TPU v7x, 32 devices: a whole 2x2x4 slice. The times are simulated.
32 devices in a mesh: terms: 8 (over y, x, core), sectors: 4 (over z).
Axes of the slice: x: 2, y: 2, z: 4, core: 2. Of those that a mesh axis runs over, the one named last changes fastest.
Arguments:
- trial: float32 [4, 128, 128], P('sectors'), may hold values from -6 to 6
- precond: float32 [4, 128, 128], P('sectors'), may hold values from 1 to 8
- block_rows: int32 [4], replicated, may hold values from 64 to 128
- owner_map: int32 [4], replicated, may hold values from 0 to 3, each once
- term_in: int32 [2048], P(('terms', 'sectors')), may hold values from 0 to 3
- term_out: int32 [2048], P(('terms', 'sectors')), may hold values from 0 to 3
- left_ops: bfloat16 [2048, 128, 128], P(('terms', 'sectors')), may hold values from -0.15462404 to 1.16462404
- right_ops: bfloat16 [2048, 128, 128], P(('terms', 'sectors')), may hold values from -0.0068334817 to 0.010778794
Outputs:
- vector: float32 [4, 128, 128], P('sectors')
- energies: float32 [3], replicated
All inputs are finite; a program needn't handle non-finite values.
Results may differ from a plain program's by a relative error of at most 0.0036.
Values may be sent and summed in bfloat16 or wider, within the bound.
No kernel may reach another device: no remote copies, remote signals or barrier semaphores. Data moves between devices by JAX's collectives and lax.ppermute only.
A program may use at most 64 MiB of HBM per device.

v0:
```python
import jax
import jax.numpy as jnp
from jax import lax
from jax.sharding import PartitionSpec as P

STEPS = 3


def on_device(trial, precond, block_rows, owner_map, term_in, term_out, left_ops, right_ops):
    sec_local = trial.shape[0]
    sec_devices = lax.axis_size("sectors")
    sector_count = sec_local * sec_devices
    rows_all = trial.shape[1]
    cols_all = trial.shape[2]
    slots = jnp.arange(sector_count, dtype=jnp.int32)
    slot_of = jnp.zeros((sector_count,), jnp.int32).at[owner_map].set(slots)
    in_slot = slot_of[term_in]
    out_slot = slot_of[term_out]
    onehot_out = (out_slot[:, None] == slots[None, :]).astype(jnp.float32)
    first_slot = lax.axis_index("sectors") * sec_local
    rows_live = lax.dynamic_slice_in_dim(block_rows, first_slot, sec_local)
    rows_index = jnp.arange(rows_all, dtype=jnp.int32)
    masking = (rows_index[None, :] < rows_live[:, None]).astype(jnp.float32)[:, :, None]
    vector = trial * masking
    entry_count = float(sector_count * rows_all * cols_all)
    energies = []
    for iteration in range(STEPS):
        gathered = lax.all_gather(vector.astype(jnp.bfloat16), "sectors", axis=0, tiled=True)
        picked = gathered[in_slot]
        halves = jnp.einsum(
            "kab,kbc->kac", left_ops, picked, preferred_element_type=jnp.float32
        ).astype(jnp.bfloat16)
        contrib = jnp.einsum("kac,kcd->kad", halves, right_ops, preferred_element_type=jnp.float32)
        partial_value = jnp.einsum(
            "ks,kad->sad",
            onehot_out,
            contrib,
            precision=lax.Precision.HIGHEST,
            preferred_element_type=jnp.float32,
        )
        summed = lax.psum(partial_value, "terms")
        sigma = lax.psum_scatter(summed, "sectors", scatter_dimension=0, tiled=True)
        sigma = sigma * masking - precond * vector
        sums_pair = lax.psum((jnp.sum(vector * sigma), jnp.sum(vector * vector)), "sectors")
        rayleigh = sums_pair[0] / sums_pair[1]
        updated = vector - (sigma - rayleigh * vector) / precond
        squared = lax.psum(jnp.sum(updated * updated), "sectors")
        vector = updated / jnp.sqrt(squared / entry_count + 1e-06)
        energies.append(rayleigh)
    return (vector, jnp.stack(energies))


def solution(mesh):
    return jax.shard_map(
        on_device,
        mesh=mesh,
        in_specs=(
            P("sectors", None, None),
            P("sectors", None, None),
            P(),
            P(),
            P(("terms", "sectors")),
            P(("terms", "sectors")),
            P(("terms", "sectors"), None, None),
            P(("terms", "sectors"), None, None),
        ),
        out_specs=(P("sectors", None, None), P()),
        check_vma=False,
    )
```

profile of v0, /device:TPU:0, one launch (start us, length us, event | category | flops | bytes accessed | tf_op | source)
XLA Modules:
  0.0 411.5 jit_solution(4209861230940832144)
XLA Ops:
  7.2 1.4 dynamic_slice.3
  8.6 0.6 compare_convert_fusion
  9.3 0.7 compare_select_fusion.3
  9.9 0.6 scatter_custom_fusion
  10.5 0.7 fusion.28
  11.2 3.2 compare_select_fusion.7
  14.4 3.2 fusion.20
  17.6 0.9 multiply_convert_fusion
  18.5 15.1 %all_gather.9 = bf16[4,128,128]{2,1,0:T(8,128)(2,1)S(1)} all-gather(bf16[1,128,128]{2,1,0:T(8,128)(2,1)S(1)} %multiply_convert_fusion), channel_id=1, replica_groups=mesh['terms'=8,'sectors'=4] {'sectors'}, dimensions={0}, use_global_device_ids=true | all-gather | bytes 163840 | tf_op jit(solution)/shard_map/all_gather | solution.py:28
  33.6 2.1 gather_fusion
  35.7 6.2 %fusion.14 = f32[64,128,128]{2,1,0:T(8,128)} fusion(bf16[64,128,128]{2,1,0:T(8,128)(2,1)S(1)} %copy-done, bf16[64,128,128]{2,1,0:T(8,128)(2,1)} %gather_fusion, bf16[64,128,128]{2,1,0:T(8,128)(2,1)} %param.14), kind=kOutput, calls=%fused_computation.16 | convolution fusion | flops 537919488 | bytes 10485760 | tf_op jit(solution)/shard_map/kac,kcd->kad/dot_general | solution.py:33
  42.0 5.8 %fusion.4 = f32[4,128,128]{2,0,1:T(4,128)S(1)} fusion(f32[64,128,128]{2,1,0:T(8,128)} %fusion.14, s32[64]{0:T(128)S(1)} %compare_select_fusion.7), kind=kOutput, calls=%fused_computation.8 | convolution fusion | flops 50331904 | bytes 4456704 | tf_op jit(solution)/shard_map/ks,kad->sad/dot_general | solution.py:34
  47.8 0.7 copy.32
  48.5 0.0 all-reduce.7.cloned.1.call-start
  48.6 21.1 %reduce-scatter.4.cloned.1.call-done = f32[1,128,128]{2,1,0:T(8,128)} async-done(((f32[4,128,128]{2,1,0:T(8,128)}), f32[1,128,128]{2,1,0:T(8,128)}) %reduce-scatter.4.cloned.1.call-update) | async-done | bytes 65552 | tf_op jit(solution)/shard_map/reduce_scatter | solution.py:42
  69.7 0.0 reduce-scatter.6.cloned.1.call-start
  69.7 54.0 %all-reduce.7.cloned.1.call-done = f32[1,128,128]{2,1,0:T(8,128)} async-done(((f32[1,128,128]{2,1,0:T(8,128)}), f32[1,128,128]{2,1,0:T(8,128)}) %all-reduce.7.cloned.1.call-update) | async-done | bytes 65552 | tf_op jit(solution)/shard_map/psum | solution.py:41
  123.7 1.5 multiply_reduce_fusion.7
  125.3 12.3 %all-reduce.2 = (f32[]{:T(128)}, f32[]{:T(128)}) all-reduce(f32[]{:T(128)} %get-tuple-element.7, f32[]{:T(128)} %get-tuple-element.6), channel_id=1, replica_groups=mesh['terms'=8,'sectors'=4] {'sectors'}, use_global_device_ids=true, to_apply=%region_4.0 | all-reduce | flops 2 | bytes 16 | tf_op jit(solution)/shard_map/psum | solution.py:44
  138.9 1.5 multiply_reduce_fusion.6
  140.5 9.0 %psum.87 = f32[]{:T(128)} all-reduce(f32[]{:T(128)} %get-tuple-element.22), channel_id=1, replica_groups=mesh['terms'=8,'sectors'=4] {'sectors'}, use_global_device_ids=true, to_apply=%region_8.0 | all-reduce | flops 1 | bytes 8 | tf_op jit(solution)/shard_map/psum | solution.py:47
  150.2 13.6 %all_gather.10 = bf16[4,128,128]{2,1,0:T(8,128)(2,1)S(1)} all-gather(bf16[1,128,128]{2,1,0:T(8,128)(2,1)S(1)} %fusion.26), channel_id=1, replica_groups=mesh['terms'=8,'sectors'=4] {'sectors'}, dimensions={0}, use_global_device_ids=true | all-gather | bytes 163840 | tf_op jit(solution)/shard_map/all_gather | solution.py:28
  163.8 2.1 gather_fusion.1
  165.9 6.2 %fusion.10 = f32[64,128,128]{2,1,0:T(8,128)} fusion(bf16[64,128,128]{2,1,0:T(8,128)(2,1)S(1)} %copy-done, bf16[64,128,128]{2,1,0:T(8,128)(2,1)} %gather_fusion.1, bf16[64,128,128]{2,1,0:T(8,128)(2,1)} %param.14), kind=kOutput, calls=%fused_computation.13 | convolution fusion | flops 537919488 | bytes 10485760 | tf_op jit(solution)/shard_map/kac,kcd->kad/dot_general | solution.py:33
  172.1 5.8 %fusion.2 = f32[4,128,128]{2,0,1:T(4,128)S(1)} fusion(f32[64,128,128]{2,1,0:T(8,128)} %fusion.10, s32[64]{0:T(128)S(1)} %compare_select_fusion.7), kind=kOutput, calls=%fused_computation.6 | convolution fusion | flops 50331904 | bytes 4456704 | tf_op jit(solution)/shard_map/ks,kad->sad/dot_general | solution.py:34
  177.9 0.7 copy.36
  178.6 0.0 all-reduce.9.cloned.1.call-start
  178.7 17.7 %reduce-scatter.6.cloned.1.call-done = f32[1,128,128]{2,1,0:T(8,128)} async-done(((f32[4,128,128]{2,1,0:T(8,128)}), f32[1,128,128]{2,1,0:T(8,128)}) %reduce-scatter.6.cloned.1.call-update) | async-done | bytes 65552 | tf_op jit(solution)/shard_map/reduce_scatter | solution.py:42
  196.4 0.0 reduce-scatter.8.cloned.1.call-start
  196.5 53.9 %all-reduce.9.cloned.1.call-done = f32[1,128,128]{2,1,0:T(8,128)} async-done(((f32[1,128,128]{2,1,0:T(8,128)}), f32[1,128,128]{2,1,0:T(8,128)}) %all-reduce.9.cloned.1.call-update) | async-done | bytes 65552 | tf_op jit(solution)/shard_map/psum | solution.py:41
  250.4 1.5 multiply_reduce_fusion.4
  251.9 12.3 %all-reduce.1 = (f32[]{:T(128)}, f32[]{:T(128)}) all-reduce(f32[]{:T(128)} %get-tuple-element.11, f32[]{:T(128)} %get-tuple-element.10), channel_id=1, replica_groups=mesh['terms'=8,'sectors'=4] {'sectors'}, use_global_device_ids=true, to_apply=%region_12.0 | all-reduce | flops 2 | bytes 16 | tf_op jit(solution)/shard_map/psum | solution.py:44
  265.5 1.5 multiply_reduce_fusion.3
  267.1 9.0 %psum.91 = f32[]{:T(128)} all-reduce(f32[]{:T(128)} %get-tuple-element.20), channel_id=1, replica_groups=mesh['terms'=8,'sectors'=4] {'sectors'}, use_global_device_ids=true, to_apply=%region_16.0 | all-reduce | flops 1 | bytes 8 | tf_op jit(solution)/shard_map/psum | solution.py:47
  276.8 13.7 %all_gather.11 = bf16[4,128,128]{2,1,0:T(8,128)(2,1)S(1)} all-gather(bf16[1,128,128]{2,1,0:T(8,128)(2,1)S(1)} %fusion.27), channel_id=1, replica_groups=mesh['terms'=8,'sectors'=4] {'sectors'}, dimensions={0}, use_global_device_ids=true | all-gather | bytes 163840 | tf_op jit(solution)/shard_map/all_gather | solution.py:28
  290.4 2.1 gather_fusion.2
  292.6 6.2 %fusion.6 = f32[64,128,128]{2,1,0:T(8,128)} fusion(bf16[64,128,128]{2,1,0:T(8,128)(2,1)S(1)} %copy-done, bf16[64,128,128]{2,1,0:T(8,128)(2,1)} %gather_fusion.2, bf16[64,128,128]{2,1,0:T(8,128)(2,1)} %param.14), kind=kOutput, calls=%fused_computation.10 | convolution fusion | flops 537919488 | bytes 10485760 | tf_op jit(solution)/shard_map/kac,kcd->kad/dot_general | solution.py:33
  298.8 5.8 %fusion = f32[4,128,128]{2,0,1:T(4,128)S(1)} fusion(f32[64,128,128]{2,1,0:T(8,128)} %fusion.6, s32[64]{0:T(128)S(1)} %compare_select_fusion.7), kind=kOutput, calls=%fused_computation.4 | convolution fusion | flops 50331904 | bytes 4456704 | tf_op jit(solution)/shard_map/ks,kad->sad/dot_general | solution.py:34
  304.6 0.7 copy.40
  305.3 0.0 all-reduce.11.cloned.1.call-start
  305.4 17.7 %reduce-scatter.8.cloned.1.call-done = f32[1,128,128]{2,1,0:T(8,128)} async-done(((f32[4,128,128]{2,1,0:T(8,128)}), f32[1,128,128]{2,1,0:T(8,128)}) %reduce-scatter.8.cloned.1.call-update) | async-done | bytes 65552 | tf_op jit(solution)/shard_map/reduce_scatter | solution.py:42
  323.1 54.0 %all-reduce.11.cloned.1.call-done = f32[1,128,128]{2,1,0:T(8,128)} async-done(((f32[1,128,128]{2,1,0:T(8,128)}), f32[1,128,128]{2,1,0:T(8,128)}) %all-reduce.11.cloned.1.call-update) | async-done | bytes 65552 | tf_op jit(solution)/shard_map/psum | solution.py:41
  377.1 1.5 multiply_reduce_fusion.1
  378.6 12.3 %all-reduce = (f32[]{:T(128)}, f32[]{:T(128)}) all-reduce(f32[]{:T(128)} %get-tuple-element.9, f32[]{:T(128)} %get-tuple-element.8), channel_id=1, replica_groups=mesh['terms'=8,'sectors'=4] {'sectors'}, use_global_device_ids=true, to_apply=%region_20.0 | all-reduce | flops 2 | bytes 16 | tf_op jit(solution)/shard_map/psum | solution.py:44
  392.2 1.5 multiply_reduce_fusion
  393.8 9.0 %psum.95 = f32[]{:T(128)} all-reduce(f32[]{:T(128)} %get-tuple-element.18), channel_id=1, replica_groups=mesh['terms'=8,'sectors'=4] {'sectors'}, use_global_device_ids=true, to_apply=%region_24.0 | all-reduce | flops 1 | bytes 8 | tf_op jit(solution)/shard_map/psum | solution.py:47
  403.4 0.6 broadcast_divide_fusion
  404.1 0.6 pad_maximum_fusion
  (17 shorter events, 0.2 us)
Async XLA Ops:
  7.2 28.6 %copy-start = (bf16[64,128,128]{2,1,0:T(8,128)(2,1)S(1)}, bf16[64,128,128]{2,1,0:T(8,128)(2,1)}, u32[]{:S(2)}) copy-start(bf16[64,128,128]{2,1,0:T(8,128)(2,1)} %param.15) | copy-start | bytes 6291460
  7.2 62.5 %reduce-scatter.4.cloned.1.call-start = ((), (), s32[]{:S(2)}) async-start(), calls=%async_computation.3 | async-start | bytes 327680 | tf_op jit(solution)/shard_map/reduce_scatter | solution.py:42
  42.0 81.8 %copy-start.1 = (f32[1,128,128]{2,1,0:T(8,128)S(1)}, f32[1,128,128]{2,1,0:T(8,128)}, u32[]{:S(2)}) copy-start(f32[1,128,128]{2,1,0:T(8,128)} %param.9) | copy-start | bytes 196612
  42.0 81.8 %copy-start.2 = (f32[1,128,128]{2,1,0:T(8,128)S(1)}, f32[1,128,128]{2,1,0:T(8,128)}, u32[]{:S(2)}) copy-start(f32[1,128,128]{2,1,0:T(8,128)} %param.8) | copy-start | bytes 196612
  48.5 75.2 %all-reduce.7.cloned.1.call-start = ((), (), s32[]{:S(2)}) async-start(), calls=%async_computation.4 | async-start | bytes 131072 | tf_op jit(solution)/shard_map/psum | solution.py:41
  69.7 126.7 %reduce-scatter.6.cloned.1.call-start = ((), (), s32[]{:S(2)}) async-start(), calls=%async_computation.5 | async-start | bytes 327680 | tf_op jit(solution)/shard_map/reduce_scatter | solution.py:42
  178.6 71.7 %all-reduce.9.cloned.1.call-start = ((), (), s32[]{:S(2)}) async-start(), calls=%async_computation.6 | async-start | bytes 131072 | tf_op jit(solution)/shard_map/psum | solution.py:41
  196.4 126.6 %reduce-scatter.8.cloned.1.call-start = ((), (), s32[]{:S(2)}) async-start(), calls=%async_computation.7 | async-start | bytes 327680 | tf_op jit(solution)/shard_map/reduce_scatter | solution.py:42
  305.3 71.8 %all-reduce.11.cloned.1.call-start = ((), (), s32[]{:S(2)}) async-start(), calls=%async_computation.8 | async-start | bytes 131072 | tf_op jit(solution)/shard_map/psum | solution.py:41
Sparse Core Ops, SparseCore 0:
  48.6 20.9 reduce-scatter.3
  73.0 50.7 all-reduce.6
  178.8 17.5 reduce-scatter.5
  199.6 50.7 all-reduce.8
  305.4 17.5 reduce-scatter.7
  326.2 50.8 all-reduce.10
where the time goes:
time: 412 us
  waiting for transfers between devices  219 us (53%)
  blocking collectives  106 us (26%)
  matrix products  36 us (9%)
  between operations  20.3 us (5%)
  other arithmetic  19.1 us (5%)
  local copies, waits for them, and re-layouts  11.2 us (3%)
    psum x3, waiting for transfers between devices, on_device(): summed = lax.psum(partial_value, 'terms')  162 us
    reduce_scatter x3, waiting for transfers between devices, on_device(): sigma = lax.psum_scatter(summed, 'sectors', scatter_dimension=0, tiled=True)  56.5 us
    all_gather x3, blocking collectives, on_device(): lax.all_gather(vector.astype(jnp.bfloat16), 'sectors', axis=0, tiled=True)  42.3 us
    psum x3, blocking collectives, on_device(): lax.psum((jnp.sum(vector * sigma), jnp.sum(vector * vector)), 'sectors')  36.9 us
    psum x3, blocking collectives, on_device(): squared = lax.psum(jnp.sum(updated * updated), 'sectors')  26.9 us
    dot_general x3, matrix products, on_device(): jnp.einsum('kac,kcd->kad', halves, right_ops, preferred_element_type=jnp....  18.7 us
    dot_general x3, matrix products, on_device(): jnp.einsum('ks,kad->sad', onehot_out, contrib, precision=lax.Precision.HI...  17.3 us
  transfers between devices with their start and end apart: 6, of which 6 were waited for; matrix products, arithmetic and copies ran while one was open for 0% of the time, Pallas kernels for 0%

commit v1 on v0

v1 whole, which is shorter than its diff:
```python
import functools
import math

import jax
import jax.numpy as jnp
from jax import lax
from jax.experimental import pallas as pl
from jax.experimental.pallas import tpu as pltpu
from jax.sharding import PartitionSpec as P

STEPS = 3
UNROLL = 16
LEFT_MAX = 1.16462404
RIGHT_MAX = 0.010778794
VMEM = pl.BlockSpec(memory_space=pltpu.VMEM)
SMEM = pl.BlockSpec(memory_space=pltpu.SMEM)
F32 = jnp.float32
BF16 = jnp.bfloat16
HALF = jnp.float16


def total(tile):
    return jnp.sum(jnp.sum(tile, axis=0, keepdims=True), axis=1, keepdims=True)


def lanes(x):
    rows, cols = x.shape
    return jnp.sum(x.reshape(rows // 8, 8, cols), axis=0)


def live(rows_ref, g, shape):
    return lax.broadcasted_iota(jnp.int32, shape, 0) < rows_ref[g]


def apply_ops(wire, square, blocks, slot, acc, refs, keep, send):
    owner, term_in, term_out, left, right = refs
    sectors, rows, cols = acc.shape
    for i in range(sectors):
        slot[owner[i]] = i
    acc[...] = jnp.zeros_like(acc)
    terms = left.shape[0]
    unroll = math.gcd(UNROLL, terms)

    def group(j, carry):
        for u in range(unroll):
            k = j * unroll + u
            half = jnp.dot(left[k], blocks[slot[term_in[k]]], preferred_element_type=F32)
            acc[slot[term_out[k]]] += jnp.dot(half.astype(BF16), right[k], preferred_element_type=F32)
        return carry

    lax.fori_loop(0, terms // unroll, group, 0)
    gain = (wire / jnp.sqrt(square / (sectors * rows * cols)))[None]
    h = sectors // 2
    low = lax.axis_index("terms") % 2
    keep[...] = acc[pl.ds(low * h, h)] * gain
    send[...] = acc[pl.ds((1 - low) * h, h)] * gain


def first_kernel(wire, mine, other, rows_live, owner, term_in, term_out, left, right,
                 vec, pre, state, keep, send, blocks, slot, acc):
    sectors, rows, cols = acc.shape
    low = lax.axis_index("terms") % 2

    def load(trial, precond):
        for g in range(sectors):
            vec[g] = jnp.where(live(rows_live, g, (rows, cols)), trial[g], 0.0)
            pre[g] = precond[g]

    @pl.when(low == 0)
    def _():
        load(mine, other)

    @pl.when(low == 1)
    def _():
        load(other, mine)

    tile = jnp.zeros((8, cols), F32)
    for g in range(sectors):
        v = vec[g]
        blocks[g] = v.astype(BF16)
        tile = tile + lanes(v * v)
    square = jnp.maximum(total(tile), 1e-30)
    state[...] = jnp.broadcast_to(square, state.shape)
    apply_ops(wire, square, blocks, slot, acc, (owner, term_in, term_out, left, right), keep, send)


def update(wire, own, far, rows_live, vec, pre, square, full, out):
    sectors, rows, cols = full.shape
    h = sectors // 2
    low = lax.axis_index("terms") % 2
    full[pl.ds(low * h, h)] = own[...]
    full[pl.ds((1 - low) * h, h)] = far[...]
    gain = jnp.sqrt(square / (sectors * rows * cols)) / wire
    tile = jnp.zeros((8, cols), F32)
    for g in range(sectors):
        v = vec[g]
        summed = jnp.where(live(rows_live, g, (rows, cols)), full[g] * gain, 0.0)
        full[g] = summed
        tile = tile + lanes(v * (summed - pre[g] * v))
    rayleigh = total(tile) / square
    tile = jnp.zeros((8, cols), F32)
    for g in range(sectors):
        v = vec[g]
        u = 2.0 * v - (full[g] - rayleigh * v) / pre[g]
        out[g] = u
        tile = tile + lanes(u * u)
    scale = 1.0 / jnp.sqrt(total(tile) / (sectors * rows * cols) + 1e-06)
    return rayleigh, scale


def middle_kernel(wire, step, own, far, vec_in, pre, state_in, rows_live, owner, term_in, term_out, left, right,
                  vec, state, keep, send, full, blocks, slot, acc):
    sectors, rows, cols = acc.shape
    old = state_in[...]
    rayleigh, scale = update(wire, own, far, rows_live, vec_in, pre, old[0:1, 0:1], full, vec)
    tile = jnp.zeros((8, cols), F32)
    for g in range(sectors):
        v = vec[g] * scale
        vec[g] = v
        blocks[g] = v.astype(BF16)
        tile = tile + lanes(v * v)
    square = jnp.maximum(total(tile), 1e-30)
    line = lax.broadcasted_iota(jnp.int32, old.shape, 0)
    state[...] = jnp.where(line == 0, square, jnp.where(line == step, rayleigh, old))
    apply_ops(wire, square, blocks, slot, acc, (owner, term_in, term_out, left, right), keep, send)


def last_kernel(wire, step, own, far, vec_in, pre, state_in, rows_live, out, energies, full, fresh):
    held = out.shape[0]
    old = state_in[...]
    rayleigh, scale = update(wire, own, far, rows_live, vec_in, pre, old[0:1, 0:1], full, fresh)
    first = lax.axis_index("sectors") * held
    out[...] = fresh[pl.ds(first, held)] * scale[None]
    line = lax.broadcasted_iota(jnp.int32, old.shape, 0)
    energies[...] = jnp.where(line == step, rayleigh, old)


def place_kernel(axis, low_bits, bits, *refs):
    parts, out = refs[:-1], refs[-1]
    size = parts[0].shape[0]
    at = (lax.axis_index(axis) >> low_bits) & ((1 << bits) - 1)
    for mask, part in enumerate(parts):
        out[pl.ds((at ^ mask) * size, size)] = part[...]


def params():
    return pltpu.CompilerParams(vmem_limit_bytes=24 << 20)


def swap(x, axis, mask):
    return lax.ppermute(x, axis, [(i, i ^ mask) for i in range(lax.axis_size(axis))])


def bit_groups(axis, first):
    count = lax.axis_size(axis).bit_length() - 1
    return [(low, min(2, count - low)) for low in range(first, count, 2)]


def sum_stage(x, axis, low, bits):
    got = [x] + [swap(x, axis, mask << low) for mask in range(1, 1 << bits)]
    got = [g.astype(F32) for g in got]
    while len(got) > 1:
        got = [got[i] + got[i + 1] for i in range(0, len(got), 2)]
    return got[0]


def reduce_half(keep, send):
    x = keep + swap(send, "terms", 1)
    for axis, first in (("sectors", 0), ("terms", 1)):
        for low, bits in bit_groups(axis, first):
            x = sum_stage(lax.optimization_barrier(x.astype(HALF)), axis, low, bits)
    return x


def gather(x):
    for low, bits in bit_groups("sectors", 0):
        parts = [x] + [swap(x, "sectors", mask << low) for mask in range(1, 1 << bits)]
        x = pl.pallas_call(
            functools.partial(place_kernel, "sectors", low, bits),
            out_shape=jax.ShapeDtypeStruct((x.shape[0] << bits, *x.shape[1:]), x.dtype),
            in_specs=[VMEM] * len(parts),
            out_specs=VMEM,
        )(*parts)
    return x


def on_device(trial, precond, block_rows, owner_map, term_in, term_out, left_ops, right_ops):
    sec_local, rows, cols = trial.shape
    sectors = sec_local * lax.axis_size("sectors")
    terms = left_ops.shape[0] * lax.axis_size("sectors") * lax.axis_size("terms")
    bound = 1.02 * LEFT_MAX * RIGHT_MAX * math.sqrt(rows * cols) * math.sqrt(sectors * rows * cols) * terms
    wire = 2.0 ** -max(0, math.ceil(math.log2(bound / 65504.0)))
    whole = jax.ShapeDtypeStruct((sectors, rows, cols), F32)
    part = jax.ShapeDtypeStruct((sectors // 2, rows, cols), F32)
    state_shape = jax.ShapeDtypeStruct((8, cols), F32)
    full = pltpu.VMEM((sectors, rows, cols), F32)
    scratch = [pltpu.VMEM((sectors, rows, cols), BF16), pltpu.SMEM((sectors,), jnp.int32), full]
    ints = (block_rows, owner_map, term_in, term_out)

    mine = gather(jnp.where(lax.axis_index("terms") % 2 == 0, trial, precond))
    other = swap(mine, "terms", 1)
    vec, pre, state, keep, send = pl.pallas_call(
        functools.partial(first_kernel, wire),
        out_shape=(whole, whole, state_shape, part, part),
        in_specs=[VMEM] * 2 + [SMEM] * 4 + [VMEM] * 2,
        out_specs=(VMEM,) * 5,
        scratch_shapes=scratch,
        compiler_params=params(),
    )(mine, other, *ints, left_ops, right_ops)
    for step in range(1, STEPS):
        own = reduce_half(keep, send)
        far = swap(own, "terms", 1)
        vec, state, keep, send = pl.pallas_call(
            functools.partial(middle_kernel, wire, step),
            out_shape=(whole, state_shape, part, part),
            in_specs=[VMEM] * 5 + [SMEM] * 4 + [VMEM] * 2,
            out_specs=(VMEM,) * 4,
            scratch_shapes=[full] + scratch,
            compiler_params=params(),
        )(own, far, vec, pre, state, *ints, left_ops, right_ops)
    own = reduce_half(keep, send)
    far = swap(own, "terms", 1)
    vector, energies = pl.pallas_call(
        functools.partial(last_kernel, wire, STEPS),
        out_shape=(jax.ShapeDtypeStruct(trial.shape, F32), state_shape),
        in_specs=[VMEM] * 5 + [SMEM],
        out_specs=(VMEM,) * 2,
        scratch_shapes=[full, full],
        compiler_params=params(),
    )(own, far, vec, pre, state, block_rows)
    return vector, energies[1 : STEPS + 1, 0]


def solution(mesh):
    return jax.shard_map(
        on_device,
        mesh=mesh,
        in_specs=(
            P("sectors", None, None),
            P("sectors", None, None),
            P(),
            P(),
            P(("terms", "sectors")),
            P(("terms", "sectors")),
            P(("terms", "sectors"), None, None),
            P(("terms", "sectors"), None, None),
        ),
        out_specs=(P("sectors", None, None), P()),
        check_vma=False,
    )
```

time: 412 us -> 91.8 us (0.22)
  waiting for transfers between devices: 219 us -> 37.7 us
  blocking collectives: 106 us -> 0 us
  matrix products: 36 us -> 0 us
  starting transfers between devices: 0.24 us -> 30.6 us
  between operations: 20.3 us -> 0.78 us
  other arithmetic: 19.1 us -> 1.14 us
  Pallas kernels: 0 us -> 12.6 us
    psum x3 -> x0, waiting for transfers between devices: 162 us -> none  [on_device(): summed = lax.psum(partial_value, 'terms')]
    psum x6 -> x0, blocking collectives: 63.8 us -> none  [the longest x3 36.9 us: on_device(): lax.psum((jnp.sum(vector * sigma), jnp.sum(vector * vector)), 'sectors')]
    reduce_scatter x3 -> x0, waiting for transfers between devices: 56.5 us -> none  [on_device(): sigma = lax.psum_scatter(summed, 'sectors', scatter_dimension=0, tiled=True)]
    all_gather x3 -> x0, blocking collectives: 42.3 us -> none  [on_device(): lax.all_gather(vector.astype(jnp.bfloat16), 'sectors', axis=0, tiled=True)]
    ppermute x0 -> x28, waiting for transfers between devices: none -> 37.7 us  [swap(): lax.ppermute(x, axis, [(i, i ^ mask) for i in range(lax.axis_size(axis))])]
    dot_general x6 -> x0, matrix products: 36 us -> none  [the longest x3 18.7 us: on_device(): jnp.einsum('kac,kcd->kad', halves, right_ops, preferred_element_type=jnp....]
    ppermute x0 -> x28, starting transfers between devices: none -> 30.6 us  [swap(): lax.ppermute(x, axis, [(i, i ^ mask) for i in range(lax.axis_size(axis))])]
    pallas_call x0 -> x5, Pallas kernels: none -> 12.6 us  [the longest x2 6.47 us: on_device(): pl.pallas_call(functools.partial(middle_kernel, wire, step), out_shape=(w...]
  transfers between devices with their start and end apart: 6 -> 28, of which waited for: 6 -> 24; matrix products, arithmetic and copies ran while one was open for 0% -> 0% of each run, Pallas kernels for 0% -> 0%
where the time goes in v1:
time: 91.8 us; the launch traced here: 91.5 us
  waiting for transfers between devices  37.7 us (41%)
  starting transfers between devices  30.6 us (33%)
  Pallas kernels  12.6 us (14%)
  local copies, waits for them, and re-layouts  8.63 us (9%)
  other arithmetic  1.14 us (1%)
    ppermute x28, waiting for transfers between devices, swap(): lax.ppermute(x, axis, [(i, i ^ mask) for i in range(lax.axis_size(axis))])  37.7 us
    ppermute x28, starting transfers between devices, swap(): lax.ppermute(x, axis, [(i, i ^ mask) for i in range(lax.axis_size(axis))])  30.6 us
    unnamed x26, local copies, waits for them, and re-layouts  8 us
    pallas_call x2, Pallas kernels, on_device(): pl.pallas_call(functools.partial(middle_kernel, wire, step), out_shape=(w...  6.47 us
    pallas_call x1, Pallas kernels, on_device(): pl.pallas_call(functools.partial(first_kernel, wire), out_shape=(whole, w...  2.87 us
  transfers between devices with their start and end apart: 28, of which 24 were waited for; matrix products, arithmetic and copies ran while one was open for 0% of the time, Pallas kernels for 0%

profile of v1, /device:TPU:0, one launch (start us, length us, event | category | flops | bytes accessed | tf_op | source)
XLA Modules:
  0.0 91.5 jit_solution(5425687727645622876)
XLA Ops:
  0.6 0.9 broadcast_select_fusion.refs_0_
  1.5 5.1 %collective-permute-start.2 = (f32[1,128,128]{2,1,0:T(8,128)S(1)}, f32[1,128,128]{2,1,0:T(8,128)S(1)}, u32[]{:S(2)}, u32[]{:S(2)}) collective-permute-start(f32[1,128,128]{2,1,0:T(8,128)S(1)} %broadcast_select_fusion.refs_0_), channel_id=1, source_target_pairs={{0,3},{1,2},{2,1},{3,0},{4,7},{5,6},{6,5},{7,4},{8,11},{9,10},{10,... | collective-permute-start | bytes 196616 | tf_op jit(solution)/shard_map/ppermute | solution.py:151
  6.6 0.6 collective-permute-start
  7.3 1.9 %collective-permute-done.2.refs_3_ = f32[1,128,128]{2,1,0:T(8,128)S(1)} collective-permute-done((f32[1,128,128]{2,1,0:T(8,128)S(1)}, f32[1,128,128]{2,1,0:T(8,128)S(1)}, u32[]{:S(2)}, u32[]{:S(2)}) %collective-permute-start.2) | collective-permute-done | bytes 65568 | tf_op jit(solution)/shard_map/ppermute | solution.py:151
  9.2 3.0 %collective-permute-done.1.refs_2_ = f32[1,128,128]{2,1,0:T(8,128)S(1)} collective-permute-done((f32[1,128,128]{2,1,0:T(8,128)S(1)}, f32[1,128,128]{2,1,0:T(8,128)S(1)}, u32[]{:S(2)}, u32[]{:S(2)}) %collective-permute-start.1) | collective-permute-done | bytes 65568 | tf_op jit(solution)/shard_map/ppermute | solution.py:151
  12.9 0.6 copy-done.12
  13.5 1.7 %shard_map.95.mine = f32[4,128,128]{2,1,0:T(8,128)} custom-call(f32[1,128,128]{2,1,0:T(8,128)} %copy-done.9, f32[1,128,128]{2,1,0:T(8,128)} %copy-done.12, f32[1,128,128]{2,1,0:T(8,128)} %copy-done.11, f32[1,128,128]{2,1,0:T(8,128)} %copy-done.10), custom_call_target="tpu_custom_call" | custom-call | tf_op jit(solution)/shard_map/pallas_call | solution.py:178
  15.1 1.7 %collective-permute-done.3.other = f32[4,128,128]{2,1,0:T(8,128)S(1)} collective-permute-done((f32[4,128,128]{2,1,0:T(8,128)}, f32[4,128,128]{2,1,0:T(8,128)S(1)}, u32[]{:S(2)}, u32[]{:S(2)}) %collective-permute-start.3) | collective-permute-done | bytes 262176 | tf_op jit(solution)/shard_map/ppermute | solution.py:151
  16.9 1.6 %copy-done = bf16[64,128,128]{2,1,0:T(8,128)(2,1)S(1)} copy-done((bf16[64,128,128]{2,1,0:T(8,128)(2,1)S(1)}, bf16[64,128,128]{2,1,0:T(8,128)(2,1)}, u32[]{:S(2)}) %copy-start) | copy-done | bytes 2097176
  18.5 1.6 %copy-done.2 = bf16[64,128,128]{2,1,0:T(8,128)(2,1)S(1)} copy-done((bf16[64,128,128]{2,1,0:T(8,128)(2,1)S(1)}, bf16[64,128,128]{2,1,0:T(8,128)(2,1)}, u32[]{:S(2)}) %copy-start.2) | copy-done | bytes 2097176
  20.1 0.9 %copy-done.4 = f32[4,128,128]{2,1,0:T(8,128)S(1)} copy-done((f32[4,128,128]{2,1,0:T(8,128)S(1)}, f32[4,128,128]{2,1,0:T(8,128)}, u32[]{:S(2)}) %copy-start.4) | copy-done | bytes 262168
  21.0 0.7 copy-done.5
  21.7 0.7 copy-done.6
  22.3 0.7 copy-done.7
  23.0 0.7 copy-done.8
  23.7 2.9 %shard_map.96 = (f32[4,128,128]{2,1,0:T(8,128)S(1)}, f32[4,128,128]{2,1,0:T(8,128)S(1)}, f32[8,128]{1,0:T(8,128)S(1)}, f32[2,128,128]{2,1,0:T(8,128)S(1)}, f32[2,128,128]{2,1,0:T(8,128)S(1)}) custom-call(f32[4,128,128]{2,1,0:T(8,128)S(1)} %copy-done.4, f32[4,128,128]{2,1,0:T(8,128)S(1)} %collective-permute-done.3.other, s32[4]{0:T(128)S(1)} %copy-done.5, ...), custom_call_target="tpu_custom_call" | custom-call | tf_op jit(solution)/shard_map/pallas_call | solution.py:202
  26.7 1.2 %collective-permute-done.4 = f32[2,128,128]{2,1,0:T(8,128)S(1)} collective-permute-done((f32[2,128,128]{2,1,0:T(8,128)S(1)}, f32[2,128,128]{2,1,0:T(8,128)S(1)}, u32[]{:S(2)}, u32[]{:S(2)}) %collective-permute-start.4) | collective-permute-done | bytes 131104 | tf_op jit(solution)/shard_map/ppermute | solution.py:151
  28.0 2.8 %collective-permute-start.7 = (f16[2,128,128]{2,1,0:T(8,128)(2,1)S(1)}, f16[2,128,128]{2,1,0:T(8,128)(2,1)S(1)}, u32[]{:S(2)}, u32[]{:S(2)}) collective-permute-start(f16[2,128,128]{2,1,0:T(8,128)(2,1)S(1)} %add_convert_fusion.5), channel_id=1, source_target_pairs={{0,3},{1,2},{2,1},{3,0},{4,7},{5,6},{6,5},{7,4},{8,11},{9,10},{10,... | collective-permute-start | bytes 196616 | tf_op jit(solution)/shard_map/ppermute | solution.py:151
  30.7 1.7 %collective-permute-start.5 = (f16[2,128,128]{2,1,0:T(8,128)(2,1)S(1)}, f16[2,128,128]{2,1,0:T(8,128)(2,1)S(1)}, u32[]{:S(2)}, u32[]{:S(2)}) collective-permute-start(f16[2,128,128]{2,1,0:T(8,128)(2,1)S(1)} %add_convert_fusion.5), channel_id=1, source_target_pairs={{0,1},{1,0},{2,3},{3,2},{4,5},{5,4},{6,7},{7,6},{8,9},{9,8},{10,11... | collective-permute-start | bytes 196616 | tf_op jit(solution)/shard_map/ppermute | solution.py:151
  32.4 2.3 %collective-permute-done.7 = f16[2,128,128]{2,1,0:T(8,128)(2,1)S(1)} collective-permute-done((f16[2,128,128]{2,1,0:T(8,128)(2,1)S(1)}, f16[2,128,128]{2,1,0:T(8,128)(2,1)S(1)}, u32[]{:S(2)}, u32[]{:S(2)}) %collective-permute-start.7) | collective-permute-done | bytes 65568 | tf_op jit(solution)/shard_map/ppermute | solution.py:151
  34.7 2.0 %collective-permute-done.6 = f16[2,128,128]{2,1,0:T(8,128)(2,1)S(1)} collective-permute-done((f16[2,128,128]{2,1,0:T(8,128)(2,1)S(1)}, f16[2,128,128]{2,1,0:T(8,128)(2,1)S(1)}, u32[]{:S(2)}, u32[]{:S(2)}) %collective-permute-start.6) | collective-permute-done | bytes 65568 | tf_op jit(solution)/shard_map/ppermute | solution.py:151
  36.8 2.5 %collective-permute-start.10 = (f16[2,128,128]{2,1,0:T(8,128)(2,1)S(1)}, f16[2,128,128]{2,1,0:T(8,128)(2,1)S(1)}, u32[]{:S(2)}, u32[]{:S(2)}) collective-permute-start(f16[2,128,128]{2,1,0:T(8,128)(2,1)S(1)} %add_convert_fusion.4), channel_id=1, source_target_pairs={{0,24},{4,28},{8,16},{12,20},{16,8},{20,12},{24,0},{28,4},{1,25},{... | collective-permute-start | bytes 196616 | tf_op jit(solution)/shard_map/ppermute | solution.py:151
  40.4 1.7 %collective-permute-done.10 = f16[2,128,128]{2,1,0:T(8,128)(2,1)S(1)} collective-permute-done((f16[2,128,128]{2,1,0:T(8,128)(2,1)S(1)}, f16[2,128,128]{2,1,0:T(8,128)(2,1)S(1)}, u32[]{:S(2)}, u32[]{:S(2)}) %collective-permute-start.10) | collective-permute-done | bytes 65568 | tf_op jit(solution)/shard_map/ppermute | solution.py:151
  42.1 1.5 %collective-permute-done.9 = f16[2,128,128]{2,1,0:T(8,128)(2,1)S(1)} collective-permute-done((f16[2,128,128]{2,1,0:T(8,128)(2,1)S(1)}, f16[2,128,128]{2,1,0:T(8,128)(2,1)S(1)}, u32[]{:S(2)}, u32[]{:S(2)}) %collective-permute-start.9) | collective-permute-done | bytes 65568 | tf_op jit(solution)/shard_map/ppermute | solution.py:151
  44.2 1.3 %collective-permute-done.11.far = f32[2,128,128]{2,1,0:T(8,128)S(1)} collective-permute-done((f32[2,128,128]{2,1,0:T(8,128)S(1)}, f32[2,128,128]{2,1,0:T(8,128)S(1)}, u32[]{:S(2)}, u32[]{:S(2)}) %collective-permute-start.11) | collective-permute-done | bytes 131104 | tf_op jit(solution)/shard_map/ppermute | solution.py:151
  45.6 3.2 %shard_map.97 = (f32[4,128,128]{2,1,0:T(8,128)S(1)}, f32[8,128]{1,0:T(8,128)S(1)}, f32[2,128,128]{2,1,0:T(8,128)S(1)}, f32[2,128,128]{2,1,0:T(8,128)S(1)}) custom-call(f32[2,128,128]{2,1,0:T(8,128)S(1)} %add_add_fusion.2.own, f32[2,128,128]{2,1,0:T(8,128)S(1)} %collective-permute-done.11.far, f32[4,128,128]{2,1,0:T(8,128)S(1)} %get-tuple-element.19.vec_in, ...), custom_call_target="tpu_custom_call" | custom-call | tf_op jit(solution)/shard_map/pallas_call | solution.py:213
  49.0 1.2 %collective-permute-done.12 = f32[2,128,128]{2,1,0:T(8,128)S(1)} collective-permute-done((f32[2,128,128]{2,1,0:T(8,128)S(1)}, f32[2,128,128]{2,1,0:T(8,128)S(1)}, u32[]{:S(2)}, u32[]{:S(2)}) %collective-permute-start.12) | collective-permute-done | bytes 131104 | tf_op jit(solution)/shard_map/ppermute | solution.py:151
  50.2 2.7 %collective-permute-start.15 = (f16[2,128,128]{2,1,0:T(8,128)(2,1)S(1)}, f16[2,128,128]{2,1,0:T(8,128)(2,1)S(1)}, u32[]{:S(2)}, u32[]{:S(2)}) collective-permute-start(f16[2,128,128]{2,1,0:T(8,128)(2,1)S(1)} %add_convert_fusion.3), channel_id=1, source_target_pairs={{0,3},{1,2},{2,1},{3,0},{4,7},{5,6},{6,5},{7,4},{8,11},{9,10},{10,... | collective-permute-start | bytes 196616 | tf_op jit(solution)/shard_map/ppermute | solution.py:151
  53.0 1.7 %collective-permute-start.13 = (f16[2,128,128]{2,1,0:T(8,128)(2,1)S(1)}, f16[2,128,128]{2,1,0:T(8,128)(2,1)S(1)}, u32[]{:S(2)}, u32[]{:S(2)}) collective-permute-start(f16[2,128,128]{2,1,0:T(8,128)(2,1)S(1)} %add_convert_fusion.3), channel_id=1, source_target_pairs={{0,1},{1,0},{2,3},{3,2},{4,5},{5,4},{6,7},{7,6},{8,9},{9,8},{10,11... | collective-permute-start | bytes 196616 | tf_op jit(solution)/shard_map/ppermute | solution.py:151
  54.7 2.4 %collective-permute-done.15 = f16[2,128,128]{2,1,0:T(8,128)(2,1)S(1)} collective-permute-done((f16[2,128,128]{2,1,0:T(8,128)(2,1)S(1)}, f16[2,128,128]{2,1,0:T(8,128)(2,1)S(1)}, u32[]{:S(2)}, u32[]{:S(2)}) %collective-permute-start.15) | collective-permute-done | bytes 65568 | tf_op jit(solution)/shard_map/ppermute | solution.py:151
  57.1 2.1 %collective-permute-done.14 = f16[2,128,128]{2,1,0:T(8,128)(2,1)S(1)} collective-permute-done((f16[2,128,128]{2,1,0:T(8,128)(2,1)S(1)}, f16[2,128,128]{2,1,0:T(8,128)(2,1)S(1)}, u32[]{:S(2)}, u32[]{:S(2)}) %collective-permute-start.14) | collective-permute-done | bytes 65568 | tf_op jit(solution)/shard_map/ppermute | solution.py:151
  59.2 1.6 %collective-permute-start.18 = (f16[2,128,128]{2,1,0:T(8,128)(2,1)S(1)}, f16[2,128,128]{2,1,0:T(8,128)(2,1)S(1)}, u32[]{:S(2)}, u32[]{:S(2)}) collective-permute-start(f16[2,128,128]{2,1,0:T(8,128)(2,1)S(1)} %add_convert_fusion.2), channel_id=1, source_target_pairs={{0,24},{4,28},{8,16},{12,20},{16,8},{20,12},{24,0},{28,4},{1,25},{... | collective-permute-start | bytes 196616 | tf_op jit(solution)/shard_map/ppermute | solution.py:151
  61.3 1.4 %collective-permute-start.16 = (f16[2,128,128]{2,1,0:T(8,128)(2,1)S(1)}, f16[2,128,128]{2,1,0:T(8,128)(2,1)S(1)}, u32[]{:S(2)}, u32[]{:S(2)}) collective-permute-start(f16[2,128,128]{2,1,0:T(8,128)(2,1)S(1)} %add_convert_fusion.2), channel_id=1, source_target_pairs={{0,8},{4,12},{8,0},{12,4},{16,24},{20,28},{24,16},{28,20},{1,9},{5... | collective-permute-start | bytes 196616 | tf_op jit(solution)/shard_map/ppermute | solution.py:151
  62.7 1.8 %collective-permute-done.18 = f16[2,128,128]{2,1,0:T(8,128)(2,1)S(1)} collective-permute-done((f16[2,128,128]{2,1,0:T(8,128)(2,1)S(1)}, f16[2,128,128]{2,1,0:T(8,128)(2,1)S(1)}, u32[]{:S(2)}, u32[]{:S(2)}) %collective-permute-start.18) | collective-permute-done | bytes 65568 | tf_op jit(solution)/shard_map/ppermute | solution.py:151
  64.5 1.1 %collective-permute-done.17 = f16[2,128,128]{2,1,0:T(8,128)(2,1)S(1)} collective-permute-done((f16[2,128,128]{2,1,0:T(8,128)(2,1)S(1)}, f16[2,128,128]{2,1,0:T(8,128)(2,1)S(1)}, u32[]{:S(2)}, u32[]{:S(2)}) %collective-permute-start.17) | collective-permute-done | bytes 65568 | tf_op jit(solution)/shard_map/ppermute | solution.py:151
  65.8 1.3 %collective-permute-done.19.far = f32[2,128,128]{2,1,0:T(8,128)S(1)} collective-permute-done((f32[2,128,128]{2,1,0:T(8,128)S(1)}, f32[2,128,128]{2,1,0:T(8,128)S(1)}, u32[]{:S(2)}, u32[]{:S(2)}) %collective-permute-start.19) | collective-permute-done | bytes 131104 | tf_op jit(solution)/shard_map/ppermute | solution.py:151
  67.2 3.2 %shard_map.98 = (f32[4,128,128]{2,1,0:T(8,128)S(1)}, f32[8,128]{1,0:T(8,128)S(1)}, f32[2,128,128]{2,1,0:T(8,128)S(1)}, f32[2,128,128]{2,1,0:T(8,128)S(1)}) custom-call(f32[2,128,128]{2,1,0:T(8,128)S(1)} %add_add_fusion.1.own, f32[2,128,128]{2,1,0:T(8,128)S(1)} %collective-permute-done.19.far, f32[4,128,128]{2,1,0:T(8,128)S(1)} %get-tuple-element.24.vec_in, ...), custom_call_target="tpu_custom_call" | custom-call | tf_op jit(solution)/shard_map/pallas_call | solution.py:213
  70.6 1.2 %collective-permute-done.20 = f32[2,128,128]{2,1,0:T(8,128)S(1)} collective-permute-done((f32[2,128,128]{2,1,0:T(8,128)S(1)}, f32[2,128,128]{2,1,0:T(8,128)S(1)}, u32[]{:S(2)}, u32[]{:S(2)}) %collective-permute-start.20) | collective-permute-done | bytes 131104 | tf_op jit(solution)/shard_map/ppermute | solution.py:151
  71.9 2.5 %collective-permute-start.23 = (f16[2,128,128]{2,1,0:T(8,128)(2,1)S(1)}, f16[2,128,128]{2,1,0:T(8,128)(2,1)S(1)}, u32[]{:S(2)}, u32[]{:S(2)}) collective-permute-start(f16[2,128,128]{2,1,0:T(8,128)(2,1)S(1)} %add_convert_fusion.1), channel_id=1, source_target_pairs={{0,3},{1,2},{2,1},{3,0},{4,7},{5,6},{6,5},{7,4},{8,11},{9,10},{10,... | collective-permute-start | bytes 196616 | tf_op jit(solution)/shard_map/ppermute | solution.py:151
  74.4 1.9 %collective-permute-start.21 = (f16[2,128,128]{2,1,0:T(8,128)(2,1)S(1)}, f16[2,128,128]{2,1,0:T(8,128)(2,1)S(1)}, u32[]{:S(2)}, u32[]{:S(2)}) collective-permute-start(f16[2,128,128]{2,1,0:T(8,128)(2,1)S(1)} %add_convert_fusion.1), channel_id=1, source_target_pairs={{0,1},{1,0},{2,3},{3,2},{4,5},{5,4},{6,7},{7,6},{8,9},{9,8},{10,11... | collective-permute-start | bytes 196616 | tf_op jit(solution)/shard_map/ppermute | solution.py:151
  76.3 2.4 %collective-permute-done.23 = f16[2,128,128]{2,1,0:T(8,128)(2,1)S(1)} collective-permute-done((f16[2,128,128]{2,1,0:T(8,128)(2,1)S(1)}, f16[2,128,128]{2,1,0:T(8,128)(2,1)S(1)}, u32[]{:S(2)}, u32[]{:S(2)}) %collective-permute-start.23) | collective-permute-done | bytes 65568 | tf_op jit(solution)/shard_map/ppermute | solution.py:151
  78.7 2.0 %collective-permute-done.22 = f16[2,128,128]{2,1,0:T(8,128)(2,1)S(1)} collective-permute-done((f16[2,128,128]{2,1,0:T(8,128)(2,1)S(1)}, f16[2,128,128]{2,1,0:T(8,128)(2,1)S(1)}, u32[]{:S(2)}, u32[]{:S(2)}) %collective-permute-start.22) | collective-permute-done | bytes 65568 | tf_op jit(solution)/shard_map/ppermute | solution.py:151
  80.7 2.3 %collective-permute-start.26 = (f16[2,128,128]{2,1,0:T(8,128)(2,1)S(1)}, f16[2,128,128]{2,1,0:T(8,128)(2,1)S(1)}, u32[]{:S(2)}, u32[]{:S(2)}) collective-permute-start(f16[2,128,128]{2,1,0:T(8,128)(2,1)S(1)} %add_convert_fusion), channel_id=1, source_target_pairs={{0,24},{4,28},{8,16},{12,20},{16,8},{20,12},{24,0},{28,4},{1,25},{... | collective-permute-start | bytes 196616 | tf_op jit(solution)/shard_map/ppermute | solution.py:151
  83.5 0.7 collective-permute-start.24
  84.3 1.7 %collective-permute-done.26 = f16[2,128,128]{2,1,0:T(8,128)(2,1)S(1)} collective-permute-done((f16[2,128,128]{2,1,0:T(8,128)(2,1)S(1)}, f16[2,128,128]{2,1,0:T(8,128)(2,1)S(1)}, u32[]{:S(2)}, u32[]{:S(2)}) %collective-permute-start.26) | collective-permute-done | bytes 65568 | tf_op jit(solution)/shard_map/ppermute | solution.py:151
  86.0 1.3 %collective-permute-done.25 = f16[2,128,128]{2,1,0:T(8,128)(2,1)S(1)} collective-permute-done((f16[2,128,128]{2,1,0:T(8,128)(2,1)S(1)}, f16[2,128,128]{2,1,0:T(8,128)(2,1)S(1)}, u32[]{:S(2)}, u32[]{:S(2)}) %collective-permute-start.25) | collective-permute-done | bytes 65568 | tf_op jit(solution)/shard_map/ppermute | solution.py:151
  87.9 1.3 %collective-permute-done.27.far = f32[2,128,128]{2,1,0:T(8,128)S(1)} collective-permute-done((f32[2,128,128]{2,1,0:T(8,128)S(1)}, f32[2,128,128]{2,1,0:T(8,128)S(1)}, u32[]{:S(2)}, u32[]{:S(2)}) %collective-permute-start.27) | collective-permute-done | bytes 131104 | tf_op jit(solution)/shard_map/ppermute | solution.py:151
  89.3 1.6 %shard_map.99 = (f32[1,128,128]{2,1,0:T(8,128)}, f32[8,128]{1,0:T(8,128)S(1)}) custom-call(f32[2,128,128]{2,1,0:T(8,128)S(1)} %add_add_fusion.own, f32[2,128,128]{2,1,0:T(8,128)S(1)} %collective-permute-done.27.far, f32[4,128,128]{2,1,0:T(8,128)S(1)} %get-tuple-element.28.vec_in, f32[4,128,128]{2,1,0:T(8,128)S(1)} %get-tuple-element.20.pre, ...), custom_call_target="tpu_custom_call" | custom-call | tf_op jit(solution)/shard_map/pallas_call | solution.py:223
  (50 shorter events, 5.5 us)
Async XLA Ops:
  1.5 10.7 %copy-start.9 = (f32[1,128,128]{2,1,0:T(8,128)}, f32[1,128,128]{2,1,0:T(8,128)S(1)}, u32[]{:S(2)}) copy-start(f32[1,128,128]{2,1,0:T(8,128)S(1)} %broadcast_select_fusion.refs_0_) | copy-start | bytes 196612
  1.5 7.7 %collective-permute-start.2 = (f32[1,128,128]{2,1,0:T(8,128)S(1)}, f32[1,128,128]{2,1,0:T(8,128)S(1)}, u32[]{:S(2)}, u32[]{:S(2)}) collective-permute-start(f32[1,128,128]{2,1,0:T(8,128)S(1)} %broadcast_select_fusion.refs_0_), channel_id=1, source_target_pairs={{0,3},{1,2},{2,1},{3,0},{4,7},{5,6},{6,5},{7,4},{8,11},{9,10},{10,... | collective-permute-start | bytes 196616 | tf_op jit(solution)/shard_map/ppermute | solution.py:151
  6.6 5.6 %collective-permute-start.1 = (f32[1,128,128]{2,1,0:T(8,128)S(1)}, f32[1,128,128]{2,1,0:T(8,128)S(1)}, u32[]{:S(2)}, u32[]{:S(2)}) collective-permute-start(f32[1,128,128]{2,1,0:T(8,128)S(1)} %broadcast_select_fusion.refs_0_), channel_id=1, source_target_pairs={{0,2},{1,3},{2,0},{3,1},{4,6},{5,7},{6,4},{7,5},{8,10},{9,11},{10,... | collective-permute-start | bytes 196616 | tf_op jit(solution)/shard_map/ppermute | solution.py:151
  6.6 5.6 %collective-permute-start = (f32[1,128,128]{2,1,0:T(8,128)S(1)}, f32[1,128,128]{2,1,0:T(8,128)S(1)}, u32[]{:S(2)}, u32[]{:S(2)}) collective-permute-start(f32[1,128,128]{2,1,0:T(8,128)S(1)} %broadcast_select_fusion.refs_0_), channel_id=1, source_target_pairs={{0,1},{1,0},{2,3},{3,2},{4,5},{5,4},{6,7},{7,6},{8,9},{9,8},{10,11... | collective-permute-start | bytes 196616 | tf_op jit(solution)/shard_map/ppermute | solution.py:151
  9.2 3.0 %copy-start.10 = (f32[1,128,128]{2,1,0:T(8,128)}, f32[1,128,128]{2,1,0:T(8,128)S(1)}, u32[]{:S(2)}) copy-start(f32[1,128,128]{2,1,0:T(8,128)S(1)} %collective-permute-done.2.refs_3_) | copy-start | bytes 196612
  12.2 0.6 copy-start.11
  12.9 0.6 copy-start.12
  15.1 1.7 %collective-permute-start.3 = (f32[4,128,128]{2,1,0:T(8,128)}, f32[4,128,128]{2,1,0:T(8,128)S(1)}, u32[]{:S(2)}, u32[]{:S(2)}) collective-permute-start(f32[4,128,128]{2,1,0:T(8,128)} %shard_map.95.mine), channel_id=1, source_target_pairs={{0,4},{4,0},{8,12},{12,8},{16,20},{20,16},{24,28},{28,24},{1,5},{5... | collective-permute-start | bytes 786440 | tf_op jit(solution)/shard_map/ppermute | solution.py:151
  16.9 1.6 %copy-start = (bf16[64,128,128]{2,1,0:T(8,128)(2,1)S(1)}, bf16[64,128,128]{2,1,0:T(8,128)(2,1)}, u32[]{:S(2)}) copy-start(bf16[64,128,128]{2,1,0:T(8,128)(2,1)} %left.5) | copy-start | bytes 6291460
  18.5 1.6 %copy-start.2 = (bf16[64,128,128]{2,1,0:T(8,128)(2,1)S(1)}, bf16[64,128,128]{2,1,0:T(8,128)(2,1)}, u32[]{:S(2)}) copy-start(bf16[64,128,128]{2,1,0:T(8,128)(2,1)} %right.5) | copy-start | bytes 6291460
  20.1 0.9 %copy-start.4 = (f32[4,128,128]{2,1,0:T(8,128)S(1)}, f32[4,128,128]{2,1,0:T(8,128)}, u32[]{:S(2)}) copy-start(f32[4,128,128]{2,1,0:T(8,128)} %shard_map.95.mine) | copy-start | bytes 786436
  21.0 0.7 copy-start.5
  21.7 0.7 copy-start.6
  22.3 0.7 copy-start.7
  23.0 0.7 copy-start.8
  23.6 21.9 %copy-start.1 = (bf16[64,128,128]{2,1,0:T(8,128)(2,1)S(1)}, bf16[64,128,128]{2,1,0:T(8,128)(2,1)}, u32[]{:S(2)}) copy-start(bf16[64,128,128]{2,1,0:T(8,128)(2,1)} %left.5) | copy-start | bytes 6291460
  23.6 21.9 %copy-start.3 = (bf16[64,128,128]{2,1,0:T(8,128)(2,1)S(1)}, bf16[64,128,128]{2,1,0:T(8,128)(2,1)}, u32[]{:S(2)}) copy-start(bf16[64,128,128]{2,1,0:T(8,128)(2,1)} %right.5) | copy-start | bytes 6291460
  26.5 1.4 %collective-permute-start.4 = (f32[2,128,128]{2,1,0:T(8,128)S(1)}, f32[2,128,128]{2,1,0:T(8,128)S(1)}, u32[]{:S(2)}, u32[]{:S(2)}) collective-permute-start(f32[2,128,128]{2,1,0:T(8,128)S(1)} %get-tuple-element.18), channel_id=1, source_target_pairs={{0,4},{4,0},{8,12},{12,8},{16,20},{20,16},{24,28},{28,24},{1,5},{5... | collective-permute-start | bytes 393224 | tf_op jit(solution)/shard_map/ppermute | solution.py:151
  28.0 6.8 %collective-permute-start.7 = (f16[2,128,128]{2,1,0:T(8,128)(2,1)S(1)}, f16[2,128,128]{2,1,0:T(8,128)(2,1)S(1)}, u32[]{:S(2)}, u32[]{:S(2)}) collective-permute-start(f16[2,128,128]{2,1,0:T(8,128)(2,1)S(1)} %add_convert_fusion.5), channel_id=1, source_target_pairs={{0,3},{1,2},{2,1},{3,0},{4,7},{5,6},{6,5},{7,4},{8,11},{9,10},{10,... | collective-permute-start | bytes 196616 | tf_op jit(solution)/shard_map/ppermute | solution.py:151
  30.7 6.0 %collective-permute-start.6 = (f16[2,128,128]{2,1,0:T(8,128)(2,1)S(1)}, f16[2,128,128]{2,1,0:T(8,128)(2,1)S(1)}, u32[]{:S(2)}, u32[]{:S(2)}) collective-permute-start(f16[2,128,128]{2,1,0:T(8,128)(2,1)S(1)} %add_convert_fusion.5), channel_id=1, source_target_pairs={{0,2},{1,3},{2,0},{3,1},{4,6},{5,7},{6,4},{7,5},{8,10},{9,11},{10,... | collective-permute-start | bytes 196616 | tf_op jit(solution)/shard_map/ppermute | solution.py:151
  30.7 6.0 %collective-permute-start.5 = (f16[2,128,128]{2,1,0:T(8,128)(2,1)S(1)}, f16[2,128,128]{2,1,0:T(8,128)(2,1)S(1)}, u32[]{:S(2)}, u32[]{:S(2)}) collective-permute-start(f16[2,128,128]{2,1,0:T(8,128)(2,1)S(1)} %add_convert_fusion.5), channel_id=1, source_target_pairs={{0,1},{1,0},{2,3},{3,2},{4,5},{5,4},{6,7},{7,6},{8,9},{9,8},{10,11... | collective-permute-start | bytes 196616 | tf_op jit(solution)/shard_map/ppermute | solution.py:151
  36.8 5.3 %collective-permute-start.10 = (f16[2,128,128]{2,1,0:T(8,128)(2,1)S(1)}, f16[2,128,128]{2,1,0:T(8,128)(2,1)S(1)}, u32[]{:S(2)}, u32[]{:S(2)}) collective-permute-start(f16[2,128,128]{2,1,0:T(8,128)(2,1)S(1)} %add_convert_fusion.4), channel_id=1, source_target_pairs={{0,24},{4,28},{8,16},{12,20},{16,8},{20,12},{24,0},{28,4},{1,25},{... | collective-permute-start | bytes 196616 | tf_op jit(solution)/shard_map/ppermute | solution.py:151
  39.3 4.3 %collective-permute-start.9 = (f16[2,128,128]{2,1,0:T(8,128)(2,1)S(1)}, f16[2,128,128]{2,1,0:T(8,128)(2,1)S(1)}, u32[]{:S(2)}, u32[]{:S(2)}) collective-permute-start(f16[2,128,128]{2,1,0:T(8,128)(2,1)S(1)} %add_convert_fusion.4), channel_id=1, source_target_pairs={{0,16},{4,20},{8,24},{12,28},{16,0},{20,4},{24,8},{28,12},{1,17},{... | collective-permute-start | bytes 196616 | tf_op jit(solution)/shard_map/ppermute | solution.py:151
  39.8 4.3 %collective-permute-start.8 = (f16[2,128,128]{2,1,0:T(8,128)(2,1)S(1)}, f16[2,128,128]{2,1,0:T(8,128)(2,1)S(1)}, u32[]{:S(2)}, u32[]{:S(2)}) collective-permute-start(f16[2,128,128]{2,1,0:T(8,128)(2,1)S(1)} %add_convert_fusion.4), channel_id=1, source_target_pairs={{0,8},{4,12},{8,0},{12,4},{16,24},{20,28},{24,16},{28,20},{1,9},{5... | collective-permute-start | bytes 196616 | tf_op jit(solution)/shard_map/ppermute | solution.py:151
  44.1 1.4 %collective-permute-start.11 = (f32[2,128,128]{2,1,0:T(8,128)S(1)}, f32[2,128,128]{2,1,0:T(8,128)S(1)}, u32[]{:S(2)}, u32[]{:S(2)}) collective-permute-start(f32[2,128,128]{2,1,0:T(8,128)S(1)} %add_add_fusion.2.own), channel_id=1, source_target_pairs={{0,4},{4,0},{8,12},{12,8},{16,20},{20,16},{24,28},{28,24},{1,5},{5... | collective-permute-start | bytes 393224 | tf_op jit(solution)/shard_map/ppermute | solution.py:151
  48.8 1.4 %collective-permute-start.12 = (f32[2,128,128]{2,1,0:T(8,128)S(1)}, f32[2,128,128]{2,1,0:T(8,128)S(1)}, u32[]{:S(2)}, u32[]{:S(2)}) collective-permute-start(f32[2,128,128]{2,1,0:T(8,128)S(1)} %get-tuple-element.23), channel_id=1, source_target_pairs={{0,4},{4,0},{8,12},{12,8},{16,20},{20,16},{24,28},{28,24},{1,5},{5... | collective-permute-start | bytes 393224 | tf_op jit(solution)/shard_map/ppermute | solution.py:151
  50.2 6.8 %collective-permute-start.15 = (f16[2,128,128]{2,1,0:T(8,128)(2,1)S(1)}, f16[2,128,128]{2,1,0:T(8,128)(2,1)S(1)}, u32[]{:S(2)}, u32[]{:S(2)}) collective-permute-start(f16[2,128,128]{2,1,0:T(8,128)(2,1)S(1)} %add_convert_fusion.3), channel_id=1, source_target_pairs={{0,3},{1,2},{2,1},{3,0},{4,7},{5,6},{6,5},{7,4},{8,11},{9,10},{10,... | collective-permute-start | bytes 196616 | tf_op jit(solution)/shard_map/ppermute | solution.py:151
  53.0 6.2 %collective-permute-start.14 = (f16[2,128,128]{2,1,0:T(8,128)(2,1)S(1)}, f16[2,128,128]{2,1,0:T(8,128)(2,1)S(1)}, u32[]{:S(2)}, u32[]{:S(2)}) collective-permute-start(f16[2,128,128]{2,1,0:T(8,128)(2,1)S(1)} %add_convert_fusion.3), channel_id=1, source_target_pairs={{0,2},{1,3},{2,0},{3,1},{4,6},{5,7},{6,4},{7,5},{8,10},{9,11},{10,... | collective-permute-start | bytes 196616 | tf_op jit(solution)/shard_map/ppermute | solution.py:151
  53.0 6.2 %collective-permute-start.13 = (f16[2,128,128]{2,1,0:T(8,128)(2,1)S(1)}, f16[2,128,128]{2,1,0:T(8,128)(2,1)S(1)}, u32[]{:S(2)}, u32[]{:S(2)}) collective-permute-start(f16[2,128,128]{2,1,0:T(8,128)(2,1)S(1)} %add_convert_fusion.3), channel_id=1, source_target_pairs={{0,1},{1,0},{2,3},{3,2},{4,5},{5,4},{6,7},{7,6},{8,9},{9,8},{10,11... | collective-permute-start | bytes 196616 | tf_op jit(solution)/shard_map/ppermute | solution.py:151
  59.2 5.3 %collective-permute-start.18 = (f16[2,128,128]{2,1,0:T(8,128)(2,1)S(1)}, f16[2,128,128]{2,1,0:T(8,128)(2,1)S(1)}, u32[]{:S(2)}, u32[]{:S(2)}) collective-permute-start(f16[2,128,128]{2,1,0:T(8,128)(2,1)S(1)} %add_convert_fusion.2), channel_id=1, source_target_pairs={{0,24},{4,28},{8,16},{12,20},{16,8},{20,12},{24,0},{28,4},{1,25},{... | collective-permute-start | bytes 196616 | tf_op jit(solution)/shard_map/ppermute | solution.py:151
  60.7 4.9 %collective-permute-start.17 = (f16[2,128,128]{2,1,0:T(8,128)(2,1)S(1)}, f16[2,128,128]{2,1,0:T(8,128)(2,1)S(1)}, u32[]{:S(2)}, u32[]{:S(2)}) collective-permute-start(f16[2,128,128]{2,1,0:T(8,128)(2,1)S(1)} %add_convert_fusion.2), channel_id=1, source_target_pairs={{0,16},{4,20},{8,24},{12,28},{16,0},{20,4},{24,8},{28,12},{1,17},{... | collective-permute-start | bytes 196616 | tf_op jit(solution)/shard_map/ppermute | solution.py:151
  61.3 4.4 %collective-permute-start.16 = (f16[2,128,128]{2,1,0:T(8,128)(2,1)S(1)}, f16[2,128,128]{2,1,0:T(8,128)(2,1)S(1)}, u32[]{:S(2)}, u32[]{:S(2)}) collective-permute-start(f16[2,128,128]{2,1,0:T(8,128)(2,1)S(1)} %add_convert_fusion.2), channel_id=1, source_target_pairs={{0,8},{4,12},{8,0},{12,4},{16,24},{20,28},{24,16},{28,20},{1,9},{5... | collective-permute-start | bytes 196616 | tf_op jit(solution)/shard_map/ppermute | solution.py:151
  65.8 1.4 %collective-permute-start.19 = (f32[2,128,128]{2,1,0:T(8,128)S(1)}, f32[2,128,128]{2,1,0:T(8,128)S(1)}, u32[]{:S(2)}, u32[]{:S(2)}) collective-permute-start(f32[2,128,128]{2,1,0:T(8,128)S(1)} %add_add_fusion.1.own), channel_id=1, source_target_pairs={{0,4},{4,0},{8,12},{12,8},{16,20},{20,16},{24,28},{28,24},{1,5},{5... | collective-permute-start | bytes 393224 | tf_op jit(solution)/shard_map/ppermute | solution.py:151
  70.4 1.4 %collective-permute-start.20 = (f32[2,128,128]{2,1,0:T(8,128)S(1)}, f32[2,128,128]{2,1,0:T(8,128)S(1)}, u32[]{:S(2)}, u32[]{:S(2)}) collective-permute-start(f32[2,128,128]{2,1,0:T(8,128)S(1)} %get-tuple-element.27), channel_id=1, source_target_pairs={{0,4},{4,0},{8,12},{12,8},{16,20},{20,16},{24,28},{28,24},{1,5},{5... | collective-permute-start | bytes 393224 | tf_op jit(solution)/shard_map/ppermute | solution.py:151
  71.9 6.8 %collective-permute-start.23 = (f16[2,128,128]{2,1,0:T(8,128)(2,1)S(1)}, f16[2,128,128]{2,1,0:T(8,128)(2,1)S(1)}, u32[]{:S(2)}, u32[]{:S(2)}) collective-permute-start(f16[2,128,128]{2,1,0:T(8,128)(2,1)S(1)} %add_convert_fusion.1), channel_id=1, source_target_pairs={{0,3},{1,2},{2,1},{3,0},{4,7},{5,6},{6,5},{7,4},{8,11},{9,10},{10,... | collective-permute-start | bytes 196616 | tf_op jit(solution)/shard_map/ppermute | solution.py:151
  74.4 6.3 %collective-permute-start.22 = (f16[2,128,128]{2,1,0:T(8,128)(2,1)S(1)}, f16[2,128,128]{2,1,0:T(8,128)(2,1)S(1)}, u32[]{:S(2)}, u32[]{:S(2)}) collective-permute-start(f16[2,128,128]{2,1,0:T(8,128)(2,1)S(1)} %add_convert_fusion.1), channel_id=1, source_target_pairs={{0,2},{1,3},{2,0},{3,1},{4,6},{5,7},{6,4},{7,5},{8,10},{9,11},{10,... | collective-permute-start | bytes 196616 | tf_op jit(solution)/shard_map/ppermute | solution.py:151
  74.4 6.3 %collective-permute-start.21 = (f16[2,128,128]{2,1,0:T(8,128)(2,1)S(1)}, f16[2,128,128]{2,1,0:T(8,128)(2,1)S(1)}, u32[]{:S(2)}, u32[]{:S(2)}) collective-permute-start(f16[2,128,128]{2,1,0:T(8,128)(2,1)S(1)} %add_convert_fusion.1), channel_id=1, source_target_pairs={{0,1},{1,0},{2,3},{3,2},{4,5},{5,4},{6,7},{7,6},{8,9},{9,8},{10,11... | collective-permute-start | bytes 196616 | tf_op jit(solution)/shard_map/ppermute | solution.py:151
  80.7 5.3 %collective-permute-start.26 = (f16[2,128,128]{2,1,0:T(8,128)(2,1)S(1)}, f16[2,128,128]{2,1,0:T(8,128)(2,1)S(1)}, u32[]{:S(2)}, u32[]{:S(2)}) collective-permute-start(f16[2,128,128]{2,1,0:T(8,128)(2,1)S(1)} %add_convert_fusion), channel_id=1, source_target_pairs={{0,24},{4,28},{8,16},{12,20},{16,8},{20,12},{24,0},{28,4},{1,25},{... | collective-permute-start | bytes 196616 | tf_op jit(solution)/shard_map/ppermute | solution.py:151
  83.0 4.3 %collective-permute-start.25 = (f16[2,128,128]{2,1,0:T(8,128)(2,1)S(1)}, f16[2,128,128]{2,1,0:T(8,128)(2,1)S(1)}, u32[]{:S(2)}, u32[]{:S(2)}) collective-permute-start(f16[2,128,128]{2,1,0:T(8,128)(2,1)S(1)} %add_convert_fusion), channel_id=1, source_target_pairs={{0,16},{4,20},{8,24},{12,28},{16,0},{20,4},{24,8},{28,12},{1,17},{... | collective-permute-start | bytes 196616 | tf_op jit(solution)/shard_map/ppermute | solution.py:151
  83.5 4.3 %collective-permute-start.24 = (f16[2,128,128]{2,1,0:T(8,128)(2,1)S(1)}, f16[2,128,128]{2,1,0:T(8,128)(2,1)S(1)}, u32[]{:S(2)}, u32[]{:S(2)}) collective-permute-start(f16[2,128,128]{2,1,0:T(8,128)(2,1)S(1)} %add_convert_fusion), channel_id=1, source_target_pairs={{0,8},{4,12},{8,0},{12,4},{16,24},{20,28},{24,16},{28,20},{1,9},{5... | collective-permute-start | bytes 196616 | tf_op jit(solution)/shard_map/ppermute | solution.py:151
  87.8 1.4 %collective-permute-start.27 = (f32[2,128,128]{2,1,0:T(8,128)S(1)}, f32[2,128,128]{2,1,0:T(8,128)S(1)}, u32[]{:S(2)}, u32[]{:S(2)}) collective-permute-start(f32[2,128,128]{2,1,0:T(8,128)S(1)} %add_add_fusion.own), channel_id=1, source_target_pairs={{0,4},{4,0},{8,12},{12,8},{16,20},{20,16},{24,28},{28,24},{1,5},{5... | collective-permute-start | bytes 393224 | tf_op jit(solution)/shard_map/ppermute | solution.py:151

commit v2 on v1

v2 whole, which is shorter than its diff:
```python
import functools
import math

import jax
import jax.numpy as jnp
from jax import lax
from jax.experimental import pallas as pl
from jax.experimental.pallas import tpu as pltpu
from jax.sharding import PartitionSpec as P

STEPS = 3
UNROLL = 16
LEFT_MAX = 1.16462404
RIGHT_MAX = 0.010778794
VMEM = pl.BlockSpec(memory_space=pltpu.VMEM)
HBM = pl.BlockSpec(memory_space=pltpu.HBM)
SMEM = pl.BlockSpec(memory_space=pltpu.SMEM)
F32 = jnp.float32
BF16 = jnp.bfloat16
HALF = jnp.float16


def total(tile):
    return jnp.sum(jnp.sum(tile, axis=0, keepdims=True), axis=1, keepdims=True)


def lanes(x):
    rows, cols = x.shape
    return jnp.sum(x.reshape(rows // 8, 8, cols), axis=0)


def live(table, g, acc):
    sectors, rows, cols = acc.shape
    return lax.broadcasted_iota(jnp.int32, (rows, cols), 0) < table[table.shape[0] - sectors + g]


def apply_ops(wire, square, blocks, acc, table, left, right, keep, send):
    sectors, rows, cols = acc.shape
    acc[...] = jnp.zeros_like(acc)
    terms = left.shape[0]
    unroll = math.gcd(UNROLL, terms)

    def group(j, carry):
        for u in range(unroll):
            k = j * unroll + u
            half = jnp.dot(left[k], blocks[table[k]], preferred_element_type=F32)
            acc[table[terms + k]] += jnp.dot(half.astype(BF16), right[k], preferred_element_type=F32)
        return carry

    lax.fori_loop(0, terms // unroll, group, 0)
    gain = (wire / jnp.sqrt(square / (sectors * rows * cols)))[None]
    h = sectors // 2
    low = lax.axis_index("terms") % 2
    keep[...] = acc[pl.ds(low * h, h)] * gain
    send[...] = acc[pl.ds((1 - low) * h, h)] * gain


def load_kernel(rows_hbm, owner_hbm, in_hbm, out_hbm, left_hbm, right_hbm, left, right, table,
                rows_live, owner, term_in, term_out, slot, sems):
    pairs = ((owner_hbm, owner), (in_hbm, term_in), (out_hbm, term_out), (rows_hbm, rows_live),
             (left_hbm, left), (right_hbm, right))
    copies = [pltpu.make_async_copy(src, dst, sems.at[i]) for i, (src, dst) in enumerate(pairs)]
    for copy in copies:
        copy.start()
    for copy in copies[:4]:
        copy.wait()
    sectors, terms = owner.shape[0], term_in.shape[0]
    for i in range(sectors):
        slot[owner[i]] = i
        table[2 * terms + i] = rows_live[i]
    for k in range(terms):
        table[k] = slot[term_in[k]]
        table[terms + k] = slot[term_out[k]]
    for copy in copies[4:]:
        copy.wait()


def first_kernel(wire, *refs):
    table, left, right, vec, pre, state, keep, send, blocks, acc = refs[-10:]
    sectors, rows, cols = acc.shape
    parts = (len(refs) - 10) // 2
    mine, other = refs[:parts], refs[parts : 2 * parts]
    held = sectors // parts
    low = lax.axis_index("terms") % 2
    here = lax.axis_index("sectors")

    def load(trial, precond):
        for mask in range(parts):
            for i in range(held):
                g = (here ^ mask) * held + i
                vec[g] = jnp.where(live(table, g, acc), trial[mask][i], 0.0)
                pre[g] = precond[mask][i]

    @pl.when(low == 0)
    def _():
        load(mine, other)

    @pl.when(low == 1)
    def _():
        load(other, mine)

    tile = jnp.zeros((8, cols), F32)
    for g in range(sectors):
        v = vec[g]
        blocks[g] = v.astype(BF16)
        tile = tile + lanes(v * v)
    square = jnp.maximum(total(tile), 1e-30)
    state[...] = jnp.broadcast_to(square, state.shape)
    apply_ops(wire, square, blocks, acc, table, left, right, keep, send)


def update(wire, own, far, table, vec, pre, square, full, out):
    sectors, rows, cols = full.shape
    h = sectors // 2
    low = lax.axis_index("terms") % 2
    full[pl.ds(low * h, h)] = own[...]
    full[pl.ds((1 - low) * h, h)] = far[...]
    gain = jnp.sqrt(square / (sectors * rows * cols)) / wire
    tile = jnp.zeros((8, cols), F32)
    for g in range(sectors):
        v = vec[g]
        summed = jnp.where(live(table, g, full), full[g] * gain, 0.0)
        full[g] = summed
        tile = tile + lanes(v * (summed - pre[g] * v))
    rayleigh = total(tile) / square
    tile = jnp.zeros((8, cols), F32)
    for g in range(sectors):
        v = vec[g]
        u = 2.0 * v - (full[g] - rayleigh * v) / pre[g]
        out[g] = u
        tile = tile + lanes(u * u)
    scale = 1.0 / jnp.sqrt(total(tile) / (sectors * rows * cols) + 1e-06)
    return rayleigh, scale


def middle_kernel(wire, step, own, far, vec_in, pre, state_in, table, left, right,
                  vec, state, keep, send, full, blocks, acc):
    sectors, rows, cols = acc.shape
    old = state_in[...]
    rayleigh, scale = update(wire, own, far, table, vec_in, pre, old[0:1, 0:1], full, vec)
    tile = jnp.zeros((8, cols), F32)
    for g in range(sectors):
        v = vec[g] * scale
        vec[g] = v
        blocks[g] = v.astype(BF16)
        tile = tile + lanes(v * v)
    square = jnp.maximum(total(tile), 1e-30)
    line = lax.broadcasted_iota(jnp.int32, old.shape, 0)
    state[...] = jnp.where(line == 0, square, jnp.where(line == step, rayleigh, old))
    apply_ops(wire, square, blocks, acc, table, left, right, keep, send)


def last_kernel(wire, step, own, far, vec_in, pre, state_in, table, out, energies, full, fresh):
    held = out.shape[0]
    old = state_in[...]
    rayleigh, scale = update(wire, own, far, table, vec_in, pre, old[0:1, 0:1], full, fresh)
    first = lax.axis_index("sectors") * held
    out[...] = fresh[pl.ds(first, held)] * scale[None]
    line = lax.broadcasted_iota(jnp.int32, old.shape, 0)
    energies[...] = jnp.where(line == step, rayleigh, old)


def params():
    return pltpu.CompilerParams(vmem_limit_bytes=24 << 20)


def swap(x, axis, mask):
    return lax.ppermute(x, axis, [(i, i ^ mask) for i in range(lax.axis_size(axis))])


def bit_groups(axis, first):
    count = lax.axis_size(axis).bit_length() - 1
    return [(low, min(2, count - low)) for low in range(first, count, 2)]


def sum_stage(x, axis, low, bits):
    got = [x] + [swap(x, axis, mask << low) for mask in range(1, 1 << bits)]
    got = [g.astype(F32) for g in got]
    while len(got) > 1:
        got = [got[i] + got[i + 1] for i in range(0, len(got), 2)]
    return got[0]


def reduce_half(keep, send):
    x = keep + swap(send, "terms", 1)
    for axis, first in (("sectors", 0), ("terms", 1)):
        for low, bits in bit_groups(axis, first):
            x = sum_stage(lax.optimization_barrier(x.astype(HALF)), axis, low, bits)
    return x


def on_device(trial, precond, block_rows, owner_map, term_in, term_out, left_ops, right_ops):
    sec_local, rows, cols = trial.shape
    sectors = sec_local * lax.axis_size("sectors")
    terms = left_ops.shape[0] * lax.axis_size("sectors") * lax.axis_size("terms")
    bound = 1.02 * LEFT_MAX * RIGHT_MAX * math.sqrt(rows * cols) * math.sqrt(sectors * rows * cols) * terms
    wire = 2.0 ** -max(0, math.ceil(math.log2(bound / 65504.0)))
    whole = jax.ShapeDtypeStruct((sectors, rows, cols), F32)
    part = jax.ShapeDtypeStruct((sectors // 2, rows, cols), F32)
    state_shape = jax.ShapeDtypeStruct((8, cols), F32)
    full = pltpu.VMEM((sectors, rows, cols), F32)
    scratch = [pltpu.VMEM((sectors, rows, cols), BF16), full]

    count, entries = left_ops.shape[0], 2 * left_ops.shape[0] + sectors
    ints = [pltpu.SMEM((n,), jnp.int32) for n in (sectors, sectors, count, count, sectors)]
    left, right, table = pl.pallas_call(
        load_kernel,
        out_shape=(
            jax.ShapeDtypeStruct(left_ops.shape, BF16),
            jax.ShapeDtypeStruct(right_ops.shape, BF16),
            jax.ShapeDtypeStruct((entries,), jnp.int32),
        ),
        in_specs=[HBM] * 6,
        out_specs=(VMEM, VMEM, SMEM),
        scratch_shapes=ints + [pltpu.SemaphoreType.DMA((6,))],
        compiler_params=params(),
        cost_estimate=pl.CostEstimate(flops=0, bytes_accessed=4 * left_ops.size, transcendentals=0),
    )(*(pltpu.with_memory_space_constraint(x, pltpu.HBM) for x in (block_rows, owner_map, term_in, term_out, left_ops, right_ops)))

    picked = jnp.where(lax.axis_index("terms") % 2 == 0, trial, precond)
    mine = [picked] + [swap(picked, "sectors", mask) for mask in range(1, lax.axis_size("sectors"))]
    mine, (left, right, table) = lax.optimization_barrier((mine, (left, right, table)))
    other = [swap(x, "terms", 1) for x in mine]
    vec, pre, state, keep, send = pl.pallas_call(
        functools.partial(first_kernel, wire),
        out_shape=(whole, whole, state_shape, part, part),
        in_specs=[VMEM] * (2 * len(mine)) + [SMEM] + [VMEM] * 2,
        out_specs=(VMEM,) * 5,
        scratch_shapes=scratch,
        compiler_params=params(),
    )(*mine, *other, table, left, right)
    for step in range(1, STEPS):
        own = reduce_half(keep, send)
        far = swap(own, "terms", 1)
        vec, state, keep, send = pl.pallas_call(
            functools.partial(middle_kernel, wire, step),
            out_shape=(whole, state_shape, part, part),
            in_specs=[VMEM] * 5 + [SMEM] + [VMEM] * 2,
            out_specs=(VMEM,) * 4,
            scratch_shapes=[full] + scratch,
            compiler_params=params(),
        )(own, far, vec, pre, state, table, left, right)
    own = reduce_half(keep, send)
    far = swap(own, "terms", 1)
    vector, energies = pl.pallas_call(
        functools.partial(last_kernel, wire, STEPS),
        out_shape=(jax.ShapeDtypeStruct(trial.shape, F32), state_shape),
        in_specs=[VMEM] * 5 + [SMEM],
        out_specs=(VMEM,) * 2,
        scratch_shapes=[full, full],
        compiler_params=params(),
    )(own, far, vec, pre, state, table)
    return vector, energies[1 : STEPS + 1, 0]


def solution(mesh):
    return jax.shard_map(
        on_device,
        mesh=mesh,
        in_specs=(
            P("sectors", None, None),
            P("sectors", None, None),
            P(),
            P(),
            P(("terms", "sectors")),
            P(("terms", "sectors")),
            P(("terms", "sectors"), None, None),
            P(("terms", "sectors"), None, None),
        ),
        out_specs=(P("sectors", None, None), P()),
        check_vma=False,
    )
```

time: 91.8 us -> 82.4 us (0.90)
  local copies, waits for them, and re-layouts: 8.63 us -> 0.63 us
  waiting for transfers between devices: 37.7 us -> 34 us
  Pallas kernels: 12.6 us -> 13.9 us
  starting transfers between devices: 30.6 us -> 31.9 us
    unnamed x26 -> x0, local copies, waits for them, and re-layouts: 8 us -> none
    ppermute x28 -> x31, waiting for transfers between devices: 37.7 us -> 34 us  [swap(): lax.ppermute(x, axis, [(i, i ^ mask) for i in range(lax.axis_size(axis))])]
    ppermute x28 -> x31, starting transfers between devices: 30.6 us -> 31.9 us  [swap(): lax.ppermute(x, axis, [(i, i ^ mask) for i in range(lax.axis_size(axis))])]
    pallas_call x1, Pallas kernels: 1.65 us -> 2.88 us  [on_device(): pl.pallas_call(load_kernel, out_shape=(jax.ShapeDtypeStruct(left_ops.shap...]
  transfers between devices with their start and end apart: 28 -> 31, of which waited for: 24 -> 26; matrix products, arithmetic and copies ran while one was open for 0% -> 0% of each run, Pallas kernels for 0% -> 3%
where the time goes in v2:
time: 82.4 us; the launch traced here: 82.3 us
  waiting for transfers between devices  34 us (41%)
  starting transfers between devices  31.9 us (39%)
  Pallas kernels  13.9 us (17%)
  other arithmetic  1.15 us (1%)
    ppermute x31, waiting for transfers between devices, swap(): lax.ppermute(x, axis, [(i, i ^ mask) for i in range(lax.axis_size(axis))])  34 us
    ppermute x31, starting transfers between devices, swap(): lax.ppermute(x, axis, [(i, i ^ mask) for i in range(lax.axis_size(axis))])  31.9 us
    pallas_call x2, Pallas kernels, on_device(): pl.pallas_call(functools.partial(middle_kernel, wire, step), out_shape=(w...  6.49 us
    pallas_call x1, Pallas kernels, on_device(): pl.pallas_call(functools.partial(first_kernel, wire), out_shape=(whole, w...  2.9 us
    pallas_call x1, Pallas kernels, on_device(): pl.pallas_call(load_kernel, out_shape=(jax.ShapeDtypeStruct(left_ops.shap...  2.88 us
  transfers between devices with their start and end apart: 31, of which 26 were waited for; matrix products, arithmetic and copies ran while one was open for 0% of the time, Pallas kernels for 3%

profile of v2, /device:TPU:0, one launch (start us, length us, event | category | flops | bytes accessed | tf_op | source)
XLA Modules:
  0.0 82.3 jit_solution(5194133063365772573)
XLA Ops:
  0.6 0.9 %broadcast_select_fusion.refs_0_ = f32[1,128,128]{2,1,0:T(8,128)S(1)} fusion(f32[1,128,128]{2,1,0:T(8,128)} %param.8, f32[1,128,128]{2,1,0:T(8,128)} %param.9, pred[]{:T(512)S(6)} %eq.5), kind=kLoop, calls=%fused_computation.9 | loop fusion | flops 16384 | bytes 196609 | tf_op jit(solution)/shard_map/jit(_where)/select_n | solution.py:220
  1.5 5.1 %collective-permute-start.2 = (f32[1,128,128]{2,1,0:T(8,128)S(1)}, f32[1,128,128]{2,1,0:T(8,128)S(1)}, u32[]{:S(2)}, u32[]{:S(2)}) collective-permute-start(f32[1,128,128]{2,1,0:T(8,128)S(1)} %broadcast_select_fusion.refs_0_), channel_id=1, source_target_pairs={{0,3},{1,2},{2,1},{3,0},{4,7},{5,6},{6,5},{7,4},{8,11},{9,10},{10,... | collective-permute-start | bytes 196616 | tf_op jit(solution)/shard_map/ppermute | solution.py:168
  6.6 0.6 collective-permute-start
  7.3 2.9 %shard_map.95 = (bf16[64,128,128]{2,1,0:T(8,128)(2,1)S(1)}, bf16[64,128,128]{2,1,0:T(8,128)(2,1)S(1)}, s32[132]{0:T(256)S(1)}) custom-call(s32[4]{0:T(128)} %rows_hbm.1, s32[4]{0:T(128)} %owner_hbm.1, s32[64]{0:T(128)} %in_hbm.1, s32[64]{0:T(128)} %out_hbm.1, bf16[64,128,128]{2,1,0:T(8,128)(2,1)} %left_hbm.1, bf16[64,128,128]{2,1,0:T(8,128)(2,1)} %right_hbm.1), custom_call_target="tpu_custom_call" | custom-call | bytes 4194304 | tf_op jit(solution)/shard_map/pallas_call | solution.py:206
  10.2 2.1 %collective-permute-done.1.refs_2_ = f32[1,128,128]{2,1,0:T(8,128)S(1)} collective-permute-done((f32[1,128,128]{2,1,0:T(8,128)S(1)}, f32[1,128,128]{2,1,0:T(8,128)S(1)}, u32[]{:S(2)}, u32[]{:S(2)}) %collective-permute-start.1) | collective-permute-done | bytes 65568 | tf_op jit(solution)/shard_map/ppermute | solution.py:168
  12.2 0.5 collective-permute-start.4
  12.7 0.5 collective-permute-start.6
  14.2 2.9 %shard_map.96 = (f32[4,128,128]{2,1,0:T(8,128)S(1)}, f32[4,128,128]{2,1,0:T(8,128)S(1)}, f32[8,128]{1,0:T(8,128)S(1)}, f32[2,128,128]{2,1,0:T(8,128)S(1)}, f32[2,128,128]{2,1,0:T(8,128)S(1)}) custom-call(f32[1,128,128]{2,1,0:T(8,128)S(1)} %broadcast_select_fusion.refs_0_, f32[1,128,128]{2,1,0:T(8,128)S(1)} %collective-permute-done.refs_1_, ...), custom_call_target="tpu_custom_call" | custom-call | tf_op jit(solution)/shard_map/pallas_call | solution.py:224
  17.1 0.4 collective-permute-start.7
  17.5 1.0 %collective-permute-done.7 = f32[2,128,128]{2,1,0:T(8,128)S(1)} collective-permute-done((f32[2,128,128]{2,1,0:T(8,128)S(1)}, f32[2,128,128]{2,1,0:T(8,128)S(1)}, u32[]{:S(2)}, u32[]{:S(2)}) %collective-permute-start.7) | collective-permute-done | bytes 131104 | tf_op jit(solution)/shard_map/ppermute | solution.py:168
  18.5 2.8 %collective-permute-start.10 = (f16[2,128,128]{2,1,0:T(8,128)(2,1)S(1)}, f16[2,128,128]{2,1,0:T(8,128)(2,1)S(1)}, u32[]{:S(2)}, u32[]{:S(2)}) collective-permute-start(f16[2,128,128]{2,1,0:T(8,128)(2,1)S(1)} %add_convert_fusion.5), channel_id=1, source_target_pairs={{0,3},{1,2},{2,1},{3,0},{4,7},{5,6},{6,5},{7,4},{8,11},{9,10},{10,... | collective-permute-start | bytes 196616 | tf_op jit(solution)/shard_map/ppermute | solution.py:168
  21.3 1.7 %collective-permute-start.8 = (f16[2,128,128]{2,1,0:T(8,128)(2,1)S(1)}, f16[2,128,128]{2,1,0:T(8,128)(2,1)S(1)}, u32[]{:S(2)}, u32[]{:S(2)}) collective-permute-start(f16[2,128,128]{2,1,0:T(8,128)(2,1)S(1)} %add_convert_fusion.5), channel_id=1, source_target_pairs={{0,1},{1,0},{2,3},{3,2},{4,5},{5,4},{6,7},{7,6},{8,9},{9,8},{10,11... | collective-permute-start | bytes 196616 | tf_op jit(solution)/shard_map/ppermute | solution.py:168
  22.9 2.4 %collective-permute-done.10 = f16[2,128,128]{2,1,0:T(8,128)(2,1)S(1)} collective-permute-done((f16[2,128,128]{2,1,0:T(8,128)(2,1)S(1)}, f16[2,128,128]{2,1,0:T(8,128)(2,1)S(1)}, u32[]{:S(2)}, u32[]{:S(2)}) %collective-permute-start.10) | collective-permute-done | bytes 65568 | tf_op jit(solution)/shard_map/ppermute | solution.py:168
  25.4 2.2 %collective-permute-done.9 = f16[2,128,128]{2,1,0:T(8,128)(2,1)S(1)} collective-permute-done((f16[2,128,128]{2,1,0:T(8,128)(2,1)S(1)}, f16[2,128,128]{2,1,0:T(8,128)(2,1)S(1)}, u32[]{:S(2)}, u32[]{:S(2)}) %collective-permute-start.9) | collective-permute-done | bytes 65568 | tf_op jit(solution)/shard_map/ppermute | solution.py:168
  27.6 2.5 %collective-permute-start.13 = (f16[2,128,128]{2,1,0:T(8,128)(2,1)S(1)}, f16[2,128,128]{2,1,0:T(8,128)(2,1)S(1)}, u32[]{:S(2)}, u32[]{:S(2)}) collective-permute-start(f16[2,128,128]{2,1,0:T(8,128)(2,1)S(1)} %add_convert_fusion.4), channel_id=1, source_target_pairs={{0,24},{4,28},{8,16},{12,20},{16,8},{20,12},{24,0},{28,4},{1,25},{... | collective-permute-start | bytes 196616 | tf_op jit(solution)/shard_map/ppermute | solution.py:168
  30.2 0.5 collective-permute-start.12
  30.7 0.5 collective-permute-start.11
  31.2 1.7 %collective-permute-done.13 = f16[2,128,128]{2,1,0:T(8,128)(2,1)S(1)} collective-permute-done((f16[2,128,128]{2,1,0:T(8,128)(2,1)S(1)}, f16[2,128,128]{2,1,0:T(8,128)(2,1)S(1)}, u32[]{:S(2)}, u32[]{:S(2)}) %collective-permute-start.13) | collective-permute-done | bytes 65568 | tf_op jit(solution)/shard_map/ppermute | solution.py:168
  32.9 1.5 %collective-permute-done.12 = f16[2,128,128]{2,1,0:T(8,128)(2,1)S(1)} collective-permute-done((f16[2,128,128]{2,1,0:T(8,128)(2,1)S(1)}, f16[2,128,128]{2,1,0:T(8,128)(2,1)S(1)}, u32[]{:S(2)}, u32[]{:S(2)}) %collective-permute-start.12) | collective-permute-done | bytes 65568 | tf_op jit(solution)/shard_map/ppermute | solution.py:168
  34.4 0.5 collective-permute-done.11
  35.1 1.3 %collective-permute-done.14.far = f32[2,128,128]{2,1,0:T(8,128)S(1)} collective-permute-done((f32[2,128,128]{2,1,0:T(8,128)S(1)}, f32[2,128,128]{2,1,0:T(8,128)S(1)}, u32[]{:S(2)}, u32[]{:S(2)}) %collective-permute-start.14) | collective-permute-done | bytes 131104 | tf_op jit(solution)/shard_map/ppermute | solution.py:168
  36.4 3.2 %shard_map.97 = (f32[4,128,128]{2,1,0:T(8,128)S(1)}, f32[8,128]{1,0:T(8,128)S(1)}, f32[2,128,128]{2,1,0:T(8,128)S(1)}, f32[2,128,128]{2,1,0:T(8,128)S(1)}) custom-call(f32[2,128,128]{2,1,0:T(8,128)S(1)} %add_add_fusion.2.own, f32[2,128,128]{2,1,0:T(8,128)S(1)} %collective-permute-done.14.far, f32[4,128,128]{2,1,0:T(8,128)S(1)} %get-tuple-element.39.vec_in, ...), custom_call_target="tpu_custom_call" | custom-call | tf_op jit(solution)/shard_map/pallas_call | solution.py:235
  39.9 1.2 %collective-permute-done.15 = f32[2,128,128]{2,1,0:T(8,128)S(1)} collective-permute-done((f32[2,128,128]{2,1,0:T(8,128)S(1)}, f32[2,128,128]{2,1,0:T(8,128)S(1)}, u32[]{:S(2)}, u32[]{:S(2)}) %collective-permute-start.15) | collective-permute-done | bytes 131104 | tf_op jit(solution)/shard_map/ppermute | solution.py:168
  41.1 2.6 %collective-permute-start.18 = (f16[2,128,128]{2,1,0:T(8,128)(2,1)S(1)}, f16[2,128,128]{2,1,0:T(8,128)(2,1)S(1)}, u32[]{:S(2)}, u32[]{:S(2)}) collective-permute-start(f16[2,128,128]{2,1,0:T(8,128)(2,1)S(1)} %add_convert_fusion.3), channel_id=1, source_target_pairs={{0,3},{1,2},{2,1},{3,0},{4,7},{5,6},{6,5},{7,4},{8,11},{9,10},{10,... | collective-permute-start | bytes 196616 | tf_op jit(solution)/shard_map/ppermute | solution.py:168
  43.7 1.8 %collective-permute-start.16 = (f16[2,128,128]{2,1,0:T(8,128)(2,1)S(1)}, f16[2,128,128]{2,1,0:T(8,128)(2,1)S(1)}, u32[]{:S(2)}, u32[]{:S(2)}) collective-permute-start(f16[2,128,128]{2,1,0:T(8,128)(2,1)S(1)} %add_convert_fusion.3), channel_id=1, source_target_pairs={{0,1},{1,0},{2,3},{3,2},{4,5},{5,4},{6,7},{7,6},{8,9},{9,8},{10,11... | collective-permute-start | bytes 196616 | tf_op jit(solution)/shard_map/ppermute | solution.py:168
  45.5 2.4 %collective-permute-done.18 = f16[2,128,128]{2,1,0:T(8,128)(2,1)S(1)} collective-permute-done((f16[2,128,128]{2,1,0:T(8,128)(2,1)S(1)}, f16[2,128,128]{2,1,0:T(8,128)(2,1)S(1)}, u32[]{:S(2)}, u32[]{:S(2)}) %collective-permute-start.18) | collective-permute-done | bytes 65568 | tf_op jit(solution)/shard_map/ppermute | solution.py:168
  47.9 2.0 %collective-permute-done.17 = f16[2,128,128]{2,1,0:T(8,128)(2,1)S(1)} collective-permute-done((f16[2,128,128]{2,1,0:T(8,128)(2,1)S(1)}, f16[2,128,128]{2,1,0:T(8,128)(2,1)S(1)}, u32[]{:S(2)}, u32[]{:S(2)}) %collective-permute-start.17) | collective-permute-done | bytes 65568 | tf_op jit(solution)/shard_map/ppermute | solution.py:168
  50.0 1.6 %collective-permute-start.21 = (f16[2,128,128]{2,1,0:T(8,128)(2,1)S(1)}, f16[2,128,128]{2,1,0:T(8,128)(2,1)S(1)}, u32[]{:S(2)}, u32[]{:S(2)}) collective-permute-start(f16[2,128,128]{2,1,0:T(8,128)(2,1)S(1)} %add_convert_fusion.2), channel_id=1, source_target_pairs={{0,24},{4,28},{8,16},{12,20},{16,8},{20,12},{24,0},{28,4},{1,25},{... | collective-permute-start | bytes 196616 | tf_op jit(solution)/shard_map/ppermute | solution.py:168
  51.6 0.7 collective-permute-start.20
  52.2 1.3 %collective-permute-start.19 = (f16[2,128,128]{2,1,0:T(8,128)(2,1)S(1)}, f16[2,128,128]{2,1,0:T(8,128)(2,1)S(1)}, u32[]{:S(2)}, u32[]{:S(2)}) collective-permute-start(f16[2,128,128]{2,1,0:T(8,128)(2,1)S(1)} %add_convert_fusion.2), channel_id=1, source_target_pairs={{0,8},{4,12},{8,0},{12,4},{16,24},{20,28},{24,16},{28,20},{1,9},{5... | collective-permute-start | bytes 196616 | tf_op jit(solution)/shard_map/ppermute | solution.py:168
  53.5 1.8 %collective-permute-done.21 = f16[2,128,128]{2,1,0:T(8,128)(2,1)S(1)} collective-permute-done((f16[2,128,128]{2,1,0:T(8,128)(2,1)S(1)}, f16[2,128,128]{2,1,0:T(8,128)(2,1)S(1)}, u32[]{:S(2)}, u32[]{:S(2)}) %collective-permute-start.21) | collective-permute-done | bytes 65568 | tf_op jit(solution)/shard_map/ppermute | solution.py:168
  55.4 1.0 %collective-permute-done.20 = f16[2,128,128]{2,1,0:T(8,128)(2,1)S(1)} collective-permute-done((f16[2,128,128]{2,1,0:T(8,128)(2,1)S(1)}, f16[2,128,128]{2,1,0:T(8,128)(2,1)S(1)}, u32[]{:S(2)}, u32[]{:S(2)}) %collective-permute-start.20) | collective-permute-done | bytes 65568 | tf_op jit(solution)/shard_map/ppermute | solution.py:168
  56.6 1.3 %collective-permute-done.22.far = f32[2,128,128]{2,1,0:T(8,128)S(1)} collective-permute-done((f32[2,128,128]{2,1,0:T(8,128)S(1)}, f32[2,128,128]{2,1,0:T(8,128)S(1)}, u32[]{:S(2)}, u32[]{:S(2)}) %collective-permute-start.22) | collective-permute-done | bytes 131104 | tf_op jit(solution)/shard_map/ppermute | solution.py:168
  57.9 3.2 %shard_map.98 = (f32[4,128,128]{2,1,0:T(8,128)S(1)}, f32[8,128]{1,0:T(8,128)S(1)}, f32[2,128,128]{2,1,0:T(8,128)S(1)}, f32[2,128,128]{2,1,0:T(8,128)S(1)}) custom-call(f32[2,128,128]{2,1,0:T(8,128)S(1)} %add_add_fusion.1.own, f32[2,128,128]{2,1,0:T(8,128)S(1)} %collective-permute-done.22.far, f32[4,128,128]{2,1,0:T(8,128)S(1)} %get-tuple-element.44.vec_in, ...), custom_call_target="tpu_custom_call" | custom-call | tf_op jit(solution)/shard_map/pallas_call | solution.py:235
  61.4 1.2 %collective-permute-done.23 = f32[2,128,128]{2,1,0:T(8,128)S(1)} collective-permute-done((f32[2,128,128]{2,1,0:T(8,128)S(1)}, f32[2,128,128]{2,1,0:T(8,128)S(1)}, u32[]{:S(2)}, u32[]{:S(2)}) %collective-permute-start.23) | collective-permute-done | bytes 131104 | tf_op jit(solution)/shard_map/ppermute | solution.py:168
  62.6 2.5 %collective-permute-start.26 = (f16[2,128,128]{2,1,0:T(8,128)(2,1)S(1)}, f16[2,128,128]{2,1,0:T(8,128)(2,1)S(1)}, u32[]{:S(2)}, u32[]{:S(2)}) collective-permute-start(f16[2,128,128]{2,1,0:T(8,128)(2,1)S(1)} %add_convert_fusion.1), channel_id=1, source_target_pairs={{0,3},{1,2},{2,1},{3,0},{4,7},{5,6},{6,5},{7,4},{8,11},{9,10},{10,... | collective-permute-start | bytes 196616 | tf_op jit(solution)/shard_map/ppermute | solution.py:168
  65.2 1.9 %collective-permute-start.24 = (f16[2,128,128]{2,1,0:T(8,128)(2,1)S(1)}, f16[2,128,128]{2,1,0:T(8,128)(2,1)S(1)}, u32[]{:S(2)}, u32[]{:S(2)}) collective-permute-start(f16[2,128,128]{2,1,0:T(8,128)(2,1)S(1)} %add_convert_fusion.1), channel_id=1, source_target_pairs={{0,1},{1,0},{2,3},{3,2},{4,5},{5,4},{6,7},{7,6},{8,9},{9,8},{10,11... | collective-permute-start | bytes 196616 | tf_op jit(solution)/shard_map/ppermute | solution.py:168
  67.1 2.4 %collective-permute-done.26 = f16[2,128,128]{2,1,0:T(8,128)(2,1)S(1)} collective-permute-done((f16[2,128,128]{2,1,0:T(8,128)(2,1)S(1)}, f16[2,128,128]{2,1,0:T(8,128)(2,1)S(1)}, u32[]{:S(2)}, u32[]{:S(2)}) %collective-permute-start.26) | collective-permute-done | bytes 65568 | tf_op jit(solution)/shard_map/ppermute | solution.py:168
  69.4 2.0 %collective-permute-done.25 = f16[2,128,128]{2,1,0:T(8,128)(2,1)S(1)} collective-permute-done((f16[2,128,128]{2,1,0:T(8,128)(2,1)S(1)}, f16[2,128,128]{2,1,0:T(8,128)(2,1)S(1)}, u32[]{:S(2)}, u32[]{:S(2)}) %collective-permute-start.25) | collective-permute-done | bytes 65568 | tf_op jit(solution)/shard_map/ppermute | solution.py:168
  71.5 2.3 %collective-permute-start.29 = (f16[2,128,128]{2,1,0:T(8,128)(2,1)S(1)}, f16[2,128,128]{2,1,0:T(8,128)(2,1)S(1)}, u32[]{:S(2)}, u32[]{:S(2)}) collective-permute-start(f16[2,128,128]{2,1,0:T(8,128)(2,1)S(1)} %add_convert_fusion), channel_id=1, source_target_pairs={{0,24},{4,28},{8,16},{12,20},{16,8},{20,12},{24,0},{28,4},{1,25},{... | collective-permute-start | bytes 196616 | tf_op jit(solution)/shard_map/ppermute | solution.py:168
  73.8 0.5 collective-permute-start.28
  74.3 0.7 collective-permute-start.27
  75.0 1.7 %collective-permute-done.29 = f16[2,128,128]{2,1,0:T(8,128)(2,1)S(1)} collective-permute-done((f16[2,128,128]{2,1,0:T(8,128)(2,1)S(1)}, f16[2,128,128]{2,1,0:T(8,128)(2,1)S(1)}, u32[]{:S(2)}, u32[]{:S(2)}) %collective-permute-start.29) | collective-permute-done | bytes 65568 | tf_op jit(solution)/shard_map/ppermute | solution.py:168
  76.8 1.3 %collective-permute-done.28 = f16[2,128,128]{2,1,0:T(8,128)(2,1)S(1)} collective-permute-done((f16[2,128,128]{2,1,0:T(8,128)(2,1)S(1)}, f16[2,128,128]{2,1,0:T(8,128)(2,1)S(1)}, u32[]{:S(2)}, u32[]{:S(2)}) %collective-permute-start.28) | collective-permute-done | bytes 65568 | tf_op jit(solution)/shard_map/ppermute | solution.py:168
  78.1 0.5 collective-permute-done.27
  78.7 1.3 %collective-permute-done.30.far = f32[2,128,128]{2,1,0:T(8,128)S(1)} collective-permute-done((f32[2,128,128]{2,1,0:T(8,128)S(1)}, f32[2,128,128]{2,1,0:T(8,128)S(1)}, u32[]{:S(2)}, u32[]{:S(2)}) %collective-permute-start.30) | collective-permute-done | bytes 131104 | tf_op jit(solution)/shard_map/ppermute | solution.py:168
  80.1 1.6 %shard_map.99 = (f32[1,128,128]{2,1,0:T(8,128)}, f32[8,128]{1,0:T(8,128)S(1)}) custom-call(f32[2,128,128]{2,1,0:T(8,128)S(1)} %add_add_fusion.own, f32[2,128,128]{2,1,0:T(8,128)S(1)} %collective-permute-done.30.far, f32[4,128,128]{2,1,0:T(8,128)S(1)} %get-tuple-element.48.vec_in, f32[4,128,128]{2,1,0:T(8,128)S(1)} %get-tuple-element.40.pre, ...), custom_call_target="tpu_custom_call" | custom-call | tf_op jit(solution)/shard_map/pallas_call | solution.py:245
  81.7 0.6 slice_reduce_fusion
  (30 shorter events, 1.9 us)
Async XLA Ops:
  1.5 8.6 %collective-permute-start.2 = (f32[1,128,128]{2,1,0:T(8,128)S(1)}, f32[1,128,128]{2,1,0:T(8,128)S(1)}, u32[]{:S(2)}, u32[]{:S(2)}) collective-permute-start(f32[1,128,128]{2,1,0:T(8,128)S(1)} %broadcast_select_fusion.refs_0_), channel_id=1, source_target_pairs={{0,3},{1,2},{2,1},{3,0},{4,7},{5,6},{6,5},{7,4},{8,11},{9,10},{10,... | collective-permute-start | bytes 196616 | tf_op jit(solution)/shard_map/ppermute | solution.py:168
  6.6 5.6 %collective-permute-start.1 = (f32[1,128,128]{2,1,0:T(8,128)S(1)}, f32[1,128,128]{2,1,0:T(8,128)S(1)}, u32[]{:S(2)}, u32[]{:S(2)}) collective-permute-start(f32[1,128,128]{2,1,0:T(8,128)S(1)} %broadcast_select_fusion.refs_0_), channel_id=1, source_target_pairs={{0,2},{1,3},{2,0},{3,1},{4,6},{5,7},{6,4},{7,5},{8,10},{9,11},{10,... | collective-permute-start | bytes 196616 | tf_op jit(solution)/shard_map/ppermute | solution.py:168
  6.6 5.6 %collective-permute-start = (f32[1,128,128]{2,1,0:T(8,128)S(1)}, f32[1,128,128]{2,1,0:T(8,128)S(1)}, u32[]{:S(2)}, u32[]{:S(2)}) collective-permute-start(f32[1,128,128]{2,1,0:T(8,128)S(1)} %broadcast_select_fusion.refs_0_), channel_id=1, source_target_pairs={{0,1},{1,0},{2,3},{3,2},{4,5},{5,4},{6,7},{7,6},{8,9},{9,8},{10,11... | collective-permute-start | bytes 196616 | tf_op jit(solution)/shard_map/ppermute | solution.py:168
  12.2 1.3 %collective-permute-start.3 = (f32[1,128,128]{2,1,0:T(8,128)S(1)}, f32[1,128,128]{2,1,0:T(8,128)S(1)}, u32[]{:S(2)}, u32[]{:S(2)}) collective-permute-start(f32[1,128,128]{2,1,0:T(8,128)S(1)} %broadcast_select_fusion.refs_0_), channel_id=1, source_target_pairs={{0,4},{4,0},{8,12},{12,8},{16,20},{20,16},{24,28},{28,24},{1,5},{5... | collective-permute-start | bytes 196616 | tf_op jit(solution)/shard_map/ppermute | solution.py:168
  12.2 1.4 %collective-permute-start.4 = (f32[1,128,128]{2,1,0:T(8,128)S(1)}, f32[1,128,128]{2,1,0:T(8,128)S(1)}, u32[]{:S(2)}, u32[]{:S(2)}) collective-permute-start(f32[1,128,128]{2,1,0:T(8,128)S(1)} %collective-permute-done.refs_1_), channel_id=1, source_target_pairs={{0,4},{4,0},{8,12},{12,8},{16,20},{20,16},{24,28},{28,24},{1,5},{5... | collective-permute-start | bytes 196616 | tf_op jit(solution)/shard_map/ppermute | solution.py:168
  12.7 1.3 %collective-permute-start.5 = (f32[1,128,128]{2,1,0:T(8,128)S(1)}, f32[1,128,128]{2,1,0:T(8,128)S(1)}, u32[]{:S(2)}, u32[]{:S(2)}) collective-permute-start(f32[1,128,128]{2,1,0:T(8,128)S(1)} %collective-permute-done.1.refs_2_), channel_id=1, source_target_pairs={{0,4},{4,0},{8,12},{12,8},{16,20},{20,16},{24,28},{28,24},{1,5},{5... | collective-permute-start | bytes 196616 | tf_op jit(solution)/shard_map/ppermute | solution.py:168
  12.7 1.4 %collective-permute-start.6 = (f32[1,128,128]{2,1,0:T(8,128)S(1)}, f32[1,128,128]{2,1,0:T(8,128)S(1)}, u32[]{:S(2)}, u32[]{:S(2)}) collective-permute-start(f32[1,128,128]{2,1,0:T(8,128)S(1)} %collective-permute-done.2.refs_3_), channel_id=1, source_target_pairs={{0,4},{4,0},{8,12},{12,8},{16,20},{20,16},{24,28},{28,24},{1,5},{5... | collective-permute-start | bytes 196616 | tf_op jit(solution)/shard_map/ppermute | solution.py:168
  17.1 1.4 %collective-permute-start.7 = (f32[2,128,128]{2,1,0:T(8,128)S(1)}, f32[2,128,128]{2,1,0:T(8,128)S(1)}, u32[]{:S(2)}, u32[]{:S(2)}) collective-permute-start(f32[2,128,128]{2,1,0:T(8,128)S(1)} %get-tuple-element.38), channel_id=1, source_target_pairs={{0,4},{4,0},{8,12},{12,8},{16,20},{20,16},{24,28},{28,24},{1,5},{5... | collective-permute-start | bytes 393224 | tf_op jit(solution)/shard_map/ppermute | solution.py:168
  18.5 6.9 %collective-permute-start.10 = (f16[2,128,128]{2,1,0:T(8,128)(2,1)S(1)}, f16[2,128,128]{2,1,0:T(8,128)(2,1)S(1)}, u32[]{:S(2)}, u32[]{:S(2)}) collective-permute-start(f16[2,128,128]{2,1,0:T(8,128)(2,1)S(1)} %add_convert_fusion.5), channel_id=1, source_target_pairs={{0,3},{1,2},{2,1},{3,0},{4,7},{5,6},{6,5},{7,4},{8,11},{9,10},{10,... | collective-permute-start | bytes 196616 | tf_op jit(solution)/shard_map/ppermute | solution.py:168
  21.3 6.3 %collective-permute-start.9 = (f16[2,128,128]{2,1,0:T(8,128)(2,1)S(1)}, f16[2,128,128]{2,1,0:T(8,128)(2,1)S(1)}, u32[]{:S(2)}, u32[]{:S(2)}) collective-permute-start(f16[2,128,128]{2,1,0:T(8,128)(2,1)S(1)} %add_convert_fusion.5), channel_id=1, source_target_pairs={{0,2},{1,3},{2,0},{3,1},{4,6},{5,7},{6,4},{7,5},{8,10},{9,11},{10,... | collective-permute-start | bytes 196616 | tf_op jit(solution)/shard_map/ppermute | solution.py:168
  21.3 6.3 %collective-permute-start.8 = (f16[2,128,128]{2,1,0:T(8,128)(2,1)S(1)}, f16[2,128,128]{2,1,0:T(8,128)(2,1)S(1)}, u32[]{:S(2)}, u32[]{:S(2)}) collective-permute-start(f16[2,128,128]{2,1,0:T(8,128)(2,1)S(1)} %add_convert_fusion.5), channel_id=1, source_target_pairs={{0,1},{1,0},{2,3},{3,2},{4,5},{5,4},{6,7},{7,6},{8,9},{9,8},{10,11... | collective-permute-start | bytes 196616 | tf_op jit(solution)/shard_map/ppermute | solution.py:168
  27.6 5.3 %collective-permute-start.13 = (f16[2,128,128]{2,1,0:T(8,128)(2,1)S(1)}, f16[2,128,128]{2,1,0:T(8,128)(2,1)S(1)}, u32[]{:S(2)}, u32[]{:S(2)}) collective-permute-start(f16[2,128,128]{2,1,0:T(8,128)(2,1)S(1)} %add_convert_fusion.4), channel_id=1, source_target_pairs={{0,24},{4,28},{8,16},{12,20},{16,8},{20,12},{24,0},{28,4},{1,25},{... | collective-permute-start | bytes 196616 | tf_op jit(solution)/shard_map/ppermute | solution.py:168
  30.2 4.3 %collective-permute-start.12 = (f16[2,128,128]{2,1,0:T(8,128)(2,1)S(1)}, f16[2,128,128]{2,1,0:T(8,128)(2,1)S(1)}, u32[]{:S(2)}, u32[]{:S(2)}) collective-permute-start(f16[2,128,128]{2,1,0:T(8,128)(2,1)S(1)} %add_convert_fusion.4), channel_id=1, source_target_pairs={{0,16},{4,20},{8,24},{12,28},{16,0},{20,4},{24,8},{28,12},{1,17},{... | collective-permute-start | bytes 196616 | tf_op jit(solution)/shard_map/ppermute | solution.py:168
  30.7 4.3 %collective-permute-start.11 = (f16[2,128,128]{2,1,0:T(8,128)(2,1)S(1)}, f16[2,128,128]{2,1,0:T(8,128)(2,1)S(1)}, u32[]{:S(2)}, u32[]{:S(2)}) collective-permute-start(f16[2,128,128]{2,1,0:T(8,128)(2,1)S(1)} %add_convert_fusion.4), channel_id=1, source_target_pairs={{0,8},{4,12},{8,0},{12,4},{16,24},{20,28},{24,16},{28,20},{1,9},{5... | collective-permute-start | bytes 196616 | tf_op jit(solution)/shard_map/ppermute | solution.py:168
  35.0 1.4 %collective-permute-start.14 = (f32[2,128,128]{2,1,0:T(8,128)S(1)}, f32[2,128,128]{2,1,0:T(8,128)S(1)}, u32[]{:S(2)}, u32[]{:S(2)}) collective-permute-start(f32[2,128,128]{2,1,0:T(8,128)S(1)} %add_add_fusion.2.own), channel_id=1, source_target_pairs={{0,4},{4,0},{8,12},{12,8},{16,20},{20,16},{24,28},{28,24},{1,5},{5... | collective-permute-start | bytes 393224 | tf_op jit(solution)/shard_map/ppermute | solution.py:168
  39.6 1.4 %collective-permute-start.15 = (f32[2,128,128]{2,1,0:T(8,128)S(1)}, f32[2,128,128]{2,1,0:T(8,128)S(1)}, u32[]{:S(2)}, u32[]{:S(2)}) collective-permute-start(f32[2,128,128]{2,1,0:T(8,128)S(1)} %get-tuple-element.43), channel_id=1, source_target_pairs={{0,4},{4,0},{8,12},{12,8},{16,20},{20,16},{24,28},{28,24},{1,5},{5... | collective-permute-start | bytes 393224 | tf_op jit(solution)/shard_map/ppermute | solution.py:168
  41.1 6.8 %collective-permute-start.18 = (f16[2,128,128]{2,1,0:T(8,128)(2,1)S(1)}, f16[2,128,128]{2,1,0:T(8,128)(2,1)S(1)}, u32[]{:S(2)}, u32[]{:S(2)}) collective-permute-start(f16[2,128,128]{2,1,0:T(8,128)(2,1)S(1)} %add_convert_fusion.3), channel_id=1, source_target_pairs={{0,3},{1,2},{2,1},{3,0},{4,7},{5,6},{6,5},{7,4},{8,11},{9,10},{10,... | collective-permute-start | bytes 196616 | tf_op jit(solution)/shard_map/ppermute | solution.py:168
  43.7 6.2 %collective-permute-start.17 = (f16[2,128,128]{2,1,0:T(8,128)(2,1)S(1)}, f16[2,128,128]{2,1,0:T(8,128)(2,1)S(1)}, u32[]{:S(2)}, u32[]{:S(2)}) collective-permute-start(f16[2,128,128]{2,1,0:T(8,128)(2,1)S(1)} %add_convert_fusion.3), channel_id=1, source_target_pairs={{0,2},{1,3},{2,0},{3,1},{4,6},{5,7},{6,4},{7,5},{8,10},{9,11},{10,... | collective-permute-start | bytes 196616 | tf_op jit(solution)/shard_map/ppermute | solution.py:168
  43.7 6.2 %collective-permute-start.16 = (f16[2,128,128]{2,1,0:T(8,128)(2,1)S(1)}, f16[2,128,128]{2,1,0:T(8,128)(2,1)S(1)}, u32[]{:S(2)}, u32[]{:S(2)}) collective-permute-start(f16[2,128,128]{2,1,0:T(8,128)(2,1)S(1)} %add_convert_fusion.3), channel_id=1, source_target_pairs={{0,1},{1,0},{2,3},{3,2},{4,5},{5,4},{6,7},{7,6},{8,9},{9,8},{10,11... | collective-permute-start | bytes 196616 | tf_op jit(solution)/shard_map/ppermute | solution.py:168
  50.0 5.4 %collective-permute-start.21 = (f16[2,128,128]{2,1,0:T(8,128)(2,1)S(1)}, f16[2,128,128]{2,1,0:T(8,128)(2,1)S(1)}, u32[]{:S(2)}, u32[]{:S(2)}) collective-permute-start(f16[2,128,128]{2,1,0:T(8,128)(2,1)S(1)} %add_convert_fusion.2), channel_id=1, source_target_pairs={{0,24},{4,28},{8,16},{12,20},{16,8},{20,12},{24,0},{28,4},{1,25},{... | collective-permute-start | bytes 196616 | tf_op jit(solution)/shard_map/ppermute | solution.py:168
  51.6 4.9 %collective-permute-start.20 = (f16[2,128,128]{2,1,0:T(8,128)(2,1)S(1)}, f16[2,128,128]{2,1,0:T(8,128)(2,1)S(1)}, u32[]{:S(2)}, u32[]{:S(2)}) collective-permute-start(f16[2,128,128]{2,1,0:T(8,128)(2,1)S(1)} %add_convert_fusion.2), channel_id=1, source_target_pairs={{0,16},{4,20},{8,24},{12,28},{16,0},{20,4},{24,8},{28,12},{1,17},{... | collective-permute-start | bytes 196616 | tf_op jit(solution)/shard_map/ppermute | solution.py:168
  52.2 4.3 %collective-permute-start.19 = (f16[2,128,128]{2,1,0:T(8,128)(2,1)S(1)}, f16[2,128,128]{2,1,0:T(8,128)(2,1)S(1)}, u32[]{:S(2)}, u32[]{:S(2)}) collective-permute-start(f16[2,128,128]{2,1,0:T(8,128)(2,1)S(1)} %add_convert_fusion.2), channel_id=1, source_target_pairs={{0,8},{4,12},{8,0},{12,4},{16,24},{20,28},{24,16},{28,20},{1,9},{5... | collective-permute-start | bytes 196616 | tf_op jit(solution)/shard_map/ppermute | solution.py:168
  56.5 1.4 %collective-permute-start.22 = (f32[2,128,128]{2,1,0:T(8,128)S(1)}, f32[2,128,128]{2,1,0:T(8,128)S(1)}, u32[]{:S(2)}, u32[]{:S(2)}) collective-permute-start(f32[2,128,128]{2,1,0:T(8,128)S(1)} %add_add_fusion.1.own), channel_id=1, source_target_pairs={{0,4},{4,0},{8,12},{12,8},{16,20},{20,16},{24,28},{28,24},{1,5},{5... | collective-permute-start | bytes 393224 | tf_op jit(solution)/shard_map/ppermute | solution.py:168
  61.2 1.4 %collective-permute-start.23 = (f32[2,128,128]{2,1,0:T(8,128)S(1)}, f32[2,128,128]{2,1,0:T(8,128)S(1)}, u32[]{:S(2)}, u32[]{:S(2)}) collective-permute-start(f32[2,128,128]{2,1,0:T(8,128)S(1)} %get-tuple-element.47), channel_id=1, source_target_pairs={{0,4},{4,0},{8,12},{12,8},{16,20},{20,16},{24,28},{28,24},{1,5},{5... | collective-permute-start | bytes 393224 | tf_op jit(solution)/shard_map/ppermute | solution.py:168
  62.6 6.8 %collective-permute-start.26 = (f16[2,128,128]{2,1,0:T(8,128)(2,1)S(1)}, f16[2,128,128]{2,1,0:T(8,128)(2,1)S(1)}, u32[]{:S(2)}, u32[]{:S(2)}) collective-permute-start(f16[2,128,128]{2,1,0:T(8,128)(2,1)S(1)} %add_convert_fusion.1), channel_id=1, source_target_pairs={{0,3},{1,2},{2,1},{3,0},{4,7},{5,6},{6,5},{7,4},{8,11},{9,10},{10,... | collective-permute-start | bytes 196616 | tf_op jit(solution)/shard_map/ppermute | solution.py:168
  65.2 6.3 %collective-permute-start.25 = (f16[2,128,128]{2,1,0:T(8,128)(2,1)S(1)}, f16[2,128,128]{2,1,0:T(8,128)(2,1)S(1)}, u32[]{:S(2)}, u32[]{:S(2)}) collective-permute-start(f16[2,128,128]{2,1,0:T(8,128)(2,1)S(1)} %add_convert_fusion.1), channel_id=1, source_target_pairs={{0,2},{1,3},{2,0},{3,1},{4,6},{5,7},{6,4},{7,5},{8,10},{9,11},{10,... | collective-permute-start | bytes 196616 | tf_op jit(solution)/shard_map/ppermute | solution.py:168
  65.2 6.3 %collective-permute-start.24 = (f16[2,128,128]{2,1,0:T(8,128)(2,1)S(1)}, f16[2,128,128]{2,1,0:T(8,128)(2,1)S(1)}, u32[]{:S(2)}, u32[]{:S(2)}) collective-permute-start(f16[2,128,128]{2,1,0:T(8,128)(2,1)S(1)} %add_convert_fusion.1), channel_id=1, source_target_pairs={{0,1},{1,0},{2,3},{3,2},{4,5},{5,4},{6,7},{7,6},{8,9},{9,8},{10,11... | collective-permute-start | bytes 196616 | tf_op jit(solution)/shard_map/ppermute | solution.py:168
  71.5 5.3 %collective-permute-start.29 = (f16[2,128,128]{2,1,0:T(8,128)(2,1)S(1)}, f16[2,128,128]{2,1,0:T(8,128)(2,1)S(1)}, u32[]{:S(2)}, u32[]{:S(2)}) collective-permute-start(f16[2,128,128]{2,1,0:T(8,128)(2,1)S(1)} %add_convert_fusion), channel_id=1, source_target_pairs={{0,24},{4,28},{8,16},{12,20},{16,8},{20,12},{24,0},{28,4},{1,25},{... | collective-permute-start | bytes 196616 | tf_op jit(solution)/shard_map/ppermute | solution.py:168
  73.8 4.3 %collective-permute-start.28 = (f16[2,128,128]{2,1,0:T(8,128)(2,1)S(1)}, f16[2,128,128]{2,1,0:T(8,128)(2,1)S(1)}, u32[]{:S(2)}, u32[]{:S(2)}) collective-permute-start(f16[2,128,128]{2,1,0:T(8,128)(2,1)S(1)} %add_convert_fusion), channel_id=1, source_target_pairs={{0,16},{4,20},{8,24},{12,28},{16,0},{20,4},{24,8},{28,12},{1,17},{... | collective-permute-start | bytes 196616 | tf_op jit(solution)/shard_map/ppermute | solution.py:168
  74.3 4.3 %collective-permute-start.27 = (f16[2,128,128]{2,1,0:T(8,128)(2,1)S(1)}, f16[2,128,128]{2,1,0:T(8,128)(2,1)S(1)}, u32[]{:S(2)}, u32[]{:S(2)}) collective-permute-start(f16[2,128,128]{2,1,0:T(8,128)(2,1)S(1)} %add_convert_fusion), channel_id=1, source_target_pairs={{0,8},{4,12},{8,0},{12,4},{16,24},{20,28},{24,16},{28,20},{1,9},{5... | collective-permute-start | bytes 196616 | tf_op jit(solution)/shard_map/ppermute | solution.py:168
  78.7 1.4 %collective-permute-start.30 = (f32[2,128,128]{2,1,0:T(8,128)S(1)}, f32[2,128,128]{2,1,0:T(8,128)S(1)}, u32[]{:S(2)}, u32[]{:S(2)}) collective-permute-start(f32[2,128,128]{2,1,0:T(8,128)S(1)} %add_add_fusion.own), channel_id=1, source_target_pairs={{0,4},{4,0},{8,12},{12,8},{16,20},{20,16},{24,28},{28,24},{1,5},{5... | collective-permute-start | bytes 393224 | tf_op jit(solution)/shard_map/ppermute | solution.py:168

commit v3 on v2

--- a/solution.py
+++ b/solution.py
@@ -9,7 +9,7 @@
 from jax.sharding import PartitionSpec as P
 
 STEPS = 3
-UNROLL = 16
+UNROLL = 64
 LEFT_MAX = 1.16462404
 RIGHT_MAX = 0.010778794
 VMEM = pl.BlockSpec(memory_space=pltpu.VMEM)
@@ -75,30 +75,19 @@
         copy.wait()
 
 
+def place(parts, whole, fill):
+    here = lax.axis_index("sectors")
+    held = parts[0].shape[0]
+    for mask, part in enumerate(parts):
+        for i in range(held):
+            g = (here ^ mask) * held + i
+            whole[g] = fill(g, part[i])
+
+
 def first_kernel(wire, *refs):
-    table, left, right, vec, pre, state, keep, send, blocks, acc = refs[-10:]
-    sectors, rows, cols = acc.shape
-    parts = (len(refs) - 10) // 2
-    mine, other = refs[:parts], refs[parts : 2 * parts]
-    held = sectors // parts
-    low = lax.axis_index("terms") % 2
-    here = lax.axis_index("sectors")
-
-    def load(trial, precond):
-        for mask in range(parts):
-            for i in range(held):
-                g = (here ^ mask) * held + i
-                vec[g] = jnp.where(live(table, g, acc), trial[mask][i], 0.0)
-                pre[g] = precond[mask][i]
-
-    @pl.when(low == 0)
-    def _():
-        load(mine, other)
-
-    @pl.when(low == 1)
-    def _():
-        load(other, mine)
-
+    table, left, right, vec, state, keep, send, blocks, acc = refs[-9:]
+    sectors, rows, cols = acc.shape
+    place(refs[:-9], vec, lambda g, block: jnp.where(live(table, g, acc), block, 0.0))
     tile = jnp.zeros((8, cols), F32)
     for g in range(sectors):
         v = vec[g]
@@ -133,9 +122,13 @@
     return rayleigh, scale
 
 
-def middle_kernel(wire, step, own, far, vec_in, pre, state_in, table, left, right,
-                  vec, state, keep, send, full, blocks, acc):
-    sectors, rows, cols = acc.shape
+def middle_kernel(wire, step, parts, own, far, vec_in, state_in, table, left, right, *refs):
+    vec, state, keep, send, full, blocks, acc = refs[-7:]
+    sectors, rows, cols = acc.shape
+    pre = refs[0]
+    if parts > 1:
+        pre = refs[parts]
+        place(refs[:parts], pre, lambda g, block: block)
     old = state_in[...]
     rayleigh, scale = update(wire, own, far, table, vec_in, pre, old[0:1, 0:1], full, vec)
     tile = jnp.zeros((8, cols), F32)
@@ -150,14 +143,15 @@
     apply_ops(wire, square, blocks, acc, table, left, right, keep, send)
 
 
-def last_kernel(wire, step, own, far, vec_in, pre, state_in, table, out, energies, full, fresh):
+def last_kernel(wire, step, own, far, vec_in, state_in, table, pre, out, energies, full, fresh):
     held = out.shape[0]
     old = state_in[...]
     rayleigh, scale = update(wire, own, far, table, vec_in, pre, old[0:1, 0:1], full, fresh)
     first = lax.axis_index("sectors") * held
     out[...] = fresh[pl.ds(first, held)] * scale[None]
-    line = lax.broadcasted_iota(jnp.int32, old.shape, 0)
-    energies[...] = jnp.where(line == step, rayleigh, old)
+    for i in range(1, step):
+        energies[i - 1] = jnp.sum(old[i : i + 1, 0:1])
+    energies[step - 1] = jnp.sum(rayleigh)
 
 
 def params():
@@ -183,7 +177,7 @@
 
 def reduce_half(keep, send):
     x = keep + swap(send, "terms", 1)
-    for axis, first in (("sectors", 0), ("terms", 1)):
+    for axis, first in (("terms", 1), ("sectors", 0)):
         for low, bits in bit_groups(axis, first):
             x = sum_stage(lax.optimization_barrier(x.astype(HALF)), axis, low, bits)
     return x
@@ -217,40 +211,44 @@
         cost_estimate=pl.CostEstimate(flops=0, bytes_accessed=4 * left_ops.size, transcendentals=0),
     )(*(pltpu.with_memory_space_constraint(x, pltpu.HBM) for x in (block_rows, owner_map, term_in, term_out, left_ops, right_ops)))
 
-    picked = jnp.where(lax.axis_index("terms") % 2 == 0, trial, precond)
-    mine = [picked] + [swap(picked, "sectors", mask) for mask in range(1, lax.axis_size("sectors"))]
+    masks = range(1, lax.axis_size("sectors"))
+    mine = [trial] + [swap(trial, "sectors", mask) for mask in masks]
+    precond, left, right, table = lax.optimization_barrier((precond, left, right, table))
+    pre = [precond] + [swap(precond, "sectors", mask) for mask in masks]
     mine, (left, right, table) = lax.optimization_barrier((mine, (left, right, table)))
-    other = [swap(x, "terms", 1) for x in mine]
-    vec, pre, state, keep, send = pl.pallas_call(
+    vec, state, keep, send = pl.pallas_call(
         functools.partial(first_kernel, wire),
-        out_shape=(whole, whole, state_shape, part, part),
-        in_specs=[VMEM] * (2 * len(mine)) + [SMEM] + [VMEM] * 2,
-        out_specs=(VMEM,) * 5,
+        out_shape=(whole, state_shape, part, part),
+        in_specs=[VMEM] * len(mine) + [SMEM] + [VMEM] * 2,
+        out_specs=(VMEM,) * 4,
         scratch_shapes=scratch,
         compiler_params=params(),
-    )(*mine, *other, table, left, right)
+    )(*mine, table, left, right)
+    pre, (keep, send) = lax.optimization_barrier((pre, (keep, send)))
     for step in range(1, STEPS):
         own = reduce_half(keep, send)
         far = swap(own, "terms", 1)
-        vec, state, keep, send = pl.pallas_call(
-            functools.partial(middle_kernel, wire, step),
-            out_shape=(whole, state_shape, part, part),
-            in_specs=[VMEM] * 5 + [SMEM] + [VMEM] * 2,
-            out_specs=(VMEM,) * 4,
+        placed = [whole] if len(pre) > 1 else []
+        got = pl.pallas_call(
+            functools.partial(middle_kernel, wire, step, len(pre)),
+            out_shape=(*placed, whole, state_shape, part, part),
+            in_specs=[VMEM] * 4 + [SMEM] + [VMEM] * (2 + len(pre)),
+            out_specs=(VMEM,) * (4 + len(placed)),
             scratch_shapes=[full] + scratch,
             compiler_params=params(),
-        )(own, far, vec, pre, state, table, left, right)
+        )(own, far, vec, state, table, left, right, *pre)
+        pre = [got[0]] if placed else pre
+        vec, state, keep, send = got[-4:]
     own = reduce_half(keep, send)
     far = swap(own, "terms", 1)
-    vector, energies = pl.pallas_call(
+    return pl.pallas_call(
         functools.partial(last_kernel, wire, STEPS),
-        out_shape=(jax.ShapeDtypeStruct(trial.shape, F32), state_shape),
-        in_specs=[VMEM] * 5 + [SMEM],
-        out_specs=(VMEM,) * 2,
+        out_shape=(jax.ShapeDtypeStruct(trial.shape, F32), jax.ShapeDtypeStruct((STEPS,), F32)),
+        in_specs=[VMEM] * 4 + [SMEM] + [VMEM] * len(pre),
+        out_specs=(VMEM, SMEM),
         scratch_shapes=[full, full],
         compiler_params=params(),
-    )(own, far, vec, pre, state, table)
-    return vector, energies[1 : STEPS + 1, 0]
+    )(own, far, vec, state, table, *pre)
 
 
 def solution(mesh):

time: 82.4 us -> 80.3 us (0.975)
  starting transfers between devices: 31.9 us -> 34.9 us
  Pallas kernels: 13.9 us -> 11.3 us
  waiting for transfers between devices: 34 us -> 32.8 us
  other arithmetic: 1.15 us -> 0.3 us
    ppermute x31 -> x30, starting transfers between devices: 31.9 us -> 34.9 us  [swap(): lax.ppermute(x, axis, [(i, i ^ mask) for i in range(lax.axis_size(axis))])]
    pallas_call x3, Pallas kernels: 9.39 us -> 6.86 us  [the longest x2 4.88 us: on_device(): pl.pallas_call(functools.partial(middle_kernel, wire, step, len(pre)), ou...]
    ppermute x31 -> x30, waiting for transfers between devices: 34 us -> 32.8 us  [swap(): lax.ppermute(x, axis, [(i, i ^ mask) for i in range(lax.axis_size(axis))])]
    select_n x1 -> x0, other arithmetic: 0.86 us -> none  [on_device(): picked = jnp.where(lax.axis_index('terms') % 2 == 0, trial, precond)]
  transfers between devices with their start and end apart: 31 -> 30, of which waited for: 26 -> 23; matrix products, arithmetic and copies ran while one was open for 0% -> 0% of each run, Pallas kernels for 3% -> 6%
where the time goes in v3:
time: 80.3 us; the launch traced here: 80.1 us
  starting transfers between devices  34.9 us (43%)
  waiting for transfers between devices  32.8 us (41%)
  Pallas kernels  11.3 us (14%)
    ppermute x30, starting transfers between devices, swap(): lax.ppermute(x, axis, [(i, i ^ mask) for i in range(lax.axis_size(axis))])  34.9 us
    ppermute x30, waiting for transfers between devices, swap(): lax.ppermute(x, axis, [(i, i ^ mask) for i in range(lax.axis_size(axis))])  32.8 us
    pallas_call x2, Pallas kernels, on_device(): pl.pallas_call(functools.partial(middle_kernel, wire, step, len(pre)), ou...  4.88 us
    pallas_call x1, Pallas kernels, on_device(): pl.pallas_call(load_kernel, out_shape=(jax.ShapeDtypeStruct(left_ops.shap...  2.88 us
    pallas_call x1, Pallas kernels, on_device(): pl.pallas_call(functools.partial(first_kernel, wire), out_shape=(whole, s...  1.98 us
  transfers between devices with their start and end apart: 30, of which 23 were waited for; matrix products, arithmetic and copies ran while one was open for 0% of the time, Pallas kernels for 6%

profile of v3, /device:TPU:0, one launch (start us, length us, event | category | flops | bytes accessed | tf_op | source)
XLA Modules:
  0.0 80.1 jit_solution(5775162858785430638)
XLA Ops:
  0.7 4.1 %collective-permute-start.4 = (f32[1,128,128]{2,1,0:T(8,128)}, f32[1,128,128]{2,1,0:T(8,128)S(1)}, u32[]{:S(2)}, u32[]{:S(2)}) collective-permute-start(f32[1,128,128]{2,1,0:T(8,128)} %refs_0_), channel_id=1, source_target_pairs={{0,2},{1,3},{2,0},{3,1},{4,6},{5,7},{6,4},{7,5},{8,10},{9,11},{10,... | collective-permute-start | bytes 196616 | tf_op jit(solution)/shard_map/ppermute | solution.py:162
  4.8 1.6 %collective-permute-start.3 = (f32[1,128,128]{2,1,0:T(8,128)}, f32[1,128,128]{2,1,0:T(8,128)S(1)}, u32[]{:S(2)}, u32[]{:S(2)}) collective-permute-start(f32[1,128,128]{2,1,0:T(8,128)} %refs_0_), channel_id=1, source_target_pairs={{0,1},{1,0},{2,3},{3,2},{4,5},{5,4},{6,7},{7,6},{8,9},{9,8},{10,11... | collective-permute-start | bytes 196616 | tf_op jit(solution)/shard_map/ppermute | solution.py:162
  6.3 2.9 %shard_map.95 = (bf16[64,128,128]{2,1,0:T(8,128)(2,1)S(1)}, bf16[64,128,128]{2,1,0:T(8,128)(2,1)S(1)}, s32[132]{0:T(256)S(1)}) custom-call(s32[4]{0:T(128)} %rows_hbm.1, s32[4]{0:T(128)} %owner_hbm.1, s32[64]{0:T(128)} %in_hbm.1, s32[64]{0:T(128)} %out_hbm.1, bf16[64,128,128]{2,1,0:T(8,128)(2,1)} %left_hbm.1, bf16[64,128,128]{2,1,0:T(8,128)(2,1)} %right_hbm.1), custom_call_target="tpu_custom_call" | custom-call | bytes 4194304 | tf_op jit(solution)/shard_map/pallas_call | solution.py:200
  9.2 3.9 %collective-permute-start.2 = (f32[1,128,128]{2,1,0:T(8,128)S(1)}, f32[1,128,128]{2,1,0:T(8,128)S(1)}, u32[]{:S(2)}, u32[]{:S(2)}) collective-permute-start(f32[1,128,128]{2,1,0:T(8,128)S(1)} %copy-done.1), channel_id=1, source_target_pairs={{0,3},{1,2},{2,1},{3,0},{4,7},{5,6},{6,5},{7,4},{8,11},{9,10},{10,... | collective-permute-start | bytes 196616 | tf_op jit(solution)/shard_map/ppermute | solution.py:162
  13.1 0.6 collective-permute-start
  13.8 2.0 %shard_map.96 = (f32[4,128,128]{2,1,0:T(8,128)S(1)}, f32[8,128]{1,0:T(8,128)S(1)}, f32[2,128,128]{2,1,0:T(8,128)S(1)}, f32[2,128,128]{2,1,0:T(8,128)S(1)}) custom-call(f32[1,128,128]{2,1,0:T(8,128)S(1)} %copy-done, f32[1,128,128]{2,1,0:T(8,128)S(1)} %collective-permute-done.3.refs_1_, f32[1,128,128]{2,1,0:T(8,128)S(1)} %collective-permute-done.4.refs_2_, ...), custom_call_target="tpu_custom_call" | custom-call | tf_op jit(solution)/shard_map/pallas_call | solution.py:219
  15.8 2.6 %collective-permute-done.1.refs_2_ = f32[1,128,128]{2,1,0:T(8,128)S(1)} collective-permute-done((f32[1,128,128]{2,1,0:T(8,128)S(1)}, f32[1,128,128]{2,1,0:T(8,128)S(1)}, u32[]{:S(2)}, u32[]{:S(2)}) %collective-permute-start.1) | collective-permute-done | bytes 65568 | tf_op jit(solution)/shard_map/ppermute | solution.py:162
  18.5 1.3 %collective-permute-done.6 = f32[2,128,128]{2,1,0:T(8,128)S(1)} collective-permute-done((f32[2,128,128]{2,1,0:T(8,128)S(1)}, f32[2,128,128]{2,1,0:T(8,128)S(1)}, u32[]{:S(2)}, u32[]{:S(2)}) %collective-permute-start.6) | collective-permute-done | bytes 131104 | tf_op jit(solution)/shard_map/ppermute | solution.py:162
  19.9 2.6 %collective-permute-start.9 = (f16[2,128,128]{2,1,0:T(8,128)(2,1)S(1)}, f16[2,128,128]{2,1,0:T(8,128)(2,1)S(1)}, u32[]{:S(2)}, u32[]{:S(2)}) collective-permute-start(f16[2,128,128]{2,1,0:T(8,128)(2,1)S(1)} %add_convert_fusion.5), channel_id=1, source_target_pairs={{0,24},{4,28},{8,16},{12,20},{16,8},{20,12},{24,0},{28,4},{1,25},{... | collective-permute-start | bytes 196616 | tf_op jit(solution)/shard_map/ppermute | solution.py:162
  22.5 0.5 collective-permute-start.8
  23.0 0.5 collective-permute-start.7
  23.4 1.7 %collective-permute-done.9 = f16[2,128,128]{2,1,0:T(8,128)(2,1)S(1)} collective-permute-done((f16[2,128,128]{2,1,0:T(8,128)(2,1)S(1)}, f16[2,128,128]{2,1,0:T(8,128)(2,1)S(1)}, u32[]{:S(2)}, u32[]{:S(2)}) %collective-permute-start.9) | collective-permute-done | bytes 65568 | tf_op jit(solution)/shard_map/ppermute | solution.py:162
  25.1 1.6 %collective-permute-done.8 = f16[2,128,128]{2,1,0:T(8,128)(2,1)S(1)} collective-permute-done((f16[2,128,128]{2,1,0:T(8,128)(2,1)S(1)}, f16[2,128,128]{2,1,0:T(8,128)(2,1)S(1)}, u32[]{:S(2)}, u32[]{:S(2)}) %collective-permute-start.8) | collective-permute-done | bytes 65568 | tf_op jit(solution)/shard_map/ppermute | solution.py:162
  26.7 0.5 collective-permute-done.7
  27.3 2.1 %collective-permute-start.12 = (f16[2,128,128]{2,1,0:T(8,128)(2,1)S(1)}, f16[2,128,128]{2,1,0:T(8,128)(2,1)S(1)}, u32[]{:S(2)}, u32[]{:S(2)}) collective-permute-start(f16[2,128,128]{2,1,0:T(8,128)(2,1)S(1)} %add_convert_fusion.4), channel_id=1, source_target_pairs={{0,3},{1,2},{2,1},{3,0},{4,7},{5,6},{6,5},{7,4},{8,11},{9,10},{10,... | collective-permute-start | bytes 196616 | tf_op jit(solution)/shard_map/ppermute | solution.py:162
  29.4 2.4 %collective-permute-start.10 = (f16[2,128,128]{2,1,0:T(8,128)(2,1)S(1)}, f16[2,128,128]{2,1,0:T(8,128)(2,1)S(1)}, u32[]{:S(2)}, u32[]{:S(2)}) collective-permute-start(f16[2,128,128]{2,1,0:T(8,128)(2,1)S(1)} %add_convert_fusion.4), channel_id=1, source_target_pairs={{0,1},{1,0},{2,3},{3,2},{4,5},{5,4},{6,7},{7,6},{8,9},{9,8},{10,11... | collective-permute-start | bytes 196616 | tf_op jit(solution)/shard_map/ppermute | solution.py:162
  31.7 2.0 %collective-permute-done.12 = f16[2,128,128]{2,1,0:T(8,128)(2,1)S(1)} collective-permute-done((f16[2,128,128]{2,1,0:T(8,128)(2,1)S(1)}, f16[2,128,128]{2,1,0:T(8,128)(2,1)S(1)}, u32[]{:S(2)}, u32[]{:S(2)}) %collective-permute-start.12) | collective-permute-done | bytes 65568 | tf_op jit(solution)/shard_map/ppermute | solution.py:162
  33.7 1.5 %collective-permute-done.11 = f16[2,128,128]{2,1,0:T(8,128)(2,1)S(1)} collective-permute-done((f16[2,128,128]{2,1,0:T(8,128)(2,1)S(1)}, f16[2,128,128]{2,1,0:T(8,128)(2,1)S(1)}, u32[]{:S(2)}, u32[]{:S(2)}) %collective-permute-start.11) | collective-permute-done | bytes 65568 | tf_op jit(solution)/shard_map/ppermute | solution.py:162
  35.3 1.3 %collective-permute-done.13.far = f32[2,128,128]{2,1,0:T(8,128)S(1)} collective-permute-done((f32[2,128,128]{2,1,0:T(8,128)S(1)}, f32[2,128,128]{2,1,0:T(8,128)S(1)}, u32[]{:S(2)}, u32[]{:S(2)}) %collective-permute-start.13) | collective-permute-done | bytes 131104 | tf_op jit(solution)/shard_map/ppermute | solution.py:162
  36.6 2.4 %shard_map.97 = (f32[4,128,128]{2,1,0:T(8,128)S(1)}, f32[4,128,128]{2,1,0:T(8,128)S(1)}, f32[8,128]{1,0:T(8,128)S(1)}, f32[2,128,128]{2,1,0:T(8,128)S(1)}, f32[2,128,128]{2,1,0:T(8,128)S(1)}) custom-call(f32[2,128,128]{2,1,0:T(8,128)S(1)} %add_add_fusion.2.own, f32[2,128,128]{2,1,0:T(8,128)S(1)} %collective-permute-done.13.far, ...), custom_call_target="tpu_custom_call" | custom-call | tf_op jit(solution)/shard_map/pallas_call | solution.py:232
  39.1 0.2 collective-permute-start.14
  39.3 1.2 %collective-permute-done.14 = f32[2,128,128]{2,1,0:T(8,128)S(1)} collective-permute-done((f32[2,128,128]{2,1,0:T(8,128)S(1)}, f32[2,128,128]{2,1,0:T(8,128)S(1)}, u32[]{:S(2)}, u32[]{:S(2)}) %collective-permute-start.14) | collective-permute-done | bytes 131104 | tf_op jit(solution)/shard_map/ppermute | solution.py:162
  40.5 1.8 %collective-permute-start.17 = (f16[2,128,128]{2,1,0:T(8,128)(2,1)S(1)}, f16[2,128,128]{2,1,0:T(8,128)(2,1)S(1)}, u32[]{:S(2)}, u32[]{:S(2)}) collective-permute-start(f16[2,128,128]{2,1,0:T(8,128)(2,1)S(1)} %add_convert_fusion.3), channel_id=1, source_target_pairs={{0,24},{4,28},{8,16},{12,20},{16,8},{20,12},{24,0},{28,4},{1,25},{... | collective-permute-start | bytes 196616 | tf_op jit(solution)/shard_map/ppermute | solution.py:162
  42.3 1.2 %collective-permute-start.16 = (f16[2,128,128]{2,1,0:T(8,128)(2,1)S(1)}, f16[2,128,128]{2,1,0:T(8,128)(2,1)S(1)}, u32[]{:S(2)}, u32[]{:S(2)}) collective-permute-start(f16[2,128,128]{2,1,0:T(8,128)(2,1)S(1)} %add_convert_fusion.3), channel_id=1, source_target_pairs={{0,16},{4,20},{8,24},{12,28},{16,0},{20,4},{24,8},{28,12},{1,17},{... | collective-permute-start | bytes 196616 | tf_op jit(solution)/shard_map/ppermute | solution.py:162
  43.5 0.6 collective-permute-start.15
  44.1 1.7 %collective-permute-done.17 = f16[2,128,128]{2,1,0:T(8,128)(2,1)S(1)} collective-permute-done((f16[2,128,128]{2,1,0:T(8,128)(2,1)S(1)}, f16[2,128,128]{2,1,0:T(8,128)(2,1)S(1)}, u32[]{:S(2)}, u32[]{:S(2)}) %collective-permute-start.17) | collective-permute-done | bytes 65568 | tf_op jit(solution)/shard_map/ppermute | solution.py:162
  45.8 1.2 %collective-permute-done.16 = f16[2,128,128]{2,1,0:T(8,128)(2,1)S(1)} collective-permute-done((f16[2,128,128]{2,1,0:T(8,128)(2,1)S(1)}, f16[2,128,128]{2,1,0:T(8,128)(2,1)S(1)}, u32[]{:S(2)}, u32[]{:S(2)}) %collective-permute-start.16) | collective-permute-done | bytes 65568 | tf_op jit(solution)/shard_map/ppermute | solution.py:162
  47.0 0.7 collective-permute-done.15
  47.8 2.7 %collective-permute-start.20 = (f16[2,128,128]{2,1,0:T(8,128)(2,1)S(1)}, f16[2,128,128]{2,1,0:T(8,128)(2,1)S(1)}, u32[]{:S(2)}, u32[]{:S(2)}) collective-permute-start(f16[2,128,128]{2,1,0:T(8,128)(2,1)S(1)} %add_convert_fusion.2), channel_id=1, source_target_pairs={{0,3},{1,2},{2,1},{3,0},{4,7},{5,6},{6,5},{7,4},{8,11},{9,10},{10,... | collective-permute-start | bytes 196616 | tf_op jit(solution)/shard_map/ppermute | solution.py:162
  50.5 1.8 %collective-permute-start.18 = (f16[2,128,128]{2,1,0:T(8,128)(2,1)S(1)}, f16[2,128,128]{2,1,0:T(8,128)(2,1)S(1)}, u32[]{:S(2)}, u32[]{:S(2)}) collective-permute-start(f16[2,128,128]{2,1,0:T(8,128)(2,1)S(1)} %add_convert_fusion.2), channel_id=1, source_target_pairs={{0,1},{1,0},{2,3},{3,2},{4,5},{5,4},{6,7},{7,6},{8,9},{9,8},{10,11... | collective-permute-start | bytes 196616 | tf_op jit(solution)/shard_map/ppermute | solution.py:162
  52.3 2.1 %collective-permute-done.20 = f16[2,128,128]{2,1,0:T(8,128)(2,1)S(1)} collective-permute-done((f16[2,128,128]{2,1,0:T(8,128)(2,1)S(1)}, f16[2,128,128]{2,1,0:T(8,128)(2,1)S(1)}, u32[]{:S(2)}, u32[]{:S(2)}) %collective-permute-start.20) | collective-permute-done | bytes 65568 | tf_op jit(solution)/shard_map/ppermute | solution.py:162
  54.3 1.7 %collective-permute-done.19 = f16[2,128,128]{2,1,0:T(8,128)(2,1)S(1)} collective-permute-done((f16[2,128,128]{2,1,0:T(8,128)(2,1)S(1)}, f16[2,128,128]{2,1,0:T(8,128)(2,1)S(1)}, u32[]{:S(2)}, u32[]{:S(2)}) %collective-permute-start.19) | collective-permute-done | bytes 65568 | tf_op jit(solution)/shard_map/ppermute | solution.py:162
  56.2 1.3 %collective-permute-done.21.far = f32[2,128,128]{2,1,0:T(8,128)S(1)} collective-permute-done((f32[2,128,128]{2,1,0:T(8,128)S(1)}, f32[2,128,128]{2,1,0:T(8,128)S(1)}, u32[]{:S(2)}, u32[]{:S(2)}) %collective-permute-start.21) | collective-permute-done | bytes 131104 | tf_op jit(solution)/shard_map/ppermute | solution.py:162
  57.5 2.4 %shard_map.98 = (f32[4,128,128]{2,1,0:T(8,128)S(1)}, f32[8,128]{1,0:T(8,128)S(1)}, f32[2,128,128]{2,1,0:T(8,128)S(1)}, f32[2,128,128]{2,1,0:T(8,128)S(1)}) custom-call(f32[2,128,128]{2,1,0:T(8,128)S(1)} %add_add_fusion.1.own, f32[2,128,128]{2,1,0:T(8,128)S(1)} %collective-permute-done.21.far, f32[4,128,128]{2,1,0:T(8,128)S(1)} %get-tuple-element.61.vec_in, ...), custom_call_target="tpu_custom_call" | custom-call | tf_op jit(solution)/shard_map/pallas_call | solution.py:232
  60.0 0.2 collective-permute-start.22
  60.2 1.2 %collective-permute-done.22 = f32[2,128,128]{2,1,0:T(8,128)S(1)} collective-permute-done((f32[2,128,128]{2,1,0:T(8,128)S(1)}, f32[2,128,128]{2,1,0:T(8,128)S(1)}, u32[]{:S(2)}, u32[]{:S(2)}) %collective-permute-start.22) | collective-permute-done | bytes 131104 | tf_op jit(solution)/shard_map/ppermute | solution.py:162
  61.4 2.2 %collective-permute-start.25 = (f16[2,128,128]{2,1,0:T(8,128)(2,1)S(1)}, f16[2,128,128]{2,1,0:T(8,128)(2,1)S(1)}, u32[]{:S(2)}, u32[]{:S(2)}) collective-permute-start(f16[2,128,128]{2,1,0:T(8,128)(2,1)S(1)} %add_convert_fusion.1), channel_id=1, source_target_pairs={{0,24},{4,28},{8,16},{12,20},{16,8},{20,12},{24,0},{28,4},{1,25},{... | collective-permute-start | bytes 196616 | tf_op jit(solution)/shard_map/ppermute | solution.py:162
  63.5 0.5 collective-permute-start.24
  64.1 0.9 %collective-permute-start.23 = (f16[2,128,128]{2,1,0:T(8,128)(2,1)S(1)}, f16[2,128,128]{2,1,0:T(8,128)(2,1)S(1)}, u32[]{:S(2)}, u32[]{:S(2)}) collective-permute-start(f16[2,128,128]{2,1,0:T(8,128)(2,1)S(1)} %add_convert_fusion.1), channel_id=1, source_target_pairs={{0,8},{4,12},{8,0},{12,4},{16,24},{20,28},{24,16},{28,20},{1,9},{5... | collective-permute-start | bytes 196616 | tf_op jit(solution)/shard_map/ppermute | solution.py:162
  65.0 1.7 %collective-permute-done.25 = f16[2,128,128]{2,1,0:T(8,128)(2,1)S(1)} collective-permute-done((f16[2,128,128]{2,1,0:T(8,128)(2,1)S(1)}, f16[2,128,128]{2,1,0:T(8,128)(2,1)S(1)}, u32[]{:S(2)}, u32[]{:S(2)}) %collective-permute-start.25) | collective-permute-done | bytes 65568 | tf_op jit(solution)/shard_map/ppermute | solution.py:162
  66.7 1.3 %collective-permute-done.24 = f16[2,128,128]{2,1,0:T(8,128)(2,1)S(1)} collective-permute-done((f16[2,128,128]{2,1,0:T(8,128)(2,1)S(1)}, f16[2,128,128]{2,1,0:T(8,128)(2,1)S(1)}, u32[]{:S(2)}, u32[]{:S(2)}) %collective-permute-start.24) | collective-permute-done | bytes 65568 | tf_op jit(solution)/shard_map/ppermute | solution.py:162
  68.0 0.3 collective-permute-done.23
  68.4 2.5 %collective-permute-start.28 = (f16[2,128,128]{2,1,0:T(8,128)(2,1)S(1)}, f16[2,128,128]{2,1,0:T(8,128)(2,1)S(1)}, u32[]{:S(2)}, u32[]{:S(2)}) collective-permute-start(f16[2,128,128]{2,1,0:T(8,128)(2,1)S(1)} %add_convert_fusion), channel_id=1, source_target_pairs={{0,3},{1,2},{2,1},{3,0},{4,7},{5,6},{6,5},{7,4},{8,11},{9,10},{10,... | collective-permute-start | bytes 196616 | tf_op jit(solution)/shard_map/ppermute | solution.py:162
  70.9 2.0 %collective-permute-start.26 = (f16[2,128,128]{2,1,0:T(8,128)(2,1)S(1)}, f16[2,128,128]{2,1,0:T(8,128)(2,1)S(1)}, u32[]{:S(2)}, u32[]{:S(2)}) collective-permute-start(f16[2,128,128]{2,1,0:T(8,128)(2,1)S(1)} %add_convert_fusion), channel_id=1, source_target_pairs={{0,1},{1,0},{2,3},{3,2},{4,5},{5,4},{6,7},{7,6},{8,9},{9,8},{10,11... | collective-permute-start | bytes 196616 | tf_op jit(solution)/shard_map/ppermute | solution.py:162
  72.8 2.1 %collective-permute-done.28 = f16[2,128,128]{2,1,0:T(8,128)(2,1)S(1)} collective-permute-done((f16[2,128,128]{2,1,0:T(8,128)(2,1)S(1)}, f16[2,128,128]{2,1,0:T(8,128)(2,1)S(1)}, u32[]{:S(2)}, u32[]{:S(2)}) %collective-permute-start.28) | collective-permute-done | bytes 65568 | tf_op jit(solution)/shard_map/ppermute | solution.py:162
  74.9 2.2 %collective-permute-done.27 = f16[2,128,128]{2,1,0:T(8,128)(2,1)S(1)} collective-permute-done((f16[2,128,128]{2,1,0:T(8,128)(2,1)S(1)}, f16[2,128,128]{2,1,0:T(8,128)(2,1)S(1)}, u32[]{:S(2)}, u32[]{:S(2)}) %collective-permute-start.27) | collective-permute-done | bytes 65568 | tf_op jit(solution)/shard_map/ppermute | solution.py:162
  77.2 1.3 %collective-permute-done.29.far = f32[2,128,128]{2,1,0:T(8,128)S(1)} collective-permute-done((f32[2,128,128]{2,1,0:T(8,128)S(1)}, f32[2,128,128]{2,1,0:T(8,128)S(1)}, u32[]{:S(2)}, u32[]{:S(2)}) %collective-permute-start.29) | collective-permute-done | bytes 131104 | tf_op jit(solution)/shard_map/ppermute | solution.py:162
  78.5 1.6 %shard_map.99 = (f32[1,128,128]{2,1,0:T(8,128)}, f32[3]{0:T(128)}) custom-call(f32[2,128,128]{2,1,0:T(8,128)S(1)} %add_add_fusion.own, f32[2,128,128]{2,1,0:T(8,128)S(1)} %collective-permute-done.29.far, f32[4,128,128]{2,1,0:T(8,128)S(1)} %get-tuple-element.66.vec_in, f32[8,128]{1,0:T(8,128)S(1)} %get-tuple-element.67.state_in, ...), custom_call_target="tpu_custom_call" | custom-call | tf_op jit(solution)/shard_map/pallas_call | solution.py:244
  (30 shorter events, 0.7 us)
Async XLA Ops:
  0.6 13.1 %copy-start = (f32[1,128,128]{2,1,0:T(8,128)S(1)}, f32[1,128,128]{2,1,0:T(8,128)}, u32[]{:S(2)}) copy-start(f32[1,128,128]{2,1,0:T(8,128)} %refs_0_) | copy-start | bytes 196612
  0.6 8.6 %copy-start.1 = (f32[1,128,128]{2,1,0:T(8,128)S(1)}, f32[1,128,128]{2,1,0:T(8,128)}, u32[]{:S(2)}) copy-start(f32[1,128,128]{2,1,0:T(8,128)} %refs_0_.1) | copy-start | bytes 196612
  0.7 12.5 %collective-permute-start.4 = (f32[1,128,128]{2,1,0:T(8,128)}, f32[1,128,128]{2,1,0:T(8,128)S(1)}, u32[]{:S(2)}, u32[]{:S(2)}) collective-permute-start(f32[1,128,128]{2,1,0:T(8,128)} %refs_0_), channel_id=1, source_target_pairs={{0,2},{1,3},{2,0},{3,1},{4,6},{5,7},{6,4},{7,5},{8,10},{9,11},{10,... | collective-permute-start | bytes 196616 | tf_op jit(solution)/shard_map/ppermute | solution.py:162
  4.8 9.0 %collective-permute-start.3 = (f32[1,128,128]{2,1,0:T(8,128)}, f32[1,128,128]{2,1,0:T(8,128)S(1)}, u32[]{:S(2)}, u32[]{:S(2)}) collective-permute-start(f32[1,128,128]{2,1,0:T(8,128)} %refs_0_), channel_id=1, source_target_pairs={{0,1},{1,0},{2,3},{3,2},{4,5},{5,4},{6,7},{7,6},{8,9},{9,8},{10,11... | collective-permute-start | bytes 196616 | tf_op jit(solution)/shard_map/ppermute | solution.py:162
  6.3 7.4 %collective-permute-start.5 = (f32[1,128,128]{2,1,0:T(8,128)}, f32[1,128,128]{2,1,0:T(8,128)S(1)}, u32[]{:S(2)}, u32[]{:S(2)}) collective-permute-start(f32[1,128,128]{2,1,0:T(8,128)} %refs_0_), channel_id=1, source_target_pairs={{0,3},{1,2},{2,1},{3,0},{4,7},{5,6},{6,5},{7,4},{8,11},{9,10},{10,... | collective-permute-start | bytes 196616 | tf_op jit(solution)/shard_map/ppermute | solution.py:162
  9.2 6.5 %collective-permute-start.2 = (f32[1,128,128]{2,1,0:T(8,128)S(1)}, f32[1,128,128]{2,1,0:T(8,128)S(1)}, u32[]{:S(2)}, u32[]{:S(2)}) collective-permute-start(f32[1,128,128]{2,1,0:T(8,128)S(1)} %copy-done.1), channel_id=1, source_target_pairs={{0,3},{1,2},{2,1},{3,0},{4,7},{5,6},{6,5},{7,4},{8,11},{9,10},{10,... | collective-permute-start | bytes 196616 | tf_op jit(solution)/shard_map/ppermute | solution.py:162
  13.1 5.2 %collective-permute-start.1 = (f32[1,128,128]{2,1,0:T(8,128)S(1)}, f32[1,128,128]{2,1,0:T(8,128)S(1)}, u32[]{:S(2)}, u32[]{:S(2)}) collective-permute-start(f32[1,128,128]{2,1,0:T(8,128)S(1)} %copy-done.1), channel_id=1, source_target_pairs={{0,2},{1,3},{2,0},{3,1},{4,6},{5,7},{6,4},{7,5},{8,10},{9,11},{10,... | collective-permute-start | bytes 196616 | tf_op jit(solution)/shard_map/ppermute | solution.py:162
  13.1 5.4 %collective-permute-start = (f32[1,128,128]{2,1,0:T(8,128)S(1)}, f32[1,128,128]{2,1,0:T(8,128)S(1)}, u32[]{:S(2)}, u32[]{:S(2)}) collective-permute-start(f32[1,128,128]{2,1,0:T(8,128)S(1)} %copy-done.1), channel_id=1, source_target_pairs={{0,1},{1,0},{2,3},{3,2},{4,5},{5,4},{6,7},{7,6},{8,9},{9,8},{10,11... | collective-permute-start | bytes 196616 | tf_op jit(solution)/shard_map/ppermute | solution.py:162
  18.5 1.3 %collective-permute-start.6 = (f32[2,128,128]{2,1,0:T(8,128)S(1)}, f32[2,128,128]{2,1,0:T(8,128)S(1)}, u32[]{:S(2)}, u32[]{:S(2)}) collective-permute-start(f32[2,128,128]{2,1,0:T(8,128)S(1)} %get-tuple-element.52), channel_id=1, source_target_pairs={{0,4},{4,0},{8,12},{12,8},{16,20},{20,16},{24,28},{28,24},{1,5},{5... | collective-permute-start | bytes 393224 | tf_op jit(solution)/shard_map/ppermute | solution.py:162
  19.9 5.2 %collective-permute-start.9 = (f16[2,128,128]{2,1,0:T(8,128)(2,1)S(1)}, f16[2,128,128]{2,1,0:T(8,128)(2,1)S(1)}, u32[]{:S(2)}, u32[]{:S(2)}) collective-permute-start(f16[2,128,128]{2,1,0:T(8,128)(2,1)S(1)} %add_convert_fusion.5), channel_id=1, source_target_pairs={{0,24},{4,28},{8,16},{12,20},{16,8},{20,12},{24,0},{28,4},{1,25},{... | collective-permute-start | bytes 196616 | tf_op jit(solution)/shard_map/ppermute | solution.py:162
  22.5 4.3 %collective-permute-start.8 = (f16[2,128,128]{2,1,0:T(8,128)(2,1)S(1)}, f16[2,128,128]{2,1,0:T(8,128)(2,1)S(1)}, u32[]{:S(2)}, u32[]{:S(2)}) collective-permute-start(f16[2,128,128]{2,1,0:T(8,128)(2,1)S(1)} %add_convert_fusion.5), channel_id=1, source_target_pairs={{0,16},{4,20},{8,24},{12,28},{16,0},{20,4},{24,8},{28,12},{1,17},{... | collective-permute-start | bytes 196616 | tf_op jit(solution)/shard_map/ppermute | solution.py:162
  23.0 4.3 %collective-permute-start.7 = (f16[2,128,128]{2,1,0:T(8,128)(2,1)S(1)}, f16[2,128,128]{2,1,0:T(8,128)(2,1)S(1)}, u32[]{:S(2)}, u32[]{:S(2)}) collective-permute-start(f16[2,128,128]{2,1,0:T(8,128)(2,1)S(1)} %add_convert_fusion.5), channel_id=1, source_target_pairs={{0,8},{4,12},{8,0},{12,4},{16,24},{20,28},{24,16},{28,20},{1,9},{5... | collective-permute-start | bytes 196616 | tf_op jit(solution)/shard_map/ppermute | solution.py:162
  27.3 6.4 %collective-permute-start.12 = (f16[2,128,128]{2,1,0:T(8,128)(2,1)S(1)}, f16[2,128,128]{2,1,0:T(8,128)(2,1)S(1)}, u32[]{:S(2)}, u32[]{:S(2)}) collective-permute-start(f16[2,128,128]{2,1,0:T(8,128)(2,1)S(1)} %add_convert_fusion.4), channel_id=1, source_target_pairs={{0,3},{1,2},{2,1},{3,0},{4,7},{5,6},{6,5},{7,4},{8,11},{9,10},{10,... | collective-permute-start | bytes 196616 | tf_op jit(solution)/shard_map/ppermute | solution.py:162
  29.4 5.8 %collective-permute-start.11 = (f16[2,128,128]{2,1,0:T(8,128)(2,1)S(1)}, f16[2,128,128]{2,1,0:T(8,128)(2,1)S(1)}, u32[]{:S(2)}, u32[]{:S(2)}) collective-permute-start(f16[2,128,128]{2,1,0:T(8,128)(2,1)S(1)} %add_convert_fusion.4), channel_id=1, source_target_pairs={{0,2},{1,3},{2,0},{3,1},{4,6},{5,7},{6,4},{7,5},{8,10},{9,11},{10,... | collective-permute-start | bytes 196616 | tf_op jit(solution)/shard_map/ppermute | solution.py:162
  29.4 5.8 %collective-permute-start.10 = (f16[2,128,128]{2,1,0:T(8,128)(2,1)S(1)}, f16[2,128,128]{2,1,0:T(8,128)(2,1)S(1)}, u32[]{:S(2)}, u32[]{:S(2)}) collective-permute-start(f16[2,128,128]{2,1,0:T(8,128)(2,1)S(1)} %add_convert_fusion.4), channel_id=1, source_target_pairs={{0,1},{1,0},{2,3},{3,2},{4,5},{5,4},{6,7},{7,6},{8,9},{9,8},{10,11... | collective-permute-start | bytes 196616 | tf_op jit(solution)/shard_map/ppermute | solution.py:162
  35.2 1.4 %collective-permute-start.13 = (f32[2,128,128]{2,1,0:T(8,128)S(1)}, f32[2,128,128]{2,1,0:T(8,128)S(1)}, u32[]{:S(2)}, u32[]{:S(2)}) collective-permute-start(f32[2,128,128]{2,1,0:T(8,128)S(1)} %add_add_fusion.2.own), channel_id=1, source_target_pairs={{0,4},{4,0},{8,12},{12,8},{16,20},{20,16},{24,28},{28,24},{1,5},{5... | collective-permute-start | bytes 393224 | tf_op jit(solution)/shard_map/ppermute | solution.py:162
  39.1 1.4 %collective-permute-start.14 = (f32[2,128,128]{2,1,0:T(8,128)S(1)}, f32[2,128,128]{2,1,0:T(8,128)S(1)}, u32[]{:S(2)}, u32[]{:S(2)}) collective-permute-start(f32[2,128,128]{2,1,0:T(8,128)S(1)} %get-tuple-element.60), channel_id=1, source_target_pairs={{0,4},{4,0},{8,12},{12,8},{16,20},{20,16},{24,28},{28,24},{1,5},{5... | collective-permute-start | bytes 393224 | tf_op jit(solution)/shard_map/ppermute | solution.py:162
  40.5 5.3 %collective-permute-start.17 = (f16[2,128,128]{2,1,0:T(8,128)(2,1)S(1)}, f16[2,128,128]{2,1,0:T(8,128)(2,1)S(1)}, u32[]{:S(2)}, u32[]{:S(2)}) collective-permute-start(f16[2,128,128]{2,1,0:T(8,128)(2,1)S(1)} %add_convert_fusion.3), channel_id=1, source_target_pairs={{0,24},{4,28},{8,16},{12,20},{16,8},{20,12},{24,0},{28,4},{1,25},{... | collective-permute-start | bytes 196616 | tf_op jit(solution)/shard_map/ppermute | solution.py:162
  42.3 4.7 %collective-permute-start.16 = (f16[2,128,128]{2,1,0:T(8,128)(2,1)S(1)}, f16[2,128,128]{2,1,0:T(8,128)(2,1)S(1)}, u32[]{:S(2)}, u32[]{:S(2)}) collective-permute-start(f16[2,128,128]{2,1,0:T(8,128)(2,1)S(1)} %add_convert_fusion.3), channel_id=1, source_target_pairs={{0,16},{4,20},{8,24},{12,28},{16,0},{20,4},{24,8},{28,12},{1,17},{... | collective-permute-start | bytes 196616 | tf_op jit(solution)/shard_map/ppermute | solution.py:162
  43.5 4.3 %collective-permute-start.15 = (f16[2,128,128]{2,1,0:T(8,128)(2,1)S(1)}, f16[2,128,128]{2,1,0:T(8,128)(2,1)S(1)}, u32[]{:S(2)}, u32[]{:S(2)}) collective-permute-start(f16[2,128,128]{2,1,0:T(8,128)(2,1)S(1)} %add_convert_fusion.3), channel_id=1, source_target_pairs={{0,8},{4,12},{8,0},{12,4},{16,24},{20,28},{24,16},{28,20},{1,9},{5... | collective-permute-start | bytes 196616 | tf_op jit(solution)/shard_map/ppermute | solution.py:162
  47.8 6.5 %collective-permute-start.20 = (f16[2,128,128]{2,1,0:T(8,128)(2,1)S(1)}, f16[2,128,128]{2,1,0:T(8,128)(2,1)S(1)}, u32[]{:S(2)}, u32[]{:S(2)}) collective-permute-start(f16[2,128,128]{2,1,0:T(8,128)(2,1)S(1)} %add_convert_fusion.2), channel_id=1, source_target_pairs={{0,3},{1,2},{2,1},{3,0},{4,7},{5,6},{6,5},{7,4},{8,11},{9,10},{10,... | collective-permute-start | bytes 196616 | tf_op jit(solution)/shard_map/ppermute | solution.py:162
  50.5 5.6 %collective-permute-start.19 = (f16[2,128,128]{2,1,0:T(8,128)(2,1)S(1)}, f16[2,128,128]{2,1,0:T(8,128)(2,1)S(1)}, u32[]{:S(2)}, u32[]{:S(2)}) collective-permute-start(f16[2,128,128]{2,1,0:T(8,128)(2,1)S(1)} %add_convert_fusion.2), channel_id=1, source_target_pairs={{0,2},{1,3},{2,0},{3,1},{4,6},{5,7},{6,4},{7,5},{8,10},{9,11},{10,... | collective-permute-start | bytes 196616 | tf_op jit(solution)/shard_map/ppermute | solution.py:162
  50.5 5.6 %collective-permute-start.18 = (f16[2,128,128]{2,1,0:T(8,128)(2,1)S(1)}, f16[2,128,128]{2,1,0:T(8,128)(2,1)S(1)}, u32[]{:S(2)}, u32[]{:S(2)}) collective-permute-start(f16[2,128,128]{2,1,0:T(8,128)(2,1)S(1)} %add_convert_fusion.2), channel_id=1, source_target_pairs={{0,1},{1,0},{2,3},{3,2},{4,5},{5,4},{6,7},{7,6},{8,9},{9,8},{10,11... | collective-permute-start | bytes 196616 | tf_op jit(solution)/shard_map/ppermute | solution.py:162
  56.1 1.4 %collective-permute-start.21 = (f32[2,128,128]{2,1,0:T(8,128)S(1)}, f32[2,128,128]{2,1,0:T(8,128)S(1)}, u32[]{:S(2)}, u32[]{:S(2)}) collective-permute-start(f32[2,128,128]{2,1,0:T(8,128)S(1)} %add_add_fusion.1.own), channel_id=1, source_target_pairs={{0,4},{4,0},{8,12},{12,8},{16,20},{20,16},{24,28},{28,24},{1,5},{5... | collective-permute-start | bytes 393224 | tf_op jit(solution)/shard_map/ppermute | solution.py:162
  60.0 1.4 %collective-permute-start.22 = (f32[2,128,128]{2,1,0:T(8,128)S(1)}, f32[2,128,128]{2,1,0:T(8,128)S(1)}, u32[]{:S(2)}, u32[]{:S(2)}) collective-permute-start(f32[2,128,128]{2,1,0:T(8,128)S(1)} %get-tuple-element.65), channel_id=1, source_target_pairs={{0,4},{4,0},{8,12},{12,8},{16,20},{20,16},{24,28},{28,24},{1,5},{5... | collective-permute-start | bytes 393224 | tf_op jit(solution)/shard_map/ppermute | solution.py:162
  61.4 5.3 %collective-permute-start.25 = (f16[2,128,128]{2,1,0:T(8,128)(2,1)S(1)}, f16[2,128,128]{2,1,0:T(8,128)(2,1)S(1)}, u32[]{:S(2)}, u32[]{:S(2)}) collective-permute-start(f16[2,128,128]{2,1,0:T(8,128)(2,1)S(1)} %add_convert_fusion.1), channel_id=1, source_target_pairs={{0,24},{4,28},{8,16},{12,20},{16,8},{20,12},{24,0},{28,4},{1,25},{... | collective-permute-start | bytes 196616 | tf_op jit(solution)/shard_map/ppermute | solution.py:162
  63.5 4.5 %collective-permute-start.24 = (f16[2,128,128]{2,1,0:T(8,128)(2,1)S(1)}, f16[2,128,128]{2,1,0:T(8,128)(2,1)S(1)}, u32[]{:S(2)}, u32[]{:S(2)}) collective-permute-start(f16[2,128,128]{2,1,0:T(8,128)(2,1)S(1)} %add_convert_fusion.1), channel_id=1, source_target_pairs={{0,16},{4,20},{8,24},{12,28},{16,0},{20,4},{24,8},{28,12},{1,17},{... | collective-permute-start | bytes 196616 | tf_op jit(solution)/shard_map/ppermute | solution.py:162
  64.1 4.3 %collective-permute-start.23 = (f16[2,128,128]{2,1,0:T(8,128)(2,1)S(1)}, f16[2,128,128]{2,1,0:T(8,128)(2,1)S(1)}, u32[]{:S(2)}, u32[]{:S(2)}) collective-permute-start(f16[2,128,128]{2,1,0:T(8,128)(2,1)S(1)} %add_convert_fusion.1), channel_id=1, source_target_pairs={{0,8},{4,12},{8,0},{12,4},{16,24},{20,28},{24,16},{28,20},{1,9},{5... | collective-permute-start | bytes 196616 | tf_op jit(solution)/shard_map/ppermute | solution.py:162
  68.4 6.5 %collective-permute-start.28 = (f16[2,128,128]{2,1,0:T(8,128)(2,1)S(1)}, f16[2,128,128]{2,1,0:T(8,128)(2,1)S(1)}, u32[]{:S(2)}, u32[]{:S(2)}) collective-permute-start(f16[2,128,128]{2,1,0:T(8,128)(2,1)S(1)} %add_convert_fusion), channel_id=1, source_target_pairs={{0,3},{1,2},{2,1},{3,0},{4,7},{5,6},{6,5},{7,4},{8,11},{9,10},{10,... | collective-permute-start | bytes 196616 | tf_op jit(solution)/shard_map/ppermute | solution.py:162
  70.9 6.2 %collective-permute-start.27 = (f16[2,128,128]{2,1,0:T(8,128)(2,1)S(1)}, f16[2,128,128]{2,1,0:T(8,128)(2,1)S(1)}, u32[]{:S(2)}, u32[]{:S(2)}) collective-permute-start(f16[2,128,128]{2,1,0:T(8,128)(2,1)S(1)} %add_convert_fusion), channel_id=1, source_target_pairs={{0,2},{1,3},{2,0},{3,1},{4,6},{5,7},{6,4},{7,5},{8,10},{9,11},{10,... | collective-permute-start | bytes 196616 | tf_op jit(solution)/shard_map/ppermute | solution.py:162
  70.9 6.2 %collective-permute-start.26 = (f16[2,128,128]{2,1,0:T(8,128)(2,1)S(1)}, f16[2,128,128]{2,1,0:T(8,128)(2,1)S(1)}, u32[]{:S(2)}, u32[]{:S(2)}) collective-permute-start(f16[2,128,128]{2,1,0:T(8,128)(2,1)S(1)} %add_convert_fusion), channel_id=1, source_target_pairs={{0,1},{1,0},{2,3},{3,2},{4,5},{5,4},{6,7},{7,6},{8,9},{9,8},{10,11... | collective-permute-start | bytes 196616 | tf_op jit(solution)/shard_map/ppermute | solution.py:162
  77.1 1.4 %collective-permute-start.29 = (f32[2,128,128]{2,1,0:T(8,128)S(1)}, f32[2,128,128]{2,1,0:T(8,128)S(1)}, u32[]{:S(2)}, u32[]{:S(2)}) collective-permute-start(f32[2,128,128]{2,1,0:T(8,128)S(1)} %add_add_fusion.own), channel_id=1, source_target_pairs={{0,4},{4,0},{8,12},{12,8},{16,20},{20,16},{24,28},{28,24},{1,5},{5... | collective-permute-start | bytes 393224 | tf_op jit(solution)/shard_map/ppermute | solution.py:162

commit v4 on v2

--- a/solution.py
+++ b/solution.py
@@ -9,7 +9,7 @@
 from jax.sharding import PartitionSpec as P
 
 STEPS = 3
-UNROLL = 16
+UNROLL = 64
 LEFT_MAX = 1.16462404
 RIGHT_MAX = 0.010778794
 VMEM = pl.BlockSpec(memory_space=pltpu.VMEM)
@@ -75,21 +75,25 @@
         copy.wait()
 
 
+def place(parts, whole, fill):
+    here = lax.axis_index("sectors")
+    held = parts[0].shape[0]
+    for mask, part in enumerate(parts):
+        for i in range(held):
+            g = (here ^ mask) * held + i
+            whole[g] = fill(g, part[i])
+
+
 def first_kernel(wire, *refs):
     table, left, right, vec, pre, state, keep, send, blocks, acc = refs[-10:]
     sectors, rows, cols = acc.shape
     parts = (len(refs) - 10) // 2
     mine, other = refs[:parts], refs[parts : 2 * parts]
-    held = sectors // parts
     low = lax.axis_index("terms") % 2
-    here = lax.axis_index("sectors")
 
     def load(trial, precond):
-        for mask in range(parts):
-            for i in range(held):
-                g = (here ^ mask) * held + i
-                vec[g] = jnp.where(live(table, g, acc), trial[mask][i], 0.0)
-                pre[g] = precond[mask][i]
+        place(trial, vec, lambda g, block: jnp.where(live(table, g, acc), block, 0.0))
+        place(precond, pre, lambda g, block: block)
 
     @pl.when(low == 0)
     def _():
@@ -156,8 +160,9 @@
     rayleigh, scale = update(wire, own, far, table, vec_in, pre, old[0:1, 0:1], full, fresh)
     first = lax.axis_index("sectors") * held
     out[...] = fresh[pl.ds(first, held)] * scale[None]
-    line = lax.broadcasted_iota(jnp.int32, old.shape, 0)
-    energies[...] = jnp.where(line == step, rayleigh, old)
+    for i in range(1, step):
+        energies[i - 1] = jnp.sum(old[i : i + 1, 0:1])
+    energies[step - 1] = jnp.sum(rayleigh)
 
 
 def params():
@@ -168,24 +173,31 @@
     return lax.ppermute(x, axis, [(i, i ^ mask) for i in range(lax.axis_size(axis))])
 
 
-def bit_groups(axis, first):
+def stages(axis, first):
     count = lax.axis_size(axis).bit_length() - 1
-    return [(low, min(2, count - low)) for low in range(first, count, 2)]
-
-
-def sum_stage(x, axis, low, bits):
-    got = [x] + [swap(x, axis, mask << low) for mask in range(1, 1 << bits)]
-    got = [g.astype(F32) for g in got]
-    while len(got) > 1:
-        got = [got[i] + got[i + 1] for i in range(0, len(got), 2)]
-    return got[0]
+    one = 1 if axis == "sectors" else lax.axis_size("sectors")
+    return [[mask * one << low for mask in range(1, 1 << min(2, count - low))] for low in range(first, count, 2)]
+
+
+def exchange(x, masks):
+    sectors = lax.axis_size("sectors")
+    devices = range(sectors * lax.axis_size("terms"))
+    return lax.ppermute(x, ("terms", "sectors"), [(d, d ^ masks[d // sectors % 2]) for d in devices])
 
 
 def reduce_half(keep, send):
     x = keep + swap(send, "terms", 1)
-    for axis, first in (("sectors", 0), ("terms", 1)):
-        for low, bits in bit_groups(axis, first):
-            x = sum_stage(lax.optimization_barrier(x.astype(HALF)), axis, low, bits)
+    along, across = stages("terms", 1), stages("sectors", 0)
+    orders = along + across, across + along
+    if [len(s) for s in orders[0]] != [len(s) for s in orders[1]]:
+        orders = orders[0], orders[0]
+    for even, odd in zip(*orders):
+        x = lax.optimization_barrier(x.astype(HALF))
+        got = [x] + [exchange(x, masks) for masks in zip(even, odd)]
+        got = [g.astype(F32) for g in got]
+        while len(got) > 1:
+            got = [got[i] + got[i + 1] for i in range(0, len(got), 2)]
+        x = got[0]
     return x
 
 
@@ -218,9 +230,11 @@
     )(*(pltpu.with_memory_space_constraint(x, pltpu.HBM) for x in (block_rows, owner_map, term_in, term_out, left_ops, right_ops)))
 
     picked = jnp.where(lax.axis_index("terms") % 2 == 0, trial, precond)
-    mine = [picked] + [swap(picked, "sectors", mask) for mask in range(1, lax.axis_size("sectors"))]
+    swapped = swap(picked, "terms", 1)
+    mine = [swap(picked, "sectors", mask) for mask in range(1, lax.axis_size("sectors"))]
     mine, (left, right, table) = lax.optimization_barrier((mine, (left, right, table)))
-    other = [swap(x, "terms", 1) for x in mine]
+    other = [swapped] + [swap(x, "terms", 1) for x in mine]
+    mine = [picked] + mine
     vec, pre, state, keep, send = pl.pallas_call(
         functools.partial(first_kernel, wire),
         out_shape=(whole, whole, state_shape, part, part),
@@ -242,15 +256,14 @@
         )(own, far, vec, pre, state, table, left, right)
     own = reduce_half(keep, send)
     far = swap(own, "terms", 1)
-    vector, energies = pl.pallas_call(
+    return pl.pallas_call(
         functools.partial(last_kernel, wire, STEPS),
-        out_shape=(jax.ShapeDtypeStruct(trial.shape, F32), state_shape),
+        out_shape=(jax.ShapeDtypeStruct(trial.shape, F32), jax.ShapeDtypeStruct((STEPS,), F32)),
         in_specs=[VMEM] * 5 + [SMEM],
-        out_specs=(VMEM,) * 2,
+        out_specs=(VMEM, SMEM),
         scratch_shapes=[full, full],
         compiler_params=params(),
     )(own, far, vec, pre, state, table)
-    return vector, energies[1 : STEPS + 1, 0]
 
 
 def solution(mesh):

time: 82.4 us -> 75.8 us (0.920)
  waiting for transfers between devices: 34 us -> 31.2 us
  Pallas kernels: 13.9 us -> 11.4 us
    ppermute x31 -> x13, starting transfers between devices: 31.9 us -> 7.14 us  [swap(): lax.ppermute(x, axis, [(i, i ^ mask) for i in range(lax.axis_size(axis))])]
    ppermute x0 -> x18, starting transfers between devices: none -> 24 us  [exchange(): lax.ppermute(x, ('terms', 'sectors'), [(d, d ^ masks[d // sectors % 2]) f...]
    ppermute x31 -> x13, waiting for transfers between devices: 34 us -> 10.9 us  [swap(): lax.ppermute(x, axis, [(i, i ^ mask) for i in range(lax.axis_size(axis))])]
    ppermute x0 -> x18, waiting for transfers between devices: none -> 20.3 us  [exchange(): lax.ppermute(x, ('terms', 'sectors'), [(d, d ^ masks[d // sectors % 2]) f...]
    pallas_call x2, Pallas kernels: 6.49 us -> 4.88 us  [on_device(): pl.pallas_call(functools.partial(middle_kernel, wire, step), out_shape=(w...]
    pallas_call x1, Pallas kernels: 2.9 us -> 2.02 us  [on_device(): pl.pallas_call(functools.partial(first_kernel, wire), out_shape=(whole, w...]
  transfers between devices with their start and end apart: 31 -> 31, of which waited for: 26 -> 25; matrix products, arithmetic and copies ran while one was open for 0% -> 0% of each run, Pallas kernels for 3% -> 4%
where the time goes in v4:
time: 75.8 us; the launch traced here: 75.7 us
  starting transfers between devices  31.2 us (41%)
  waiting for transfers between devices  31.2 us (41%)
  Pallas kernels  11.4 us (15%)
  other arithmetic  1.15 us (2%)
  between operations  0.76 us (1%)
    ppermute x18, starting transfers between devices, exchange(): lax.ppermute(x, ('terms', 'sectors'), [(d, d ^ masks[d // sectors % 2]) f...  24 us
    ppermute x18, waiting for transfers between devices, exchange(): lax.ppermute(x, ('terms', 'sectors'), [(d, d ^ masks[d // sectors % 2]) f...  20.3 us
    ppermute x13, waiting for transfers between devices, swap(): lax.ppermute(x, axis, [(i, i ^ mask) for i in range(lax.axis_size(axis))])  10.9 us
    ppermute x13, starting transfers between devices, swap(): lax.ppermute(x, axis, [(i, i ^ mask) for i in range(lax.axis_size(axis))])  7.14 us
    pallas_call x2, Pallas kernels, on_device(): pl.pallas_call(functools.partial(middle_kernel, wire, step), out_shape=(w...  4.88 us
    pallas_call x1, Pallas kernels, on_device(): pl.pallas_call(load_kernel, out_shape=(jax.ShapeDtypeStruct(left_ops.shap...  2.88 us
    pallas_call x1, Pallas kernels, on_device(): pl.pallas_call(functools.partial(first_kernel, wire), out_shape=(whole, w...  2.02 us
    pallas_call x1, Pallas kernels, on_device(): pl.pallas_call(functools.partial(last_kernel, wire, STEPS), out_shape=(ja...  1.6 us
  transfers between devices with their start and end apart: 31, of which 25 were waited for; matrix products, arithmetic and copies ran while one was open for 0% of the time, Pallas kernels for 4%

profile of v4, /device:TPU:0, one launch (start us, length us, event | category | flops | bytes accessed | tf_op | source)
XLA Modules:
  0.0 75.7 jit_solution(8876627735354097965)
XLA Ops:
  0.6 0.9 %broadcast_select_fusion.refs_0_ = f32[1,128,128]{2,1,0:T(8,128)S(1)} fusion(f32[1,128,128]{2,1,0:T(8,128)} %param.8, f32[1,128,128]{2,1,0:T(8,128)} %param.9, pred[]{:T(512)S(6)} %eq.5), kind=kLoop, calls=%fused_computation.9 | loop fusion | flops 16384 | bytes 196609 | tf_op jit(solution)/shard_map/jit(_where)/select_n | solution.py:232
  1.5 5.1 %collective-permute-start.2 = (f32[1,128,128]{2,1,0:T(8,128)S(1)}, f32[1,128,128]{2,1,0:T(8,128)S(1)}, u32[]{:S(2)}, u32[]{:S(2)}) collective-permute-start(f32[1,128,128]{2,1,0:T(8,128)S(1)} %broadcast_select_fusion.refs_0_), channel_id=1, source_target_pairs={{0,3},{1,2},{2,1},{3,0},{4,7},{5,6},{6,5},{7,4},{8,11},{9,10},{10,... | collective-permute-start | bytes 196616 | tf_op jit(solution)/shard_map/ppermute | solution.py:173
  6.6 0.6 collective-permute-start
  7.3 2.9 %shard_map.95 = (bf16[64,128,128]{2,1,0:T(8,128)(2,1)S(1)}, bf16[64,128,128]{2,1,0:T(8,128)(2,1)S(1)}, s32[132]{0:T(256)S(1)}) custom-call(s32[4]{0:T(128)} %rows_hbm.1, s32[4]{0:T(128)} %owner_hbm.1, s32[64]{0:T(128)} %in_hbm.1, s32[64]{0:T(128)} %out_hbm.1, bf16[64,128,128]{2,1,0:T(8,128)(2,1)} %left_hbm.1, bf16[64,128,128]{2,1,0:T(8,128)(2,1)} %right_hbm.1), custom_call_target="tpu_custom_call" | custom-call | bytes 4194304 | tf_op jit(solution)/shard_map/pallas_call | solution.py:218
  10.2 2.1 %collective-permute-done.1.refs_2_ = f32[1,128,128]{2,1,0:T(8,128)S(1)} collective-permute-done((f32[1,128,128]{2,1,0:T(8,128)S(1)}, f32[1,128,128]{2,1,0:T(8,128)S(1)}, u32[]{:S(2)}, u32[]{:S(2)}) %collective-permute-start.1) | collective-permute-done | bytes 65568 | tf_op jit(solution)/shard_map/ppermute | solution.py:173
  12.2 0.5 collective-permute-start.5
  12.7 0.7 collective-permute-done.4.refs_5_
  13.6 0.4 collective-permute-done.6.refs_7_
  14.0 2.0 %shard_map.96 = (f32[4,128,128]{2,1,0:T(8,128)S(1)}, f32[4,128,128]{2,1,0:T(8,128)S(1)}, f32[8,128]{1,0:T(8,128)S(1)}, f32[2,128,128]{2,1,0:T(8,128)S(1)}, f32[2,128,128]{2,1,0:T(8,128)S(1)}) custom-call(f32[1,128,128]{2,1,0:T(8,128)S(1)} %broadcast_select_fusion.refs_0_, f32[1,128,128]{2,1,0:T(8,128)S(1)} %collective-permute-done.refs_1_, ...), custom_call_target="tpu_custom_call" | custom-call | tf_op jit(solution)/shard_map/pallas_call | solution.py:238
  16.2 1.2 %collective-permute-done.7 = f32[2,128,128]{2,1,0:T(8,128)S(1)} collective-permute-done((f32[2,128,128]{2,1,0:T(8,128)S(1)}, f32[2,128,128]{2,1,0:T(8,128)S(1)}, u32[]{:S(2)}, u32[]{:S(2)}) %collective-permute-start.7) | collective-permute-done | bytes 131104 | tf_op jit(solution)/shard_map/ppermute | solution.py:173
  17.5 2.5 %collective-permute-start.10 = (f16[2,128,128]{2,1,0:T(8,128)(2,1)S(1)}, f16[2,128,128]{2,1,0:T(8,128)(2,1)S(1)}, u32[]{:S(2)}, u32[]{:S(2)}) collective-permute-start(f16[2,128,128]{2,1,0:T(8,128)(2,1)S(1)} %add_convert_fusion.5), channel_id=1, source_target_pairs={{0,24},{1,25},{2,26},{3,27},{4,7},{5,6},{6,5},{7,4},{8,16},{9,17},... | collective-permute-start | bytes 196616 | tf_op jit(solution)/shard_map/ppermute | solution.py:185
  20.0 0.5 collective-permute-start.9
  20.5 0.5 collective-permute-start.8
  21.0 1.7 %collective-permute-done.10 = f16[2,128,128]{2,1,0:T(8,128)(2,1)S(1)} collective-permute-done((f16[2,128,128]{2,1,0:T(8,128)(2,1)S(1)}, f16[2,128,128]{2,1,0:T(8,128)(2,1)S(1)}, u32[]{:S(2)}, u32[]{:S(2)}) %collective-permute-start.10) | collective-permute-done | bytes 65568 | tf_op jit(solution)/shard_map/ppermute | solution.py:185
  22.7 1.5 %collective-permute-done.9 = f16[2,128,128]{2,1,0:T(8,128)(2,1)S(1)} collective-permute-done((f16[2,128,128]{2,1,0:T(8,128)(2,1)S(1)}, f16[2,128,128]{2,1,0:T(8,128)(2,1)S(1)}, u32[]{:S(2)}, u32[]{:S(2)}) %collective-permute-start.9) | collective-permute-done | bytes 65568 | tf_op jit(solution)/shard_map/ppermute | solution.py:185
  24.2 0.5 collective-permute-done.8
  24.8 2.8 %collective-permute-start.13 = (f16[2,128,128]{2,1,0:T(8,128)(2,1)S(1)}, f16[2,128,128]{2,1,0:T(8,128)(2,1)S(1)}, u32[]{:S(2)}, u32[]{:S(2)}) collective-permute-start(f16[2,128,128]{2,1,0:T(8,128)(2,1)S(1)} %add_convert_fusion.4), channel_id=1, source_target_pairs={{0,3},{1,2},{2,1},{3,0},{4,28},{5,29},{6,30},{7,31},{8,11},{9,10},... | collective-permute-start | bytes 196616 | tf_op jit(solution)/shard_map/ppermute | solution.py:185
  27.6 1.7 %collective-permute-start.11 = (f16[2,128,128]{2,1,0:T(8,128)(2,1)S(1)}, f16[2,128,128]{2,1,0:T(8,128)(2,1)S(1)}, u32[]{:S(2)}, u32[]{:S(2)}) collective-permute-start(f16[2,128,128]{2,1,0:T(8,128)(2,1)S(1)} %add_convert_fusion.4), channel_id=1, source_target_pairs={{0,1},{1,0},{2,3},{3,2},{4,12},{5,13},{6,14},{7,15},{8,9},{9,8},{1... | collective-permute-start | bytes 196616 | tf_op jit(solution)/shard_map/ppermute | solution.py:185
  29.2 1.7 %collective-permute-done.13 = f16[2,128,128]{2,1,0:T(8,128)(2,1)S(1)} collective-permute-done((f16[2,128,128]{2,1,0:T(8,128)(2,1)S(1)}, f16[2,128,128]{2,1,0:T(8,128)(2,1)S(1)}, u32[]{:S(2)}, u32[]{:S(2)}) %collective-permute-start.13) | collective-permute-done | bytes 65568 | tf_op jit(solution)/shard_map/ppermute | solution.py:185
  30.9 1.8 %collective-permute-done.12 = f16[2,128,128]{2,1,0:T(8,128)(2,1)S(1)} collective-permute-done((f16[2,128,128]{2,1,0:T(8,128)(2,1)S(1)}, f16[2,128,128]{2,1,0:T(8,128)(2,1)S(1)}, u32[]{:S(2)}, u32[]{:S(2)}) %collective-permute-start.12) | collective-permute-done | bytes 65568 | tf_op jit(solution)/shard_map/ppermute | solution.py:185
  32.9 1.3 %collective-permute-done.14.far = f32[2,128,128]{2,1,0:T(8,128)S(1)} collective-permute-done((f32[2,128,128]{2,1,0:T(8,128)S(1)}, f32[2,128,128]{2,1,0:T(8,128)S(1)}, u32[]{:S(2)}, u32[]{:S(2)}) %collective-permute-start.14) | collective-permute-done | bytes 131104 | tf_op jit(solution)/shard_map/ppermute | solution.py:173
  34.2 2.4 %shard_map.97 = (f32[4,128,128]{2,1,0:T(8,128)S(1)}, f32[8,128]{1,0:T(8,128)S(1)}, f32[2,128,128]{2,1,0:T(8,128)S(1)}, f32[2,128,128]{2,1,0:T(8,128)S(1)}) custom-call(f32[2,128,128]{2,1,0:T(8,128)S(1)} %add_add_fusion.2.own, f32[2,128,128]{2,1,0:T(8,128)S(1)} %collective-permute-done.14.far, f32[4,128,128]{2,1,0:T(8,128)S(1)} %get-tuple-element.35.vec_in, ...), custom_call_target="tpu_custom_call" | custom-call | tf_op jit(solution)/shard_map/pallas_call | solution.py:249
  36.9 1.2 %collective-permute-done.15 = f32[2,128,128]{2,1,0:T(8,128)S(1)} collective-permute-done((f32[2,128,128]{2,1,0:T(8,128)S(1)}, f32[2,128,128]{2,1,0:T(8,128)S(1)}, u32[]{:S(2)}, u32[]{:S(2)}) %collective-permute-start.15) | collective-permute-done | bytes 131104 | tf_op jit(solution)/shard_map/ppermute | solution.py:173
  38.1 1.6 %collective-permute-start.18 = (f16[2,128,128]{2,1,0:T(8,128)(2,1)S(1)}, f16[2,128,128]{2,1,0:T(8,128)(2,1)S(1)}, u32[]{:S(2)}, u32[]{:S(2)}) collective-permute-start(f16[2,128,128]{2,1,0:T(8,128)(2,1)S(1)} %add_convert_fusion.3), channel_id=1, source_target_pairs={{0,24},{1,25},{2,26},{3,27},{4,7},{5,6},{6,5},{7,4},{8,16},{9,17},... | collective-permute-start | bytes 196616 | tf_op jit(solution)/shard_map/ppermute | solution.py:185
  39.6 0.5 collective-permute-start.17
  40.1 1.5 %collective-permute-start.16 = (f16[2,128,128]{2,1,0:T(8,128)(2,1)S(1)}, f16[2,128,128]{2,1,0:T(8,128)(2,1)S(1)}, u32[]{:S(2)}, u32[]{:S(2)}) collective-permute-start(f16[2,128,128]{2,1,0:T(8,128)(2,1)S(1)} %add_convert_fusion.3), channel_id=1, source_target_pairs={{0,8},{1,9},{2,10},{3,11},{4,5},{5,4},{6,7},{7,6},{8,0},{9,1},{10,... | collective-permute-start | bytes 196616 | tf_op jit(solution)/shard_map/ppermute | solution.py:185
  41.6 1.7 %collective-permute-done.18 = f16[2,128,128]{2,1,0:T(8,128)(2,1)S(1)} collective-permute-done((f16[2,128,128]{2,1,0:T(8,128)(2,1)S(1)}, f16[2,128,128]{2,1,0:T(8,128)(2,1)S(1)}, u32[]{:S(2)}, u32[]{:S(2)}) %collective-permute-start.18) | collective-permute-done | bytes 65568 | tf_op jit(solution)/shard_map/ppermute | solution.py:185
  43.3 0.7 collective-permute-done.17
  44.0 0.4 collective-permute-done.16
  44.5 2.4 %collective-permute-start.21 = (f16[2,128,128]{2,1,0:T(8,128)(2,1)S(1)}, f16[2,128,128]{2,1,0:T(8,128)(2,1)S(1)}, u32[]{:S(2)}, u32[]{:S(2)}) collective-permute-start(f16[2,128,128]{2,1,0:T(8,128)(2,1)S(1)} %add_convert_fusion.2), channel_id=1, source_target_pairs={{0,3},{1,2},{2,1},{3,0},{4,28},{5,29},{6,30},{7,31},{8,11},{9,10},... | collective-permute-start | bytes 196616 | tf_op jit(solution)/shard_map/ppermute | solution.py:185
  46.8 2.1 %collective-permute-start.19 = (f16[2,128,128]{2,1,0:T(8,128)(2,1)S(1)}, f16[2,128,128]{2,1,0:T(8,128)(2,1)S(1)}, u32[]{:S(2)}, u32[]{:S(2)}) collective-permute-start(f16[2,128,128]{2,1,0:T(8,128)(2,1)S(1)} %add_convert_fusion.2), channel_id=1, source_target_pairs={{0,1},{1,0},{2,3},{3,2},{4,12},{5,13},{6,14},{7,15},{8,9},{9,8},{1... | collective-permute-start | bytes 196616 | tf_op jit(solution)/shard_map/ppermute | solution.py:185
  48.9 1.7 %collective-permute-done.21 = f16[2,128,128]{2,1,0:T(8,128)(2,1)S(1)} collective-permute-done((f16[2,128,128]{2,1,0:T(8,128)(2,1)S(1)}, f16[2,128,128]{2,1,0:T(8,128)(2,1)S(1)}, u32[]{:S(2)}, u32[]{:S(2)}) %collective-permute-start.21) | collective-permute-done | bytes 65568 | tf_op jit(solution)/shard_map/ppermute | solution.py:185
  50.6 1.8 %collective-permute-done.20 = f16[2,128,128]{2,1,0:T(8,128)(2,1)S(1)} collective-permute-done((f16[2,128,128]{2,1,0:T(8,128)(2,1)S(1)}, f16[2,128,128]{2,1,0:T(8,128)(2,1)S(1)}, u32[]{:S(2)}, u32[]{:S(2)}) %collective-permute-start.20) | collective-permute-done | bytes 65568 | tf_op jit(solution)/shard_map/ppermute | solution.py:185
  52.5 1.3 %collective-permute-done.22.far = f32[2,128,128]{2,1,0:T(8,128)S(1)} collective-permute-done((f32[2,128,128]{2,1,0:T(8,128)S(1)}, f32[2,128,128]{2,1,0:T(8,128)S(1)}, u32[]{:S(2)}, u32[]{:S(2)}) %collective-permute-start.22) | collective-permute-done | bytes 131104 | tf_op jit(solution)/shard_map/ppermute | solution.py:173
  53.9 2.4 %shard_map.98 = (f32[4,128,128]{2,1,0:T(8,128)S(1)}, f32[8,128]{1,0:T(8,128)S(1)}, f32[2,128,128]{2,1,0:T(8,128)S(1)}, f32[2,128,128]{2,1,0:T(8,128)S(1)}) custom-call(f32[2,128,128]{2,1,0:T(8,128)S(1)} %add_add_fusion.1.own, f32[2,128,128]{2,1,0:T(8,128)S(1)} %collective-permute-done.22.far, f32[4,128,128]{2,1,0:T(8,128)S(1)} %get-tuple-element.40.vec_in, ...), custom_call_target="tpu_custom_call" | custom-call | tf_op jit(solution)/shard_map/pallas_call | solution.py:249
  56.5 1.2 %collective-permute-done.23 = f32[2,128,128]{2,1,0:T(8,128)S(1)} collective-permute-done((f32[2,128,128]{2,1,0:T(8,128)S(1)}, f32[2,128,128]{2,1,0:T(8,128)S(1)}, u32[]{:S(2)}, u32[]{:S(2)}) %collective-permute-start.23) | collective-permute-done | bytes 131104 | tf_op jit(solution)/shard_map/ppermute | solution.py:173
  57.7 2.5 %collective-permute-start.26 = (f16[2,128,128]{2,1,0:T(8,128)(2,1)S(1)}, f16[2,128,128]{2,1,0:T(8,128)(2,1)S(1)}, u32[]{:S(2)}, u32[]{:S(2)}) collective-permute-start(f16[2,128,128]{2,1,0:T(8,128)(2,1)S(1)} %add_convert_fusion.1), channel_id=1, source_target_pairs={{0,24},{1,25},{2,26},{3,27},{4,7},{5,6},{6,5},{7,4},{8,16},{9,17},... | collective-permute-start | bytes 196616 | tf_op jit(solution)/shard_map/ppermute | solution.py:185
  60.3 0.5 collective-permute-start.25
  60.8 0.5 collective-permute-start.24
  61.3 1.7 %collective-permute-done.26 = f16[2,128,128]{2,1,0:T(8,128)(2,1)S(1)} collective-permute-done((f16[2,128,128]{2,1,0:T(8,128)(2,1)S(1)}, f16[2,128,128]{2,1,0:T(8,128)(2,1)S(1)}, u32[]{:S(2)}, u32[]{:S(2)}) %collective-permute-start.26) | collective-permute-done | bytes 65568 | tf_op jit(solution)/shard_map/ppermute | solution.py:185
  63.0 1.5 %collective-permute-done.25 = f16[2,128,128]{2,1,0:T(8,128)(2,1)S(1)} collective-permute-done((f16[2,128,128]{2,1,0:T(8,128)(2,1)S(1)}, f16[2,128,128]{2,1,0:T(8,128)(2,1)S(1)}, u32[]{:S(2)}, u32[]{:S(2)}) %collective-permute-start.25) | collective-permute-done | bytes 65568 | tf_op jit(solution)/shard_map/ppermute | solution.py:185
  64.5 0.5 collective-permute-done.24
  65.1 2.1 %collective-permute-start.29 = (f16[2,128,128]{2,1,0:T(8,128)(2,1)S(1)}, f16[2,128,128]{2,1,0:T(8,128)(2,1)S(1)}, u32[]{:S(2)}, u32[]{:S(2)}) collective-permute-start(f16[2,128,128]{2,1,0:T(8,128)(2,1)S(1)} %add_convert_fusion), channel_id=1, source_target_pairs={{0,3},{1,2},{2,1},{3,0},{4,28},{5,29},{6,30},{7,31},{8,11},{9,10},... | collective-permute-start | bytes 196616 | tf_op jit(solution)/shard_map/ppermute | solution.py:185
  67.4 2.2 %collective-permute-start.27 = (f16[2,128,128]{2,1,0:T(8,128)(2,1)S(1)}, f16[2,128,128]{2,1,0:T(8,128)(2,1)S(1)}, u32[]{:S(2)}, u32[]{:S(2)}) collective-permute-start(f16[2,128,128]{2,1,0:T(8,128)(2,1)S(1)} %add_convert_fusion), channel_id=1, source_target_pairs={{0,1},{1,0},{2,3},{3,2},{4,12},{5,13},{6,14},{7,15},{8,9},{9,8},{1... | collective-permute-start | bytes 196616 | tf_op jit(solution)/shard_map/ppermute | solution.py:185
  69.5 1.7 %collective-permute-done.29 = f16[2,128,128]{2,1,0:T(8,128)(2,1)S(1)} collective-permute-done((f16[2,128,128]{2,1,0:T(8,128)(2,1)S(1)}, f16[2,128,128]{2,1,0:T(8,128)(2,1)S(1)}, u32[]{:S(2)}, u32[]{:S(2)}) %collective-permute-start.29) | collective-permute-done | bytes 65568 | tf_op jit(solution)/shard_map/ppermute | solution.py:185
  71.2 1.4 %collective-permute-done.28 = f16[2,128,128]{2,1,0:T(8,128)(2,1)S(1)} collective-permute-done((f16[2,128,128]{2,1,0:T(8,128)(2,1)S(1)}, f16[2,128,128]{2,1,0:T(8,128)(2,1)S(1)}, u32[]{:S(2)}, u32[]{:S(2)}) %collective-permute-start.28) | collective-permute-done | bytes 65568 | tf_op jit(solution)/shard_map/ppermute | solution.py:185
  72.7 1.3 %collective-permute-done.30.far = f32[2,128,128]{2,1,0:T(8,128)S(1)} collective-permute-done((f32[2,128,128]{2,1,0:T(8,128)S(1)}, f32[2,128,128]{2,1,0:T(8,128)S(1)}, u32[]{:S(2)}, u32[]{:S(2)}) %collective-permute-start.30) | collective-permute-done | bytes 131104 | tf_op jit(solution)/shard_map/ppermute | solution.py:173
  74.1 1.6 %shard_map.99 = (f32[1,128,128]{2,1,0:T(8,128)}, f32[3]{0:T(128)}) custom-call(f32[2,128,128]{2,1,0:T(8,128)S(1)} %add_add_fusion.own, f32[2,128,128]{2,1,0:T(8,128)S(1)} %collective-permute-done.30.far, f32[4,128,128]{2,1,0:T(8,128)S(1)} %get-tuple-element.44.vec_in, f32[4,128,128]{2,1,0:T(8,128)S(1)} %get-tuple-element.36.pre, ...), custom_call_target="tpu_custom_call" | custom-call | tf_op jit(solution)/shard_map/pallas_call | solution.py:259
  (29 shorter events, 1.6 us)
Async XLA Ops:
  1.5 8.6 %collective-permute-start.2 = (f32[1,128,128]{2,1,0:T(8,128)S(1)}, f32[1,128,128]{2,1,0:T(8,128)S(1)}, u32[]{:S(2)}, u32[]{:S(2)}) collective-permute-start(f32[1,128,128]{2,1,0:T(8,128)S(1)} %broadcast_select_fusion.refs_0_), channel_id=1, source_target_pairs={{0,3},{1,2},{2,1},{3,0},{4,7},{5,6},{6,5},{7,4},{8,11},{9,10},{10,... | collective-permute-start | bytes 196616 | tf_op jit(solution)/shard_map/ppermute | solution.py:173
  6.6 5.6 %collective-permute-start.1 = (f32[1,128,128]{2,1,0:T(8,128)S(1)}, f32[1,128,128]{2,1,0:T(8,128)S(1)}, u32[]{:S(2)}, u32[]{:S(2)}) collective-permute-start(f32[1,128,128]{2,1,0:T(8,128)S(1)} %broadcast_select_fusion.refs_0_), channel_id=1, source_target_pairs={{0,2},{1,3},{2,0},{3,1},{4,6},{5,7},{6,4},{7,5},{8,10},{9,11},{10,... | collective-permute-start | bytes 196616 | tf_op jit(solution)/shard_map/ppermute | solution.py:173
  6.6 5.6 %collective-permute-start = (f32[1,128,128]{2,1,0:T(8,128)S(1)}, f32[1,128,128]{2,1,0:T(8,128)S(1)}, u32[]{:S(2)}, u32[]{:S(2)}) collective-permute-start(f32[1,128,128]{2,1,0:T(8,128)S(1)} %broadcast_select_fusion.refs_0_), channel_id=1, source_target_pairs={{0,1},{1,0},{2,3},{3,2},{4,5},{5,4},{6,7},{7,6},{8,9},{9,8},{10,11... | collective-permute-start | bytes 196616 | tf_op jit(solution)/shard_map/ppermute | solution.py:173
  7.3 5.5 %collective-permute-start.3 = (f32[1,128,128]{2,1,0:T(8,128)S(1)}, f32[1,128,128]{2,1,0:T(8,128)S(1)}, u32[]{:S(2)}, u32[]{:S(2)}) collective-permute-start(f32[1,128,128]{2,1,0:T(8,128)S(1)} %broadcast_select_fusion.refs_0_), channel_id=1, source_target_pairs={{0,4},{4,0},{8,12},{12,8},{16,20},{20,16},{24,28},{28,24},{1,5},{5... | collective-permute-start | bytes 196616 | tf_op jit(solution)/shard_map/ppermute | solution.py:173
  12.2 1.3 %collective-permute-start.4 = (f32[1,128,128]{2,1,0:T(8,128)S(1)}, f32[1,128,128]{2,1,0:T(8,128)S(1)}, u32[]{:S(2)}, u32[]{:S(2)}) collective-permute-start(f32[1,128,128]{2,1,0:T(8,128)S(1)} %collective-permute-done.refs_1_), channel_id=1, source_target_pairs={{0,4},{4,0},{8,12},{12,8},{16,20},{20,16},{24,28},{28,24},{1,5},{5... | collective-permute-start | bytes 196616 | tf_op jit(solution)/shard_map/ppermute | solution.py:173
  12.2 1.4 %collective-permute-start.5 = (f32[1,128,128]{2,1,0:T(8,128)S(1)}, f32[1,128,128]{2,1,0:T(8,128)S(1)}, u32[]{:S(2)}, u32[]{:S(2)}) collective-permute-start(f32[1,128,128]{2,1,0:T(8,128)S(1)} %collective-permute-done.1.refs_2_), channel_id=1, source_target_pairs={{0,4},{4,0},{8,12},{12,8},{16,20},{20,16},{24,28},{28,24},{1,5},{5... | collective-permute-start | bytes 196616 | tf_op jit(solution)/shard_map/ppermute | solution.py:173
  12.7 1.3 %collective-permute-start.6 = (f32[1,128,128]{2,1,0:T(8,128)S(1)}, f32[1,128,128]{2,1,0:T(8,128)S(1)}, u32[]{:S(2)}, u32[]{:S(2)}) collective-permute-start(f32[1,128,128]{2,1,0:T(8,128)S(1)} %collective-permute-done.2.refs_3_), channel_id=1, source_target_pairs={{0,4},{4,0},{8,12},{12,8},{16,20},{20,16},{24,28},{28,24},{1,5},{5... | collective-permute-start | bytes 196616 | tf_op jit(solution)/shard_map/ppermute | solution.py:173
  16.0 1.4 %collective-permute-start.7 = (f32[2,128,128]{2,1,0:T(8,128)S(1)}, f32[2,128,128]{2,1,0:T(8,128)S(1)}, u32[]{:S(2)}, u32[]{:S(2)}) collective-permute-start(f32[2,128,128]{2,1,0:T(8,128)S(1)} %get-tuple-element.34), channel_id=1, source_target_pairs={{0,4},{4,0},{8,12},{12,8},{16,20},{20,16},{24,28},{28,24},{1,5},{5... | collective-permute-start | bytes 393224 | tf_op jit(solution)/shard_map/ppermute | solution.py:173
  17.5 5.2 %collective-permute-start.10 = (f16[2,128,128]{2,1,0:T(8,128)(2,1)S(1)}, f16[2,128,128]{2,1,0:T(8,128)(2,1)S(1)}, u32[]{:S(2)}, u32[]{:S(2)}) collective-permute-start(f16[2,128,128]{2,1,0:T(8,128)(2,1)S(1)} %add_convert_fusion.5), channel_id=1, source_target_pairs={{0,24},{1,25},{2,26},{3,27},{4,7},{5,6},{6,5},{7,4},{8,16},{9,17},... | collective-permute-start | bytes 196616 | tf_op jit(solution)/shard_map/ppermute | solution.py:185
  20.0 4.3 %collective-permute-start.9 = (f16[2,128,128]{2,1,0:T(8,128)(2,1)S(1)}, f16[2,128,128]{2,1,0:T(8,128)(2,1)S(1)}, u32[]{:S(2)}, u32[]{:S(2)}) collective-permute-start(f16[2,128,128]{2,1,0:T(8,128)(2,1)S(1)} %add_convert_fusion.5), channel_id=1, source_target_pairs={{0,16},{1,17},{2,18},{3,19},{4,6},{5,7},{6,4},{7,5},{8,24},{9,25},... | collective-permute-start | bytes 196616 | tf_op jit(solution)/shard_map/ppermute | solution.py:185
  20.5 4.3 %collective-permute-start.8 = (f16[2,128,128]{2,1,0:T(8,128)(2,1)S(1)}, f16[2,128,128]{2,1,0:T(8,128)(2,1)S(1)}, u32[]{:S(2)}, u32[]{:S(2)}) collective-permute-start(f16[2,128,128]{2,1,0:T(8,128)(2,1)S(1)} %add_convert_fusion.5), channel_id=1, source_target_pairs={{0,8},{1,9},{2,10},{3,11},{4,5},{5,4},{6,7},{7,6},{8,0},{9,1},{10,... | collective-permute-start | bytes 196616 | tf_op jit(solution)/shard_map/ppermute | solution.py:185
  24.8 6.1 %collective-permute-start.13 = (f16[2,128,128]{2,1,0:T(8,128)(2,1)S(1)}, f16[2,128,128]{2,1,0:T(8,128)(2,1)S(1)}, u32[]{:S(2)}, u32[]{:S(2)}) collective-permute-start(f16[2,128,128]{2,1,0:T(8,128)(2,1)S(1)} %add_convert_fusion.4), channel_id=1, source_target_pairs={{0,3},{1,2},{2,1},{3,0},{4,28},{5,29},{6,30},{7,31},{8,11},{9,10},... | collective-permute-start | bytes 196616 | tf_op jit(solution)/shard_map/ppermute | solution.py:185
  27.6 5.2 %collective-permute-start.12 = (f16[2,128,128]{2,1,0:T(8,128)(2,1)S(1)}, f16[2,128,128]{2,1,0:T(8,128)(2,1)S(1)}, u32[]{:S(2)}, u32[]{:S(2)}) collective-permute-start(f16[2,128,128]{2,1,0:T(8,128)(2,1)S(1)} %add_convert_fusion.4), channel_id=1, source_target_pairs={{0,2},{1,3},{2,0},{3,1},{4,20},{5,21},{6,22},{7,23},{8,10},{9,11},... | collective-permute-start | bytes 196616 | tf_op jit(solution)/shard_map/ppermute | solution.py:185
  27.6 5.2 %collective-permute-start.11 = (f16[2,128,128]{2,1,0:T(8,128)(2,1)S(1)}, f16[2,128,128]{2,1,0:T(8,128)(2,1)S(1)}, u32[]{:S(2)}, u32[]{:S(2)}) collective-permute-start(f16[2,128,128]{2,1,0:T(8,128)(2,1)S(1)} %add_convert_fusion.4), channel_id=1, source_target_pairs={{0,1},{1,0},{2,3},{3,2},{4,12},{5,13},{6,14},{7,15},{8,9},{9,8},{1... | collective-permute-start | bytes 196616 | tf_op jit(solution)/shard_map/ppermute | solution.py:185
  32.8 1.4 %collective-permute-start.14 = (f32[2,128,128]{2,1,0:T(8,128)S(1)}, f32[2,128,128]{2,1,0:T(8,128)S(1)}, u32[]{:S(2)}, u32[]{:S(2)}) collective-permute-start(f32[2,128,128]{2,1,0:T(8,128)S(1)} %add_add_fusion.2.own), channel_id=1, source_target_pairs={{0,4},{4,0},{8,12},{12,8},{16,20},{20,16},{24,28},{28,24},{1,5},{5... | collective-permute-start | bytes 393224 | tf_op jit(solution)/shard_map/ppermute | solution.py:173
  36.6 1.4 %collective-permute-start.15 = (f32[2,128,128]{2,1,0:T(8,128)S(1)}, f32[2,128,128]{2,1,0:T(8,128)S(1)}, u32[]{:S(2)}, u32[]{:S(2)}) collective-permute-start(f32[2,128,128]{2,1,0:T(8,128)S(1)} %get-tuple-element.39), channel_id=1, source_target_pairs={{0,4},{4,0},{8,12},{12,8},{16,20},{20,16},{24,28},{28,24},{1,5},{5... | collective-permute-start | bytes 393224 | tf_op jit(solution)/shard_map/ppermute | solution.py:173
  38.1 5.2 %collective-permute-start.18 = (f16[2,128,128]{2,1,0:T(8,128)(2,1)S(1)}, f16[2,128,128]{2,1,0:T(8,128)(2,1)S(1)}, u32[]{:S(2)}, u32[]{:S(2)}) collective-permute-start(f16[2,128,128]{2,1,0:T(8,128)(2,1)S(1)} %add_convert_fusion.3), channel_id=1, source_target_pairs={{0,24},{1,25},{2,26},{3,27},{4,7},{5,6},{6,5},{7,4},{8,16},{9,17},... | collective-permute-start | bytes 196616 | tf_op jit(solution)/shard_map/ppermute | solution.py:185
  39.6 4.4 %collective-permute-start.17 = (f16[2,128,128]{2,1,0:T(8,128)(2,1)S(1)}, f16[2,128,128]{2,1,0:T(8,128)(2,1)S(1)}, u32[]{:S(2)}, u32[]{:S(2)}) collective-permute-start(f16[2,128,128]{2,1,0:T(8,128)(2,1)S(1)} %add_convert_fusion.3), channel_id=1, source_target_pairs={{0,16},{1,17},{2,18},{3,19},{4,6},{5,7},{6,4},{7,5},{8,24},{9,25},... | collective-permute-start | bytes 196616 | tf_op jit(solution)/shard_map/ppermute | solution.py:185
  40.1 4.3 %collective-permute-start.16 = (f16[2,128,128]{2,1,0:T(8,128)(2,1)S(1)}, f16[2,128,128]{2,1,0:T(8,128)(2,1)S(1)}, u32[]{:S(2)}, u32[]{:S(2)}) collective-permute-start(f16[2,128,128]{2,1,0:T(8,128)(2,1)S(1)} %add_convert_fusion.3), channel_id=1, source_target_pairs={{0,8},{1,9},{2,10},{3,11},{4,5},{5,4},{6,7},{7,6},{8,0},{9,1},{10,... | collective-permute-start | bytes 196616 | tf_op jit(solution)/shard_map/ppermute | solution.py:185
  44.5 6.1 %collective-permute-start.21 = (f16[2,128,128]{2,1,0:T(8,128)(2,1)S(1)}, f16[2,128,128]{2,1,0:T(8,128)(2,1)S(1)}, u32[]{:S(2)}, u32[]{:S(2)}) collective-permute-start(f16[2,128,128]{2,1,0:T(8,128)(2,1)S(1)} %add_convert_fusion.2), channel_id=1, source_target_pairs={{0,3},{1,2},{2,1},{3,0},{4,28},{5,29},{6,30},{7,31},{8,11},{9,10},... | collective-permute-start | bytes 196616 | tf_op jit(solution)/shard_map/ppermute | solution.py:185
  46.8 5.6 %collective-permute-start.20 = (f16[2,128,128]{2,1,0:T(8,128)(2,1)S(1)}, f16[2,128,128]{2,1,0:T(8,128)(2,1)S(1)}, u32[]{:S(2)}, u32[]{:S(2)}) collective-permute-start(f16[2,128,128]{2,1,0:T(8,128)(2,1)S(1)} %add_convert_fusion.2), channel_id=1, source_target_pairs={{0,2},{1,3},{2,0},{3,1},{4,20},{5,21},{6,22},{7,23},{8,10},{9,11},... | collective-permute-start | bytes 196616 | tf_op jit(solution)/shard_map/ppermute | solution.py:185
  46.8 5.6 %collective-permute-start.19 = (f16[2,128,128]{2,1,0:T(8,128)(2,1)S(1)}, f16[2,128,128]{2,1,0:T(8,128)(2,1)S(1)}, u32[]{:S(2)}, u32[]{:S(2)}) collective-permute-start(f16[2,128,128]{2,1,0:T(8,128)(2,1)S(1)} %add_convert_fusion.2), channel_id=1, source_target_pairs={{0,1},{1,0},{2,3},{3,2},{4,12},{5,13},{6,14},{7,15},{8,9},{9,8},{1... | collective-permute-start | bytes 196616 | tf_op jit(solution)/shard_map/ppermute | solution.py:185
  52.4 1.4 %collective-permute-start.22 = (f32[2,128,128]{2,1,0:T(8,128)S(1)}, f32[2,128,128]{2,1,0:T(8,128)S(1)}, u32[]{:S(2)}, u32[]{:S(2)}) collective-permute-start(f32[2,128,128]{2,1,0:T(8,128)S(1)} %add_add_fusion.1.own), channel_id=1, source_target_pairs={{0,4},{4,0},{8,12},{12,8},{16,20},{20,16},{24,28},{28,24},{1,5},{5... | collective-permute-start | bytes 393224 | tf_op jit(solution)/shard_map/ppermute | solution.py:173
  56.3 1.4 %collective-permute-start.23 = (f32[2,128,128]{2,1,0:T(8,128)S(1)}, f32[2,128,128]{2,1,0:T(8,128)S(1)}, u32[]{:S(2)}, u32[]{:S(2)}) collective-permute-start(f32[2,128,128]{2,1,0:T(8,128)S(1)} %get-tuple-element.43), channel_id=1, source_target_pairs={{0,4},{4,0},{8,12},{12,8},{16,20},{20,16},{24,28},{28,24},{1,5},{5... | collective-permute-start | bytes 393224 | tf_op jit(solution)/shard_map/ppermute | solution.py:173
  57.7 5.2 %collective-permute-start.26 = (f16[2,128,128]{2,1,0:T(8,128)(2,1)S(1)}, f16[2,128,128]{2,1,0:T(8,128)(2,1)S(1)}, u32[]{:S(2)}, u32[]{:S(2)}) collective-permute-start(f16[2,128,128]{2,1,0:T(8,128)(2,1)S(1)} %add_convert_fusion.1), channel_id=1, source_target_pairs={{0,24},{1,25},{2,26},{3,27},{4,7},{5,6},{6,5},{7,4},{8,16},{9,17},... | collective-permute-start | bytes 196616 | tf_op jit(solution)/shard_map/ppermute | solution.py:185
  60.3 4.3 %collective-permute-start.25 = (f16[2,128,128]{2,1,0:T(8,128)(2,1)S(1)}, f16[2,128,128]{2,1,0:T(8,128)(2,1)S(1)}, u32[]{:S(2)}, u32[]{:S(2)}) collective-permute-start(f16[2,128,128]{2,1,0:T(8,128)(2,1)S(1)} %add_convert_fusion.1), channel_id=1, source_target_pairs={{0,16},{1,17},{2,18},{3,19},{4,6},{5,7},{6,4},{7,5},{8,24},{9,25},... | collective-permute-start | bytes 196616 | tf_op jit(solution)/shard_map/ppermute | solution.py:185
  60.8 4.3 %collective-permute-start.24 = (f16[2,128,128]{2,1,0:T(8,128)(2,1)S(1)}, f16[2,128,128]{2,1,0:T(8,128)(2,1)S(1)}, u32[]{:S(2)}, u32[]{:S(2)}) collective-permute-start(f16[2,128,128]{2,1,0:T(8,128)(2,1)S(1)} %add_convert_fusion.1), channel_id=1, source_target_pairs={{0,8},{1,9},{2,10},{3,11},{4,5},{5,4},{6,7},{7,6},{8,0},{9,1},{10,... | collective-permute-start | bytes 196616 | tf_op jit(solution)/shard_map/ppermute | solution.py:185
  65.1 6.1 %collective-permute-start.29 = (f16[2,128,128]{2,1,0:T(8,128)(2,1)S(1)}, f16[2,128,128]{2,1,0:T(8,128)(2,1)S(1)}, u32[]{:S(2)}, u32[]{:S(2)}) collective-permute-start(f16[2,128,128]{2,1,0:T(8,128)(2,1)S(1)} %add_convert_fusion), channel_id=1, source_target_pairs={{0,3},{1,2},{2,1},{3,0},{4,28},{5,29},{6,30},{7,31},{8,11},{9,10},... | collective-permute-start | bytes 196616 | tf_op jit(solution)/shard_map/ppermute | solution.py:185
  67.1 5.5 %collective-permute-start.28 = (f16[2,128,128]{2,1,0:T(8,128)(2,1)S(1)}, f16[2,128,128]{2,1,0:T(8,128)(2,1)S(1)}, u32[]{:S(2)}, u32[]{:S(2)}) collective-permute-start(f16[2,128,128]{2,1,0:T(8,128)(2,1)S(1)} %add_convert_fusion), channel_id=1, source_target_pairs={{0,2},{1,3},{2,0},{3,1},{4,20},{5,21},{6,22},{7,23},{8,10},{9,11},... | collective-permute-start | bytes 196616 | tf_op jit(solution)/shard_map/ppermute | solution.py:185
  67.4 5.2 %collective-permute-start.27 = (f16[2,128,128]{2,1,0:T(8,128)(2,1)S(1)}, f16[2,128,128]{2,1,0:T(8,128)(2,1)S(1)}, u32[]{:S(2)}, u32[]{:S(2)}) collective-permute-start(f16[2,128,128]{2,1,0:T(8,128)(2,1)S(1)} %add_convert_fusion), channel_id=1, source_target_pairs={{0,1},{1,0},{2,3},{3,2},{4,12},{5,13},{6,14},{7,15},{8,9},{9,8},{1... | collective-permute-start | bytes 196616 | tf_op jit(solution)/shard_map/ppermute | solution.py:185
  72.7 1.4 %collective-permute-start.30 = (f32[2,128,128]{2,1,0:T(8,128)S(1)}, f32[2,128,128]{2,1,0:T(8,128)S(1)}, u32[]{:S(2)}, u32[]{:S(2)}) collective-permute-start(f32[2,128,128]{2,1,0:T(8,128)S(1)} %add_add_fusion.own), channel_id=1, source_target_pairs={{0,4},{4,0},{8,12},{12,8},{16,20},{20,16},{24,28},{28,24},{1,5},{5... | collective-permute-start | bytes 393224 | tf_op jit(solution)/shard_map/ppermute | solution.py:173

commit v5 on v4

--- a/solution.py
+++ b/solution.py
@@ -13,6 +13,7 @@
 LEFT_MAX = 1.16462404
 RIGHT_MAX = 0.010778794
 VMEM = pl.BlockSpec(memory_space=pltpu.VMEM)
+ANY = pl.BlockSpec(memory_space=pl.ANY)
 HBM = pl.BlockSpec(memory_space=pltpu.HBM)
 SMEM = pl.BlockSpec(memory_space=pltpu.SMEM)
 F32 = jnp.float32
@@ -32,6 +33,12 @@
 def live(table, g, acc):
     sectors, rows, cols = acc.shape
     return lax.broadcasted_iota(jnp.int32, (rows, cols), 0) < table[table.shape[0] - sectors + g]
+
+
+def halves(sectors):
+    h = sectors // 2
+    low = lax.axis_index("terms") % 2
+    return low * h, (1 - low) * h
 
 
 def apply_ops(wire, square, blocks, acc, table, left, right, keep, send):
@@ -49,10 +56,17 @@
 
     lax.fori_loop(0, terms // unroll, group, 0)
     gain = (wire / jnp.sqrt(square / (sectors * rows * cols)))[None]
-    h = sectors // 2
-    low = lax.axis_index("terms") % 2
-    keep[...] = acc[pl.ds(low * h, h)] * gain
-    send[...] = acc[pl.ds((1 - low) * h, h)] * gain
+    own, far = halves(sectors)
+    keep[...] = acc[pl.ds(own, sectors // 2)] * gain
+    send[...] = acc[pl.ds(far, sectors // 2)] * gain
+
+
+def note(state, old, values):
+    line = lax.broadcasted_iota(jnp.int32, state.shape, 0)
+    tile = old
+    for row, value in values:
+        tile = jnp.where(line == row, value, tile)
+    state[...] = tile
 
 
 def load_kernel(rows_hbm, owner_hbm, in_hbm, out_hbm, left_hbm, right_hbm, left, right, table,
@@ -85,9 +99,9 @@
 
 
 def first_kernel(wire, *refs):
-    table, left, right, vec, pre, state, keep, send, blocks, acc = refs[-10:]
+    table, left, right, vec, pre, inv, state, keep, send, blocks, acc = refs[-11:]
     sectors, rows, cols = acc.shape
-    parts = (len(refs) - 10) // 2
+    parts = (len(refs) - 11) // 2
     mine, other = refs[:parts], refs[parts : 2 * parts]
     low = lax.axis_index("terms") % 2
 
@@ -103,65 +117,71 @@
     def _():
         load(other, mine)
 
-    tile = jnp.zeros((8, cols), F32)
+    squares = weighted = jnp.zeros((8, cols), F32)
     for g in range(sectors):
         v = vec[g]
         blocks[g] = v.astype(BF16)
-        tile = tile + lanes(v * v)
-    square = jnp.maximum(total(tile), 1e-30)
-    state[...] = jnp.broadcast_to(square, state.shape)
+        inv[g] = jnp.where(live(table, g, acc), 1.0 / pre[g], 0.0)
+        squares = squares + lanes(v * v)
+        weighted = weighted + lanes(pre[g] * (v * v))
+    square = jnp.maximum(total(squares), 1e-30)
+    note(state, jnp.zeros(state.shape, F32), ((0, square), (1, total(weighted))))
     apply_ops(wire, square, blocks, acc, table, left, right, keep, send)
 
 
-def update(wire, own, far, table, vec, pre, square, full, out):
-    sectors, rows, cols = full.shape
-    h = sectors // 2
-    low = lax.axis_index("terms") % 2
-    full[pl.ds(low * h, h)] = own[...]
-    full[pl.ds((1 - low) * h, h)] = far[...]
+def update(wire, sums, vec, inv, old, out):
+    sectors, rows, cols = out.shape
+    zero = jnp.zeros((8, cols), F32)
+    square, weighted = old[0:1, 0:1], old[1:2, 0:1]
     gain = jnp.sqrt(square / (sectors * rows * cols)) / wire
-    tile = jnp.zeros((8, cols), F32)
-    for g in range(sectors):
-        v = vec[g]
-        summed = jnp.where(live(table, g, full), full[g] * gain, 0.0)
-        full[g] = summed
-        tile = tile + lanes(v * (summed - pre[g] * v))
-    rayleigh = total(tile) / square
-    tile = jnp.zeros((8, cols), F32)
-    for g in range(sectors):
-        v = vec[g]
-        u = 2.0 * v - (full[g] - rayleigh * v) / pre[g]
-        out[g] = u
-        tile = tile + lanes(u * u)
-    scale = 1.0 / jnp.sqrt(total(tile) / (sectors * rows * cols) + 1e-06)
+    tiles = []
+    for base, part in zip(halves(sectors), sums):
+        tile = zero
+        for j in range(sectors // 2):
+            tile = tile + lanes(vec[base + j] * part[j])
+        tiles.append(tile)
+    rayleigh = (total(tiles[0] + tiles[1]) * gain - weighted) / square
+    tiles = []
+    for base, part in zip(halves(sectors), sums):
+        tile = zero
+        for j in range(sectors // 2):
+            v = vec[base + j]
+            u = 2.0 * v - (part[j] * gain - rayleigh * v) * inv[base + j]
+            out[base + j] = u
+            tile = tile + lanes(u * u)
+        tiles.append(tile)
+    scale = 1.0 / jnp.sqrt(total(tiles[0] + tiles[1]) / (sectors * rows * cols) + 1e-06)
     return rayleigh, scale
 
 
-def middle_kernel(wire, step, own, far, vec_in, pre, state_in, table, left, right,
-                  vec, state, keep, send, full, blocks, acc):
+def middle_kernel(wire, step, own, far, vec_in, pre, inv, state_in, table_in, left, right,
+                  vec, state, keep, send, blocks, acc, table, sem):
     sectors, rows, cols = acc.shape
+    copy = pltpu.make_async_copy(table_in, table, sem)
+    copy.start()
     old = state_in[...]
-    rayleigh, scale = update(wire, own, far, table, vec_in, pre, old[0:1, 0:1], full, vec)
-    tile = jnp.zeros((8, cols), F32)
+    rayleigh, scale = update(wire, (own, far), vec_in, inv, old, vec)
+    squares = weighted = jnp.zeros((8, cols), F32)
     for g in range(sectors):
         v = vec[g] * scale
         vec[g] = v
         blocks[g] = v.astype(BF16)
-        tile = tile + lanes(v * v)
-    square = jnp.maximum(total(tile), 1e-30)
-    line = lax.broadcasted_iota(jnp.int32, old.shape, 0)
-    state[...] = jnp.where(line == 0, square, jnp.where(line == step, rayleigh, old))
+        squares = squares + lanes(v * v)
+        weighted = weighted + lanes(pre[g] * (v * v))
+    square = jnp.maximum(total(squares), 1e-30)
+    note(state, old, ((0, square), (1, total(weighted)), (1 + step, rayleigh)))
+    copy.wait()
     apply_ops(wire, square, blocks, acc, table, left, right, keep, send)
 
 
-def last_kernel(wire, step, own, far, vec_in, pre, state_in, table, out, energies, full, fresh):
+def last_kernel(wire, step, own, far, vec, inv, state, out, energies, fresh):
     held = out.shape[0]
-    old = state_in[...]
-    rayleigh, scale = update(wire, own, far, table, vec_in, pre, old[0:1, 0:1], full, fresh)
+    old = state[...]
+    rayleigh, scale = update(wire, (own, far), vec, inv, old, fresh)
     first = lax.axis_index("sectors") * held
     out[...] = fresh[pl.ds(first, held)] * scale[None]
     for i in range(1, step):
-        energies[i - 1] = jnp.sum(old[i : i + 1, 0:1])
+        energies[i - 1] = jnp.sum(old[i + 1 : i + 2, 0:1])
     energies[step - 1] = jnp.sum(rayleigh)
 
 
@@ -235,11 +255,11 @@
     mine, (left, right, table) = lax.optimization_barrier((mine, (left, right, table)))
     other = [swapped] + [swap(x, "terms", 1) for x in mine]
     mine = [picked] + mine
-    vec, pre, state, keep, send = pl.pallas_call(
+    vec, pre, inv, state, keep, send = pl.pallas_call(
         functools.partial(first_kernel, wire),
-        out_shape=(whole, whole, state_shape, part, part),
+        out_shape=(whole, whole, whole, state_shape, part, part),
         in_specs=[VMEM] * (2 * len(mine)) + [SMEM] + [VMEM] * 2,
-        out_specs=(VMEM,) * 5,
+        out_specs=(VMEM,) * 6,
         scratch_shapes=scratch,
         compiler_params=params(),
     )(*mine, *other, table, left, right)
@@ -249,21 +269,21 @@
         vec, state, keep, send = pl.pallas_call(
             functools.partial(middle_kernel, wire, step),
             out_shape=(whole, state_shape, part, part),
-            in_specs=[VMEM] * 5 + [SMEM] + [VMEM] * 2,
+            in_specs=[VMEM] * 6 + [ANY] + [VMEM] * 2,
             out_specs=(VMEM,) * 4,
-            scratch_shapes=[full] + scratch,
+            scratch_shapes=scratch + [pltpu.SMEM(table.shape, jnp.int32), pltpu.SemaphoreType.DMA],
             compiler_params=params(),
-        )(own, far, vec, pre, state, table, left, right)
+        )(own, far, vec, pre, inv, state, table, left, right)
     own = reduce_half(keep, send)
     far = swap(own, "terms", 1)
     return pl.pallas_call(
         functools.partial(last_kernel, wire, STEPS),
         out_shape=(jax.ShapeDtypeStruct(trial.shape, F32), jax.ShapeDtypeStruct((STEPS,), F32)),
-        in_specs=[VMEM] * 5 + [SMEM],
+        in_specs=[VMEM] * 5,
         out_specs=(VMEM, SMEM),
-        scratch_shapes=[full, full],
+        scratch_shapes=[full],
         compiler_params=params(),
-    )(own, far, vec, pre, state, table)
+    )(own, far, vec, inv, state)
 
 
 def solution(mesh):

time: 75.8 us -> 75.1 us (level)
  Pallas kernels: 11.4 us -> 10.6 us
where the time goes in v5:
time: 75.1 us; the launch traced here: 74.9 us
  starting transfers between devices  31.2 us (42%)
  waiting for transfers between devices  31.2 us (42%)
  Pallas kernels  10.6 us (14%)
  other arithmetic  1.15 us (2%)
  between operations  0.76 us (1%)
    ppermute x18, starting transfers between devices, exchange(): lax.ppermute(x, ('terms', 'sectors'), [(d, d ^ masks[d // sectors % 2]) f...  24 us
    ppermute x18, waiting for transfers between devices, exchange(): lax.ppermute(x, ('terms', 'sectors'), [(d, d ^ masks[d // sectors % 2]) f...  20.3 us
    ppermute x13, waiting for transfers between devices, swap(): lax.ppermute(x, axis, [(i, i ^ mask) for i in range(lax.axis_size(axis))])  10.9 us
    ppermute x13, starting transfers between devices, swap(): lax.ppermute(x, axis, [(i, i ^ mask) for i in range(lax.axis_size(axis))])  7.14 us
    pallas_call x2, Pallas kernels, on_device(): pl.pallas_call(functools.partial(middle_kernel, wire, step), out_shape=(w...  4.68 us
    pallas_call x1, Pallas kernels, on_device(): pl.pallas_call(load_kernel, out_shape=(jax.ShapeDtypeStruct(left_ops.shap...  2.88 us
    pallas_call x1, Pallas kernels, on_device(): pl.pallas_call(functools.partial(first_kernel, wire), out_shape=(whole, w...  2.07 us
  transfers between devices with their start and end apart: 31, of which 25 were waited for; matrix products, arithmetic and copies ran while one was open for 0% of the time, Pallas kernels for 4%

profile of v5, /device:TPU:0, one launch (start us, length us, event | category | flops | bytes accessed | tf_op | source)
XLA Modules:
  0.0 74.9 jit_solution(4311157622163510148)
XLA Ops:
  0.6 0.9 %broadcast_select_fusion.refs_0_ = f32[1,128,128]{2,1,0:T(8,128)S(1)} fusion(f32[1,128,128]{2,1,0:T(8,128)} %param.8, f32[1,128,128]{2,1,0:T(8,128)} %param.9, pred[]{:T(512)S(6)} %eq.5), kind=kLoop, calls=%fused_computation.9 | loop fusion | flops 16384 | bytes 196609 | tf_op jit(solution)/shard_map/jit(_where)/select_n | solution.py:252
  1.5 5.1 %collective-permute-start.2 = (f32[1,128,128]{2,1,0:T(8,128)S(1)}, f32[1,128,128]{2,1,0:T(8,128)S(1)}, u32[]{:S(2)}, u32[]{:S(2)}) collective-permute-start(f32[1,128,128]{2,1,0:T(8,128)S(1)} %broadcast_select_fusion.refs_0_), channel_id=1, source_target_pairs={{0,3},{1,2},{2,1},{3,0},{4,7},{5,6},{6,5},{7,4},{8,11},{9,10},{10,... | collective-permute-start | bytes 196616 | tf_op jit(solution)/shard_map/ppermute | solution.py:193
  6.6 0.6 collective-permute-start
  7.3 2.9 %shard_map.95 = (bf16[64,128,128]{2,1,0:T(8,128)(2,1)S(1)}, bf16[64,128,128]{2,1,0:T(8,128)(2,1)S(1)}, s32[132]{0:T(256)S(1)}) custom-call(s32[4]{0:T(128)} %rows_hbm.1, s32[4]{0:T(128)} %owner_hbm.1, s32[64]{0:T(128)} %in_hbm.1, s32[64]{0:T(128)} %out_hbm.1, bf16[64,128,128]{2,1,0:T(8,128)(2,1)} %left_hbm.1, bf16[64,128,128]{2,1,0:T(8,128)(2,1)} %right_hbm.1), custom_call_target="tpu_custom_call" | custom-call | bytes 4194304 | tf_op jit(solution)/shard_map/pallas_call | solution.py:238
  10.2 2.1 %collective-permute-done.1.refs_2_ = f32[1,128,128]{2,1,0:T(8,128)S(1)} collective-permute-done((f32[1,128,128]{2,1,0:T(8,128)S(1)}, f32[1,128,128]{2,1,0:T(8,128)S(1)}, u32[]{:S(2)}, u32[]{:S(2)}) %collective-permute-start.1) | collective-permute-done | bytes 65568 | tf_op jit(solution)/shard_map/ppermute | solution.py:193
  12.2 0.5 collective-permute-start.5
  12.7 0.7 collective-permute-done.4.refs_5_
  13.6 0.4 collective-permute-done.6.refs_7_
  14.0 2.1 %shard_map.96 = (f32[4,128,128]{2,1,0:T(8,128)S(1)}, f32[4,128,128]{2,1,0:T(8,128)S(1)}, f32[4,128,128]{2,1,0:T(8,128)S(1)}, f32[8,128]{1,0:T(8,128)S(1)}, f32[2...) custom-call(f32[1,128,128]{2,1,0:T(8,128)S(1)} %broadcast_select_fusion.refs_0_, ...), custom_call_target="tpu_custom_call" | custom-call | tf_op jit(solution)/shard_map/pallas_call | solution.py:258
  16.3 1.2 %collective-permute-done.7 = f32[2,128,128]{2,1,0:T(8,128)S(1)} collective-permute-done((f32[2,128,128]{2,1,0:T(8,128)S(1)}, f32[2,128,128]{2,1,0:T(8,128)S(1)}, u32[]{:S(2)}, u32[]{:S(2)}) %collective-permute-start.7) | collective-permute-done | bytes 131104 | tf_op jit(solution)/shard_map/ppermute | solution.py:193
  17.5 2.5 %collective-permute-start.10 = (f16[2,128,128]{2,1,0:T(8,128)(2,1)S(1)}, f16[2,128,128]{2,1,0:T(8,128)(2,1)S(1)}, u32[]{:S(2)}, u32[]{:S(2)}) collective-permute-start(f16[2,128,128]{2,1,0:T(8,128)(2,1)S(1)} %add_convert_fusion.5), channel_id=1, source_target_pairs={{0,24},{1,25},{2,26},{3,27},{4,7},{5,6},{6,5},{7,4},{8,16},{9,17},... | collective-permute-start | bytes 196616 | tf_op jit(solution)/shard_map/ppermute | solution.py:205
  20.0 0.5 collective-permute-start.9
  20.5 0.5 collective-permute-start.8
  21.1 1.7 %collective-permute-done.10 = f16[2,128,128]{2,1,0:T(8,128)(2,1)S(1)} collective-permute-done((f16[2,128,128]{2,1,0:T(8,128)(2,1)S(1)}, f16[2,128,128]{2,1,0:T(8,128)(2,1)S(1)}, u32[]{:S(2)}, u32[]{:S(2)}) %collective-permute-start.10) | collective-permute-done | bytes 65568 | tf_op jit(solution)/shard_map/ppermute | solution.py:205
  22.7 1.6 %collective-permute-done.9 = f16[2,128,128]{2,1,0:T(8,128)(2,1)S(1)} collective-permute-done((f16[2,128,128]{2,1,0:T(8,128)(2,1)S(1)}, f16[2,128,128]{2,1,0:T(8,128)(2,1)S(1)}, u32[]{:S(2)}, u32[]{:S(2)}) %collective-permute-start.9) | collective-permute-done | bytes 65568 | tf_op jit(solution)/shard_map/ppermute | solution.py:205
  24.3 0.5 collective-permute-done.8
  24.8 2.8 %collective-permute-start.13 = (f16[2,128,128]{2,1,0:T(8,128)(2,1)S(1)}, f16[2,128,128]{2,1,0:T(8,128)(2,1)S(1)}, u32[]{:S(2)}, u32[]{:S(2)}) collective-permute-start(f16[2,128,128]{2,1,0:T(8,128)(2,1)S(1)} %add_convert_fusion.4), channel_id=1, source_target_pairs={{0,3},{1,2},{2,1},{3,0},{4,28},{5,29},{6,30},{7,31},{8,11},{9,10},... | collective-permute-start | bytes 196616 | tf_op jit(solution)/shard_map/ppermute | solution.py:205
  27.6 1.7 %collective-permute-start.11 = (f16[2,128,128]{2,1,0:T(8,128)(2,1)S(1)}, f16[2,128,128]{2,1,0:T(8,128)(2,1)S(1)}, u32[]{:S(2)}, u32[]{:S(2)}) collective-permute-start(f16[2,128,128]{2,1,0:T(8,128)(2,1)S(1)} %add_convert_fusion.4), channel_id=1, source_target_pairs={{0,1},{1,0},{2,3},{3,2},{4,12},{5,13},{6,14},{7,15},{8,9},{9,8},{1... | collective-permute-start | bytes 196616 | tf_op jit(solution)/shard_map/ppermute | solution.py:205
  29.3 1.7 %collective-permute-done.13 = f16[2,128,128]{2,1,0:T(8,128)(2,1)S(1)} collective-permute-done((f16[2,128,128]{2,1,0:T(8,128)(2,1)S(1)}, f16[2,128,128]{2,1,0:T(8,128)(2,1)S(1)}, u32[]{:S(2)}, u32[]{:S(2)}) %collective-permute-start.13) | collective-permute-done | bytes 65568 | tf_op jit(solution)/shard_map/ppermute | solution.py:205
  31.0 1.8 %collective-permute-done.12 = f16[2,128,128]{2,1,0:T(8,128)(2,1)S(1)} collective-permute-done((f16[2,128,128]{2,1,0:T(8,128)(2,1)S(1)}, f16[2,128,128]{2,1,0:T(8,128)(2,1)S(1)}, u32[]{:S(2)}, u32[]{:S(2)}) %collective-permute-start.12) | collective-permute-done | bytes 65568 | tf_op jit(solution)/shard_map/ppermute | solution.py:205
  32.9 1.3 %collective-permute-done.14.far = f32[2,128,128]{2,1,0:T(8,128)S(1)} collective-permute-done((f32[2,128,128]{2,1,0:T(8,128)S(1)}, f32[2,128,128]{2,1,0:T(8,128)S(1)}, u32[]{:S(2)}, u32[]{:S(2)}) %collective-permute-start.14) | collective-permute-done | bytes 131104 | tf_op jit(solution)/shard_map/ppermute | solution.py:193
  34.2 2.3 %shard_map.97 = (f32[4,128,128]{2,1,0:T(8,128)S(1)}, f32[8,128]{1,0:T(8,128)S(1)}, f32[2,128,128]{2,1,0:T(8,128)S(1)}, f32[2,128,128]{2,1,0:T(8,128)S(1)}) custom-call(f32[2,128,128]{2,1,0:T(8,128)S(1)} %add_add_fusion.2.own, f32[2,128,128]{2,1,0:T(8,128)S(1)} %collective-permute-done.14.far, f32[4,128,128]{2,1,0:T(8,128)S(1)} %get-tuple-element.36.vec_in, ...), custom_call_target="tpu_custom_call" | custom-call | tf_op jit(solution)/shard_map/pallas_call | solution.py:269
  36.8 1.2 %collective-permute-done.15 = f32[2,128,128]{2,1,0:T(8,128)S(1)} collective-permute-done((f32[2,128,128]{2,1,0:T(8,128)S(1)}, f32[2,128,128]{2,1,0:T(8,128)S(1)}, u32[]{:S(2)}, u32[]{:S(2)}) %collective-permute-start.15) | collective-permute-done | bytes 131104 | tf_op jit(solution)/shard_map/ppermute | solution.py:193
  38.0 1.6 %collective-permute-start.18 = (f16[2,128,128]{2,1,0:T(8,128)(2,1)S(1)}, f16[2,128,128]{2,1,0:T(8,128)(2,1)S(1)}, u32[]{:S(2)}, u32[]{:S(2)}) collective-permute-start(f16[2,128,128]{2,1,0:T(8,128)(2,1)S(1)} %add_convert_fusion.3), channel_id=1, source_target_pairs={{0,24},{1,25},{2,26},{3,27},{4,7},{5,6},{6,5},{7,4},{8,16},{9,17},... | collective-permute-start | bytes 196616 | tf_op jit(solution)/shard_map/ppermute | solution.py:205
  39.6 0.5 collective-permute-start.17
  40.1 1.5 %collective-permute-start.16 = (f16[2,128,128]{2,1,0:T(8,128)(2,1)S(1)}, f16[2,128,128]{2,1,0:T(8,128)(2,1)S(1)}, u32[]{:S(2)}, u32[]{:S(2)}) collective-permute-start(f16[2,128,128]{2,1,0:T(8,128)(2,1)S(1)} %add_convert_fusion.3), channel_id=1, source_target_pairs={{0,8},{1,9},{2,10},{3,11},{4,5},{5,4},{6,7},{7,6},{8,0},{9,1},{10,... | collective-permute-start | bytes 196616 | tf_op jit(solution)/shard_map/ppermute | solution.py:205
  41.6 1.7 %collective-permute-done.18 = f16[2,128,128]{2,1,0:T(8,128)(2,1)S(1)} collective-permute-done((f16[2,128,128]{2,1,0:T(8,128)(2,1)S(1)}, f16[2,128,128]{2,1,0:T(8,128)(2,1)S(1)}, u32[]{:S(2)}, u32[]{:S(2)}) %collective-permute-start.18) | collective-permute-done | bytes 65568 | tf_op jit(solution)/shard_map/ppermute | solution.py:205
  43.3 0.7 collective-permute-done.17
  44.0 0.4 collective-permute-done.16
  44.4 2.4 %collective-permute-start.21 = (f16[2,128,128]{2,1,0:T(8,128)(2,1)S(1)}, f16[2,128,128]{2,1,0:T(8,128)(2,1)S(1)}, u32[]{:S(2)}, u32[]{:S(2)}) collective-permute-start(f16[2,128,128]{2,1,0:T(8,128)(2,1)S(1)} %add_convert_fusion.2), channel_id=1, source_target_pairs={{0,3},{1,2},{2,1},{3,0},{4,28},{5,29},{6,30},{7,31},{8,11},{9,10},... | collective-permute-start | bytes 196616 | tf_op jit(solution)/shard_map/ppermute | solution.py:205
  46.8 2.1 %collective-permute-start.19 = (f16[2,128,128]{2,1,0:T(8,128)(2,1)S(1)}, f16[2,128,128]{2,1,0:T(8,128)(2,1)S(1)}, u32[]{:S(2)}, u32[]{:S(2)}) collective-permute-start(f16[2,128,128]{2,1,0:T(8,128)(2,1)S(1)} %add_convert_fusion.2), channel_id=1, source_target_pairs={{0,1},{1,0},{2,3},{3,2},{4,12},{5,13},{6,14},{7,15},{8,9},{9,8},{1... | collective-permute-start | bytes 196616 | tf_op jit(solution)/shard_map/ppermute | solution.py:205
  48.9 1.7 %collective-permute-done.21 = f16[2,128,128]{2,1,0:T(8,128)(2,1)S(1)} collective-permute-done((f16[2,128,128]{2,1,0:T(8,128)(2,1)S(1)}, f16[2,128,128]{2,1,0:T(8,128)(2,1)S(1)}, u32[]{:S(2)}, u32[]{:S(2)}) %collective-permute-start.21) | collective-permute-done | bytes 65568 | tf_op jit(solution)/shard_map/ppermute | solution.py:205
  50.5 1.8 %collective-permute-done.20 = f16[2,128,128]{2,1,0:T(8,128)(2,1)S(1)} collective-permute-done((f16[2,128,128]{2,1,0:T(8,128)(2,1)S(1)}, f16[2,128,128]{2,1,0:T(8,128)(2,1)S(1)}, u32[]{:S(2)}, u32[]{:S(2)}) %collective-permute-start.20) | collective-permute-done | bytes 65568 | tf_op jit(solution)/shard_map/ppermute | solution.py:205
  52.5 1.3 %collective-permute-done.22.far = f32[2,128,128]{2,1,0:T(8,128)S(1)} collective-permute-done((f32[2,128,128]{2,1,0:T(8,128)S(1)}, f32[2,128,128]{2,1,0:T(8,128)S(1)}, u32[]{:S(2)}, u32[]{:S(2)}) %collective-permute-start.22) | collective-permute-done | bytes 131104 | tf_op jit(solution)/shard_map/ppermute | solution.py:193
  53.8 2.3 %shard_map.98 = (f32[4,128,128]{2,1,0:T(8,128)S(1)}, f32[8,128]{1,0:T(8,128)S(1)}, f32[2,128,128]{2,1,0:T(8,128)S(1)}, f32[2,128,128]{2,1,0:T(8,128)S(1)}) custom-call(f32[2,128,128]{2,1,0:T(8,128)S(1)} %add_add_fusion.1.own, f32[2,128,128]{2,1,0:T(8,128)S(1)} %collective-permute-done.22.far, f32[4,128,128]{2,1,0:T(8,128)S(1)} %get-tuple-element.42.vec_in, ...), custom_call_target="tpu_custom_call" | custom-call | tf_op jit(solution)/shard_map/pallas_call | solution.py:269
  56.4 1.2 %collective-permute-done.23 = f32[2,128,128]{2,1,0:T(8,128)S(1)} collective-permute-done((f32[2,128,128]{2,1,0:T(8,128)S(1)}, f32[2,128,128]{2,1,0:T(8,128)S(1)}, u32[]{:S(2)}, u32[]{:S(2)}) %collective-permute-start.23) | collective-permute-done | bytes 131104 | tf_op jit(solution)/shard_map/ppermute | solution.py:193
  57.6 2.5 %collective-permute-start.26 = (f16[2,128,128]{2,1,0:T(8,128)(2,1)S(1)}, f16[2,128,128]{2,1,0:T(8,128)(2,1)S(1)}, u32[]{:S(2)}, u32[]{:S(2)}) collective-permute-start(f16[2,128,128]{2,1,0:T(8,128)(2,1)S(1)} %add_convert_fusion.1), channel_id=1, source_target_pairs={{0,24},{1,25},{2,26},{3,27},{4,7},{5,6},{6,5},{7,4},{8,16},{9,17},... | collective-permute-start | bytes 196616 | tf_op jit(solution)/shard_map/ppermute | solution.py:205
  60.1 0.5 collective-permute-start.25
  60.6 0.5 collective-permute-start.24
  61.2 1.7 %collective-permute-done.26 = f16[2,128,128]{2,1,0:T(8,128)(2,1)S(1)} collective-permute-done((f16[2,128,128]{2,1,0:T(8,128)(2,1)S(1)}, f16[2,128,128]{2,1,0:T(8,128)(2,1)S(1)}, u32[]{:S(2)}, u32[]{:S(2)}) %collective-permute-start.26) | collective-permute-done | bytes 65568 | tf_op jit(solution)/shard_map/ppermute | solution.py:205
  62.8 1.6 %collective-permute-done.25 = f16[2,128,128]{2,1,0:T(8,128)(2,1)S(1)} collective-permute-done((f16[2,128,128]{2,1,0:T(8,128)(2,1)S(1)}, f16[2,128,128]{2,1,0:T(8,128)(2,1)S(1)}, u32[]{:S(2)}, u32[]{:S(2)}) %collective-permute-start.25) | collective-permute-done | bytes 65568 | tf_op jit(solution)/shard_map/ppermute | solution.py:205
  64.4 0.5 collective-permute-done.24
  64.9 2.1 %collective-permute-start.29 = (f16[2,128,128]{2,1,0:T(8,128)(2,1)S(1)}, f16[2,128,128]{2,1,0:T(8,128)(2,1)S(1)}, u32[]{:S(2)}, u32[]{:S(2)}) collective-permute-start(f16[2,128,128]{2,1,0:T(8,128)(2,1)S(1)} %add_convert_fusion), channel_id=1, source_target_pairs={{0,3},{1,2},{2,1},{3,0},{4,28},{5,29},{6,30},{7,31},{8,11},{9,10},... | collective-permute-start | bytes 196616 | tf_op jit(solution)/shard_map/ppermute | solution.py:205
  67.2 2.2 %collective-permute-start.27 = (f16[2,128,128]{2,1,0:T(8,128)(2,1)S(1)}, f16[2,128,128]{2,1,0:T(8,128)(2,1)S(1)}, u32[]{:S(2)}, u32[]{:S(2)}) collective-permute-start(f16[2,128,128]{2,1,0:T(8,128)(2,1)S(1)} %add_convert_fusion), channel_id=1, source_target_pairs={{0,1},{1,0},{2,3},{3,2},{4,12},{5,13},{6,14},{7,15},{8,9},{9,8},{1... | collective-permute-start | bytes 196616 | tf_op jit(solution)/shard_map/ppermute | solution.py:205
  69.4 1.7 %collective-permute-done.29 = f16[2,128,128]{2,1,0:T(8,128)(2,1)S(1)} collective-permute-done((f16[2,128,128]{2,1,0:T(8,128)(2,1)S(1)}, f16[2,128,128]{2,1,0:T(8,128)(2,1)S(1)}, u32[]{:S(2)}, u32[]{:S(2)}) %collective-permute-start.29) | collective-permute-done | bytes 65568 | tf_op jit(solution)/shard_map/ppermute | solution.py:205
  71.1 1.4 %collective-permute-done.28 = f16[2,128,128]{2,1,0:T(8,128)(2,1)S(1)} collective-permute-done((f16[2,128,128]{2,1,0:T(8,128)(2,1)S(1)}, f16[2,128,128]{2,1,0:T(8,128)(2,1)S(1)}, u32[]{:S(2)}, u32[]{:S(2)}) %collective-permute-start.28) | collective-permute-done | bytes 65568 | tf_op jit(solution)/shard_map/ppermute | solution.py:205
  72.6 1.3 %collective-permute-done.30.far = f32[2,128,128]{2,1,0:T(8,128)S(1)} collective-permute-done((f32[2,128,128]{2,1,0:T(8,128)S(1)}, f32[2,128,128]{2,1,0:T(8,128)S(1)}, u32[]{:S(2)}, u32[]{:S(2)}) %collective-permute-start.30) | collective-permute-done | bytes 131104 | tf_op jit(solution)/shard_map/ppermute | solution.py:193
  73.9 1.0 %shard_map.99 = (f32[1,128,128]{2,1,0:T(8,128)}, f32[3]{0:T(128)}) custom-call(f32[2,128,128]{2,1,0:T(8,128)S(1)} %add_add_fusion.own, f32[2,128,128]{2,1,0:T(8,128)S(1)} %collective-permute-done.30.far, f32[4,128,128]{2,1,0:T(8,128)S(1)} %get-tuple-element.46.vec, f32[4,128,128]{2,1,0:T(8,128)S(1)} %get-tuple-element.38.inv, ...), custom_call_target="tpu_custom_call" | custom-call | tf_op jit(solution)/shard_map/pallas_call | solution.py:279
  (29 shorter events, 1.6 us)
Async XLA Ops:
  1.5 8.6 %collective-permute-start.2 = (f32[1,128,128]{2,1,0:T(8,128)S(1)}, f32[1,128,128]{2,1,0:T(8,128)S(1)}, u32[]{:S(2)}, u32[]{:S(2)}) collective-permute-start(f32[1,128,128]{2,1,0:T(8,128)S(1)} %broadcast_select_fusion.refs_0_), channel_id=1, source_target_pairs={{0,3},{1,2},{2,1},{3,0},{4,7},{5,6},{6,5},{7,4},{8,11},{9,10},{10,... | collective-permute-start | bytes 196616 | tf_op jit(solution)/shard_map/ppermute | solution.py:193
  6.6 5.6 %collective-permute-start.1 = (f32[1,128,128]{2,1,0:T(8,128)S(1)}, f32[1,128,128]{2,1,0:T(8,128)S(1)}, u32[]{:S(2)}, u32[]{:S(2)}) collective-permute-start(f32[1,128,128]{2,1,0:T(8,128)S(1)} %broadcast_select_fusion.refs_0_), channel_id=1, source_target_pairs={{0,2},{1,3},{2,0},{3,1},{4,6},{5,7},{6,4},{7,5},{8,10},{9,11},{10,... | collective-permute-start | bytes 196616 | tf_op jit(solution)/shard_map/ppermute | solution.py:193
  6.6 5.6 %collective-permute-start = (f32[1,128,128]{2,1,0:T(8,128)S(1)}, f32[1,128,128]{2,1,0:T(8,128)S(1)}, u32[]{:S(2)}, u32[]{:S(2)}) collective-permute-start(f32[1,128,128]{2,1,0:T(8,128)S(1)} %broadcast_select_fusion.refs_0_), channel_id=1, source_target_pairs={{0,1},{1,0},{2,3},{3,2},{4,5},{5,4},{6,7},{7,6},{8,9},{9,8},{10,11... | collective-permute-start | bytes 196616 | tf_op jit(solution)/shard_map/ppermute | solution.py:193
  7.3 5.5 %collective-permute-start.3 = (f32[1,128,128]{2,1,0:T(8,128)S(1)}, f32[1,128,128]{2,1,0:T(8,128)S(1)}, u32[]{:S(2)}, u32[]{:S(2)}) collective-permute-start(f32[1,128,128]{2,1,0:T(8,128)S(1)} %broadcast_select_fusion.refs_0_), channel_id=1, source_target_pairs={{0,4},{4,0},{8,12},{12,8},{16,20},{20,16},{24,28},{28,24},{1,5},{5... | collective-permute-start | bytes 196616 | tf_op jit(solution)/shard_map/ppermute | solution.py:193
  12.2 1.3 %collective-permute-start.4 = (f32[1,128,128]{2,1,0:T(8,128)S(1)}, f32[1,128,128]{2,1,0:T(8,128)S(1)}, u32[]{:S(2)}, u32[]{:S(2)}) collective-permute-start(f32[1,128,128]{2,1,0:T(8,128)S(1)} %collective-permute-done.refs_1_), channel_id=1, source_target_pairs={{0,4},{4,0},{8,12},{12,8},{16,20},{20,16},{24,28},{28,24},{1,5},{5... | collective-permute-start | bytes 196616 | tf_op jit(solution)/shard_map/ppermute | solution.py:193
  12.2 1.4 %collective-permute-start.5 = (f32[1,128,128]{2,1,0:T(8,128)S(1)}, f32[1,128,128]{2,1,0:T(8,128)S(1)}, u32[]{:S(2)}, u32[]{:S(2)}) collective-permute-start(f32[1,128,128]{2,1,0:T(8,128)S(1)} %collective-permute-done.1.refs_2_), channel_id=1, source_target_pairs={{0,4},{4,0},{8,12},{12,8},{16,20},{20,16},{24,28},{28,24},{1,5},{5... | collective-permute-start | bytes 196616 | tf_op jit(solution)/shard_map/ppermute | solution.py:193
  12.7 1.3 %collective-permute-start.6 = (f32[1,128,128]{2,1,0:T(8,128)S(1)}, f32[1,128,128]{2,1,0:T(8,128)S(1)}, u32[]{:S(2)}, u32[]{:S(2)}) collective-permute-start(f32[1,128,128]{2,1,0:T(8,128)S(1)} %collective-permute-done.2.refs_3_), channel_id=1, source_target_pairs={{0,4},{4,0},{8,12},{12,8},{16,20},{20,16},{24,28},{28,24},{1,5},{5... | collective-permute-start | bytes 196616 | tf_op jit(solution)/shard_map/ppermute | solution.py:193
  16.1 1.4 %collective-permute-start.7 = (f32[2,128,128]{2,1,0:T(8,128)S(1)}, f32[2,128,128]{2,1,0:T(8,128)S(1)}, u32[]{:S(2)}, u32[]{:S(2)}) collective-permute-start(f32[2,128,128]{2,1,0:T(8,128)S(1)} %get-tuple-element.35), channel_id=1, source_target_pairs={{0,4},{4,0},{8,12},{12,8},{16,20},{20,16},{24,28},{28,24},{1,5},{5... | collective-permute-start | bytes 393224 | tf_op jit(solution)/shard_map/ppermute | solution.py:193
  17.5 5.2 %collective-permute-start.10 = (f16[2,128,128]{2,1,0:T(8,128)(2,1)S(1)}, f16[2,128,128]{2,1,0:T(8,128)(2,1)S(1)}, u32[]{:S(2)}, u32[]{:S(2)}) collective-permute-start(f16[2,128,128]{2,1,0:T(8,128)(2,1)S(1)} %add_convert_fusion.5), channel_id=1, source_target_pairs={{0,24},{1,25},{2,26},{3,27},{4,7},{5,6},{6,5},{7,4},{8,16},{9,17},... | collective-permute-start | bytes 196616 | tf_op jit(solution)/shard_map/ppermute | solution.py:205
  20.0 4.3 %collective-permute-start.9 = (f16[2,128,128]{2,1,0:T(8,128)(2,1)S(1)}, f16[2,128,128]{2,1,0:T(8,128)(2,1)S(1)}, u32[]{:S(2)}, u32[]{:S(2)}) collective-permute-start(f16[2,128,128]{2,1,0:T(8,128)(2,1)S(1)} %add_convert_fusion.5), channel_id=1, source_target_pairs={{0,16},{1,17},{2,18},{3,19},{4,6},{5,7},{6,4},{7,5},{8,24},{9,25},... | collective-permute-start | bytes 196616 | tf_op jit(solution)/shard_map/ppermute | solution.py:205
  20.5 4.3 %collective-permute-start.8 = (f16[2,128,128]{2,1,0:T(8,128)(2,1)S(1)}, f16[2,128,128]{2,1,0:T(8,128)(2,1)S(1)}, u32[]{:S(2)}, u32[]{:S(2)}) collective-permute-start(f16[2,128,128]{2,1,0:T(8,128)(2,1)S(1)} %add_convert_fusion.5), channel_id=1, source_target_pairs={{0,8},{1,9},{2,10},{3,11},{4,5},{5,4},{6,7},{7,6},{8,0},{9,1},{10,... | collective-permute-start | bytes 196616 | tf_op jit(solution)/shard_map/ppermute | solution.py:205
  24.8 6.1 %collective-permute-start.13 = (f16[2,128,128]{2,1,0:T(8,128)(2,1)S(1)}, f16[2,128,128]{2,1,0:T(8,128)(2,1)S(1)}, u32[]{:S(2)}, u32[]{:S(2)}) collective-permute-start(f16[2,128,128]{2,1,0:T(8,128)(2,1)S(1)} %add_convert_fusion.4), channel_id=1, source_target_pairs={{0,3},{1,2},{2,1},{3,0},{4,28},{5,29},{6,30},{7,31},{8,11},{9,10},... | collective-permute-start | bytes 196616 | tf_op jit(solution)/shard_map/ppermute | solution.py:205
  27.6 5.2 %collective-permute-start.12 = (f16[2,128,128]{2,1,0:T(8,128)(2,1)S(1)}, f16[2,128,128]{2,1,0:T(8,128)(2,1)S(1)}, u32[]{:S(2)}, u32[]{:S(2)}) collective-permute-start(f16[2,128,128]{2,1,0:T(8,128)(2,1)S(1)} %add_convert_fusion.4), channel_id=1, source_target_pairs={{0,2},{1,3},{2,0},{3,1},{4,20},{5,21},{6,22},{7,23},{8,10},{9,11},... | collective-permute-start | bytes 196616 | tf_op jit(solution)/shard_map/ppermute | solution.py:205
  27.6 5.2 %collective-permute-start.11 = (f16[2,128,128]{2,1,0:T(8,128)(2,1)S(1)}, f16[2,128,128]{2,1,0:T(8,128)(2,1)S(1)}, u32[]{:S(2)}, u32[]{:S(2)}) collective-permute-start(f16[2,128,128]{2,1,0:T(8,128)(2,1)S(1)} %add_convert_fusion.4), channel_id=1, source_target_pairs={{0,1},{1,0},{2,3},{3,2},{4,12},{5,13},{6,14},{7,15},{8,9},{9,8},{1... | collective-permute-start | bytes 196616 | tf_op jit(solution)/shard_map/ppermute | solution.py:205
  32.8 1.4 %collective-permute-start.14 = (f32[2,128,128]{2,1,0:T(8,128)S(1)}, f32[2,128,128]{2,1,0:T(8,128)S(1)}, u32[]{:S(2)}, u32[]{:S(2)}) collective-permute-start(f32[2,128,128]{2,1,0:T(8,128)S(1)} %add_add_fusion.2.own), channel_id=1, source_target_pairs={{0,4},{4,0},{8,12},{12,8},{16,20},{20,16},{24,28},{28,24},{1,5},{5... | collective-permute-start | bytes 393224 | tf_op jit(solution)/shard_map/ppermute | solution.py:193
  36.6 1.4 %collective-permute-start.15 = (f32[2,128,128]{2,1,0:T(8,128)S(1)}, f32[2,128,128]{2,1,0:T(8,128)S(1)}, u32[]{:S(2)}, u32[]{:S(2)}) collective-permute-start(f32[2,128,128]{2,1,0:T(8,128)S(1)} %get-tuple-element.41), channel_id=1, source_target_pairs={{0,4},{4,0},{8,12},{12,8},{16,20},{20,16},{24,28},{28,24},{1,5},{5... | collective-permute-start | bytes 393224 | tf_op jit(solution)/shard_map/ppermute | solution.py:193
  38.0 5.2 %collective-permute-start.18 = (f16[2,128,128]{2,1,0:T(8,128)(2,1)S(1)}, f16[2,128,128]{2,1,0:T(8,128)(2,1)S(1)}, u32[]{:S(2)}, u32[]{:S(2)}) collective-permute-start(f16[2,128,128]{2,1,0:T(8,128)(2,1)S(1)} %add_convert_fusion.3), channel_id=1, source_target_pairs={{0,24},{1,25},{2,26},{3,27},{4,7},{5,6},{6,5},{7,4},{8,16},{9,17},... | collective-permute-start | bytes 196616 | tf_op jit(solution)/shard_map/ppermute | solution.py:205
  39.6 4.4 %collective-permute-start.17 = (f16[2,128,128]{2,1,0:T(8,128)(2,1)S(1)}, f16[2,128,128]{2,1,0:T(8,128)(2,1)S(1)}, u32[]{:S(2)}, u32[]{:S(2)}) collective-permute-start(f16[2,128,128]{2,1,0:T(8,128)(2,1)S(1)} %add_convert_fusion.3), channel_id=1, source_target_pairs={{0,16},{1,17},{2,18},{3,19},{4,6},{5,7},{6,4},{7,5},{8,24},{9,25},... | collective-permute-start | bytes 196616 | tf_op jit(solution)/shard_map/ppermute | solution.py:205
  40.1 4.3 %collective-permute-start.16 = (f16[2,128,128]{2,1,0:T(8,128)(2,1)S(1)}, f16[2,128,128]{2,1,0:T(8,128)(2,1)S(1)}, u32[]{:S(2)}, u32[]{:S(2)}) collective-permute-start(f16[2,128,128]{2,1,0:T(8,128)(2,1)S(1)} %add_convert_fusion.3), channel_id=1, source_target_pairs={{0,8},{1,9},{2,10},{3,11},{4,5},{5,4},{6,7},{7,6},{8,0},{9,1},{10,... | collective-permute-start | bytes 196616 | tf_op jit(solution)/shard_map/ppermute | solution.py:205
  44.4 6.1 %collective-permute-start.21 = (f16[2,128,128]{2,1,0:T(8,128)(2,1)S(1)}, f16[2,128,128]{2,1,0:T(8,128)(2,1)S(1)}, u32[]{:S(2)}, u32[]{:S(2)}) collective-permute-start(f16[2,128,128]{2,1,0:T(8,128)(2,1)S(1)} %add_convert_fusion.2), channel_id=1, source_target_pairs={{0,3},{1,2},{2,1},{3,0},{4,28},{5,29},{6,30},{7,31},{8,11},{9,10},... | collective-permute-start | bytes 196616 | tf_op jit(solution)/shard_map/ppermute | solution.py:205
  46.8 5.6 %collective-permute-start.20 = (f16[2,128,128]{2,1,0:T(8,128)(2,1)S(1)}, f16[2,128,128]{2,1,0:T(8,128)(2,1)S(1)}, u32[]{:S(2)}, u32[]{:S(2)}) collective-permute-start(f16[2,128,128]{2,1,0:T(8,128)(2,1)S(1)} %add_convert_fusion.2), channel_id=1, source_target_pairs={{0,2},{1,3},{2,0},{3,1},{4,20},{5,21},{6,22},{7,23},{8,10},{9,11},... | collective-permute-start | bytes 196616 | tf_op jit(solution)/shard_map/ppermute | solution.py:205
  46.8 5.6 %collective-permute-start.19 = (f16[2,128,128]{2,1,0:T(8,128)(2,1)S(1)}, f16[2,128,128]{2,1,0:T(8,128)(2,1)S(1)}, u32[]{:S(2)}, u32[]{:S(2)}) collective-permute-start(f16[2,128,128]{2,1,0:T(8,128)(2,1)S(1)} %add_convert_fusion.2), channel_id=1, source_target_pairs={{0,1},{1,0},{2,3},{3,2},{4,12},{5,13},{6,14},{7,15},{8,9},{9,8},{1... | collective-permute-start | bytes 196616 | tf_op jit(solution)/shard_map/ppermute | solution.py:205
  52.4 1.4 %collective-permute-start.22 = (f32[2,128,128]{2,1,0:T(8,128)S(1)}, f32[2,128,128]{2,1,0:T(8,128)S(1)}, u32[]{:S(2)}, u32[]{:S(2)}) collective-permute-start(f32[2,128,128]{2,1,0:T(8,128)S(1)} %add_add_fusion.1.own), channel_id=1, source_target_pairs={{0,4},{4,0},{8,12},{12,8},{16,20},{20,16},{24,28},{28,24},{1,5},{5... | collective-permute-start | bytes 393224 | tf_op jit(solution)/shard_map/ppermute | solution.py:193
  56.2 1.4 %collective-permute-start.23 = (f32[2,128,128]{2,1,0:T(8,128)S(1)}, f32[2,128,128]{2,1,0:T(8,128)S(1)}, u32[]{:S(2)}, u32[]{:S(2)}) collective-permute-start(f32[2,128,128]{2,1,0:T(8,128)S(1)} %get-tuple-element.45), channel_id=1, source_target_pairs={{0,4},{4,0},{8,12},{12,8},{16,20},{20,16},{24,28},{28,24},{1,5},{5... | collective-permute-start | bytes 393224 | tf_op jit(solution)/shard_map/ppermute | solution.py:193
  57.6 5.2 %collective-permute-start.26 = (f16[2,128,128]{2,1,0:T(8,128)(2,1)S(1)}, f16[2,128,128]{2,1,0:T(8,128)(2,1)S(1)}, u32[]{:S(2)}, u32[]{:S(2)}) collective-permute-start(f16[2,128,128]{2,1,0:T(8,128)(2,1)S(1)} %add_convert_fusion.1), channel_id=1, source_target_pairs={{0,24},{1,25},{2,26},{3,27},{4,7},{5,6},{6,5},{7,4},{8,16},{9,17},... | collective-permute-start | bytes 196616 | tf_op jit(solution)/shard_map/ppermute | solution.py:205
  60.1 4.3 %collective-permute-start.25 = (f16[2,128,128]{2,1,0:T(8,128)(2,1)S(1)}, f16[2,128,128]{2,1,0:T(8,128)(2,1)S(1)}, u32[]{:S(2)}, u32[]{:S(2)}) collective-permute-start(f16[2,128,128]{2,1,0:T(8,128)(2,1)S(1)} %add_convert_fusion.1), channel_id=1, source_target_pairs={{0,16},{1,17},{2,18},{3,19},{4,6},{5,7},{6,4},{7,5},{8,24},{9,25},... | collective-permute-start | bytes 196616 | tf_op jit(solution)/shard_map/ppermute | solution.py:205
  60.6 4.3 %collective-permute-start.24 = (f16[2,128,128]{2,1,0:T(8,128)(2,1)S(1)}, f16[2,128,128]{2,1,0:T(8,128)(2,1)S(1)}, u32[]{:S(2)}, u32[]{:S(2)}) collective-permute-start(f16[2,128,128]{2,1,0:T(8,128)(2,1)S(1)} %add_convert_fusion.1), channel_id=1, source_target_pairs={{0,8},{1,9},{2,10},{3,11},{4,5},{5,4},{6,7},{7,6},{8,0},{9,1},{10,... | collective-permute-start | bytes 196616 | tf_op jit(solution)/shard_map/ppermute | solution.py:205
  64.9 6.1 %collective-permute-start.29 = (f16[2,128,128]{2,1,0:T(8,128)(2,1)S(1)}, f16[2,128,128]{2,1,0:T(8,128)(2,1)S(1)}, u32[]{:S(2)}, u32[]{:S(2)}) collective-permute-start(f16[2,128,128]{2,1,0:T(8,128)(2,1)S(1)} %add_convert_fusion), channel_id=1, source_target_pairs={{0,3},{1,2},{2,1},{3,0},{4,28},{5,29},{6,30},{7,31},{8,11},{9,10},... | collective-permute-start | bytes 196616 | tf_op jit(solution)/shard_map/ppermute | solution.py:205
  67.0 5.5 %collective-permute-start.28 = (f16[2,128,128]{2,1,0:T(8,128)(2,1)S(1)}, f16[2,128,128]{2,1,0:T(8,128)(2,1)S(1)}, u32[]{:S(2)}, u32[]{:S(2)}) collective-permute-start(f16[2,128,128]{2,1,0:T(8,128)(2,1)S(1)} %add_convert_fusion), channel_id=1, source_target_pairs={{0,2},{1,3},{2,0},{3,1},{4,20},{5,21},{6,22},{7,23},{8,10},{9,11},... | collective-permute-start | bytes 196616 | tf_op jit(solution)/shard_map/ppermute | solution.py:205
  67.2 5.2 %collective-permute-start.27 = (f16[2,128,128]{2,1,0:T(8,128)(2,1)S(1)}, f16[2,128,128]{2,1,0:T(8,128)(2,1)S(1)}, u32[]{:S(2)}, u32[]{:S(2)}) collective-permute-start(f16[2,128,128]{2,1,0:T(8,128)(2,1)S(1)} %add_convert_fusion), channel_id=1, source_target_pairs={{0,1},{1,0},{2,3},{3,2},{4,12},{5,13},{6,14},{7,15},{8,9},{9,8},{1... | collective-permute-start | bytes 196616 | tf_op jit(solution)/shard_map/ppermute | solution.py:205
  72.5 1.4 %collective-permute-start.30 = (f32[2,128,128]{2,1,0:T(8,128)S(1)}, f32[2,128,128]{2,1,0:T(8,128)S(1)}, u32[]{:S(2)}, u32[]{:S(2)}) collective-permute-start(f32[2,128,128]{2,1,0:T(8,128)S(1)} %add_add_fusion.own), channel_id=1, source_target_pairs={{0,4},{4,0},{8,12},{12,8},{16,20},{20,16},{24,28},{28,24},{1,5},{5... | collective-permute-start | bytes 393224 | tf_op jit(solution)/shard_map/ppermute | solution.py:193

commit v6 on v5

--- a/solution.py
+++ b/solution.py
@@ -89,33 +89,40 @@
         copy.wait()
 
 
-def place(parts, whole, fill):
+def pack_kernel(trial, precond, both, picked, sems):
+    held = trial.shape[0]
+    copies = [
+        pltpu.make_async_copy(src, both.at[pl.ds(i * held, held)], sems.at[i]) for i, src in enumerate((trial, precond))
+    ]
+    for copy in copies:
+        copy.start()
+    for copy in copies:
+        copy.wait()
+    picked[...] = both[pl.ds(lax.axis_index("terms") % 2 * held, held)]
+
+
+def first_kernel(wire, pairs, last, *refs):
+    table, left, right, vec, pre, inv, state, keep, send, blocks, acc = refs[-11:]
+    packed, *moved = refs[:-11]
+    mine, other = moved[: len(moved) // 2], moved[len(moved) // 2 :]
+    sectors, rows, cols = acc.shape
+    held = packed.shape[0] // 2
+    low = lax.axis_index("terms") % 2
     here = lax.axis_index("sectors")
-    held = parts[0].shape[0]
-    for mask, part in enumerate(parts):
-        for i in range(held):
-            g = (here ^ mask) * held + i
-            whole[g] = fill(g, part[i])
-
-
-def first_kernel(wire, *refs):
-    table, left, right, vec, pre, inv, state, keep, send, blocks, acc = refs[-11:]
-    sectors, rows, cols = acc.shape
-    parts = (len(refs) - 11) // 2
-    mine, other = refs[:parts], refs[parts : 2 * parts]
-    low = lax.axis_index("terms") % 2
-
-    def load(trial, precond):
-        place(trial, vec, lambda g, block: jnp.where(live(table, g, acc), block, 0.0))
-        place(precond, pre, lambda g, block: block)
-
-    @pl.when(low == 0)
-    def _():
-        load(mine, other)
-
-    @pl.when(low == 1)
-    def _():
-        load(other, mine)
+
+    def place(mask, i, v, p):
+        g = (here ^ mask) * held + i
+        vec[g] = jnp.where(live(table, g, acc), v, 0.0)
+        pre[g] = p
+
+    for i in range(held):
+        place(0, i, packed[i], packed[held + i])
+        for (even, odd), near, far in zip(pairs, mine, other):
+            place(jnp.where(low == 0, even, odd), i, near[i], near[held + i])
+            place(jnp.where(low == 0, odd, even), i, far[i], far[held + i])
+        if last:
+            near, far = mine[-1][i], other[-1][i]
+            place(last, i, jnp.where(low == 0, near, far), jnp.where(low == 0, far, near))
 
     squares = weighted = jnp.zeros((8, cols), F32)
     for g in range(sectors):
@@ -249,20 +256,30 @@
         cost_estimate=pl.CostEstimate(flops=0, bytes_accessed=4 * left_ops.size, transcendentals=0),
     )(*(pltpu.with_memory_space_constraint(x, pltpu.HBM) for x in (block_rows, owner_map, term_in, term_out, left_ops, right_ops)))
 
-    picked = jnp.where(lax.axis_index("terms") % 2 == 0, trial, precond)
-    swapped = swap(picked, "terms", 1)
-    mine = [swap(picked, "sectors", mask) for mask in range(1, lax.axis_size("sectors"))]
+    masks = list(range(1, lax.axis_size("sectors")))
+    pairs = [tuple(masks[i : i + 2]) for i in range(0, len(masks) - 1, 2)]
+    last = masks[-1] if len(masks) % 2 else 0
+    both, picked = pl.pallas_call(
+        pack_kernel,
+        out_shape=(jax.ShapeDtypeStruct((2 * sec_local, rows, cols), F32), jax.ShapeDtypeStruct(trial.shape, F32)),
+        in_specs=[HBM] * 2,
+        out_specs=(VMEM,) * 2,
+        scratch_shapes=[pltpu.SemaphoreType.DMA((2,))],
+        compiler_params=params(),
+    )(*(pltpu.with_memory_space_constraint(x, pltpu.HBM) for x in (trial, precond)))
+    mine = [exchange(both, pair) for pair in pairs]
+    if last:
+        mine.append(swap(picked, "sectors", last))
     mine, (left, right, table) = lax.optimization_barrier((mine, (left, right, table)))
-    other = [swapped] + [swap(x, "terms", 1) for x in mine]
-    mine = [picked] + mine
+    other = [swap(x, "terms", 1) for x in mine]
     vec, pre, inv, state, keep, send = pl.pallas_call(
-        functools.partial(first_kernel, wire),
+        functools.partial(first_kernel, wire, pairs, last),
         out_shape=(whole, whole, whole, state_shape, part, part),
-        in_specs=[VMEM] * (2 * len(mine)) + [SMEM] + [VMEM] * 2,
+        in_specs=[VMEM] * (1 + 2 * len(mine)) + [SMEM] + [VMEM] * 2,
         out_specs=(VMEM,) * 6,
         scratch_shapes=scratch,
         compiler_params=params(),
-    )(*mine, *other, table, left, right)
+    )(both, *mine, *other, table, left, right)
     for step in range(1, STEPS):
         own = reduce_half(keep, send)
         far = swap(own, "terms", 1)

time: 75.1 us -> 74.7 us (level)
  Pallas kernels: 10.6 us -> 11.7 us
  other arithmetic: 1.15 us -> 0.29 us
    ppermute x13 -> x9, starting transfers between devices: 7.14 us -> 4.01 us  [swap(): lax.ppermute(x, axis, [(i, i ^ mask) for i in range(lax.axis_size(axis))])]
    ppermute x18 -> x19, starting transfers between devices: 24 us -> 27.1 us  [exchange(): lax.ppermute(x, ('terms', 'sectors'), [(d, d ^ masks[d // sectors % 2]) f...]
    pallas_call x1 -> x2, Pallas kernels: 2.07 us -> 3.06 us  [the longest x1 2.16 us: on_device(): pl.pallas_call(functools.partial(first_kernel, wire, pairs, last), out_sh...]
    select_n x1 -> x0, other arithmetic: 0.86 us -> none  [on_device(): picked = jnp.where(lax.axis_index('terms') % 2 == 0, trial, precond)]
    ppermute x13 -> x9, waiting for transfers between devices: 10.9 us -> 10.1 us  [swap(): lax.ppermute(x, axis, [(i, i ^ mask) for i in range(lax.axis_size(axis))])]
    ppermute x18 -> x19, waiting for transfers between devices: 20.3 us -> 20.5 us  [exchange(): lax.ppermute(x, ('terms', 'sectors'), [(d, d ^ masks[d // sectors % 2]) f...]
  transfers between devices with their start and end apart: 31 -> 28, of which waited for: 25 -> 23; matrix products, arithmetic and copies ran while one was open for 0% -> 0% of each run, Pallas kernels for 4% -> 4%
where the time goes in v6:
time: 74.7 us; the launch traced here: 74.5 us
  starting transfers between devices  31.1 us (42%)
  waiting for transfers between devices  30.6 us (41%)
  Pallas kernels  11.7 us (16%)
    ppermute x19, starting transfers between devices, exchange(): lax.ppermute(x, ('terms', 'sectors'), [(d, d ^ masks[d // sectors % 2]) f...  27.1 us
    ppermute x19, waiting for transfers between devices, exchange(): lax.ppermute(x, ('terms', 'sectors'), [(d, d ^ masks[d // sectors % 2]) f...  20.5 us
    ppermute x9, waiting for transfers between devices, swap(): lax.ppermute(x, axis, [(i, i ^ mask) for i in range(lax.axis_size(axis))])  10.1 us
    pallas_call x2, Pallas kernels, on_device(): pl.pallas_call(functools.partial(middle_kernel, wire, step), out_shape=(w...  4.81 us
    ppermute x9, starting transfers between devices, swap(): lax.ppermute(x, axis, [(i, i ^ mask) for i in range(lax.axis_size(axis))])  4.01 us
    pallas_call x1, Pallas kernels, on_device(): pl.pallas_call(load_kernel, out_shape=(jax.ShapeDtypeStruct(left_ops.shap...  2.88 us
    pallas_call x1, Pallas kernels, on_device(): pl.pallas_call(functools.partial(first_kernel, wire, pairs, last), out_sh...  2.16 us
  transfers between devices with their start and end apart: 28, of which 23 were waited for; matrix products, arithmetic and copies ran while one was open for 0% of the time, Pallas kernels for 4%

profile of v6, /device:TPU:0, one launch (start us, length us, event | category | flops | bytes accessed | tf_op | source)
XLA Modules:
  0.0 74.5 jit_solution(4214043518123465171)
XLA Ops:
  0.6 0.9 %shard_map.95 = (f32[2,128,128]{2,1,0:T(8,128)S(1)}, f32[1,128,128]{2,1,0:T(8,128)S(1)}) custom-call(f32[1,128,128]{2,1,0:T(8,128)} %trial.1, f32[1,128,128]{2,1,0:T(8,128)} %precond.1), custom_call_target="tpu_custom_call" | custom-call | tf_op jit(solution)/shard_map/pallas_call | solution.py:262
  1.5 3.1 %collective-permute-start = (f32[2,128,128]{2,1,0:T(8,128)S(1)}, f32[2,128,128]{2,1,0:T(8,128)S(1)}, u32[]{:S(2)}, u32[]{:S(2)}) collective-permute-start(f32[2,128,128]{2,1,0:T(8,128)S(1)} %get-tuple-element.26.refs_0_), channel_id=1, source_target_pairs={{0,1},{1,0},{2,3},{3,2},{4,6},{5,7},{6,4},{7,5},{8,9},{9,8},{10,11... | collective-permute-start | bytes 393224 | tf_op jit(solution)/shard_map/ppermute | solution.py:212
  4.6 2.5 %collective-permute-start.1 = (f32[1,128,128]{2,1,0:T(8,128)S(1)}, f32[1,128,128]{2,1,0:T(8,128)S(1)}, u32[]{:S(2)}, u32[]{:S(2)}) collective-permute-start(f32[1,128,128]{2,1,0:T(8,128)S(1)} %get-tuple-element.27), channel_id=1, source_target_pairs={{0,3},{1,2},{2,1},{3,0},{4,7},{5,6},{6,5},{7,4},{8,11},{9,10},{10,... | collective-permute-start | bytes 196616 | tf_op jit(solution)/shard_map/ppermute | solution.py:200
  7.1 2.9 %shard_map.96 = (bf16[64,128,128]{2,1,0:T(8,128)(2,1)S(1)}, bf16[64,128,128]{2,1,0:T(8,128)(2,1)S(1)}, s32[132]{0:T(256)S(1)}) custom-call(s32[4]{0:T(128)} %rows_hbm.1, s32[4]{0:T(128)} %owner_hbm.1, s32[64]{0:T(128)} %in_hbm.1, s32[64]{0:T(128)} %out_hbm.1, bf16[64,128,128]{2,1,0:T(8,128)(2,1)} %left_hbm.1, bf16[64,128,128]{2,1,0:T(8,128)(2,1)} %right_hbm.1), custom_call_target="tpu_custom_call" | custom-call | bytes 4194304 | tf_op jit(solution)/shard_map/pallas_call | solution.py:245
  10.0 1.7 %collective-permute-done.1.refs_2_ = f32[1,128,128]{2,1,0:T(8,128)S(1)} collective-permute-done((f32[1,128,128]{2,1,0:T(8,128)S(1)}, f32[1,128,128]{2,1,0:T(8,128)S(1)}, u32[]{:S(2)}, u32[]{:S(2)}) %collective-permute-start.1) | collective-permute-done | bytes 65568 | tf_op jit(solution)/shard_map/ppermute | solution.py:200
  11.7 0.5 collective-permute-start.3
  12.2 0.9 %collective-permute-done.3.refs_4_ = f32[1,128,128]{2,1,0:T(8,128)S(1)} collective-permute-done((f32[1,128,128]{2,1,0:T(8,128)S(1)}, f32[1,128,128]{2,1,0:T(8,128)S(1)}, u32[]{:S(2)}, u32[]{:S(2)}) %collective-permute-start.3) | collective-permute-done | bytes 65568 | tf_op jit(solution)/shard_map/ppermute | solution.py:200
  13.1 2.2 %shard_map.97 = (f32[4,128,128]{2,1,0:T(8,128)S(1)}, f32[4,128,128]{2,1,0:T(8,128)S(1)}, f32[4,128,128]{2,1,0:T(8,128)S(1)}, f32[8,128]{1,0:T(8,128)S(1)}, f32[2...) custom-call(f32[2,128,128]{2,1,0:T(8,128)S(1)} %get-tuple-element.26.refs_0_, ...), custom_call_target="tpu_custom_call" | custom-call | tf_op jit(solution)/shard_map/pallas_call | solution.py:275
  15.7 1.0 %collective-permute-done.4 = f32[2,128,128]{2,1,0:T(8,128)S(1)} collective-permute-done((f32[2,128,128]{2,1,0:T(8,128)S(1)}, f32[2,128,128]{2,1,0:T(8,128)S(1)}, u32[]{:S(2)}, u32[]{:S(2)}) %collective-permute-start.4) | collective-permute-done | bytes 131104 | tf_op jit(solution)/shard_map/ppermute | solution.py:200
  16.8 2.5 %collective-permute-start.7 = (f16[2,128,128]{2,1,0:T(8,128)(2,1)S(1)}, f16[2,128,128]{2,1,0:T(8,128)(2,1)S(1)}, u32[]{:S(2)}, u32[]{:S(2)}) collective-permute-start(f16[2,128,128]{2,1,0:T(8,128)(2,1)S(1)} %add_convert_fusion.5), channel_id=1, source_target_pairs={{0,24},{1,25},{2,26},{3,27},{4,7},{5,6},{6,5},{7,4},{8,16},{9,17},... | collective-permute-start | bytes 196616 | tf_op jit(solution)/shard_map/ppermute | solution.py:212
  19.3 0.5 collective-permute-start.6
  19.8 0.5 collective-permute-start.5
  20.3 1.7 %collective-permute-done.7 = f16[2,128,128]{2,1,0:T(8,128)(2,1)S(1)} collective-permute-done((f16[2,128,128]{2,1,0:T(8,128)(2,1)S(1)}, f16[2,128,128]{2,1,0:T(8,128)(2,1)S(1)}, u32[]{:S(2)}, u32[]{:S(2)}) %collective-permute-start.7) | collective-permute-done | bytes 65568 | tf_op jit(solution)/shard_map/ppermute | solution.py:212
  22.0 1.5 %collective-permute-done.6 = f16[2,128,128]{2,1,0:T(8,128)(2,1)S(1)} collective-permute-done((f16[2,128,128]{2,1,0:T(8,128)(2,1)S(1)}, f16[2,128,128]{2,1,0:T(8,128)(2,1)S(1)}, u32[]{:S(2)}, u32[]{:S(2)}) %collective-permute-start.6) | collective-permute-done | bytes 65568 | tf_op jit(solution)/shard_map/ppermute | solution.py:212
  23.5 0.5 collective-permute-done.5
  24.1 2.6 %collective-permute-start.10 = (f16[2,128,128]{2,1,0:T(8,128)(2,1)S(1)}, f16[2,128,128]{2,1,0:T(8,128)(2,1)S(1)}, u32[]{:S(2)}, u32[]{:S(2)}) collective-permute-start(f16[2,128,128]{2,1,0:T(8,128)(2,1)S(1)} %add_convert_fusion.4), channel_id=1, source_target_pairs={{0,3},{1,2},{2,1},{3,0},{4,28},{5,29},{6,30},{7,31},{8,11},{9,10},... | collective-permute-start | bytes 196616 | tf_op jit(solution)/shard_map/ppermute | solution.py:212
  26.7 1.8 %collective-permute-start.8 = (f16[2,128,128]{2,1,0:T(8,128)(2,1)S(1)}, f16[2,128,128]{2,1,0:T(8,128)(2,1)S(1)}, u32[]{:S(2)}, u32[]{:S(2)}) collective-permute-start(f16[2,128,128]{2,1,0:T(8,128)(2,1)S(1)} %add_convert_fusion.4), channel_id=1, source_target_pairs={{0,1},{1,0},{2,3},{3,2},{4,12},{5,13},{6,14},{7,15},{8,9},{9,8},{1... | collective-permute-start | bytes 196616 | tf_op jit(solution)/shard_map/ppermute | solution.py:212
  28.5 1.7 %collective-permute-done.10 = f16[2,128,128]{2,1,0:T(8,128)(2,1)S(1)} collective-permute-done((f16[2,128,128]{2,1,0:T(8,128)(2,1)S(1)}, f16[2,128,128]{2,1,0:T(8,128)(2,1)S(1)}, u32[]{:S(2)}, u32[]{:S(2)}) %collective-permute-start.10) | collective-permute-done | bytes 65568 | tf_op jit(solution)/shard_map/ppermute | solution.py:212
  30.2 2.3 %collective-permute-done.9 = f16[2,128,128]{2,1,0:T(8,128)(2,1)S(1)} collective-permute-done((f16[2,128,128]{2,1,0:T(8,128)(2,1)S(1)}, f16[2,128,128]{2,1,0:T(8,128)(2,1)S(1)}, u32[]{:S(2)}, u32[]{:S(2)}) %collective-permute-start.9) | collective-permute-done | bytes 65568 | tf_op jit(solution)/shard_map/ppermute | solution.py:212
  32.6 1.3 %collective-permute-done.11.far = f32[2,128,128]{2,1,0:T(8,128)S(1)} collective-permute-done((f32[2,128,128]{2,1,0:T(8,128)S(1)}, f32[2,128,128]{2,1,0:T(8,128)S(1)}, u32[]{:S(2)}, u32[]{:S(2)}) %collective-permute-start.11) | collective-permute-done | bytes 131104 | tf_op jit(solution)/shard_map/ppermute | solution.py:200
  34.0 2.4 %shard_map.98 = (f32[4,128,128]{2,1,0:T(8,128)S(1)}, f32[8,128]{1,0:T(8,128)S(1)}, f32[2,128,128]{2,1,0:T(8,128)S(1)}, f32[2,128,128]{2,1,0:T(8,128)S(1)}) custom-call(f32[2,128,128]{2,1,0:T(8,128)S(1)} %add_add_fusion.2.own, f32[2,128,128]{2,1,0:T(8,128)S(1)} %collective-permute-done.11.far, f32[4,128,128]{2,1,0:T(8,128)S(1)} %get-tuple-element.38.vec_in, ...), custom_call_target="tpu_custom_call" | custom-call | tf_op jit(solution)/shard_map/pallas_call | solution.py:286
  36.6 1.2 %collective-permute-done.12 = f32[2,128,128]{2,1,0:T(8,128)S(1)} collective-permute-done((f32[2,128,128]{2,1,0:T(8,128)S(1)}, f32[2,128,128]{2,1,0:T(8,128)S(1)}, u32[]{:S(2)}, u32[]{:S(2)}) %collective-permute-start.12) | collective-permute-done | bytes 131104 | tf_op jit(solution)/shard_map/ppermute | solution.py:200
  37.8 1.6 %collective-permute-start.15 = (f16[2,128,128]{2,1,0:T(8,128)(2,1)S(1)}, f16[2,128,128]{2,1,0:T(8,128)(2,1)S(1)}, u32[]{:S(2)}, u32[]{:S(2)}) collective-permute-start(f16[2,128,128]{2,1,0:T(8,128)(2,1)S(1)} %add_convert_fusion.3), channel_id=1, source_target_pairs={{0,24},{1,25},{2,26},{3,27},{4,7},{5,6},{6,5},{7,4},{8,16},{9,17},... | collective-permute-start | bytes 196616 | tf_op jit(solution)/shard_map/ppermute | solution.py:212
  39.4 0.5 collective-permute-start.14
  39.9 1.5 %collective-permute-start.13 = (f16[2,128,128]{2,1,0:T(8,128)(2,1)S(1)}, f16[2,128,128]{2,1,0:T(8,128)(2,1)S(1)}, u32[]{:S(2)}, u32[]{:S(2)}) collective-permute-start(f16[2,128,128]{2,1,0:T(8,128)(2,1)S(1)} %add_convert_fusion.3), channel_id=1, source_target_pairs={{0,8},{1,9},{2,10},{3,11},{4,5},{5,4},{6,7},{7,6},{8,0},{9,1},{10,... | collective-permute-start | bytes 196616 | tf_op jit(solution)/shard_map/ppermute | solution.py:212
  41.4 1.7 %collective-permute-done.15 = f16[2,128,128]{2,1,0:T(8,128)(2,1)S(1)} collective-permute-done((f16[2,128,128]{2,1,0:T(8,128)(2,1)S(1)}, f16[2,128,128]{2,1,0:T(8,128)(2,1)S(1)}, u32[]{:S(2)}, u32[]{:S(2)}) %collective-permute-start.15) | collective-permute-done | bytes 65568 | tf_op jit(solution)/shard_map/ppermute | solution.py:212
  43.1 0.7 collective-permute-done.14
  43.8 0.4 collective-permute-done.13
  44.2 2.0 %collective-permute-start.18 = (f16[2,128,128]{2,1,0:T(8,128)(2,1)S(1)}, f16[2,128,128]{2,1,0:T(8,128)(2,1)S(1)}, u32[]{:S(2)}, u32[]{:S(2)}) collective-permute-start(f16[2,128,128]{2,1,0:T(8,128)(2,1)S(1)} %add_convert_fusion.2), channel_id=1, source_target_pairs={{0,3},{1,2},{2,1},{3,0},{4,28},{5,29},{6,30},{7,31},{8,11},{9,10},... | collective-permute-start | bytes 196616 | tf_op jit(solution)/shard_map/ppermute | solution.py:212
  46.2 2.4 %collective-permute-start.16 = (f16[2,128,128]{2,1,0:T(8,128)(2,1)S(1)}, f16[2,128,128]{2,1,0:T(8,128)(2,1)S(1)}, u32[]{:S(2)}, u32[]{:S(2)}) collective-permute-start(f16[2,128,128]{2,1,0:T(8,128)(2,1)S(1)} %add_convert_fusion.2), channel_id=1, source_target_pairs={{0,1},{1,0},{2,3},{3,2},{4,12},{5,13},{6,14},{7,15},{8,9},{9,8},{1... | collective-permute-start | bytes 196616 | tf_op jit(solution)/shard_map/ppermute | solution.py:212
  48.7 1.7 %collective-permute-done.18 = f16[2,128,128]{2,1,0:T(8,128)(2,1)S(1)} collective-permute-done((f16[2,128,128]{2,1,0:T(8,128)(2,1)S(1)}, f16[2,128,128]{2,1,0:T(8,128)(2,1)S(1)}, u32[]{:S(2)}, u32[]{:S(2)}) %collective-permute-start.18) | collective-permute-done | bytes 65568 | tf_op jit(solution)/shard_map/ppermute | solution.py:212
  50.3 1.4 %collective-permute-done.17 = f16[2,128,128]{2,1,0:T(8,128)(2,1)S(1)} collective-permute-done((f16[2,128,128]{2,1,0:T(8,128)(2,1)S(1)}, f16[2,128,128]{2,1,0:T(8,128)(2,1)S(1)}, u32[]{:S(2)}, u32[]{:S(2)}) %collective-permute-start.17) | collective-permute-done | bytes 65568 | tf_op jit(solution)/shard_map/ppermute | solution.py:212
  51.9 1.3 %collective-permute-done.19.far = f32[2,128,128]{2,1,0:T(8,128)S(1)} collective-permute-done((f32[2,128,128]{2,1,0:T(8,128)S(1)}, f32[2,128,128]{2,1,0:T(8,128)S(1)}, u32[]{:S(2)}, u32[]{:S(2)}) %collective-permute-start.19) | collective-permute-done | bytes 131104 | tf_op jit(solution)/shard_map/ppermute | solution.py:200
  53.2 2.4 %shard_map.99 = (f32[4,128,128]{2,1,0:T(8,128)S(1)}, f32[8,128]{1,0:T(8,128)S(1)}, f32[2,128,128]{2,1,0:T(8,128)S(1)}, f32[2,128,128]{2,1,0:T(8,128)S(1)}) custom-call(f32[2,128,128]{2,1,0:T(8,128)S(1)} %add_add_fusion.1.own, f32[2,128,128]{2,1,0:T(8,128)S(1)} %collective-permute-done.19.far, f32[4,128,128]{2,1,0:T(8,128)S(1)} %get-tuple-element.44.vec_in, ...), custom_call_target="tpu_custom_call" | custom-call | tf_op jit(solution)/shard_map/pallas_call | solution.py:286
  55.8 1.2 %collective-permute-done.20 = f32[2,128,128]{2,1,0:T(8,128)S(1)} collective-permute-done((f32[2,128,128]{2,1,0:T(8,128)S(1)}, f32[2,128,128]{2,1,0:T(8,128)S(1)}, u32[]{:S(2)}, u32[]{:S(2)}) %collective-permute-start.20) | collective-permute-done | bytes 131104 | tf_op jit(solution)/shard_map/ppermute | solution.py:200
  57.0 2.5 %collective-permute-start.23 = (f16[2,128,128]{2,1,0:T(8,128)(2,1)S(1)}, f16[2,128,128]{2,1,0:T(8,128)(2,1)S(1)}, u32[]{:S(2)}, u32[]{:S(2)}) collective-permute-start(f16[2,128,128]{2,1,0:T(8,128)(2,1)S(1)} %add_convert_fusion.1), channel_id=1, source_target_pairs={{0,24},{1,25},{2,26},{3,27},{4,7},{5,6},{6,5},{7,4},{8,16},{9,17},... | collective-permute-start | bytes 196616 | tf_op jit(solution)/shard_map/ppermute | solution.py:212
  59.5 0.5 collective-permute-start.22
  60.1 0.5 collective-permute-start.21
  60.6 1.7 %collective-permute-done.23 = f16[2,128,128]{2,1,0:T(8,128)(2,1)S(1)} collective-permute-done((f16[2,128,128]{2,1,0:T(8,128)(2,1)S(1)}, f16[2,128,128]{2,1,0:T(8,128)(2,1)S(1)}, u32[]{:S(2)}, u32[]{:S(2)}) %collective-permute-start.23) | collective-permute-done | bytes 65568 | tf_op jit(solution)/shard_map/ppermute | solution.py:212
  62.3 1.5 %collective-permute-done.22 = f16[2,128,128]{2,1,0:T(8,128)(2,1)S(1)} collective-permute-done((f16[2,128,128]{2,1,0:T(8,128)(2,1)S(1)}, f16[2,128,128]{2,1,0:T(8,128)(2,1)S(1)}, u32[]{:S(2)}, u32[]{:S(2)}) %collective-permute-start.22) | collective-permute-done | bytes 65568 | tf_op jit(solution)/shard_map/ppermute | solution.py:212
  63.8 0.5 collective-permute-done.21
  64.4 2.0 %collective-permute-start.26 = (f16[2,128,128]{2,1,0:T(8,128)(2,1)S(1)}, f16[2,128,128]{2,1,0:T(8,128)(2,1)S(1)}, u32[]{:S(2)}, u32[]{:S(2)}) collective-permute-start(f16[2,128,128]{2,1,0:T(8,128)(2,1)S(1)} %add_convert_fusion), channel_id=1, source_target_pairs={{0,3},{1,2},{2,1},{3,0},{4,28},{5,29},{6,30},{7,31},{8,11},{9,10},... | collective-permute-start | bytes 196616 | tf_op jit(solution)/shard_map/ppermute | solution.py:212
  66.4 0.7 collective-permute-start.25
  67.1 1.7 %collective-permute-start.24 = (f16[2,128,128]{2,1,0:T(8,128)(2,1)S(1)}, f16[2,128,128]{2,1,0:T(8,128)(2,1)S(1)}, u32[]{:S(2)}, u32[]{:S(2)}) collective-permute-start(f16[2,128,128]{2,1,0:T(8,128)(2,1)S(1)} %add_convert_fusion), channel_id=1, source_target_pairs={{0,1},{1,0},{2,3},{3,2},{4,12},{5,13},{6,14},{7,15},{8,9},{9,8},{1... | collective-permute-start | bytes 196616 | tf_op jit(solution)/shard_map/ppermute | solution.py:212
  68.8 1.7 %collective-permute-done.26 = f16[2,128,128]{2,1,0:T(8,128)(2,1)S(1)} collective-permute-done((f16[2,128,128]{2,1,0:T(8,128)(2,1)S(1)}, f16[2,128,128]{2,1,0:T(8,128)(2,1)S(1)}, u32[]{:S(2)}, u32[]{:S(2)}) %collective-permute-start.26) | collective-permute-done | bytes 65568 | tf_op jit(solution)/shard_map/ppermute | solution.py:212
  70.5 1.5 %collective-permute-done.25 = f16[2,128,128]{2,1,0:T(8,128)(2,1)S(1)} collective-permute-done((f16[2,128,128]{2,1,0:T(8,128)(2,1)S(1)}, f16[2,128,128]{2,1,0:T(8,128)(2,1)S(1)}, u32[]{:S(2)}, u32[]{:S(2)}) %collective-permute-start.25) | collective-permute-done | bytes 65568 | tf_op jit(solution)/shard_map/ppermute | solution.py:212
  72.2 1.3 %collective-permute-done.27.far = f32[2,128,128]{2,1,0:T(8,128)S(1)} collective-permute-done((f32[2,128,128]{2,1,0:T(8,128)S(1)}, f32[2,128,128]{2,1,0:T(8,128)S(1)}, u32[]{:S(2)}, u32[]{:S(2)}) %collective-permute-start.27) | collective-permute-done | bytes 131104 | tf_op jit(solution)/shard_map/ppermute | solution.py:200
  73.5 1.0 %shard_map.100 = (f32[1,128,128]{2,1,0:T(8,128)}, f32[3]{0:T(128)}) custom-call(f32[2,128,128]{2,1,0:T(8,128)S(1)} %add_add_fusion.own, f32[2,128,128]{2,1,0:T(8,128)S(1)} %collective-permute-done.27.far, f32[4,128,128]{2,1,0:T(8,128)S(1)} %get-tuple-element.48.vec, f32[4,128,128]{2,1,0:T(8,128)S(1)} %get-tuple-element.40.inv, ...), custom_call_target="tpu_custom_call" | custom-call | tf_op jit(solution)/shard_map/pallas_call | solution.py:296
  (23 shorter events, 1.4 us)
Async XLA Ops:
  1.5 10.2 %collective-permute-start = (f32[2,128,128]{2,1,0:T(8,128)S(1)}, f32[2,128,128]{2,1,0:T(8,128)S(1)}, u32[]{:S(2)}, u32[]{:S(2)}) collective-permute-start(f32[2,128,128]{2,1,0:T(8,128)S(1)} %get-tuple-element.26.refs_0_), channel_id=1, source_target_pairs={{0,1},{1,0},{2,3},{3,2},{4,6},{5,7},{6,4},{7,5},{8,9},{9,8},{10,11... | collective-permute-start | bytes 393224 | tf_op jit(solution)/shard_map/ppermute | solution.py:212
  4.6 7.1 %collective-permute-start.1 = (f32[1,128,128]{2,1,0:T(8,128)S(1)}, f32[1,128,128]{2,1,0:T(8,128)S(1)}, u32[]{:S(2)}, u32[]{:S(2)}) collective-permute-start(f32[1,128,128]{2,1,0:T(8,128)S(1)} %get-tuple-element.27), channel_id=1, source_target_pairs={{0,3},{1,2},{2,1},{3,0},{4,7},{5,6},{6,5},{7,4},{8,11},{9,10},{10,... | collective-permute-start | bytes 196616 | tf_op jit(solution)/shard_map/ppermute | solution.py:200
  11.7 1.4 %collective-permute-start.2 = (f32[2,128,128]{2,1,0:T(8,128)S(1)}, f32[2,128,128]{2,1,0:T(8,128)S(1)}, u32[]{:S(2)}, u32[]{:S(2)}) collective-permute-start(f32[2,128,128]{2,1,0:T(8,128)S(1)} %collective-permute-done.refs_1_), channel_id=1, source_target_pairs={{0,4},{4,0},{8,12},{12,8},{16,20},{20,16},{24,28},{28,24},{1,5},{5... | collective-permute-start | bytes 393224 | tf_op jit(solution)/shard_map/ppermute | solution.py:200
  11.7 1.4 %collective-permute-start.3 = (f32[1,128,128]{2,1,0:T(8,128)S(1)}, f32[1,128,128]{2,1,0:T(8,128)S(1)}, u32[]{:S(2)}, u32[]{:S(2)}) collective-permute-start(f32[1,128,128]{2,1,0:T(8,128)S(1)} %collective-permute-done.1.refs_2_), channel_id=1, source_target_pairs={{0,4},{4,0},{8,12},{12,8},{16,20},{20,16},{24,28},{28,24},{1,5},{5... | collective-permute-start | bytes 196616 | tf_op jit(solution)/shard_map/ppermute | solution.py:200
  15.3 1.4 %collective-permute-start.4 = (f32[2,128,128]{2,1,0:T(8,128)S(1)}, f32[2,128,128]{2,1,0:T(8,128)S(1)}, u32[]{:S(2)}, u32[]{:S(2)}) collective-permute-start(f32[2,128,128]{2,1,0:T(8,128)S(1)} %get-tuple-element.37), channel_id=1, source_target_pairs={{0,4},{4,0},{8,12},{12,8},{16,20},{20,16},{24,28},{28,24},{1,5},{5... | collective-permute-start | bytes 393224 | tf_op jit(solution)/shard_map/ppermute | solution.py:200
  16.8 5.2 %collective-permute-start.7 = (f16[2,128,128]{2,1,0:T(8,128)(2,1)S(1)}, f16[2,128,128]{2,1,0:T(8,128)(2,1)S(1)}, u32[]{:S(2)}, u32[]{:S(2)}) collective-permute-start(f16[2,128,128]{2,1,0:T(8,128)(2,1)S(1)} %add_convert_fusion.5), channel_id=1, source_target_pairs={{0,24},{1,25},{2,26},{3,27},{4,7},{5,6},{6,5},{7,4},{8,16},{9,17},... | collective-permute-start | bytes 196616 | tf_op jit(solution)/shard_map/ppermute | solution.py:212
  19.3 4.3 %collective-permute-start.6 = (f16[2,128,128]{2,1,0:T(8,128)(2,1)S(1)}, f16[2,128,128]{2,1,0:T(8,128)(2,1)S(1)}, u32[]{:S(2)}, u32[]{:S(2)}) collective-permute-start(f16[2,128,128]{2,1,0:T(8,128)(2,1)S(1)} %add_convert_fusion.5), channel_id=1, source_target_pairs={{0,16},{1,17},{2,18},{3,19},{4,6},{5,7},{6,4},{7,5},{8,24},{9,25},... | collective-permute-start | bytes 196616 | tf_op jit(solution)/shard_map/ppermute | solution.py:212
  19.8 4.3 %collective-permute-start.5 = (f16[2,128,128]{2,1,0:T(8,128)(2,1)S(1)}, f16[2,128,128]{2,1,0:T(8,128)(2,1)S(1)}, u32[]{:S(2)}, u32[]{:S(2)}) collective-permute-start(f16[2,128,128]{2,1,0:T(8,128)(2,1)S(1)} %add_convert_fusion.5), channel_id=1, source_target_pairs={{0,8},{1,9},{2,10},{3,11},{4,5},{5,4},{6,7},{7,6},{8,0},{9,1},{10,... | collective-permute-start | bytes 196616 | tf_op jit(solution)/shard_map/ppermute | solution.py:212
  24.1 6.1 %collective-permute-start.10 = (f16[2,128,128]{2,1,0:T(8,128)(2,1)S(1)}, f16[2,128,128]{2,1,0:T(8,128)(2,1)S(1)}, u32[]{:S(2)}, u32[]{:S(2)}) collective-permute-start(f16[2,128,128]{2,1,0:T(8,128)(2,1)S(1)} %add_convert_fusion.4), channel_id=1, source_target_pairs={{0,3},{1,2},{2,1},{3,0},{4,28},{5,29},{6,30},{7,31},{8,11},{9,10},... | collective-permute-start | bytes 196616 | tf_op jit(solution)/shard_map/ppermute | solution.py:212
  26.7 5.9 %collective-permute-start.9 = (f16[2,128,128]{2,1,0:T(8,128)(2,1)S(1)}, f16[2,128,128]{2,1,0:T(8,128)(2,1)S(1)}, u32[]{:S(2)}, u32[]{:S(2)}) collective-permute-start(f16[2,128,128]{2,1,0:T(8,128)(2,1)S(1)} %add_convert_fusion.4), channel_id=1, source_target_pairs={{0,2},{1,3},{2,0},{3,1},{4,20},{5,21},{6,22},{7,23},{8,10},{9,11},... | collective-permute-start | bytes 196616 | tf_op jit(solution)/shard_map/ppermute | solution.py:212
  26.7 5.8 %collective-permute-start.8 = (f16[2,128,128]{2,1,0:T(8,128)(2,1)S(1)}, f16[2,128,128]{2,1,0:T(8,128)(2,1)S(1)}, u32[]{:S(2)}, u32[]{:S(2)}) collective-permute-start(f16[2,128,128]{2,1,0:T(8,128)(2,1)S(1)} %add_convert_fusion.4), channel_id=1, source_target_pairs={{0,1},{1,0},{2,3},{3,2},{4,12},{5,13},{6,14},{7,15},{8,9},{9,8},{1... | collective-permute-start | bytes 196616 | tf_op jit(solution)/shard_map/ppermute | solution.py:212
  32.6 1.4 %collective-permute-start.11 = (f32[2,128,128]{2,1,0:T(8,128)S(1)}, f32[2,128,128]{2,1,0:T(8,128)S(1)}, u32[]{:S(2)}, u32[]{:S(2)}) collective-permute-start(f32[2,128,128]{2,1,0:T(8,128)S(1)} %add_add_fusion.2.own), channel_id=1, source_target_pairs={{0,4},{4,0},{8,12},{12,8},{16,20},{20,16},{24,28},{28,24},{1,5},{5... | collective-permute-start | bytes 393224 | tf_op jit(solution)/shard_map/ppermute | solution.py:200
  36.4 1.4 %collective-permute-start.12 = (f32[2,128,128]{2,1,0:T(8,128)S(1)}, f32[2,128,128]{2,1,0:T(8,128)S(1)}, u32[]{:S(2)}, u32[]{:S(2)}) collective-permute-start(f32[2,128,128]{2,1,0:T(8,128)S(1)} %get-tuple-element.43), channel_id=1, source_target_pairs={{0,4},{4,0},{8,12},{12,8},{16,20},{20,16},{24,28},{28,24},{1,5},{5... | collective-permute-start | bytes 393224 | tf_op jit(solution)/shard_map/ppermute | solution.py:200
  37.8 5.2 %collective-permute-start.15 = (f16[2,128,128]{2,1,0:T(8,128)(2,1)S(1)}, f16[2,128,128]{2,1,0:T(8,128)(2,1)S(1)}, u32[]{:S(2)}, u32[]{:S(2)}) collective-permute-start(f16[2,128,128]{2,1,0:T(8,128)(2,1)S(1)} %add_convert_fusion.3), channel_id=1, source_target_pairs={{0,24},{1,25},{2,26},{3,27},{4,7},{5,6},{6,5},{7,4},{8,16},{9,17},... | collective-permute-start | bytes 196616 | tf_op jit(solution)/shard_map/ppermute | solution.py:212
  39.4 4.4 %collective-permute-start.14 = (f16[2,128,128]{2,1,0:T(8,128)(2,1)S(1)}, f16[2,128,128]{2,1,0:T(8,128)(2,1)S(1)}, u32[]{:S(2)}, u32[]{:S(2)}) collective-permute-start(f16[2,128,128]{2,1,0:T(8,128)(2,1)S(1)} %add_convert_fusion.3), channel_id=1, source_target_pairs={{0,16},{1,17},{2,18},{3,19},{4,6},{5,7},{6,4},{7,5},{8,24},{9,25},... | collective-permute-start | bytes 196616 | tf_op jit(solution)/shard_map/ppermute | solution.py:212
  39.9 4.3 %collective-permute-start.13 = (f16[2,128,128]{2,1,0:T(8,128)(2,1)S(1)}, f16[2,128,128]{2,1,0:T(8,128)(2,1)S(1)}, u32[]{:S(2)}, u32[]{:S(2)}) collective-permute-start(f16[2,128,128]{2,1,0:T(8,128)(2,1)S(1)} %add_convert_fusion.3), channel_id=1, source_target_pairs={{0,8},{1,9},{2,10},{3,11},{4,5},{5,4},{6,7},{7,6},{8,0},{9,1},{10,... | collective-permute-start | bytes 196616 | tf_op jit(solution)/shard_map/ppermute | solution.py:212
  44.2 6.1 %collective-permute-start.18 = (f16[2,128,128]{2,1,0:T(8,128)(2,1)S(1)}, f16[2,128,128]{2,1,0:T(8,128)(2,1)S(1)}, u32[]{:S(2)}, u32[]{:S(2)}) collective-permute-start(f16[2,128,128]{2,1,0:T(8,128)(2,1)S(1)} %add_convert_fusion.2), channel_id=1, source_target_pairs={{0,3},{1,2},{2,1},{3,0},{4,28},{5,29},{6,30},{7,31},{8,11},{9,10},... | collective-permute-start | bytes 196616 | tf_op jit(solution)/shard_map/ppermute | solution.py:212
  46.2 5.5 %collective-permute-start.17 = (f16[2,128,128]{2,1,0:T(8,128)(2,1)S(1)}, f16[2,128,128]{2,1,0:T(8,128)(2,1)S(1)}, u32[]{:S(2)}, u32[]{:S(2)}) collective-permute-start(f16[2,128,128]{2,1,0:T(8,128)(2,1)S(1)} %add_convert_fusion.2), channel_id=1, source_target_pairs={{0,2},{1,3},{2,0},{3,1},{4,20},{5,21},{6,22},{7,23},{8,10},{9,11},... | collective-permute-start | bytes 196616 | tf_op jit(solution)/shard_map/ppermute | solution.py:212
  46.2 5.5 %collective-permute-start.16 = (f16[2,128,128]{2,1,0:T(8,128)(2,1)S(1)}, f16[2,128,128]{2,1,0:T(8,128)(2,1)S(1)}, u32[]{:S(2)}, u32[]{:S(2)}) collective-permute-start(f16[2,128,128]{2,1,0:T(8,128)(2,1)S(1)} %add_convert_fusion.2), channel_id=1, source_target_pairs={{0,1},{1,0},{2,3},{3,2},{4,12},{5,13},{6,14},{7,15},{8,9},{9,8},{1... | collective-permute-start | bytes 196616 | tf_op jit(solution)/shard_map/ppermute | solution.py:212
  51.8 1.4 %collective-permute-start.19 = (f32[2,128,128]{2,1,0:T(8,128)S(1)}, f32[2,128,128]{2,1,0:T(8,128)S(1)}, u32[]{:S(2)}, u32[]{:S(2)}) collective-permute-start(f32[2,128,128]{2,1,0:T(8,128)S(1)} %add_add_fusion.1.own), channel_id=1, source_target_pairs={{0,4},{4,0},{8,12},{12,8},{16,20},{20,16},{24,28},{28,24},{1,5},{5... | collective-permute-start | bytes 393224 | tf_op jit(solution)/shard_map/ppermute | solution.py:200
  55.6 1.4 %collective-permute-start.20 = (f32[2,128,128]{2,1,0:T(8,128)S(1)}, f32[2,128,128]{2,1,0:T(8,128)S(1)}, u32[]{:S(2)}, u32[]{:S(2)}) collective-permute-start(f32[2,128,128]{2,1,0:T(8,128)S(1)} %get-tuple-element.47), channel_id=1, source_target_pairs={{0,4},{4,0},{8,12},{12,8},{16,20},{20,16},{24,28},{28,24},{1,5},{5... | collective-permute-start | bytes 393224 | tf_op jit(solution)/shard_map/ppermute | solution.py:200
  57.0 5.2 %collective-permute-start.23 = (f16[2,128,128]{2,1,0:T(8,128)(2,1)S(1)}, f16[2,128,128]{2,1,0:T(8,128)(2,1)S(1)}, u32[]{:S(2)}, u32[]{:S(2)}) collective-permute-start(f16[2,128,128]{2,1,0:T(8,128)(2,1)S(1)} %add_convert_fusion.1), channel_id=1, source_target_pairs={{0,24},{1,25},{2,26},{3,27},{4,7},{5,6},{6,5},{7,4},{8,16},{9,17},... | collective-permute-start | bytes 196616 | tf_op jit(solution)/shard_map/ppermute | solution.py:212
  59.5 4.3 %collective-permute-start.22 = (f16[2,128,128]{2,1,0:T(8,128)(2,1)S(1)}, f16[2,128,128]{2,1,0:T(8,128)(2,1)S(1)}, u32[]{:S(2)}, u32[]{:S(2)}) collective-permute-start(f16[2,128,128]{2,1,0:T(8,128)(2,1)S(1)} %add_convert_fusion.1), channel_id=1, source_target_pairs={{0,16},{1,17},{2,18},{3,19},{4,6},{5,7},{6,4},{7,5},{8,24},{9,25},... | collective-permute-start | bytes 196616 | tf_op jit(solution)/shard_map/ppermute | solution.py:212
  60.1 4.3 %collective-permute-start.21 = (f16[2,128,128]{2,1,0:T(8,128)(2,1)S(1)}, f16[2,128,128]{2,1,0:T(8,128)(2,1)S(1)}, u32[]{:S(2)}, u32[]{:S(2)}) collective-permute-start(f16[2,128,128]{2,1,0:T(8,128)(2,1)S(1)} %add_convert_fusion.1), channel_id=1, source_target_pairs={{0,8},{1,9},{2,10},{3,11},{4,5},{5,4},{6,7},{7,6},{8,0},{9,1},{10,... | collective-permute-start | bytes 196616 | tf_op jit(solution)/shard_map/ppermute | solution.py:212
  64.4 6.1 %collective-permute-start.26 = (f16[2,128,128]{2,1,0:T(8,128)(2,1)S(1)}, f16[2,128,128]{2,1,0:T(8,128)(2,1)S(1)}, u32[]{:S(2)}, u32[]{:S(2)}) collective-permute-start(f16[2,128,128]{2,1,0:T(8,128)(2,1)S(1)} %add_convert_fusion), channel_id=1, source_target_pairs={{0,3},{1,2},{2,1},{3,0},{4,28},{5,29},{6,30},{7,31},{8,11},{9,10},... | collective-permute-start | bytes 196616 | tf_op jit(solution)/shard_map/ppermute | solution.py:212
  66.4 5.6 %collective-permute-start.25 = (f16[2,128,128]{2,1,0:T(8,128)(2,1)S(1)}, f16[2,128,128]{2,1,0:T(8,128)(2,1)S(1)}, u32[]{:S(2)}, u32[]{:S(2)}) collective-permute-start(f16[2,128,128]{2,1,0:T(8,128)(2,1)S(1)} %add_convert_fusion), channel_id=1, source_target_pairs={{0,2},{1,3},{2,0},{3,1},{4,20},{5,21},{6,22},{7,23},{8,10},{9,11},... | collective-permute-start | bytes 196616 | tf_op jit(solution)/shard_map/ppermute | solution.py:212
  67.1 5.0 %collective-permute-start.24 = (f16[2,128,128]{2,1,0:T(8,128)(2,1)S(1)}, f16[2,128,128]{2,1,0:T(8,128)(2,1)S(1)}, u32[]{:S(2)}, u32[]{:S(2)}) collective-permute-start(f16[2,128,128]{2,1,0:T(8,128)(2,1)S(1)} %add_convert_fusion), channel_id=1, source_target_pairs={{0,1},{1,0},{2,3},{3,2},{4,12},{5,13},{6,14},{7,15},{8,9},{9,8},{1... | collective-permute-start | bytes 196616 | tf_op jit(solution)/shard_map/ppermute | solution.py:212
  72.1 1.4 %collective-permute-start.27 = (f32[2,128,128]{2,1,0:T(8,128)S(1)}, f32[2,128,128]{2,1,0:T(8,128)S(1)}, u32[]{:S(2)}, u32[]{:S(2)}) collective-permute-start(f32[2,128,128]{2,1,0:T(8,128)S(1)} %add_add_fusion.own), channel_id=1, source_target_pairs={{0,4},{4,0},{8,12},{12,8},{16,20},{20,16},{24,28},{28,24},{1,5},{5... | collective-permute-start | bytes 393224 | tf_op jit(solution)/shard_map/ppermute | solution.py:200

commit v7 on v6

--- a/solution.py
+++ b/solution.py
@@ -270,7 +270,7 @@
     mine = [exchange(both, pair) for pair in pairs]
     if last:
         mine.append(swap(picked, "sectors", last))
-    mine, (left, right, table) = lax.optimization_barrier((mine, (left, right, table)))
+    mine = [lax.optimization_barrier((x, table))[0] for x in mine]
     other = [swap(x, "terms", 1) for x in mine]
     vec, pre, inv, state, keep, send = pl.pallas_call(
         functools.partial(first_kernel, wire, pairs, last),

time: 74.7 us -> 74.3 us (level)
  no operation moved by 1% of the time
where the time goes in v7:
time: 74.3 us; the launch traced here: 74.2 us
  waiting for transfers between devices  30.9 us (42%)
  starting transfers between devices  30.5 us (41%)
  Pallas kernels  11.7 us (16%)
  between operations  0.76 us (1%)
    ppermute x19, starting transfers between devices, exchange(): lax.ppermute(x, ('terms', 'sectors'), [(d, d ^ masks[d // sectors % 2]) f...  27.1 us
    ppermute x19, waiting for transfers between devices, exchange(): lax.ppermute(x, ('terms', 'sectors'), [(d, d ^ masks[d // sectors % 2]) f...  20.4 us
    ppermute x9, waiting for transfers between devices, swap(): lax.ppermute(x, axis, [(i, i ^ mask) for i in range(lax.axis_size(axis))])  10.5 us
    pallas_call x2, Pallas kernels, on_device(): pl.pallas_call(functools.partial(middle_kernel, wire, step), out_shape=(w...  4.81 us
    ppermute x9, starting transfers between devices, swap(): lax.ppermute(x, axis, [(i, i ^ mask) for i in range(lax.axis_size(axis))])  3.42 us
    pallas_call x1, Pallas kernels, on_device(): pl.pallas_call(load_kernel, out_shape=(jax.ShapeDtypeStruct(left_ops.shap...  2.88 us
    pallas_call x1, Pallas kernels, on_device(): pl.pallas_call(functools.partial(first_kernel, wire, pairs, last), out_sh...  2.16 us
  transfers between devices with their start and end apart: 28, of which 23 were waited for; matrix products, arithmetic and copies ran while one was open for 0% of the time, Pallas kernels for 4%

profile of v7, /device:TPU:0, one launch (start us, length us, event | category | flops | bytes accessed | tf_op | source)
XLA Modules:
  0.0 74.2 jit_solution(8708368771683460900)
XLA Ops:
  0.6 0.9 %shard_map.95 = (f32[2,128,128]{2,1,0:T(8,128)S(1)}, f32[1,128,128]{2,1,0:T(8,128)S(1)}) custom-call(f32[1,128,128]{2,1,0:T(8,128)} %trial.1, f32[1,128,128]{2,1,0:T(8,128)} %precond.1), custom_call_target="tpu_custom_call" | custom-call | tf_op jit(solution)/shard_map/pallas_call | solution.py:262
  1.5 3.1 %collective-permute-start = (f32[2,128,128]{2,1,0:T(8,128)S(1)}, f32[2,128,128]{2,1,0:T(8,128)S(1)}, u32[]{:S(2)}, u32[]{:S(2)}) collective-permute-start(f32[2,128,128]{2,1,0:T(8,128)S(1)} %get-tuple-element.23.refs_0_), channel_id=1, source_target_pairs={{0,1},{1,0},{2,3},{3,2},{4,6},{5,7},{6,4},{7,5},{8,9},{9,8},{10,11... | collective-permute-start | bytes 393224 | tf_op jit(solution)/shard_map/ppermute | solution.py:212
  4.6 2.5 %collective-permute-start.1 = (f32[1,128,128]{2,1,0:T(8,128)S(1)}, f32[1,128,128]{2,1,0:T(8,128)S(1)}, u32[]{:S(2)}, u32[]{:S(2)}) collective-permute-start(f32[1,128,128]{2,1,0:T(8,128)S(1)} %get-tuple-element.26), channel_id=1, source_target_pairs={{0,3},{1,2},{2,1},{3,0},{4,7},{5,6},{6,5},{7,4},{8,11},{9,10},{10,... | collective-permute-start | bytes 196616 | tf_op jit(solution)/shard_map/ppermute | solution.py:200
  7.1 2.9 %shard_map.96 = (bf16[64,128,128]{2,1,0:T(8,128)(2,1)S(1)}, bf16[64,128,128]{2,1,0:T(8,128)(2,1)S(1)}, s32[132]{0:T(256)S(1)}) custom-call(s32[4]{0:T(128)} %rows_hbm.1, s32[4]{0:T(128)} %owner_hbm.1, s32[64]{0:T(128)} %in_hbm.1, s32[64]{0:T(128)} %out_hbm.1, bf16[64,128,128]{2,1,0:T(8,128)(2,1)} %left_hbm.1, bf16[64,128,128]{2,1,0:T(8,128)(2,1)} %right_hbm.1), custom_call_target="tpu_custom_call" | custom-call | bytes 4194304 | tf_op jit(solution)/shard_map/pallas_call | solution.py:245
  10.1 1.6 %collective-permute-done.1.refs_2_ = f32[1,128,128]{2,1,0:T(8,128)S(1)} collective-permute-done((f32[1,128,128]{2,1,0:T(8,128)S(1)}, f32[1,128,128]{2,1,0:T(8,128)S(1)}, u32[]{:S(2)}, u32[]{:S(2)}) %collective-permute-start.1) | collective-permute-done | bytes 65568 | tf_op jit(solution)/shard_map/ppermute | solution.py:200
  11.7 1.3 %collective-permute-done.3.refs_4_ = f32[1,128,128]{2,1,0:T(8,128)S(1)} collective-permute-done((f32[1,128,128]{2,1,0:T(8,128)S(1)}, f32[1,128,128]{2,1,0:T(8,128)S(1)}, u32[]{:S(2)}, u32[]{:S(2)}) %collective-permute-start.3) | collective-permute-done | bytes 65568 | tf_op jit(solution)/shard_map/ppermute | solution.py:200
  13.0 2.2 %shard_map.97 = (f32[4,128,128]{2,1,0:T(8,128)S(1)}, f32[4,128,128]{2,1,0:T(8,128)S(1)}, f32[4,128,128]{2,1,0:T(8,128)S(1)}, f32[8,128]{1,0:T(8,128)S(1)}, f32[2...) custom-call(f32[2,128,128]{2,1,0:T(8,128)S(1)} %get-tuple-element.23.refs_0_, ...), custom_call_target="tpu_custom_call" | custom-call | tf_op jit(solution)/shard_map/pallas_call | solution.py:275
  15.1 0.2 collective-permute-start.4
  15.4 1.2 %collective-permute-done.4 = f32[2,128,128]{2,1,0:T(8,128)S(1)} collective-permute-done((f32[2,128,128]{2,1,0:T(8,128)S(1)}, f32[2,128,128]{2,1,0:T(8,128)S(1)}, u32[]{:S(2)}, u32[]{:S(2)}) %collective-permute-start.4) | collective-permute-done | bytes 131104 | tf_op jit(solution)/shard_map/ppermute | solution.py:200
  16.6 2.5 %collective-permute-start.7 = (f16[2,128,128]{2,1,0:T(8,128)(2,1)S(1)}, f16[2,128,128]{2,1,0:T(8,128)(2,1)S(1)}, u32[]{:S(2)}, u32[]{:S(2)}) collective-permute-start(f16[2,128,128]{2,1,0:T(8,128)(2,1)S(1)} %add_convert_fusion.5), channel_id=1, source_target_pairs={{0,24},{1,25},{2,26},{3,27},{4,7},{5,6},{6,5},{7,4},{8,16},{9,17},... | collective-permute-start | bytes 196616 | tf_op jit(solution)/shard_map/ppermute | solution.py:212
  19.1 0.5 collective-permute-start.6
  19.6 0.5 collective-permute-start.5
  20.1 1.7 %collective-permute-done.7 = f16[2,128,128]{2,1,0:T(8,128)(2,1)S(1)} collective-permute-done((f16[2,128,128]{2,1,0:T(8,128)(2,1)S(1)}, f16[2,128,128]{2,1,0:T(8,128)(2,1)S(1)}, u32[]{:S(2)}, u32[]{:S(2)}) %collective-permute-start.7) | collective-permute-done | bytes 65568 | tf_op jit(solution)/shard_map/ppermute | solution.py:212
  21.8 1.5 %collective-permute-done.6 = f16[2,128,128]{2,1,0:T(8,128)(2,1)S(1)} collective-permute-done((f16[2,128,128]{2,1,0:T(8,128)(2,1)S(1)}, f16[2,128,128]{2,1,0:T(8,128)(2,1)S(1)}, u32[]{:S(2)}, u32[]{:S(2)}) %collective-permute-start.6) | collective-permute-done | bytes 65568 | tf_op jit(solution)/shard_map/ppermute | solution.py:212
  23.3 0.5 collective-permute-done.5
  23.9 2.8 %collective-permute-start.10 = (f16[2,128,128]{2,1,0:T(8,128)(2,1)S(1)}, f16[2,128,128]{2,1,0:T(8,128)(2,1)S(1)}, u32[]{:S(2)}, u32[]{:S(2)}) collective-permute-start(f16[2,128,128]{2,1,0:T(8,128)(2,1)S(1)} %add_convert_fusion.4), channel_id=1, source_target_pairs={{0,3},{1,2},{2,1},{3,0},{4,28},{5,29},{6,30},{7,31},{8,11},{9,10},... | collective-permute-start | bytes 196616 | tf_op jit(solution)/shard_map/ppermute | solution.py:212
  26.7 1.7 %collective-permute-start.8 = (f16[2,128,128]{2,1,0:T(8,128)(2,1)S(1)}, f16[2,128,128]{2,1,0:T(8,128)(2,1)S(1)}, u32[]{:S(2)}, u32[]{:S(2)}) collective-permute-start(f16[2,128,128]{2,1,0:T(8,128)(2,1)S(1)} %add_convert_fusion.4), channel_id=1, source_target_pairs={{0,1},{1,0},{2,3},{3,2},{4,12},{5,13},{6,14},{7,15},{8,9},{9,8},{1... | collective-permute-start | bytes 196616 | tf_op jit(solution)/shard_map/ppermute | solution.py:212
  28.4 1.7 %collective-permute-done.10 = f16[2,128,128]{2,1,0:T(8,128)(2,1)S(1)} collective-permute-done((f16[2,128,128]{2,1,0:T(8,128)(2,1)S(1)}, f16[2,128,128]{2,1,0:T(8,128)(2,1)S(1)}, u32[]{:S(2)}, u32[]{:S(2)}) %collective-permute-start.10) | collective-permute-done | bytes 65568 | tf_op jit(solution)/shard_map/ppermute | solution.py:212
  30.0 2.2 %collective-permute-done.9 = f16[2,128,128]{2,1,0:T(8,128)(2,1)S(1)} collective-permute-done((f16[2,128,128]{2,1,0:T(8,128)(2,1)S(1)}, f16[2,128,128]{2,1,0:T(8,128)(2,1)S(1)}, u32[]{:S(2)}, u32[]{:S(2)}) %collective-permute-start.9) | collective-permute-done | bytes 65568 | tf_op jit(solution)/shard_map/ppermute | solution.py:212
  32.3 1.3 %collective-permute-done.11.far = f32[2,128,128]{2,1,0:T(8,128)S(1)} collective-permute-done((f32[2,128,128]{2,1,0:T(8,128)S(1)}, f32[2,128,128]{2,1,0:T(8,128)S(1)}, u32[]{:S(2)}, u32[]{:S(2)}) %collective-permute-start.11) | collective-permute-done | bytes 131104 | tf_op jit(solution)/shard_map/ppermute | solution.py:200
  33.7 2.4 %shard_map.98 = (f32[4,128,128]{2,1,0:T(8,128)S(1)}, f32[8,128]{1,0:T(8,128)S(1)}, f32[2,128,128]{2,1,0:T(8,128)S(1)}, f32[2,128,128]{2,1,0:T(8,128)S(1)}) custom-call(f32[2,128,128]{2,1,0:T(8,128)S(1)} %add_add_fusion.2.own, f32[2,128,128]{2,1,0:T(8,128)S(1)} %collective-permute-done.11.far, f32[4,128,128]{2,1,0:T(8,128)S(1)} %get-tuple-element.32.vec_in, ...), custom_call_target="tpu_custom_call" | custom-call | tf_op jit(solution)/shard_map/pallas_call | solution.py:286
  36.3 1.2 %collective-permute-done.12 = f32[2,128,128]{2,1,0:T(8,128)S(1)} collective-permute-done((f32[2,128,128]{2,1,0:T(8,128)S(1)}, f32[2,128,128]{2,1,0:T(8,128)S(1)}, u32[]{:S(2)}, u32[]{:S(2)}) %collective-permute-start.12) | collective-permute-done | bytes 131104 | tf_op jit(solution)/shard_map/ppermute | solution.py:200
  37.5 1.6 %collective-permute-start.15 = (f16[2,128,128]{2,1,0:T(8,128)(2,1)S(1)}, f16[2,128,128]{2,1,0:T(8,128)(2,1)S(1)}, u32[]{:S(2)}, u32[]{:S(2)}) collective-permute-start(f16[2,128,128]{2,1,0:T(8,128)(2,1)S(1)} %add_convert_fusion.3), channel_id=1, source_target_pairs={{0,24},{1,25},{2,26},{3,27},{4,7},{5,6},{6,5},{7,4},{8,16},{9,17},... | collective-permute-start | bytes 196616 | tf_op jit(solution)/shard_map/ppermute | solution.py:212
  39.1 0.5 collective-permute-start.14
  39.6 1.5 %collective-permute-start.13 = (f16[2,128,128]{2,1,0:T(8,128)(2,1)S(1)}, f16[2,128,128]{2,1,0:T(8,128)(2,1)S(1)}, u32[]{:S(2)}, u32[]{:S(2)}) collective-permute-start(f16[2,128,128]{2,1,0:T(8,128)(2,1)S(1)} %add_convert_fusion.3), channel_id=1, source_target_pairs={{0,8},{1,9},{2,10},{3,11},{4,5},{5,4},{6,7},{7,6},{8,0},{9,1},{10,... | collective-permute-start | bytes 196616 | tf_op jit(solution)/shard_map/ppermute | solution.py:212
  41.1 1.7 %collective-permute-done.15 = f16[2,128,128]{2,1,0:T(8,128)(2,1)S(1)} collective-permute-done((f16[2,128,128]{2,1,0:T(8,128)(2,1)S(1)}, f16[2,128,128]{2,1,0:T(8,128)(2,1)S(1)}, u32[]{:S(2)}, u32[]{:S(2)}) %collective-permute-start.15) | collective-permute-done | bytes 65568 | tf_op jit(solution)/shard_map/ppermute | solution.py:212
  42.7 0.7 collective-permute-done.14
  43.4 0.4 collective-permute-done.13
  43.9 2.0 %collective-permute-start.18 = (f16[2,128,128]{2,1,0:T(8,128)(2,1)S(1)}, f16[2,128,128]{2,1,0:T(8,128)(2,1)S(1)}, u32[]{:S(2)}, u32[]{:S(2)}) collective-permute-start(f16[2,128,128]{2,1,0:T(8,128)(2,1)S(1)} %add_convert_fusion.2), channel_id=1, source_target_pairs={{0,3},{1,2},{2,1},{3,0},{4,28},{5,29},{6,30},{7,31},{8,11},{9,10},... | collective-permute-start | bytes 196616 | tf_op jit(solution)/shard_map/ppermute | solution.py:212
  45.9 2.4 %collective-permute-start.16 = (f16[2,128,128]{2,1,0:T(8,128)(2,1)S(1)}, f16[2,128,128]{2,1,0:T(8,128)(2,1)S(1)}, u32[]{:S(2)}, u32[]{:S(2)}) collective-permute-start(f16[2,128,128]{2,1,0:T(8,128)(2,1)S(1)} %add_convert_fusion.2), channel_id=1, source_target_pairs={{0,1},{1,0},{2,3},{3,2},{4,12},{5,13},{6,14},{7,15},{8,9},{9,8},{1... | collective-permute-start | bytes 196616 | tf_op jit(solution)/shard_map/ppermute | solution.py:212
  48.3 1.7 %collective-permute-done.18 = f16[2,128,128]{2,1,0:T(8,128)(2,1)S(1)} collective-permute-done((f16[2,128,128]{2,1,0:T(8,128)(2,1)S(1)}, f16[2,128,128]{2,1,0:T(8,128)(2,1)S(1)}, u32[]{:S(2)}, u32[]{:S(2)}) %collective-permute-start.18) | collective-permute-done | bytes 65568 | tf_op jit(solution)/shard_map/ppermute | solution.py:212
  50.0 1.4 %collective-permute-done.17 = f16[2,128,128]{2,1,0:T(8,128)(2,1)S(1)} collective-permute-done((f16[2,128,128]{2,1,0:T(8,128)(2,1)S(1)}, f16[2,128,128]{2,1,0:T(8,128)(2,1)S(1)}, u32[]{:S(2)}, u32[]{:S(2)}) %collective-permute-start.17) | collective-permute-done | bytes 65568 | tf_op jit(solution)/shard_map/ppermute | solution.py:212
  51.6 1.3 %collective-permute-done.19.far = f32[2,128,128]{2,1,0:T(8,128)S(1)} collective-permute-done((f32[2,128,128]{2,1,0:T(8,128)S(1)}, f32[2,128,128]{2,1,0:T(8,128)S(1)}, u32[]{:S(2)}, u32[]{:S(2)}) %collective-permute-start.19) | collective-permute-done | bytes 131104 | tf_op jit(solution)/shard_map/ppermute | solution.py:200
  52.9 2.4 %shard_map.99 = (f32[4,128,128]{2,1,0:T(8,128)S(1)}, f32[8,128]{1,0:T(8,128)S(1)}, f32[2,128,128]{2,1,0:T(8,128)S(1)}, f32[2,128,128]{2,1,0:T(8,128)S(1)}) custom-call(f32[2,128,128]{2,1,0:T(8,128)S(1)} %add_add_fusion.1.own, f32[2,128,128]{2,1,0:T(8,128)S(1)} %collective-permute-done.19.far, f32[4,128,128]{2,1,0:T(8,128)S(1)} %get-tuple-element.38.vec_in, ...), custom_call_target="tpu_custom_call" | custom-call | tf_op jit(solution)/shard_map/pallas_call | solution.py:286
  55.5 1.2 %collective-permute-done.20 = f32[2,128,128]{2,1,0:T(8,128)S(1)} collective-permute-done((f32[2,128,128]{2,1,0:T(8,128)S(1)}, f32[2,128,128]{2,1,0:T(8,128)S(1)}, u32[]{:S(2)}, u32[]{:S(2)}) %collective-permute-start.20) | collective-permute-done | bytes 131104 | tf_op jit(solution)/shard_map/ppermute | solution.py:200
  56.8 2.5 %collective-permute-start.23 = (f16[2,128,128]{2,1,0:T(8,128)(2,1)S(1)}, f16[2,128,128]{2,1,0:T(8,128)(2,1)S(1)}, u32[]{:S(2)}, u32[]{:S(2)}) collective-permute-start(f16[2,128,128]{2,1,0:T(8,128)(2,1)S(1)} %add_convert_fusion.1), channel_id=1, source_target_pairs={{0,24},{1,25},{2,26},{3,27},{4,7},{5,6},{6,5},{7,4},{8,16},{9,17},... | collective-permute-start | bytes 196616 | tf_op jit(solution)/shard_map/ppermute | solution.py:212
  59.3 0.5 collective-permute-start.22
  59.8 0.5 collective-permute-start.21
  60.3 1.7 %collective-permute-done.23 = f16[2,128,128]{2,1,0:T(8,128)(2,1)S(1)} collective-permute-done((f16[2,128,128]{2,1,0:T(8,128)(2,1)S(1)}, f16[2,128,128]{2,1,0:T(8,128)(2,1)S(1)}, u32[]{:S(2)}, u32[]{:S(2)}) %collective-permute-start.23) | collective-permute-done | bytes 65568 | tf_op jit(solution)/shard_map/ppermute | solution.py:212
  62.0 1.5 %collective-permute-done.22 = f16[2,128,128]{2,1,0:T(8,128)(2,1)S(1)} collective-permute-done((f16[2,128,128]{2,1,0:T(8,128)(2,1)S(1)}, f16[2,128,128]{2,1,0:T(8,128)(2,1)S(1)}, u32[]{:S(2)}, u32[]{:S(2)}) %collective-permute-start.22) | collective-permute-done | bytes 65568 | tf_op jit(solution)/shard_map/ppermute | solution.py:212
  63.5 0.5 collective-permute-done.21
  64.1 2.1 %collective-permute-start.26 = (f16[2,128,128]{2,1,0:T(8,128)(2,1)S(1)}, f16[2,128,128]{2,1,0:T(8,128)(2,1)S(1)}, u32[]{:S(2)}, u32[]{:S(2)}) collective-permute-start(f16[2,128,128]{2,1,0:T(8,128)(2,1)S(1)} %add_convert_fusion), channel_id=1, source_target_pairs={{0,3},{1,2},{2,1},{3,0},{4,28},{5,29},{6,30},{7,31},{8,11},{9,10},... | collective-permute-start | bytes 196616 | tf_op jit(solution)/shard_map/ppermute | solution.py:212
  66.2 0.6 collective-permute-start.25
  66.8 1.8 %collective-permute-start.24 = (f16[2,128,128]{2,1,0:T(8,128)(2,1)S(1)}, f16[2,128,128]{2,1,0:T(8,128)(2,1)S(1)}, u32[]{:S(2)}, u32[]{:S(2)}) collective-permute-start(f16[2,128,128]{2,1,0:T(8,128)(2,1)S(1)} %add_convert_fusion), channel_id=1, source_target_pairs={{0,1},{1,0},{2,3},{3,2},{4,12},{5,13},{6,14},{7,15},{8,9},{9,8},{1... | collective-permute-start | bytes 196616 | tf_op jit(solution)/shard_map/ppermute | solution.py:212
  68.5 1.7 %collective-permute-done.26 = f16[2,128,128]{2,1,0:T(8,128)(2,1)S(1)} collective-permute-done((f16[2,128,128]{2,1,0:T(8,128)(2,1)S(1)}, f16[2,128,128]{2,1,0:T(8,128)(2,1)S(1)}, u32[]{:S(2)}, u32[]{:S(2)}) %collective-permute-start.26) | collective-permute-done | bytes 65568 | tf_op jit(solution)/shard_map/ppermute | solution.py:212
  70.2 1.5 %collective-permute-done.25 = f16[2,128,128]{2,1,0:T(8,128)(2,1)S(1)} collective-permute-done((f16[2,128,128]{2,1,0:T(8,128)(2,1)S(1)}, f16[2,128,128]{2,1,0:T(8,128)(2,1)S(1)}, u32[]{:S(2)}, u32[]{:S(2)}) %collective-permute-start.25) | collective-permute-done | bytes 65568 | tf_op jit(solution)/shard_map/ppermute | solution.py:212
  71.9 1.3 %collective-permute-done.27.far = f32[2,128,128]{2,1,0:T(8,128)S(1)} collective-permute-done((f32[2,128,128]{2,1,0:T(8,128)S(1)}, f32[2,128,128]{2,1,0:T(8,128)S(1)}, u32[]{:S(2)}, u32[]{:S(2)}) %collective-permute-start.27) | collective-permute-done | bytes 131104 | tf_op jit(solution)/shard_map/ppermute | solution.py:200
  73.2 1.0 %shard_map.100 = (f32[1,128,128]{2,1,0:T(8,128)}, f32[3]{0:T(128)}) custom-call(f32[2,128,128]{2,1,0:T(8,128)S(1)} %add_add_fusion.own, f32[2,128,128]{2,1,0:T(8,128)S(1)} %collective-permute-done.27.far, f32[4,128,128]{2,1,0:T(8,128)S(1)} %get-tuple-element.42.vec, f32[4,128,128]{2,1,0:T(8,128)S(1)} %get-tuple-element.34.inv, ...), custom_call_target="tpu_custom_call" | custom-call | tf_op jit(solution)/shard_map/pallas_call | solution.py:296
  (23 shorter events, 1.0 us)
Async XLA Ops:
  1.5 8.5 %collective-permute-start = (f32[2,128,128]{2,1,0:T(8,128)S(1)}, f32[2,128,128]{2,1,0:T(8,128)S(1)}, u32[]{:S(2)}, u32[]{:S(2)}) collective-permute-start(f32[2,128,128]{2,1,0:T(8,128)S(1)} %get-tuple-element.23.refs_0_), channel_id=1, source_target_pairs={{0,1},{1,0},{2,3},{3,2},{4,6},{5,7},{6,4},{7,5},{8,9},{9,8},{10,11... | collective-permute-start | bytes 393224 | tf_op jit(solution)/shard_map/ppermute | solution.py:212
  4.6 7.1 %collective-permute-start.1 = (f32[1,128,128]{2,1,0:T(8,128)S(1)}, f32[1,128,128]{2,1,0:T(8,128)S(1)}, u32[]{:S(2)}, u32[]{:S(2)}) collective-permute-start(f32[1,128,128]{2,1,0:T(8,128)S(1)} %get-tuple-element.26), channel_id=1, source_target_pairs={{0,3},{1,2},{2,1},{3,0},{4,7},{5,6},{6,5},{7,4},{8,11},{9,10},{10,... | collective-permute-start | bytes 196616 | tf_op jit(solution)/shard_map/ppermute | solution.py:200
  10.0 3.0 %collective-permute-start.2 = (f32[2,128,128]{2,1,0:T(8,128)S(1)}, f32[2,128,128]{2,1,0:T(8,128)S(1)}, u32[]{:S(2)}, u32[]{:S(2)}) collective-permute-start(f32[2,128,128]{2,1,0:T(8,128)S(1)} %collective-permute-done.refs_1_), channel_id=1, source_target_pairs={{0,4},{4,0},{8,12},{12,8},{16,20},{20,16},{24,28},{28,24},{1,5},{5... | collective-permute-start | bytes 393224 | tf_op jit(solution)/shard_map/ppermute | solution.py:200
  11.7 1.3 %collective-permute-start.3 = (f32[1,128,128]{2,1,0:T(8,128)S(1)}, f32[1,128,128]{2,1,0:T(8,128)S(1)}, u32[]{:S(2)}, u32[]{:S(2)}) collective-permute-start(f32[1,128,128]{2,1,0:T(8,128)S(1)} %collective-permute-done.1.refs_2_), channel_id=1, source_target_pairs={{0,4},{4,0},{8,12},{12,8},{16,20},{20,16},{24,28},{28,24},{1,5},{5... | collective-permute-start | bytes 196616 | tf_op jit(solution)/shard_map/ppermute | solution.py:200
  15.1 1.4 %collective-permute-start.4 = (f32[2,128,128]{2,1,0:T(8,128)S(1)}, f32[2,128,128]{2,1,0:T(8,128)S(1)}, u32[]{:S(2)}, u32[]{:S(2)}) collective-permute-start(f32[2,128,128]{2,1,0:T(8,128)S(1)} %get-tuple-element.31), channel_id=1, source_target_pairs={{0,4},{4,0},{8,12},{12,8},{16,20},{20,16},{24,28},{28,24},{1,5},{5... | collective-permute-start | bytes 393224 | tf_op jit(solution)/shard_map/ppermute | solution.py:200
  16.6 5.2 %collective-permute-start.7 = (f16[2,128,128]{2,1,0:T(8,128)(2,1)S(1)}, f16[2,128,128]{2,1,0:T(8,128)(2,1)S(1)}, u32[]{:S(2)}, u32[]{:S(2)}) collective-permute-start(f16[2,128,128]{2,1,0:T(8,128)(2,1)S(1)} %add_convert_fusion.5), channel_id=1, source_target_pairs={{0,24},{1,25},{2,26},{3,27},{4,7},{5,6},{6,5},{7,4},{8,16},{9,17},... | collective-permute-start | bytes 196616 | tf_op jit(solution)/shard_map/ppermute | solution.py:212
  19.1 4.3 %collective-permute-start.6 = (f16[2,128,128]{2,1,0:T(8,128)(2,1)S(1)}, f16[2,128,128]{2,1,0:T(8,128)(2,1)S(1)}, u32[]{:S(2)}, u32[]{:S(2)}) collective-permute-start(f16[2,128,128]{2,1,0:T(8,128)(2,1)S(1)} %add_convert_fusion.5), channel_id=1, source_target_pairs={{0,16},{1,17},{2,18},{3,19},{4,6},{5,7},{6,4},{7,5},{8,24},{9,25},... | collective-permute-start | bytes 196616 | tf_op jit(solution)/shard_map/ppermute | solution.py:212
  19.6 4.3 %collective-permute-start.5 = (f16[2,128,128]{2,1,0:T(8,128)(2,1)S(1)}, f16[2,128,128]{2,1,0:T(8,128)(2,1)S(1)}, u32[]{:S(2)}, u32[]{:S(2)}) collective-permute-start(f16[2,128,128]{2,1,0:T(8,128)(2,1)S(1)} %add_convert_fusion.5), channel_id=1, source_target_pairs={{0,8},{1,9},{2,10},{3,11},{4,5},{5,4},{6,7},{7,6},{8,0},{9,1},{10,... | collective-permute-start | bytes 196616 | tf_op jit(solution)/shard_map/ppermute | solution.py:212
  23.9 6.1 %collective-permute-start.10 = (f16[2,128,128]{2,1,0:T(8,128)(2,1)S(1)}, f16[2,128,128]{2,1,0:T(8,128)(2,1)S(1)}, u32[]{:S(2)}, u32[]{:S(2)}) collective-permute-start(f16[2,128,128]{2,1,0:T(8,128)(2,1)S(1)} %add_convert_fusion.4), channel_id=1, source_target_pairs={{0,3},{1,2},{2,1},{3,0},{4,28},{5,29},{6,30},{7,31},{8,11},{9,10},... | collective-permute-start | bytes 196616 | tf_op jit(solution)/shard_map/ppermute | solution.py:212
  26.7 5.6 %collective-permute-start.9 = (f16[2,128,128]{2,1,0:T(8,128)(2,1)S(1)}, f16[2,128,128]{2,1,0:T(8,128)(2,1)S(1)}, u32[]{:S(2)}, u32[]{:S(2)}) collective-permute-start(f16[2,128,128]{2,1,0:T(8,128)(2,1)S(1)} %add_convert_fusion.4), channel_id=1, source_target_pairs={{0,2},{1,3},{2,0},{3,1},{4,20},{5,21},{6,22},{7,23},{8,10},{9,11},... | collective-permute-start | bytes 196616 | tf_op jit(solution)/shard_map/ppermute | solution.py:212
  26.7 5.6 %collective-permute-start.8 = (f16[2,128,128]{2,1,0:T(8,128)(2,1)S(1)}, f16[2,128,128]{2,1,0:T(8,128)(2,1)S(1)}, u32[]{:S(2)}, u32[]{:S(2)}) collective-permute-start(f16[2,128,128]{2,1,0:T(8,128)(2,1)S(1)} %add_convert_fusion.4), channel_id=1, source_target_pairs={{0,1},{1,0},{2,3},{3,2},{4,12},{5,13},{6,14},{7,15},{8,9},{9,8},{1... | collective-permute-start | bytes 196616 | tf_op jit(solution)/shard_map/ppermute | solution.py:212
  32.2 1.4 %collective-permute-start.11 = (f32[2,128,128]{2,1,0:T(8,128)S(1)}, f32[2,128,128]{2,1,0:T(8,128)S(1)}, u32[]{:S(2)}, u32[]{:S(2)}) collective-permute-start(f32[2,128,128]{2,1,0:T(8,128)S(1)} %add_add_fusion.2.own), channel_id=1, source_target_pairs={{0,4},{4,0},{8,12},{12,8},{16,20},{20,16},{24,28},{28,24},{1,5},{5... | collective-permute-start | bytes 393224 | tf_op jit(solution)/shard_map/ppermute | solution.py:200
  36.1 1.4 %collective-permute-start.12 = (f32[2,128,128]{2,1,0:T(8,128)S(1)}, f32[2,128,128]{2,1,0:T(8,128)S(1)}, u32[]{:S(2)}, u32[]{:S(2)}) collective-permute-start(f32[2,128,128]{2,1,0:T(8,128)S(1)} %get-tuple-element.37), channel_id=1, source_target_pairs={{0,4},{4,0},{8,12},{12,8},{16,20},{20,16},{24,28},{28,24},{1,5},{5... | collective-permute-start | bytes 393224 | tf_op jit(solution)/shard_map/ppermute | solution.py:200
  37.5 5.2 %collective-permute-start.15 = (f16[2,128,128]{2,1,0:T(8,128)(2,1)S(1)}, f16[2,128,128]{2,1,0:T(8,128)(2,1)S(1)}, u32[]{:S(2)}, u32[]{:S(2)}) collective-permute-start(f16[2,128,128]{2,1,0:T(8,128)(2,1)S(1)} %add_convert_fusion.3), channel_id=1, source_target_pairs={{0,24},{1,25},{2,26},{3,27},{4,7},{5,6},{6,5},{7,4},{8,16},{9,17},... | collective-permute-start | bytes 196616 | tf_op jit(solution)/shard_map/ppermute | solution.py:212
  39.1 4.4 %collective-permute-start.14 = (f16[2,128,128]{2,1,0:T(8,128)(2,1)S(1)}, f16[2,128,128]{2,1,0:T(8,128)(2,1)S(1)}, u32[]{:S(2)}, u32[]{:S(2)}) collective-permute-start(f16[2,128,128]{2,1,0:T(8,128)(2,1)S(1)} %add_convert_fusion.3), channel_id=1, source_target_pairs={{0,16},{1,17},{2,18},{3,19},{4,6},{5,7},{6,4},{7,5},{8,24},{9,25},... | collective-permute-start | bytes 196616 | tf_op jit(solution)/shard_map/ppermute | solution.py:212
  39.6 4.3 %collective-permute-start.13 = (f16[2,128,128]{2,1,0:T(8,128)(2,1)S(1)}, f16[2,128,128]{2,1,0:T(8,128)(2,1)S(1)}, u32[]{:S(2)}, u32[]{:S(2)}) collective-permute-start(f16[2,128,128]{2,1,0:T(8,128)(2,1)S(1)} %add_convert_fusion.3), channel_id=1, source_target_pairs={{0,8},{1,9},{2,10},{3,11},{4,5},{5,4},{6,7},{7,6},{8,0},{9,1},{10,... | collective-permute-start | bytes 196616 | tf_op jit(solution)/shard_map/ppermute | solution.py:212
  43.9 6.1 %collective-permute-start.18 = (f16[2,128,128]{2,1,0:T(8,128)(2,1)S(1)}, f16[2,128,128]{2,1,0:T(8,128)(2,1)S(1)}, u32[]{:S(2)}, u32[]{:S(2)}) collective-permute-start(f16[2,128,128]{2,1,0:T(8,128)(2,1)S(1)} %add_convert_fusion.2), channel_id=1, source_target_pairs={{0,3},{1,2},{2,1},{3,0},{4,28},{5,29},{6,30},{7,31},{8,11},{9,10},... | collective-permute-start | bytes 196616 | tf_op jit(solution)/shard_map/ppermute | solution.py:212
  45.9 5.5 %collective-permute-start.17 = (f16[2,128,128]{2,1,0:T(8,128)(2,1)S(1)}, f16[2,128,128]{2,1,0:T(8,128)(2,1)S(1)}, u32[]{:S(2)}, u32[]{:S(2)}) collective-permute-start(f16[2,128,128]{2,1,0:T(8,128)(2,1)S(1)} %add_convert_fusion.2), channel_id=1, source_target_pairs={{0,2},{1,3},{2,0},{3,1},{4,20},{5,21},{6,22},{7,23},{8,10},{9,11},... | collective-permute-start | bytes 196616 | tf_op jit(solution)/shard_map/ppermute | solution.py:212
  45.9 5.5 %collective-permute-start.16 = (f16[2,128,128]{2,1,0:T(8,128)(2,1)S(1)}, f16[2,128,128]{2,1,0:T(8,128)(2,1)S(1)}, u32[]{:S(2)}, u32[]{:S(2)}) collective-permute-start(f16[2,128,128]{2,1,0:T(8,128)(2,1)S(1)} %add_convert_fusion.2), channel_id=1, source_target_pairs={{0,1},{1,0},{2,3},{3,2},{4,12},{5,13},{6,14},{7,15},{8,9},{9,8},{1... | collective-permute-start | bytes 196616 | tf_op jit(solution)/shard_map/ppermute | solution.py:212
  51.5 1.4 %collective-permute-start.19 = (f32[2,128,128]{2,1,0:T(8,128)S(1)}, f32[2,128,128]{2,1,0:T(8,128)S(1)}, u32[]{:S(2)}, u32[]{:S(2)}) collective-permute-start(f32[2,128,128]{2,1,0:T(8,128)S(1)} %add_add_fusion.1.own), channel_id=1, source_target_pairs={{0,4},{4,0},{8,12},{12,8},{16,20},{20,16},{24,28},{28,24},{1,5},{5... | collective-permute-start | bytes 393224 | tf_op jit(solution)/shard_map/ppermute | solution.py:200
  55.3 1.4 %collective-permute-start.20 = (f32[2,128,128]{2,1,0:T(8,128)S(1)}, f32[2,128,128]{2,1,0:T(8,128)S(1)}, u32[]{:S(2)}, u32[]{:S(2)}) collective-permute-start(f32[2,128,128]{2,1,0:T(8,128)S(1)} %get-tuple-element.41), channel_id=1, source_target_pairs={{0,4},{4,0},{8,12},{12,8},{16,20},{20,16},{24,28},{28,24},{1,5},{5... | collective-permute-start | bytes 393224 | tf_op jit(solution)/shard_map/ppermute | solution.py:200
  56.8 5.2 %collective-permute-start.23 = (f16[2,128,128]{2,1,0:T(8,128)(2,1)S(1)}, f16[2,128,128]{2,1,0:T(8,128)(2,1)S(1)}, u32[]{:S(2)}, u32[]{:S(2)}) collective-permute-start(f16[2,128,128]{2,1,0:T(8,128)(2,1)S(1)} %add_convert_fusion.1), channel_id=1, source_target_pairs={{0,24},{1,25},{2,26},{3,27},{4,7},{5,6},{6,5},{7,4},{8,16},{9,17},... | collective-permute-start | bytes 196616 | tf_op jit(solution)/shard_map/ppermute | solution.py:212
  59.3 4.3 %collective-permute-start.22 = (f16[2,128,128]{2,1,0:T(8,128)(2,1)S(1)}, f16[2,128,128]{2,1,0:T(8,128)(2,1)S(1)}, u32[]{:S(2)}, u32[]{:S(2)}) collective-permute-start(f16[2,128,128]{2,1,0:T(8,128)(2,1)S(1)} %add_convert_fusion.1), channel_id=1, source_target_pairs={{0,16},{1,17},{2,18},{3,19},{4,6},{5,7},{6,4},{7,5},{8,24},{9,25},... | collective-permute-start | bytes 196616 | tf_op jit(solution)/shard_map/ppermute | solution.py:212
  59.8 4.3 %collective-permute-start.21 = (f16[2,128,128]{2,1,0:T(8,128)(2,1)S(1)}, f16[2,128,128]{2,1,0:T(8,128)(2,1)S(1)}, u32[]{:S(2)}, u32[]{:S(2)}) collective-permute-start(f16[2,128,128]{2,1,0:T(8,128)(2,1)S(1)} %add_convert_fusion.1), channel_id=1, source_target_pairs={{0,8},{1,9},{2,10},{3,11},{4,5},{5,4},{6,7},{7,6},{8,0},{9,1},{10,... | collective-permute-start | bytes 196616 | tf_op jit(solution)/shard_map/ppermute | solution.py:212
  64.1 6.1 %collective-permute-start.26 = (f16[2,128,128]{2,1,0:T(8,128)(2,1)S(1)}, f16[2,128,128]{2,1,0:T(8,128)(2,1)S(1)}, u32[]{:S(2)}, u32[]{:S(2)}) collective-permute-start(f16[2,128,128]{2,1,0:T(8,128)(2,1)S(1)} %add_convert_fusion), channel_id=1, source_target_pairs={{0,3},{1,2},{2,1},{3,0},{4,28},{5,29},{6,30},{7,31},{8,11},{9,10},... | collective-permute-start | bytes 196616 | tf_op jit(solution)/shard_map/ppermute | solution.py:212
  66.2 5.6 %collective-permute-start.25 = (f16[2,128,128]{2,1,0:T(8,128)(2,1)S(1)}, f16[2,128,128]{2,1,0:T(8,128)(2,1)S(1)}, u32[]{:S(2)}, u32[]{:S(2)}) collective-permute-start(f16[2,128,128]{2,1,0:T(8,128)(2,1)S(1)} %add_convert_fusion), channel_id=1, source_target_pairs={{0,2},{1,3},{2,0},{3,1},{4,20},{5,21},{6,22},{7,23},{8,10},{9,11},... | collective-permute-start | bytes 196616 | tf_op jit(solution)/shard_map/ppermute | solution.py:212
  66.8 5.0 %collective-permute-start.24 = (f16[2,128,128]{2,1,0:T(8,128)(2,1)S(1)}, f16[2,128,128]{2,1,0:T(8,128)(2,1)S(1)}, u32[]{:S(2)}, u32[]{:S(2)}) collective-permute-start(f16[2,128,128]{2,1,0:T(8,128)(2,1)S(1)} %add_convert_fusion), channel_id=1, source_target_pairs={{0,1},{1,0},{2,3},{3,2},{4,12},{5,13},{6,14},{7,15},{8,9},{9,8},{1... | collective-permute-start | bytes 196616 | tf_op jit(solution)/shard_map/ppermute | solution.py:212
  71.8 1.4 %collective-permute-start.27 = (f32[2,128,128]{2,1,0:T(8,128)S(1)}, f32[2,128,128]{2,1,0:T(8,128)S(1)}, u32[]{:S(2)}, u32[]{:S(2)}) collective-permute-start(f32[2,128,128]{2,1,0:T(8,128)S(1)} %add_add_fusion.own), channel_id=1, source_target_pairs={{0,4},{4,0},{8,12},{12,8},{16,20},{20,16},{24,28},{28,24},{1,5},{5... | collective-permute-start | bytes 393224 | tf_op jit(solution)/shard_map/ppermute | solution.py:200

commit v8 on v7

--- a/solution.py
+++ b/solution.py
@@ -203,7 +203,8 @@
 def stages(axis, first):
     count = lax.axis_size(axis).bit_length() - 1
     one = 1 if axis == "sectors" else lax.axis_size("sectors")
-    return [[mask * one << low for mask in range(1, 1 << min(2, count - low))] for low in range(first, count, 2)]
+    order = (1, 2, 3) if axis == "sectors" else (1, 3, 2)
+    return [[mask * one << low for mask in order[: (1 << min(2, count - low)) - 1]] for low in range(first, count, 2)]
 
 
 def exchange(x, masks):
@@ -213,7 +214,7 @@
 
 
 def reduce_half(keep, send):
-    x = keep + swap(send, "terms", 1)
+    x = keep + swap(send.astype(HALF), "terms", 1).astype(F32)
     along, across = stages("terms", 1), stages("sectors", 0)
     orders = along + across, across + along
     if [len(s) for s in orders[0]] != [len(s) for s in orders[1]]:

time: 74.3 us -> 74.1 us (level)
  transfers between devices with their start and end apart: 28 -> 28, of which waited for: 23 -> 22; matrix products, arithmetic and copies ran while one was open for 0% -> 0% of each run, Pallas kernels for 4% -> 4%
where the time goes in v8:
time: 74.1 us; the launch traced here: 74 us
  waiting for transfers between devices  30.6 us (41%)
  starting transfers between devices  30.5 us (41%)
  Pallas kernels  11.7 us (16%)
  between operations  0.78 us (1%)
    ppermute x19, starting transfers between devices, exchange(): lax.ppermute(x, ('terms', 'sectors'), [(d, d ^ masks[d // sectors % 2]) f...  27.1 us
    ppermute x19, waiting for transfers between devices, exchange(): lax.ppermute(x, ('terms', 'sectors'), [(d, d ^ masks[d // sectors % 2]) f...  20.4 us
    ppermute x9, waiting for transfers between devices, swap(): lax.ppermute(x, axis, [(i, i ^ mask) for i in range(lax.axis_size(axis))])  10.2 us
    pallas_call x2, Pallas kernels, on_device(): pl.pallas_call(functools.partial(middle_kernel, wire, step), out_shape=(w...  4.81 us
    ppermute x9, starting transfers between devices, swap(): lax.ppermute(x, axis, [(i, i ^ mask) for i in range(lax.axis_size(axis))])  3.41 us
    pallas_call x1, Pallas kernels, on_device(): pl.pallas_call(load_kernel, out_shape=(jax.ShapeDtypeStruct(left_ops.shap...  2.88 us
    pallas_call x1, Pallas kernels, on_device(): pl.pallas_call(functools.partial(first_kernel, wire, pairs, last), out_sh...  2.16 us
  transfers between devices with their start and end apart: 28, of which 22 were waited for; matrix products, arithmetic and copies ran while one was open for 0% of the time, Pallas kernels for 4%

profile of v8, /device:TPU:0, one launch (start us, length us, event | category | flops | bytes accessed | tf_op | source)
XLA Modules:
  0.0 74.0 jit_solution(4061214622271719924)
XLA Ops:
  0.6 0.9 %shard_map.95 = (f32[2,128,128]{2,1,0:T(8,128)S(1)}, f32[1,128,128]{2,1,0:T(8,128)S(1)}) custom-call(f32[1,128,128]{2,1,0:T(8,128)} %trial.1, f32[1,128,128]{2,1,0:T(8,128)} %precond.1), custom_call_target="tpu_custom_call" | custom-call | tf_op jit(solution)/shard_map/pallas_call | solution.py:263
  1.5 3.1 %collective-permute-start = (f32[2,128,128]{2,1,0:T(8,128)S(1)}, f32[2,128,128]{2,1,0:T(8,128)S(1)}, u32[]{:S(2)}, u32[]{:S(2)}) collective-permute-start(f32[2,128,128]{2,1,0:T(8,128)S(1)} %get-tuple-element.23.refs_0_), channel_id=1, source_target_pairs={{0,1},{1,0},{2,3},{3,2},{4,6},{5,7},{6,4},{7,5},{8,9},{9,8},{10,11... | collective-permute-start | bytes 393224 | tf_op jit(solution)/shard_map/ppermute | solution.py:213
  4.6 2.5 %collective-permute-start.1 = (f32[1,128,128]{2,1,0:T(8,128)S(1)}, f32[1,128,128]{2,1,0:T(8,128)S(1)}, u32[]{:S(2)}, u32[]{:S(2)}) collective-permute-start(f32[1,128,128]{2,1,0:T(8,128)S(1)} %get-tuple-element.26), channel_id=1, source_target_pairs={{0,3},{1,2},{2,1},{3,0},{4,7},{5,6},{6,5},{7,4},{8,11},{9,10},{10,... | collective-permute-start | bytes 196616 | tf_op jit(solution)/shard_map/ppermute | solution.py:200
  7.1 2.9 %shard_map.96 = (bf16[64,128,128]{2,1,0:T(8,128)(2,1)S(1)}, bf16[64,128,128]{2,1,0:T(8,128)(2,1)S(1)}, s32[132]{0:T(256)S(1)}) custom-call(s32[4]{0:T(128)} %rows_hbm.1, s32[4]{0:T(128)} %owner_hbm.1, s32[64]{0:T(128)} %in_hbm.1, s32[64]{0:T(128)} %out_hbm.1, bf16[64,128,128]{2,1,0:T(8,128)(2,1)} %left_hbm.1, bf16[64,128,128]{2,1,0:T(8,128)(2,1)} %right_hbm.1), custom_call_target="tpu_custom_call" | custom-call | bytes 4194304 | tf_op jit(solution)/shard_map/pallas_call | solution.py:246
  10.1 1.6 %collective-permute-done.1.refs_2_ = f32[1,128,128]{2,1,0:T(8,128)S(1)} collective-permute-done((f32[1,128,128]{2,1,0:T(8,128)S(1)}, f32[1,128,128]{2,1,0:T(8,128)S(1)}, u32[]{:S(2)}, u32[]{:S(2)}) %collective-permute-start.1) | collective-permute-done | bytes 65568 | tf_op jit(solution)/shard_map/ppermute | solution.py:200
  11.7 1.3 %collective-permute-done.3.refs_4_ = f32[1,128,128]{2,1,0:T(8,128)S(1)} collective-permute-done((f32[1,128,128]{2,1,0:T(8,128)S(1)}, f32[1,128,128]{2,1,0:T(8,128)S(1)}, u32[]{:S(2)}, u32[]{:S(2)}) %collective-permute-start.3) | collective-permute-done | bytes 65568 | tf_op jit(solution)/shard_map/ppermute | solution.py:200
  13.0 2.2 %shard_map.97 = (f32[4,128,128]{2,1,0:T(8,128)S(1)}, f32[4,128,128]{2,1,0:T(8,128)S(1)}, f32[4,128,128]{2,1,0:T(8,128)S(1)}, f32[8,128]{1,0:T(8,128)S(1)}, f32[2...) custom-call(f32[2,128,128]{2,1,0:T(8,128)S(1)} %get-tuple-element.23.refs_0_, ...), custom_call_target="tpu_custom_call" | custom-call | tf_op jit(solution)/shard_map/pallas_call | solution.py:276
  15.1 0.2 collective-permute-start.4
  15.4 1.1 %collective-permute-done.4 = f16[2,128,128]{2,1,0:T(8,128)(2,1)S(1)} collective-permute-done((f16[2,128,128]{2,1,0:T(8,128)(2,1)S(1)}, f16[2,128,128]{2,1,0:T(8,128)(2,1)S(1)}, u32[]{:S(2)}, u32[]{:S(2)}) %collective-permute-start.4) | collective-permute-done | bytes 65568 | tf_op jit(solution)/shard_map/ppermute | solution.py:200
  16.5 1.6 %collective-permute-start.7 = (f16[2,128,128]{2,1,0:T(8,128)(2,1)S(1)}, f16[2,128,128]{2,1,0:T(8,128)(2,1)S(1)}, u32[]{:S(2)}, u32[]{:S(2)}) collective-permute-start(f16[2,128,128]{2,1,0:T(8,128)(2,1)S(1)} %add_convert_fusion.5), channel_id=1, source_target_pairs={{0,16},{1,17},{2,18},{3,19},{4,7},{5,6},{6,5},{7,4},{8,24},{9,25},... | collective-permute-start | bytes 196616 | tf_op jit(solution)/shard_map/ppermute | solution.py:213
  18.1 1.4 %collective-permute-start.6 = (f16[2,128,128]{2,1,0:T(8,128)(2,1)S(1)}, f16[2,128,128]{2,1,0:T(8,128)(2,1)S(1)}, u32[]{:S(2)}, u32[]{:S(2)}) collective-permute-start(f16[2,128,128]{2,1,0:T(8,128)(2,1)S(1)} %add_convert_fusion.5), channel_id=1, source_target_pairs={{0,24},{1,25},{2,26},{3,27},{4,6},{5,7},{6,4},{7,5},{8,16},{9,17},... | collective-permute-start | bytes 196616 | tf_op jit(solution)/shard_map/ppermute | solution.py:213
  19.5 0.5 collective-permute-start.5
  20.0 0.8 %collective-permute-done.7 = f16[2,128,128]{2,1,0:T(8,128)(2,1)S(1)} collective-permute-done((f16[2,128,128]{2,1,0:T(8,128)(2,1)S(1)}, f16[2,128,128]{2,1,0:T(8,128)(2,1)S(1)}, u32[]{:S(2)}, u32[]{:S(2)}) %collective-permute-start.7) | collective-permute-done | bytes 65568 | tf_op jit(solution)/shard_map/ppermute | solution.py:213
  20.8 2.4 %collective-permute-done.6 = f16[2,128,128]{2,1,0:T(8,128)(2,1)S(1)} collective-permute-done((f16[2,128,128]{2,1,0:T(8,128)(2,1)S(1)}, f16[2,128,128]{2,1,0:T(8,128)(2,1)S(1)}, u32[]{:S(2)}, u32[]{:S(2)}) %collective-permute-start.6) | collective-permute-done | bytes 65568 | tf_op jit(solution)/shard_map/ppermute | solution.py:213
  23.2 0.5 collective-permute-done.5
  23.8 2.8 %collective-permute-start.10 = (f16[2,128,128]{2,1,0:T(8,128)(2,1)S(1)}, f16[2,128,128]{2,1,0:T(8,128)(2,1)S(1)}, u32[]{:S(2)}, u32[]{:S(2)}) collective-permute-start(f16[2,128,128]{2,1,0:T(8,128)(2,1)S(1)} %add_convert_fusion.4), channel_id=1, source_target_pairs={{0,3},{1,2},{2,1},{3,0},{4,20},{5,21},{6,22},{7,23},{8,11},{9,10},... | collective-permute-start | bytes 196616 | tf_op jit(solution)/shard_map/ppermute | solution.py:213
  26.6 1.7 %collective-permute-start.8 = (f16[2,128,128]{2,1,0:T(8,128)(2,1)S(1)}, f16[2,128,128]{2,1,0:T(8,128)(2,1)S(1)}, u32[]{:S(2)}, u32[]{:S(2)}) collective-permute-start(f16[2,128,128]{2,1,0:T(8,128)(2,1)S(1)} %add_convert_fusion.4), channel_id=1, source_target_pairs={{0,1},{1,0},{2,3},{3,2},{4,12},{5,13},{6,14},{7,15},{8,9},{9,8},{1... | collective-permute-start | bytes 196616 | tf_op jit(solution)/shard_map/ppermute | solution.py:213
  28.3 1.7 %collective-permute-done.10 = f16[2,128,128]{2,1,0:T(8,128)(2,1)S(1)} collective-permute-done((f16[2,128,128]{2,1,0:T(8,128)(2,1)S(1)}, f16[2,128,128]{2,1,0:T(8,128)(2,1)S(1)}, u32[]{:S(2)}, u32[]{:S(2)}) %collective-permute-start.10) | collective-permute-done | bytes 65568 | tf_op jit(solution)/shard_map/ppermute | solution.py:213
  30.0 2.2 %collective-permute-done.9 = f16[2,128,128]{2,1,0:T(8,128)(2,1)S(1)} collective-permute-done((f16[2,128,128]{2,1,0:T(8,128)(2,1)S(1)}, f16[2,128,128]{2,1,0:T(8,128)(2,1)S(1)}, u32[]{:S(2)}, u32[]{:S(2)}) %collective-permute-start.9) | collective-permute-done | bytes 65568 | tf_op jit(solution)/shard_map/ppermute | solution.py:213
  32.3 1.3 %collective-permute-done.11.far = f32[2,128,128]{2,1,0:T(8,128)S(1)} collective-permute-done((f32[2,128,128]{2,1,0:T(8,128)S(1)}, f32[2,128,128]{2,1,0:T(8,128)S(1)}, u32[]{:S(2)}, u32[]{:S(2)}) %collective-permute-start.11) | collective-permute-done | bytes 131104 | tf_op jit(solution)/shard_map/ppermute | solution.py:200
  33.6 2.4 %shard_map.98 = (f32[4,128,128]{2,1,0:T(8,128)S(1)}, f32[8,128]{1,0:T(8,128)S(1)}, f32[2,128,128]{2,1,0:T(8,128)S(1)}, f32[2,128,128]{2,1,0:T(8,128)S(1)}) custom-call(f32[2,128,128]{2,1,0:T(8,128)S(1)} %add_add_fusion.2.own, f32[2,128,128]{2,1,0:T(8,128)S(1)} %collective-permute-done.11.far, f32[4,128,128]{2,1,0:T(8,128)S(1)} %get-tuple-element.32.vec_in, ...), custom_call_target="tpu_custom_call" | custom-call | tf_op jit(solution)/shard_map/pallas_call | solution.py:287
  36.0 0.2 collective-permute-start.12
  36.2 1.1 %collective-permute-done.12 = f16[2,128,128]{2,1,0:T(8,128)(2,1)S(1)} collective-permute-done((f16[2,128,128]{2,1,0:T(8,128)(2,1)S(1)}, f16[2,128,128]{2,1,0:T(8,128)(2,1)S(1)}, u32[]{:S(2)}, u32[]{:S(2)}) %collective-permute-start.12) | collective-permute-done | bytes 65568 | tf_op jit(solution)/shard_map/ppermute | solution.py:200
  37.4 1.6 %collective-permute-start.15 = (f16[2,128,128]{2,1,0:T(8,128)(2,1)S(1)}, f16[2,128,128]{2,1,0:T(8,128)(2,1)S(1)}, u32[]{:S(2)}, u32[]{:S(2)}) collective-permute-start(f16[2,128,128]{2,1,0:T(8,128)(2,1)S(1)} %add_convert_fusion.3), channel_id=1, source_target_pairs={{0,16},{1,17},{2,18},{3,19},{4,7},{5,6},{6,5},{7,4},{8,24},{9,25},... | collective-permute-start | bytes 196616 | tf_op jit(solution)/shard_map/ppermute | solution.py:213
  39.0 0.9 %collective-permute-start.14 = (f16[2,128,128]{2,1,0:T(8,128)(2,1)S(1)}, f16[2,128,128]{2,1,0:T(8,128)(2,1)S(1)}, u32[]{:S(2)}, u32[]{:S(2)}) collective-permute-start(f16[2,128,128]{2,1,0:T(8,128)(2,1)S(1)} %add_convert_fusion.3), channel_id=1, source_target_pairs={{0,24},{1,25},{2,26},{3,27},{4,6},{5,7},{6,4},{7,5},{8,16},{9,17},... | collective-permute-start | bytes 196616 | tf_op jit(solution)/shard_map/ppermute | solution.py:213
  39.9 1.1 %collective-permute-start.13 = (f16[2,128,128]{2,1,0:T(8,128)(2,1)S(1)}, f16[2,128,128]{2,1,0:T(8,128)(2,1)S(1)}, u32[]{:S(2)}, u32[]{:S(2)}) collective-permute-start(f16[2,128,128]{2,1,0:T(8,128)(2,1)S(1)} %add_convert_fusion.3), channel_id=1, source_target_pairs={{0,8},{1,9},{2,10},{3,11},{4,5},{5,4},{6,7},{7,6},{8,0},{9,1},{10,... | collective-permute-start | bytes 196616 | tf_op jit(solution)/shard_map/ppermute | solution.py:213
  40.9 0.8 %collective-permute-done.15 = f16[2,128,128]{2,1,0:T(8,128)(2,1)S(1)} collective-permute-done((f16[2,128,128]{2,1,0:T(8,128)(2,1)S(1)}, f16[2,128,128]{2,1,0:T(8,128)(2,1)S(1)}, u32[]{:S(2)}, u32[]{:S(2)}) %collective-permute-start.15) | collective-permute-done | bytes 65568 | tf_op jit(solution)/shard_map/ppermute | solution.py:213
  41.7 2.4 %collective-permute-done.14 = f16[2,128,128]{2,1,0:T(8,128)(2,1)S(1)} collective-permute-done((f16[2,128,128]{2,1,0:T(8,128)(2,1)S(1)}, f16[2,128,128]{2,1,0:T(8,128)(2,1)S(1)}, u32[]{:S(2)}, u32[]{:S(2)}) %collective-permute-start.14) | collective-permute-done | bytes 65568 | tf_op jit(solution)/shard_map/ppermute | solution.py:213
  44.2 2.0 %collective-permute-start.18 = (f16[2,128,128]{2,1,0:T(8,128)(2,1)S(1)}, f16[2,128,128]{2,1,0:T(8,128)(2,1)S(1)}, u32[]{:S(2)}, u32[]{:S(2)}) collective-permute-start(f16[2,128,128]{2,1,0:T(8,128)(2,1)S(1)} %add_convert_fusion.2), channel_id=1, source_target_pairs={{0,3},{1,2},{2,1},{3,0},{4,20},{5,21},{6,22},{7,23},{8,11},{9,10},... | collective-permute-start | bytes 196616 | tf_op jit(solution)/shard_map/ppermute | solution.py:213
  46.2 2.4 %collective-permute-start.16 = (f16[2,128,128]{2,1,0:T(8,128)(2,1)S(1)}, f16[2,128,128]{2,1,0:T(8,128)(2,1)S(1)}, u32[]{:S(2)}, u32[]{:S(2)}) collective-permute-start(f16[2,128,128]{2,1,0:T(8,128)(2,1)S(1)} %add_convert_fusion.2), channel_id=1, source_target_pairs={{0,1},{1,0},{2,3},{3,2},{4,12},{5,13},{6,14},{7,15},{8,9},{9,8},{1... | collective-permute-start | bytes 196616 | tf_op jit(solution)/shard_map/ppermute | solution.py:213
  48.6 1.7 %collective-permute-done.18 = f16[2,128,128]{2,1,0:T(8,128)(2,1)S(1)} collective-permute-done((f16[2,128,128]{2,1,0:T(8,128)(2,1)S(1)}, f16[2,128,128]{2,1,0:T(8,128)(2,1)S(1)}, u32[]{:S(2)}, u32[]{:S(2)}) %collective-permute-start.18) | collective-permute-done | bytes 65568 | tf_op jit(solution)/shard_map/ppermute | solution.py:213
  50.3 1.4 %collective-permute-done.17 = f16[2,128,128]{2,1,0:T(8,128)(2,1)S(1)} collective-permute-done((f16[2,128,128]{2,1,0:T(8,128)(2,1)S(1)}, f16[2,128,128]{2,1,0:T(8,128)(2,1)S(1)}, u32[]{:S(2)}, u32[]{:S(2)}) %collective-permute-start.17) | collective-permute-done | bytes 65568 | tf_op jit(solution)/shard_map/ppermute | solution.py:213
  51.9 1.3 %collective-permute-done.19.far = f32[2,128,128]{2,1,0:T(8,128)S(1)} collective-permute-done((f32[2,128,128]{2,1,0:T(8,128)S(1)}, f32[2,128,128]{2,1,0:T(8,128)S(1)}, u32[]{:S(2)}, u32[]{:S(2)}) %collective-permute-start.19) | collective-permute-done | bytes 131104 | tf_op jit(solution)/shard_map/ppermute | solution.py:200
  53.2 2.4 %shard_map.99 = (f32[4,128,128]{2,1,0:T(8,128)S(1)}, f32[8,128]{1,0:T(8,128)S(1)}, f32[2,128,128]{2,1,0:T(8,128)S(1)}, f32[2,128,128]{2,1,0:T(8,128)S(1)}) custom-call(f32[2,128,128]{2,1,0:T(8,128)S(1)} %add_add_fusion.1.own, f32[2,128,128]{2,1,0:T(8,128)S(1)} %collective-permute-done.19.far, f32[4,128,128]{2,1,0:T(8,128)S(1)} %get-tuple-element.38.vec_in, ...), custom_call_target="tpu_custom_call" | custom-call | tf_op jit(solution)/shard_map/pallas_call | solution.py:287
  55.8 1.1 %collective-permute-done.20 = f16[2,128,128]{2,1,0:T(8,128)(2,1)S(1)} collective-permute-done((f16[2,128,128]{2,1,0:T(8,128)(2,1)S(1)}, f16[2,128,128]{2,1,0:T(8,128)(2,1)S(1)}, u32[]{:S(2)}, u32[]{:S(2)}) %collective-permute-start.20) | collective-permute-done | bytes 65568 | tf_op jit(solution)/shard_map/ppermute | solution.py:200
  57.0 1.3 %collective-permute-start.23 = (f16[2,128,128]{2,1,0:T(8,128)(2,1)S(1)}, f16[2,128,128]{2,1,0:T(8,128)(2,1)S(1)}, u32[]{:S(2)}, u32[]{:S(2)}) collective-permute-start(f16[2,128,128]{2,1,0:T(8,128)(2,1)S(1)} %add_convert_fusion.1), channel_id=1, source_target_pairs={{0,16},{1,17},{2,18},{3,19},{4,7},{5,6},{6,5},{7,4},{8,24},{9,25},... | collective-permute-start | bytes 196616 | tf_op jit(solution)/shard_map/ppermute | solution.py:213
  58.3 1.3 %collective-permute-start.22 = (f16[2,128,128]{2,1,0:T(8,128)(2,1)S(1)}, f16[2,128,128]{2,1,0:T(8,128)(2,1)S(1)}, u32[]{:S(2)}, u32[]{:S(2)}) collective-permute-start(f16[2,128,128]{2,1,0:T(8,128)(2,1)S(1)} %add_convert_fusion.1), channel_id=1, source_target_pairs={{0,24},{1,25},{2,26},{3,27},{4,6},{5,7},{6,4},{7,5},{8,16},{9,17},... | collective-permute-start | bytes 196616 | tf_op jit(solution)/shard_map/ppermute | solution.py:213
  59.6 1.0 %collective-permute-start.21 = (f16[2,128,128]{2,1,0:T(8,128)(2,1)S(1)}, f16[2,128,128]{2,1,0:T(8,128)(2,1)S(1)}, u32[]{:S(2)}, u32[]{:S(2)}) collective-permute-start(f16[2,128,128]{2,1,0:T(8,128)(2,1)S(1)} %add_convert_fusion.1), channel_id=1, source_target_pairs={{0,8},{1,9},{2,10},{3,11},{4,5},{5,4},{6,7},{7,6},{8,0},{9,1},{10,... | collective-permute-start | bytes 196616 | tf_op jit(solution)/shard_map/ppermute | solution.py:213
  60.5 0.8 %collective-permute-done.23 = f16[2,128,128]{2,1,0:T(8,128)(2,1)S(1)} collective-permute-done((f16[2,128,128]{2,1,0:T(8,128)(2,1)S(1)}, f16[2,128,128]{2,1,0:T(8,128)(2,1)S(1)}, u32[]{:S(2)}, u32[]{:S(2)}) %collective-permute-start.23) | collective-permute-done | bytes 65568 | tf_op jit(solution)/shard_map/ppermute | solution.py:213
  61.3 2.2 %collective-permute-done.22 = f16[2,128,128]{2,1,0:T(8,128)(2,1)S(1)} collective-permute-done((f16[2,128,128]{2,1,0:T(8,128)(2,1)S(1)}, f16[2,128,128]{2,1,0:T(8,128)(2,1)S(1)}, u32[]{:S(2)}, u32[]{:S(2)}) %collective-permute-start.22) | collective-permute-done | bytes 65568 | tf_op jit(solution)/shard_map/ppermute | solution.py:213
  63.5 0.4 collective-permute-done.21
  63.9 2.1 %collective-permute-start.26 = (f16[2,128,128]{2,1,0:T(8,128)(2,1)S(1)}, f16[2,128,128]{2,1,0:T(8,128)(2,1)S(1)}, u32[]{:S(2)}, u32[]{:S(2)}) collective-permute-start(f16[2,128,128]{2,1,0:T(8,128)(2,1)S(1)} %add_convert_fusion), channel_id=1, source_target_pairs={{0,3},{1,2},{2,1},{3,0},{4,20},{5,21},{6,22},{7,23},{8,11},{9,10},... | collective-permute-start | bytes 196616 | tf_op jit(solution)/shard_map/ppermute | solution.py:213
  66.0 0.6 collective-permute-start.25
  66.6 1.8 %collective-permute-start.24 = (f16[2,128,128]{2,1,0:T(8,128)(2,1)S(1)}, f16[2,128,128]{2,1,0:T(8,128)(2,1)S(1)}, u32[]{:S(2)}, u32[]{:S(2)}) collective-permute-start(f16[2,128,128]{2,1,0:T(8,128)(2,1)S(1)} %add_convert_fusion), channel_id=1, source_target_pairs={{0,1},{1,0},{2,3},{3,2},{4,12},{5,13},{6,14},{7,15},{8,9},{9,8},{1... | collective-permute-start | bytes 196616 | tf_op jit(solution)/shard_map/ppermute | solution.py:213
  68.3 1.7 %collective-permute-done.26 = f16[2,128,128]{2,1,0:T(8,128)(2,1)S(1)} collective-permute-done((f16[2,128,128]{2,1,0:T(8,128)(2,1)S(1)}, f16[2,128,128]{2,1,0:T(8,128)(2,1)S(1)}, u32[]{:S(2)}, u32[]{:S(2)}) %collective-permute-start.26) | collective-permute-done | bytes 65568 | tf_op jit(solution)/shard_map/ppermute | solution.py:213
  70.0 1.5 %collective-permute-done.25 = f16[2,128,128]{2,1,0:T(8,128)(2,1)S(1)} collective-permute-done((f16[2,128,128]{2,1,0:T(8,128)(2,1)S(1)}, f16[2,128,128]{2,1,0:T(8,128)(2,1)S(1)}, u32[]{:S(2)}, u32[]{:S(2)}) %collective-permute-start.25) | collective-permute-done | bytes 65568 | tf_op jit(solution)/shard_map/ppermute | solution.py:213
  71.6 1.3 %collective-permute-done.27.far = f32[2,128,128]{2,1,0:T(8,128)S(1)} collective-permute-done((f32[2,128,128]{2,1,0:T(8,128)S(1)}, f32[2,128,128]{2,1,0:T(8,128)S(1)}, u32[]{:S(2)}, u32[]{:S(2)}) %collective-permute-start.27) | collective-permute-done | bytes 131104 | tf_op jit(solution)/shard_map/ppermute | solution.py:200
  73.0 1.0 %shard_map.100 = (f32[1,128,128]{2,1,0:T(8,128)}, f32[3]{0:T(128)}) custom-call(f32[2,128,128]{2,1,0:T(8,128)S(1)} %add_add_fusion.own, f32[2,128,128]{2,1,0:T(8,128)S(1)} %collective-permute-done.27.far, f32[4,128,128]{2,1,0:T(8,128)S(1)} %get-tuple-element.42.vec, f32[4,128,128]{2,1,0:T(8,128)S(1)} %get-tuple-element.34.inv, ...), custom_call_target="tpu_custom_call" | custom-call | tf_op jit(solution)/shard_map/pallas_call | solution.py:297
  (26 shorter events, 0.9 us)
Async XLA Ops:
  1.5 8.5 %collective-permute-start = (f32[2,128,128]{2,1,0:T(8,128)S(1)}, f32[2,128,128]{2,1,0:T(8,128)S(1)}, u32[]{:S(2)}, u32[]{:S(2)}) collective-permute-start(f32[2,128,128]{2,1,0:T(8,128)S(1)} %get-tuple-element.23.refs_0_), channel_id=1, source_target_pairs={{0,1},{1,0},{2,3},{3,2},{4,6},{5,7},{6,4},{7,5},{8,9},{9,8},{10,11... | collective-permute-start | bytes 393224 | tf_op jit(solution)/shard_map/ppermute | solution.py:213
  4.6 7.1 %collective-permute-start.1 = (f32[1,128,128]{2,1,0:T(8,128)S(1)}, f32[1,128,128]{2,1,0:T(8,128)S(1)}, u32[]{:S(2)}, u32[]{:S(2)}) collective-permute-start(f32[1,128,128]{2,1,0:T(8,128)S(1)} %get-tuple-element.26), channel_id=1, source_target_pairs={{0,3},{1,2},{2,1},{3,0},{4,7},{5,6},{6,5},{7,4},{8,11},{9,10},{10,... | collective-permute-start | bytes 196616 | tf_op jit(solution)/shard_map/ppermute | solution.py:200
  10.0 3.0 %collective-permute-start.2 = (f32[2,128,128]{2,1,0:T(8,128)S(1)}, f32[2,128,128]{2,1,0:T(8,128)S(1)}, u32[]{:S(2)}, u32[]{:S(2)}) collective-permute-start(f32[2,128,128]{2,1,0:T(8,128)S(1)} %collective-permute-done.refs_1_), channel_id=1, source_target_pairs={{0,4},{4,0},{8,12},{12,8},{16,20},{20,16},{24,28},{28,24},{1,5},{5... | collective-permute-start | bytes 393224 | tf_op jit(solution)/shard_map/ppermute | solution.py:200
  11.7 1.3 %collective-permute-start.3 = (f32[1,128,128]{2,1,0:T(8,128)S(1)}, f32[1,128,128]{2,1,0:T(8,128)S(1)}, u32[]{:S(2)}, u32[]{:S(2)}) collective-permute-start(f32[1,128,128]{2,1,0:T(8,128)S(1)} %collective-permute-done.1.refs_2_), channel_id=1, source_target_pairs={{0,4},{4,0},{8,12},{12,8},{16,20},{20,16},{24,28},{28,24},{1,5},{5... | collective-permute-start | bytes 196616 | tf_op jit(solution)/shard_map/ppermute | solution.py:200
  15.1 1.3 %collective-permute-start.4 = (f16[2,128,128]{2,1,0:T(8,128)(2,1)S(1)}, f16[2,128,128]{2,1,0:T(8,128)(2,1)S(1)}, u32[]{:S(2)}, u32[]{:S(2)}) collective-permute-start(f16[2,128,128]{2,1,0:T(8,128)(2,1)S(1)} %convert_element_type.108), channel_id=1, source_target_pairs={{0,4},{4,0},{8,12},{12,8},{16,20},{20,16},{24,28},{28,24},{1,5},{5... | collective-permute-start | bytes 196616 | tf_op jit(solution)/shard_map/ppermute | solution.py:200
  16.5 4.3 %collective-permute-start.7 = (f16[2,128,128]{2,1,0:T(8,128)(2,1)S(1)}, f16[2,128,128]{2,1,0:T(8,128)(2,1)S(1)}, u32[]{:S(2)}, u32[]{:S(2)}) collective-permute-start(f16[2,128,128]{2,1,0:T(8,128)(2,1)S(1)} %add_convert_fusion.5), channel_id=1, source_target_pairs={{0,16},{1,17},{2,18},{3,19},{4,7},{5,6},{6,5},{7,4},{8,24},{9,25},... | collective-permute-start | bytes 196616 | tf_op jit(solution)/shard_map/ppermute | solution.py:213
  18.1 5.2 %collective-permute-start.6 = (f16[2,128,128]{2,1,0:T(8,128)(2,1)S(1)}, f16[2,128,128]{2,1,0:T(8,128)(2,1)S(1)}, u32[]{:S(2)}, u32[]{:S(2)}) collective-permute-start(f16[2,128,128]{2,1,0:T(8,128)(2,1)S(1)} %add_convert_fusion.5), channel_id=1, source_target_pairs={{0,24},{1,25},{2,26},{3,27},{4,6},{5,7},{6,4},{7,5},{8,16},{9,17},... | collective-permute-start | bytes 196616 | tf_op jit(solution)/shard_map/ppermute | solution.py:213
  19.5 4.3 %collective-permute-start.5 = (f16[2,128,128]{2,1,0:T(8,128)(2,1)S(1)}, f16[2,128,128]{2,1,0:T(8,128)(2,1)S(1)}, u32[]{:S(2)}, u32[]{:S(2)}) collective-permute-start(f16[2,128,128]{2,1,0:T(8,128)(2,1)S(1)} %add_convert_fusion.5), channel_id=1, source_target_pairs={{0,8},{1,9},{2,10},{3,11},{4,5},{5,4},{6,7},{7,6},{8,0},{9,1},{10,... | collective-permute-start | bytes 196616 | tf_op jit(solution)/shard_map/ppermute | solution.py:213
  23.8 6.1 %collective-permute-start.10 = (f16[2,128,128]{2,1,0:T(8,128)(2,1)S(1)}, f16[2,128,128]{2,1,0:T(8,128)(2,1)S(1)}, u32[]{:S(2)}, u32[]{:S(2)}) collective-permute-start(f16[2,128,128]{2,1,0:T(8,128)(2,1)S(1)} %add_convert_fusion.4), channel_id=1, source_target_pairs={{0,3},{1,2},{2,1},{3,0},{4,20},{5,21},{6,22},{7,23},{8,11},{9,10},... | collective-permute-start | bytes 196616 | tf_op jit(solution)/shard_map/ppermute | solution.py:213
  26.6 5.6 %collective-permute-start.9 = (f16[2,128,128]{2,1,0:T(8,128)(2,1)S(1)}, f16[2,128,128]{2,1,0:T(8,128)(2,1)S(1)}, u32[]{:S(2)}, u32[]{:S(2)}) collective-permute-start(f16[2,128,128]{2,1,0:T(8,128)(2,1)S(1)} %add_convert_fusion.4), channel_id=1, source_target_pairs={{0,2},{1,3},{2,0},{3,1},{4,28},{5,29},{6,30},{7,31},{8,10},{9,11},... | collective-permute-start | bytes 196616 | tf_op jit(solution)/shard_map/ppermute | solution.py:213
  26.6 5.6 %collective-permute-start.8 = (f16[2,128,128]{2,1,0:T(8,128)(2,1)S(1)}, f16[2,128,128]{2,1,0:T(8,128)(2,1)S(1)}, u32[]{:S(2)}, u32[]{:S(2)}) collective-permute-start(f16[2,128,128]{2,1,0:T(8,128)(2,1)S(1)} %add_convert_fusion.4), channel_id=1, source_target_pairs={{0,1},{1,0},{2,3},{3,2},{4,12},{5,13},{6,14},{7,15},{8,9},{9,8},{1... | collective-permute-start | bytes 196616 | tf_op jit(solution)/shard_map/ppermute | solution.py:213
  32.2 1.4 %collective-permute-start.11 = (f32[2,128,128]{2,1,0:T(8,128)S(1)}, f32[2,128,128]{2,1,0:T(8,128)S(1)}, u32[]{:S(2)}, u32[]{:S(2)}) collective-permute-start(f32[2,128,128]{2,1,0:T(8,128)S(1)} %add_add_fusion.2.own), channel_id=1, source_target_pairs={{0,4},{4,0},{8,12},{12,8},{16,20},{20,16},{24,28},{28,24},{1,5},{5... | collective-permute-start | bytes 393224 | tf_op jit(solution)/shard_map/ppermute | solution.py:200
  36.0 1.3 %collective-permute-start.12 = (f16[2,128,128]{2,1,0:T(8,128)(2,1)S(1)}, f16[2,128,128]{2,1,0:T(8,128)(2,1)S(1)}, u32[]{:S(2)}, u32[]{:S(2)}) collective-permute-start(f16[2,128,128]{2,1,0:T(8,128)(2,1)S(1)} %convert_element_type.120), channel_id=1, source_target_pairs={{0,4},{4,0},{8,12},{12,8},{16,20},{20,16},{24,28},{28,24},{1,5},{5... | collective-permute-start | bytes 196616 | tf_op jit(solution)/shard_map/ppermute | solution.py:200
  37.4 4.3 %collective-permute-start.15 = (f16[2,128,128]{2,1,0:T(8,128)(2,1)S(1)}, f16[2,128,128]{2,1,0:T(8,128)(2,1)S(1)}, u32[]{:S(2)}, u32[]{:S(2)}) collective-permute-start(f16[2,128,128]{2,1,0:T(8,128)(2,1)S(1)} %add_convert_fusion.3), channel_id=1, source_target_pairs={{0,16},{1,17},{2,18},{3,19},{4,7},{5,6},{6,5},{7,4},{8,24},{9,25},... | collective-permute-start | bytes 196616 | tf_op jit(solution)/shard_map/ppermute | solution.py:213
  39.0 5.2 %collective-permute-start.14 = (f16[2,128,128]{2,1,0:T(8,128)(2,1)S(1)}, f16[2,128,128]{2,1,0:T(8,128)(2,1)S(1)}, u32[]{:S(2)}, u32[]{:S(2)}) collective-permute-start(f16[2,128,128]{2,1,0:T(8,128)(2,1)S(1)} %add_convert_fusion.3), channel_id=1, source_target_pairs={{0,24},{1,25},{2,26},{3,27},{4,6},{5,7},{6,4},{7,5},{8,16},{9,17},... | collective-permute-start | bytes 196616 | tf_op jit(solution)/shard_map/ppermute | solution.py:213
  39.9 4.3 %collective-permute-start.13 = (f16[2,128,128]{2,1,0:T(8,128)(2,1)S(1)}, f16[2,128,128]{2,1,0:T(8,128)(2,1)S(1)}, u32[]{:S(2)}, u32[]{:S(2)}) collective-permute-start(f16[2,128,128]{2,1,0:T(8,128)(2,1)S(1)} %add_convert_fusion.3), channel_id=1, source_target_pairs={{0,8},{1,9},{2,10},{3,11},{4,5},{5,4},{6,7},{7,6},{8,0},{9,1},{10,... | collective-permute-start | bytes 196616 | tf_op jit(solution)/shard_map/ppermute | solution.py:213
  44.2 6.1 %collective-permute-start.18 = (f16[2,128,128]{2,1,0:T(8,128)(2,1)S(1)}, f16[2,128,128]{2,1,0:T(8,128)(2,1)S(1)}, u32[]{:S(2)}, u32[]{:S(2)}) collective-permute-start(f16[2,128,128]{2,1,0:T(8,128)(2,1)S(1)} %add_convert_fusion.2), channel_id=1, source_target_pairs={{0,3},{1,2},{2,1},{3,0},{4,20},{5,21},{6,22},{7,23},{8,11},{9,10},... | collective-permute-start | bytes 196616 | tf_op jit(solution)/shard_map/ppermute | solution.py:213
  46.2 5.5 %collective-permute-start.17 = (f16[2,128,128]{2,1,0:T(8,128)(2,1)S(1)}, f16[2,128,128]{2,1,0:T(8,128)(2,1)S(1)}, u32[]{:S(2)}, u32[]{:S(2)}) collective-permute-start(f16[2,128,128]{2,1,0:T(8,128)(2,1)S(1)} %add_convert_fusion.2), channel_id=1, source_target_pairs={{0,2},{1,3},{2,0},{3,1},{4,28},{5,29},{6,30},{7,31},{8,10},{9,11},... | collective-permute-start | bytes 196616 | tf_op jit(solution)/shard_map/ppermute | solution.py:213
  46.2 5.5 %collective-permute-start.16 = (f16[2,128,128]{2,1,0:T(8,128)(2,1)S(1)}, f16[2,128,128]{2,1,0:T(8,128)(2,1)S(1)}, u32[]{:S(2)}, u32[]{:S(2)}) collective-permute-start(f16[2,128,128]{2,1,0:T(8,128)(2,1)S(1)} %add_convert_fusion.2), channel_id=1, source_target_pairs={{0,1},{1,0},{2,3},{3,2},{4,12},{5,13},{6,14},{7,15},{8,9},{9,8},{1... | collective-permute-start | bytes 196616 | tf_op jit(solution)/shard_map/ppermute | solution.py:213
  51.8 1.4 %collective-permute-start.19 = (f32[2,128,128]{2,1,0:T(8,128)S(1)}, f32[2,128,128]{2,1,0:T(8,128)S(1)}, u32[]{:S(2)}, u32[]{:S(2)}) collective-permute-start(f32[2,128,128]{2,1,0:T(8,128)S(1)} %add_add_fusion.1.own), channel_id=1, source_target_pairs={{0,4},{4,0},{8,12},{12,8},{16,20},{20,16},{24,28},{28,24},{1,5},{5... | collective-permute-start | bytes 393224 | tf_op jit(solution)/shard_map/ppermute | solution.py:200
  55.6 1.3 %collective-permute-start.20 = (f16[2,128,128]{2,1,0:T(8,128)(2,1)S(1)}, f16[2,128,128]{2,1,0:T(8,128)(2,1)S(1)}, u32[]{:S(2)}, u32[]{:S(2)}) collective-permute-start(f16[2,128,128]{2,1,0:T(8,128)(2,1)S(1)} %convert_element_type.132), channel_id=1, source_target_pairs={{0,4},{4,0},{8,12},{12,8},{16,20},{20,16},{24,28},{28,24},{1,5},{5... | collective-permute-start | bytes 196616 | tf_op jit(solution)/shard_map/ppermute | solution.py:200
  57.0 4.3 %collective-permute-start.23 = (f16[2,128,128]{2,1,0:T(8,128)(2,1)S(1)}, f16[2,128,128]{2,1,0:T(8,128)(2,1)S(1)}, u32[]{:S(2)}, u32[]{:S(2)}) collective-permute-start(f16[2,128,128]{2,1,0:T(8,128)(2,1)S(1)} %add_convert_fusion.1), channel_id=1, source_target_pairs={{0,16},{1,17},{2,18},{3,19},{4,7},{5,6},{6,5},{7,4},{8,24},{9,25},... | collective-permute-start | bytes 196616 | tf_op jit(solution)/shard_map/ppermute | solution.py:213
  58.3 5.2 %collective-permute-start.22 = (f16[2,128,128]{2,1,0:T(8,128)(2,1)S(1)}, f16[2,128,128]{2,1,0:T(8,128)(2,1)S(1)}, u32[]{:S(2)}, u32[]{:S(2)}) collective-permute-start(f16[2,128,128]{2,1,0:T(8,128)(2,1)S(1)} %add_convert_fusion.1), channel_id=1, source_target_pairs={{0,24},{1,25},{2,26},{3,27},{4,6},{5,7},{6,4},{7,5},{8,16},{9,17},... | collective-permute-start | bytes 196616 | tf_op jit(solution)/shard_map/ppermute | solution.py:213
  59.6 4.3 %collective-permute-start.21 = (f16[2,128,128]{2,1,0:T(8,128)(2,1)S(1)}, f16[2,128,128]{2,1,0:T(8,128)(2,1)S(1)}, u32[]{:S(2)}, u32[]{:S(2)}) collective-permute-start(f16[2,128,128]{2,1,0:T(8,128)(2,1)S(1)} %add_convert_fusion.1), channel_id=1, source_target_pairs={{0,8},{1,9},{2,10},{3,11},{4,5},{5,4},{6,7},{7,6},{8,0},{9,1},{10,... | collective-permute-start | bytes 196616 | tf_op jit(solution)/shard_map/ppermute | solution.py:213
  63.9 6.1 %collective-permute-start.26 = (f16[2,128,128]{2,1,0:T(8,128)(2,1)S(1)}, f16[2,128,128]{2,1,0:T(8,128)(2,1)S(1)}, u32[]{:S(2)}, u32[]{:S(2)}) collective-permute-start(f16[2,128,128]{2,1,0:T(8,128)(2,1)S(1)} %add_convert_fusion), channel_id=1, source_target_pairs={{0,3},{1,2},{2,1},{3,0},{4,20},{5,21},{6,22},{7,23},{8,11},{9,10},... | collective-permute-start | bytes 196616 | tf_op jit(solution)/shard_map/ppermute | solution.py:213
  66.0 5.6 %collective-permute-start.25 = (f16[2,128,128]{2,1,0:T(8,128)(2,1)S(1)}, f16[2,128,128]{2,1,0:T(8,128)(2,1)S(1)}, u32[]{:S(2)}, u32[]{:S(2)}) collective-permute-start(f16[2,128,128]{2,1,0:T(8,128)(2,1)S(1)} %add_convert_fusion), channel_id=1, source_target_pairs={{0,2},{1,3},{2,0},{3,1},{4,28},{5,29},{6,30},{7,31},{8,10},{9,11},... | collective-permute-start | bytes 196616 | tf_op jit(solution)/shard_map/ppermute | solution.py:213
  66.6 5.0 %collective-permute-start.24 = (f16[2,128,128]{2,1,0:T(8,128)(2,1)S(1)}, f16[2,128,128]{2,1,0:T(8,128)(2,1)S(1)}, u32[]{:S(2)}, u32[]{:S(2)}) collective-permute-start(f16[2,128,128]{2,1,0:T(8,128)(2,1)S(1)} %add_convert_fusion), channel_id=1, source_target_pairs={{0,1},{1,0},{2,3},{3,2},{4,12},{5,13},{6,14},{7,15},{8,9},{9,8},{1... | collective-permute-start | bytes 196616 | tf_op jit(solution)/shard_map/ppermute | solution.py:213
  71.6 1.4 %collective-permute-start.27 = (f32[2,128,128]{2,1,0:T(8,128)S(1)}, f32[2,128,128]{2,1,0:T(8,128)S(1)}, u32[]{:S(2)}, u32[]{:S(2)}) collective-permute-start(f32[2,128,128]{2,1,0:T(8,128)S(1)} %add_add_fusion.own), channel_id=1, source_target_pairs={{0,4},{4,0},{8,12},{12,8},{16,20},{20,16},{24,28},{28,24},{1,5},{5... | collective-permute-start | bytes 393224 | tf_op jit(solution)/shard_map/ppermute | solution.py:200
